TPU v7x, 128 devices: a whole 4x4x4 slice. The times are simulated.
128 devices in a mesh: gx: 16 (over y_lo, x, core), gy: 8 (over y_hi, z).
Axes of the slice: x: 4, y: 4 (y_hi: 2, y_lo: 2; y = y_hi * 2 + y_lo), z: 4, core: 2. Of those that a mesh axis runs over, the one named last changes fastest.
Arguments:
- retained_source: bfloat16 [256, 128, 24, 128], P('gx', 'gy'), may hold values from -6 to 6
- incoming_adjoint: bfloat16 [256, 128, 24, 128], P('gx', 'gy'), may hold values from -6 to 6
- rescale_multiplier: float32 [128], replicated, may hold values from 0.25 to 1.75
- triple_projection_matrix: bfloat16 [128, 384], replicated, may hold values from -0.5 to 0.5
- w_proj: bfloat16 [128, 128], replicated, may hold values from -0.5 to 0.5
- pos_bias: float32 [4, 512, 512], replicated, may hold values from -8 to 320
Outputs:
- grad_input: bfloat16 [256, 128, 24, 128], P('gx', 'gy')
- grad_bias: float32 [4, 512, 512], replicated
- grad_proj: float32 [128, 128], replicated
- grad_qkv: float32 [128, 384], replicated
- multiplier_derivative: float32 [128], replicated
All inputs are finite; a program needn't handle non-finite values.
Results may differ from a plain program's by a relative error of at most 0.0095.
Values may be sent and summed in bfloat16 or wider, within the bound.
No kernel may reach another device: no remote copies, remote signals or barrier semaphores. Data moves between devices by JAX's collectives and lax.ppermute only.
A program may use at most 128 MiB of HBM per device.

v0:
```python
import jax
import jax.numpy as jnp
from jax import lax
from jax.sharding import PartitionSpec as P

HEADS = 4
WIN = 8
SHIFT = 4


def from_behind(shard, axis, by):
    peers = lax.axis_size(axis)
    return lax.ppermute(shard, axis, [(i, (i + by) % peers) for i in range(peers)])


def moment_summary(values):
    floats = values.astype(jnp.float32)
    center = floats - jnp.mean(floats, axis=-1, keepdims=True)
    variance = jnp.mean(center * center, axis=-1, keepdims=True)
    reciprocal_spread = lax.rsqrt(variance + 1e-05)
    return (center * reciprocal_spread, reciprocal_spread)


def regions(offset, count, length):
    places = offset + jnp.arange(count, dtype=jnp.int32)
    return (places >= length - WIN).astype(jnp.int32) + (places >= length - SHIFT).astype(jnp.int32)


def to_windows(grid):
    sx, sy, sz, feat = grid.shape
    shaped = grid.reshape(sx // WIN, WIN, sy // WIN, WIN, sz // WIN, WIN, feat)
    return shaped.transpose(0, 2, 4, 1, 3, 5, 6).reshape(-1, WIN * WIN * WIN, feat)


def from_windows(wins, sx, sy, sz):
    feat = wins.shape[-1]
    shaped = wins.reshape(sx // WIN, sy // WIN, sz // WIN, WIN, WIN, WIN, feat)
    return shaped.transpose(0, 3, 1, 4, 2, 5, 6).reshape(sx, sy, sz, feat)


def roll_forward(grid):
    from_next = from_behind(grid[:SHIFT], "gx", -1)
    grid = jnp.concatenate([grid[SHIFT:], from_next], axis=0)
    from_next = from_behind(grid[:, :SHIFT], "gy", -1)
    grid = jnp.concatenate([grid[:, SHIFT:], from_next], axis=1)
    return jnp.roll(grid, -SHIFT, axis=2)


def roll_back(grid):
    grid = jnp.roll(grid, SHIFT, axis=2)
    rows_x = grid.shape[0]
    from_prev = from_behind(grid[rows_x - SHIFT :], "gx", 1)
    grid = jnp.concatenate([from_prev, grid[: rows_x - SHIFT]], axis=0)
    rows_y = grid.shape[1]
    from_prev = from_behind(grid[:, rows_y - SHIFT :], "gy", 1)
    return jnp.concatenate([from_prev, grid[:, : rows_y - SHIFT]], axis=1)


def window_grads(qkv, result_adjoint, label, bias, w_proj):
    tokens, three = qkv.shape
    channel_extent = three // 3
    head_dim = channel_extent // HEADS
    scale = head_dim ** (-0.5)
    query = qkv[:, :channel_extent].reshape(tokens, HEADS, head_dim)
    keys = qkv[:, channel_extent : 2 * channel_extent].reshape(tokens, HEADS, head_dim)
    values = qkv[:, 2 * channel_extent :].reshape(tokens, HEADS, head_dim)
    scores = (
        jnp.einsum("qhd,khd->hqk", query, keys, preferred_element_type=jnp.float32) * scale + bias
    )
    allowed = label[:, None] == label[None, :]
    scores = jnp.where(allowed[None], scores, -1e30)
    top = jnp.max(scores, axis=-1, keepdims=True)
    expo = jnp.exp(scores - top)
    prob = expo / jnp.sum(expo, axis=-1, keepdims=True)
    prob_b = prob.astype(jnp.bfloat16)
    attended = (
        jnp.einsum("hqk,khd->qhd", prob_b, values, preferred_element_type=jnp.float32)
        .reshape(tokens, channel_extent)
        .astype(jnp.bfloat16)
    )
    grad_att = lax.dot_general(
        result_adjoint, w_proj, (((1,), (1,)), ((), ())), preferred_element_type=jnp.float32
    ).astype(jnp.bfloat16)
    proj_term = lax.dot_general(
        attended, result_adjoint, (((0,), (0,)), ((), ())), preferred_element_type=jnp.float32
    )
    grad_heads = grad_att.reshape(tokens, HEADS, head_dim)
    dprob = jnp.einsum("qhd,khd->hqk", grad_heads, values, preferred_element_type=jnp.float32)
    delta = jnp.sum(dprob * prob, axis=-1, keepdims=True)
    dscore = prob * (dprob - delta)
    ds_b = dscore.astype(jnp.bfloat16)
    dquery = jnp.einsum("hqk,khd->qhd", ds_b, keys, preferred_element_type=jnp.float32) * scale
    dkeys = jnp.einsum("hqk,qhd->khd", ds_b, query, preferred_element_type=jnp.float32) * scale
    dvalues = jnp.einsum("hqk,qhd->khd", prob_b, grad_heads, preferred_element_type=jnp.float32)
    projection_triple_adjoint = jnp.concatenate(
        [
            dquery.reshape(tokens, channel_extent),
            dkeys.reshape(tokens, channel_extent),
            dvalues.reshape(tokens, channel_extent),
        ],
        axis=1,
    ).astype(jnp.bfloat16)
    return (projection_triple_adjoint, dscore, proj_term)


def source_contributions(
    standardized_tokens,
    whitened_entries,
    reciprocal_spread,
    projection_triple_adjoint,
    result_adjoint,
    rescale_multiplier,
    triple_projection_matrix,
):
    channel_extent = standardized_tokens.shape[-1]
    flat_normed = standardized_tokens.reshape(-1, channel_extent)
    flat_dqkv = projection_triple_adjoint.reshape(-1, 3 * channel_extent)
    qkv_term = lax.dot_general(
        flat_normed, flat_dqkv, (((0,), (0,)), ((), ())), preferred_element_type=jnp.float32
    )
    standardized_adjoint = lax.dot_general(
        flat_dqkv,
        triple_projection_matrix,
        (((1,), (1,)), ((), ())),
        preferred_element_type=jnp.float32,
    ).reshape(standardized_tokens.shape)
    multiplier_contribution = jnp.sum(
        (standardized_adjoint * whitened_entries).reshape(-1, channel_extent), axis=0
    )
    multiplied_adjoint = standardized_adjoint * rescale_multiplier
    residual_path = reciprocal_spread * (
        multiplied_adjoint
        - jnp.mean(multiplied_adjoint, axis=-1, keepdims=True)
        - whitened_entries * jnp.mean(multiplied_adjoint * whitened_entries, axis=-1, keepdims=True)
    )
    grad_in = (result_adjoint.astype(jnp.float32) + residual_path).astype(jnp.bfloat16)
    return (grad_in, qkv_term, multiplier_contribution)


def body(
    retained_source,
    incoming_adjoint,
    rescale_multiplier,
    triple_projection_matrix,
    w_proj,
    pos_bias,
):
    rows_x, rows_y, depth, channel_extent = retained_source.shape
    whitened_entries, reciprocal_spread = moment_summary(retained_source)
    standardized_tokens = (whitened_entries * rescale_multiplier).astype(jnp.bfloat16)
    qkv_own = (
        jnp.dot(
            standardized_tokens.reshape(-1, channel_extent),
            triple_projection_matrix,
            preferred_element_type=jnp.float32,
        )
        .astype(jnp.bfloat16)
        .reshape(rows_x, rows_y, depth, 3 * channel_extent)
    )
    carried = jnp.concatenate([qkv_own, incoming_adjoint], axis=3)
    rolled = roll_forward(carried)
    rolled_qkv = rolled[..., : 3 * channel_extent]
    rolled_grad = rolled[..., 3 * channel_extent :]
    label_x = regions(lax.axis_index("gx") * rows_x, rows_x, rows_x * lax.axis_size("gx"))
    label_y = regions(lax.axis_index("gy") * rows_y, rows_y, rows_y * lax.axis_size("gy"))
    label_z = regions(0, depth, depth)
    label = label_x[:, None, None] * 9 + label_y[None, :, None] * 3 + label_z[None, None, :]
    label_w = to_windows(label[..., None])[..., 0]

    def step(carry, items):
        qkv_w, grad_w, lab_w = items
        projection_triple_adjoint, dscore, proj_term = window_grads(
            qkv_w, grad_w, lab_w, pos_bias, w_proj
        )
        return ((carry[0] + dscore, carry[1] + proj_term), projection_triple_adjoint)

    window_tokens = WIN * WIN * WIN
    init = (
        jnp.zeros((HEADS, window_tokens, window_tokens), jnp.float32),
        jnp.zeros((channel_extent, channel_extent), jnp.float32),
    )
    (bias_term, proj_term), dqkv_w = lax.scan(
        step, init, (to_windows(rolled_qkv), to_windows(rolled_grad), label_w)
    )
    dqkv_rolled = from_windows(dqkv_w, rows_x, rows_y, depth)
    triple_adjoint_mine = roll_back(dqkv_rolled)
    grad_input, qkv_term, multiplier_contribution = source_contributions(
        standardized_tokens,
        whitened_entries,
        reciprocal_spread,
        triple_adjoint_mine,
        incoming_adjoint,
        rescale_multiplier,
        triple_projection_matrix,
    )
    grad_bias, grad_proj, grad_qkv, multiplier_derivative = lax.psum(
        (bias_term, proj_term, qkv_term, multiplier_contribution), ("gx", "gy")
    )
    return (grad_input, grad_bias, grad_proj, grad_qkv, multiplier_derivative)


def solution(mesh):
    placed = (P("gx", "gy", None, None), P("gx", "gy", None, None), P(), P(), P(), P())
    return jax.shard_map(
        body,
        mesh=mesh,
        in_specs=placed,
        out_specs=(P("gx", "gy", None, None), P(), P(), P(), P()),
        check_vma=False,
    )
```

profile of v0, /device:TPU:1, one launch (start us, length us, event | category | flops | bytes accessed | tf_op | source)
XLA Modules:
  0.0 642.5 jit_solution(4328890476533839881)
XLA Ops:
  19.6 18.7 %collective-permute-done = bf16[4,16,24,512]{3,2,1,0:T(8,128)(2,1)S(1)} collective-permute-done((bf16[4,16,24,512]{3,2,1,0:T(8,128)(2,1)S(1)}, bf16[4,16,24,512]{3,2,1,0:T(8,128)(2,1)S(1)}, u32[]{:S(2)}, u32[]{:S(2)}) %collective-permute-start) | collective-permute-done | bytes 1572896 | tf_op jit(solution)/shard_map/ppermute | solution.py:13
  39.6 6.4 collective-permute-start.1
  48.2 5.3 copy.37
  55.7 22.6 %collective-permute-done.1 = bf16[16,4,24,512]{3,2,1,0:T(8,128)(2,1)S(1)} collective-permute-done((bf16[16,4,24,512]{3,2,1,0:T(8,128)(2,1)}, bf16[16,4,24,512]{3,2,1,0:T(8,128)(2,1)S(1)}, u32[]{:S(2)}, u32[]{:S(2)}) %collective-permute-start.1) | collective-permute-done | bytes 1572896 | tf_op jit(solution)/shard_map/ppermute | solution.py:13
  86.6 330.1 %while.15 = (s32[]{:T(128)}, f32[4,512,512]{1,2,0:T(8,128)}, f32[128,128]{1,0:T(8,128)S(1)}, bf16[12,512,384]{2,1,0:T(8,128)(2,1)}, s32[12,512]{1,0:T(8,128)S(1)...) while((s32[]{:T(128)}, f32[4,512,512]{1,2,0:T(8,128)}, ...), condition=%wide.region_6.7_spmd.clone, body=%wide.region_2.6_spmd.clone.sunk | while | flops 459116032 | bytes 131299584 | solution.py:182
  94.7 4.5 convolution_convert_fusion.9
  99.3 4.6 convolution_convert_fusion.8
  115.9 3.2 add_select_fusion.2
  122.3 4.5 convolution_convert_fusion.9
  126.8 4.6 convolution_convert_fusion.8
  143.4 3.2 add_select_fusion.2
  149.8 4.5 convolution_convert_fusion.9
  154.3 4.6 convolution_convert_fusion.8
  177.3 4.5 convolution_convert_fusion.9
  181.8 4.6 convolution_convert_fusion.8
  198.4 3.2 add_select_fusion.2
  204.8 4.5 convolution_convert_fusion.9
  209.3 4.6 convolution_convert_fusion.8
  225.9 3.2 add_select_fusion.2
  232.3 4.5 convolution_convert_fusion.9
  236.8 4.6 convolution_convert_fusion.8
  253.4 3.2 add_select_fusion.2
  259.8 4.5 convolution_convert_fusion.9
  264.3 4.6 convolution_convert_fusion.8
  280.9 3.2 add_select_fusion.2
  287.3 4.5 convolution_convert_fusion.9
  291.8 4.6 convolution_convert_fusion.8
  308.3 3.2 add_select_fusion.2
  314.7 4.5 convolution_convert_fusion.9
  319.3 4.6 convolution_convert_fusion.8
  335.8 3.2 add_select_fusion.2
  342.2 4.5 convolution_convert_fusion.9
  346.8 4.6 convolution_convert_fusion.8
  363.4 3.2 add_select_fusion.2
  369.8 4.5 convolution_convert_fusion.9
  374.3 4.6 convolution_convert_fusion.8
  390.9 3.2 add_select_fusion.2
  397.3 4.5 convolution_convert_fusion.9
  401.8 4.6 convolution_convert_fusion.8
  423.0 13.1 %collective-permute-done.2 = bf16[4,16,24,384]{3,2,1,0:T(8,128)(2,1)S(1)} collective-permute-done((bf16[4,16,24,384]{3,2,1,0:T(8,128)(2,1)S(1)}, bf16[4,16,24,384]{3,2,1,0:T(8,128)(2,1)S(1)}, u32[]{:S(2)}, u32[]{:S(2)}) %collective-permute-start.2) | collective-permute-done | bytes 1179680 | tf_op jit(solution)/shard_map/ppermute | solution.py:13
  437.6 5.5 copy.40
  443.1 24.3 %collective-permute-done.3 = bf16[16,4,24,384]{3,2,1,0:T(8,128)(2,1)} collective-permute-done((bf16[16,4,24,384]{3,2,1,0:T(8,128)(2,1)}, bf16[16,4,24,384]{3,2,1,0:T(8,128)(2,1)}, u32[]{:S(2)}, u32[]{:S(2)}) %collective-permute-start.3) | collective-permute-done | bytes 1179680 | tf_op jit(solution)/shard_map/ppermute | solution.py:13
  467.4 5.6 convolution_bitcast_fusion
  474.4 8.6 %fusion.28 = (f32[128]{0:T(128)S(1)}, f32[16,16,24]{2,1,0:T(8,128)}, f32[16,16,24]{2,1,0:T(8,128)}, f32[16,16,24,128]{3,2,1,0:T(8,128)}) fusion(bf16[16,16,24,128]{3,2,1,0:T(8,128)(2,1)S(1)} %copy-done.8, f32[16,16,24]{2,1,0:T(8,128)S(1)} %copy-done.18, f32[16,16,24]{2,1,0:T(8,128)S(1)} %copy-done.16, f32[128]{0:T(128)S(1)} %copy-done.23, ...), kind=kOutput, calls=%fused_computation.56 | convolution fusion | flops 629919616 | bytes 11994112 | tf_op jit(solution)/shard_map/dot_general | solution.py:121
  483.0 68.3 %psum.31 = f32[128]{0:T(128)} all-reduce(f32[128]{0:T(128)S(1)} %get-tuple-element.114), channel_id=1, replica_groups=mesh['gx'=16,'gy'=8] {'gx','gy'}, use_global_device_ids=true, to_apply=%region_13.14 | all-reduce | flops 128 | bytes 1024 | tf_op jit(solution)/shard_map/psum | solution.py:196
  553.1 7.5 %fusion.27 = bf16[16,16,24,128]{3,2,1,0:T(8,128)(2,1)} fusion(bf16[16,16,24,128]{3,2,1,0:T(8,128)(2,1)S(1)} %copy-done.8, bf16[16,16,24,128]{3,2,1,0:T(8,128)(2,1)S(1)} %copy-done.10, f32[16,16,24,128]{3,2,1,0:T(8,128)} %get-tuple-element.147, f32[16,16,24]{2,1,0:T(8,128)S(1)} %broadcast_multiply_fusion, f32[16,16,24]{2,1,0:T(8,128)S(1)} %broadcast_multiply_fusion.1, ...), kind=kLoop, calls=%fused_computation.55 | loop fusion | flops 8650752 | bytes 7963136 | tf_op jit(solution)/shard_map/convert_element_type | solution.py:136
  560.6 69.0 %all-reduce.3.cloned.1.call-done = (f32[4,512,512]{2,1,0:T(8,128)}, f32[128,128]{1,0:T(8,128)}, f32[128,384]{1,0:T(8,128)}) async-done(((f32[4,512,512]{2,1,0:T(8,128)}, f32[128,128]{1,0:T(8,128)}, f32[128,384]{1,0:T(8,128)}), (f32[4,512,512]{2,1,0:T(8,128)}, f32[128,128]{1,0:T(8,128)}, f32[128,384]{1,0:T(8,128)})) %all-reduce.3.cloned.1.call-update) | async-done | bytes 4456464 | tf_op jit(solution)/shard_map/psum | solution.py:196
  629.6 4.7 copy.70
  (355 shorter events, 225.9 us)
Async XLA Ops:
  7.2 8.2 %copy-start = (bf16[128,384]{1,0:T(8,128)(2,1)S(1)}, bf16[128,384]{1,0:T(8,128)(2,1)}, u32[]{:S(2)}) copy-start(bf16[128,384]{1,0:T(8,128)(2,1)} %param.11) | copy-start | bytes 294916
  7.2 5.5 copy-start.7
  7.2 622.4 %all-reduce.3.cloned.1.call-start = ((), (), s32[]{:S(2)}) async-start(), calls=%async_computation | async-start | bytes 8912896 | tf_op jit(solution)/shard_map/psum | solution.py:196
  9.7 5.7 copy-start.15
  17.6 20.8 %collective-permute-start = (bf16[4,16,24,512]{3,2,1,0:T(8,128)(2,1)S(1)}, bf16[4,16,24,512]{3,2,1,0:T(8,128)(2,1)S(1)}, u32[]{:S(2)}, u32[]{:S(2)}) collective-permute-start(bf16[4,16,24,512]{3,2,1,0:T(8,128)(2,1)S(1)} %pad_maximum_fusion.6), channel_id=1, source_target_pairs={{0,120},{8,0},{16,8},{24,16},{32,24},{40,32},{48,40},{56,48},{64,5... | collective-permute-start | bytes 4718600 | tf_op jit(solution)/shard_map/ppermute | solution.py:13
  19.6 18.7 %copy-start.6 = (bf16[12,16,24,512]{3,2,1,0:T(8,128)(2,1)}, bf16[12,16,24,512]{3,2,1,0:T(8,128)(2,1)S(1)}, u32[]{:S(2)}) copy-start(bf16[12,16,24,512]{3,2,1,0:T(8,128)(2,1)S(1)} %fusion.14) | copy-start | bytes 14155780
  39.6 38.7 %collective-permute-start.1 = (bf16[16,4,24,512]{3,2,1,0:T(8,128)(2,1)}, bf16[16,4,24,512]{3,2,1,0:T(8,128)(2,1)S(1)}, u32[]{:S(2)}, u32[]{:S(2)}) collective-permute-start(bf16[16,4,24,512]{3,2,1,0:T(8,128)(2,1)} %pad_maximum_fusion.5), channel_id=1, source_target_pairs={{0,7},{1,0},{2,1},{3,2},{4,3},{5,4},{6,5},{7,6},{8,15},{9,8},{10,9... | collective-permute-start | bytes 4718600 | tf_op jit(solution)/shard_map/ppermute | solution.py:13
  91.5 3.2 copy-start.1
  104.0 3.5 copy-start.2
  104.1 4.7 copy-start.3
  119.1 3.2 copy-start.1
  131.6 3.5 copy-start.2
  131.6 4.7 copy-start.3
  146.6 3.2 copy-start.1
  159.1 3.5 copy-start.2
  159.1 4.7 copy-start.3
  174.1 3.2 copy-start.1
  186.6 3.5 copy-start.2
  186.6 4.7 copy-start.3
  201.6 3.2 copy-start.1
  214.1 3.5 copy-start.2
  214.1 4.7 copy-start.3
  229.1 3.2 copy-start.1
  241.6 3.5 copy-start.2
  241.6 4.7 copy-start.3
  256.6 3.2 copy-start.1
  269.1 3.5 copy-start.2
  269.1 4.7 copy-start.3
  296.6 3.5 copy-start.2
  296.6 4.7 copy-start.3
  324.0 3.5 copy-start.2
  324.1 4.7 copy-start.3
  339.0 3.2 copy-start.1
  351.5 3.5 copy-start.2
  351.6 4.7 copy-start.3
  366.6 3.2 copy-start.1
  379.1 3.5 copy-start.2
  379.1 4.7 copy-start.3
  406.6 3.5 copy-start.2
  406.6 4.7 copy-start.3
  419.8 17.8 %copy-start.5 = (bf16[2,8,2,8,3,8,384]{6,5,4,3,2,1,0:T(8,128)(2,1)}, bf16[2,8,2,8,3,8,384]{6,5,4,3,2,1,0:T(8,128)(2,1)S(1)}, u32[]{:S(2)}) copy-start(bf16[2,8,2,8,3,8,384]{6,5,4,3,2,1,0:T(8,128)(2,1)S(1)} %copy.39) | copy-start | bytes 14155780
  420.2 47.1 %copy-start.13 = (bf16[16,16,4,384]{3,2,1,0:T(4,128)(2,1)}, bf16[16,16,4,384]{3,2,1,0:T(4,128)(2,1)S(1)}, u32[]{:S(2)}) copy-start(bf16[16,16,4,384]{3,2,1,0:T(4,128)(2,1)S(1)} %slice.82) | copy-start | bytes 2359300
  420.8 15.3 %collective-permute-start.2 = (bf16[4,16,24,384]{3,2,1,0:T(8,128)(2,1)S(1)}, bf16[4,16,24,384]{3,2,1,0:T(8,128)(2,1)S(1)}, u32[]{:S(2)}, u32[]{:S(2)}) collective-permute-start(bf16[4,16,24,384]{3,2,1,0:T(8,128)(2,1)S(1)} %pad_maximum_fusion.8), channel_id=1, source_target_pairs={{0,8},{8,16},{16,24},{24,32},{32,40},{40,48},{48,56},{56,64},{64,7... | collective-permute-start | bytes 3538952 | tf_op jit(solution)/shard_map/ppermute | solution.py:13
  437.6 29.7 %collective-permute-start.3 = (bf16[16,4,24,384]{3,2,1,0:T(8,128)(2,1)}, bf16[16,4,24,384]{3,2,1,0:T(8,128)(2,1)}, u32[]{:S(2)}, u32[]{:S(2)}) collective-permute-start(bf16[16,4,24,384]{3,2,1,0:T(8,128)(2,1)} %pad_maximum_fusion.7), channel_id=1, source_target_pairs={{0,1},{1,2},{2,3},{3,4},{4,5},{5,6},{6,7},{7,0},{8,9},{9,10},{10,1... | collective-permute-start | bytes 3538952 | tf_op jit(solution)/shard_map/ppermute | solution.py:13
  437.6 29.7 %copy-start.12 = (bf16[16,16,24,128]{3,2,1,0:T(8,128)(2,1)S(1)}, bf16[16,16,24,128]{3,2,1,0:T(8,128)(2,1)}, u32[]{:S(2)}) copy-start(bf16[16,16,24,128]{3,2,1,0:T(8,128)(2,1)} %copy-done.11) | copy-start | bytes 4718596
  474.4 78.7 %copy-start.10 = (bf16[16,16,24,128]{3,2,1,0:T(8,128)(2,1)S(1)}, bf16[16,16,24,128]{3,2,1,0:T(8,128)(2,1)}, u32[]{:S(2)}) copy-start(bf16[16,16,24,128]{3,2,1,0:T(8,128)(2,1)} %param.9) | copy-start | bytes 4718596
  629.6 4.7 copy-start.22
  629.6 5.3 copy-start.21
  (25 other events, 50.9 us)
Sparse Core Ops, SparseCore 0:
  473.2 156.4 all-reduce.2
where the time goes:
time: 644 us; the launch traced here: 642 us
  matrix products  219 us (34%)
  waiting for transfers between devices  148 us (23%)
  other arithmetic  97.3 us (15%)
  local copies, waits for them, and re-layouts  84.5 us (13%)
  blocking collectives  68.3 us (11%)
  between operations  14.3 us (2%)
  starting transfers between devices  10.1 us (2%)
    ppermute x4, waiting for transfers between devices, from_behind(): lax.ppermute(shard, axis, [(i, (i + by) % peers) for i in range(peers)])  78.7 us
    psum x1, waiting for transfers between devices, body(): lax.psum((bias_term, proj_term, qkv_term, multiplier_contribution), ('gx'...  69 us
    psum x1, blocking collectives, body(): lax.psum((bias_term, proj_term, qkv_term, multiplier_contribution), ('gx'...  68.3 us
    dot_general x12, matrix products, window_grads(): jnp.einsum('hqk,khd->qhd', prob_b, values, preferred_element_type=jnp.flo...  54.8 us
    dot_general x12, matrix products, window_grads(): jnp.einsum('hqk,qhd->khd', prob_b, grad_heads, preferred_element_type=jnp...  54.4 us
    dot_general x12, matrix products, window_grads(): jnp.einsum('qhd,khd->hqk', query, keys, preferred_element_type=jnp.float32)  38.4 us
    sub x12, other arithmetic, window_grads(): expo = jnp.exp(scores - top)  38.2 us
    dot_general x12, matrix products, window_grads(): jnp.einsum('qhd,khd->hqk', grad_heads, values, preferred_element_type=jnp...  37.3 us
  transfers between devices with their start and end apart: 5, of which 5 were waited for; matrix products, arithmetic and copies ran while one was open for 5% of the time, Pallas kernels for 0%

commit v1 on v0

v1 whole, which is shorter than its diff:
```python
import functools
import math

import jax
import jax.numpy as jnp
from jax import lax
from jax.experimental import pallas as pl
from jax.experimental.pallas import tpu as pltpu
from jax.sharding import PartitionSpec as P

HEADS = 4
HD = 32
C = 128
T = 512
KC = 128
SHIFT = 4
SCALE = HD**-0.5
EXPC = SCALE / math.log(2.0)
BLOCKED = -(2.0**100)
F32 = jnp.float32
BF = jnp.bfloat16


def dot(a, b):
    return lax.dot_general(a, b, (((1,), (0,)), ((), ())), preferred_element_type=F32)


def dot_nt(a, b):
    return lax.dot_general(a, b, (((1,), (1,)), ((), ())), preferred_element_type=F32)


def half_bits(shape, dim):
    token = lax.broadcasted_iota(jnp.int32, shape, dim)
    return [lax.shift_right_logical(token, s) & 1 for s in (8, 5, 2)]


def key_regions():
    lane = lax.broadcasted_iota(jnp.int32, (T, C), 1)
    out = jnp.zeros((T, C), F32)
    for n, bit in enumerate(half_bits((T, C), 0)):
        out = jnp.where(lane == 2 * n, bit.astype(F32), out)
        out = jnp.where(lane == 2 * n + 1, 1.0 - bit.astype(F32), out)
    return out.astype(BF)


def query_regions(edges):
    row = lax.broadcasted_iota(jnp.int32, (16, T), 0)
    out = jnp.zeros((16, T), F32)
    for n, (bit, edge) in enumerate(zip(half_bits((16, T), 1), edges)):
        weight = jnp.where(edge, BLOCKED, 0.0)
        out = jnp.where(row == 2 * n, (1.0 - bit.astype(F32)) * weight, out)
        out = jnp.where(row == 2 * n + 1, bit.astype(F32) * weight, out)
    return out.astype(BF)


def kernel(first, *refs):
    xs_ref, adj_ref, gamma_ref, w_ref, wT_ref, wproj_ref, bias_ref = refs[:7]
    if first:
        gin_ref, dbias_ref, small_ref = refs[7:10]
        scratch = refs[10:]
    else:
        acc_ref, accs_ref = refs[7:9]
        gin_ref, dbias_out, small_ref = refs[9:12]
        dbias_ref = refs[12]
        scratch = refs[13:]
    (biasT_s, xh_s, adj_s, rstd_s, qext_s, gz_s, kext_s, v_s, kT_s, vT_s, gT_s, attT_s, dT_s, dn_s, u_s, e_s, ds_s) = scratch
    step = pl.program_id(0)

    @pl.when(step == 0)
    def _():
        for h in range(HEADS):
            biasT_s[h] = bias_ref[h].T * (1.0 / SCALE)
        if first:
            dbias_ref[...] = jnp.zeros_like(dbias_ref)
            small_ref[...] = jnp.zeros_like(small_ref)
        else:
            dbias_ref[...] = acc_ref[...]
            small_ref[...] = accs_ref[...]
        qext_s[...] = jnp.zeros_like(qext_s)
        gz_s[...] = jnp.zeros_like(gz_s)
        vT_s[...] = jnp.ones_like(vT_s)
        kext_s[:, C:] = key_regions()

    if first:
        edge_x = edge_y = False
    else:
        edge_x = (lax.axis_index("gx") == lax.axis_size("gx") - 1) & (step != 1)
        edge_y = (lax.axis_index("gy") == lax.axis_size("gy") - 1) & (step != 0)
    ones = jnp.full((C, C), 1.0 / C, BF)
    low = lax.broadcasted_iota(jnp.int32, (64, 8, C), 1) < SHIFT
    xb=xs_ref[...].reshape(64*24,C)
    mu=dot(xb,ones)
    cen=xb.astype(F32)-mu
    var=dot((cen*cen).astype(BF),ones)
    rstd=lax.rsqrt(var+1e-5)
    rstd_s[...]=rstd.reshape(64,24,C)
    xh=(cen*rstd).reshape(64,3,8,C)
    a=adj_ref[...].reshape(64,3,8,C).astype(F32)
    for z in range(3):
        z1=(z+1)%3
        xh_s[z]=pltpu.roll(jnp.where(low,xh[:,z1],xh[:,z]),SHIFT,1).reshape(T,C)
        adj_s[z]=pltpu.roll(jnp.where(low,a[:,z1],a[:,z]),SHIFT,1).reshape(T,C).astype(BF)

    def window(z,carry):
        xhat=xh_s[z]
        nrm=(xhat*gamma_ref[...]).astype(BF)
        adj=adj_s[z]
        qkvT=dot_nt(wT_ref[...],nrm).astype(BF)
        kT_s[...]=qkvT[C:2*C]
        regions=query_regions((edge_x,edge_y,z==2))
        for h in range(HEADS):
            vT_s[h,:HD]=qkvT[2*C+HD*h:2*C+HD*(h+1)]
            qext_s[h,HD*h:HD*(h+1)]=qkvT[HD*h:HD*(h+1)]
            qext_s[h,C:C+16]=regions
        kv=dot(nrm,w_ref[:,C:]).astype(BF)
        kext_s[:,:C]=kv[:,:C]
        v_s[...]=kv[:,C:]
        gT_s[...]=dot_nt(wproj_ref[...],adj).astype(BF)
        st={}
        def A(h):
            mx=None
            for kc in range(T//KC):
                ks=slice(kc*KC,(kc+1)*KC)
                u=dot(kext_s[ks],qext_s[h])+biasT_s[h,ks]
                u_s[h%2,ks]=u
                c=jnp.max(u.reshape(KC//8,8,T),axis=0)
                mx=c if mx is None else jnp.maximum(mx,c)
            st["m",h]=jnp.max(mx,axis=0,keepdims=True)
        def B(h):
            m=st["m",h]
            o=None
            for kc in range(T//KC):
                ks=slice(kc*KC,(kc+1)*KC)
                e_s[h%2,ks]=jnp.exp2((u_s[h%2,ks]-m)*EXPC).astype(BF)
            o=dot(vT_s[h],e_s[h%2])
            hs=slice(HD*h,HD*(h+1))
            rl=1.0/o[HD:HD+1]
            gs=(gT_s[hs].astype(F32)*rl).astype(BF)
            on=o[:HD]*rl
            attT_s[hs]=on.astype(BF)
            st["delta",h]=jnp.sum(gs.astype(F32)*on,axis=0,keepdims=True)
            gz_s[h,hs]=gs
        def Cc(h):
            delta=st["delta",h]
            for kc in range(T//KC):
                ks=slice(kc*KC,(kc+1)*KC)
                dp=dot(v_s[ks],gz_s[h])
                ds=e_s[h%2,ks].astype(F32)*(dp-delta)
                ds_s[h%2,ks]=ds.astype(BF)
                dbias_ref[h,ks]+=ds
        def D(h):
            hs=slice(HD*h,HD*(h+1))
            dT_s[hs]=(dot(kT_s[hs],ds_s[h%2])*SCALE).astype(BF)
            dT_s[C+HD*h:C+HD*(h+1)]=(dot_nt(qext_s[h,hs],ds_s[h%2])*SCALE).astype(BF)
            dT_s[2*C+HD*h:2*C+HD*(h+1)]=dot_nt(gz_s[h,hs],e_s[h%2]).astype(BF)

        A(0)
        B(0)
        A(1)
        Cc(0)
        B(1)
        D(0)
        A(2)
        Cc(1)
        B(2)
        D(1)
        A(3)
        Cc(2)
        B(3)
        D(2)
        Cc(3)
        D(3)
        dT=dT_s[...]
        small_ref[:C]+=dot(attT_s[...],adj)
        small_ref[C:4*C]+=dot(dT,nrm)
        dn=dot(w_ref[...],dT).T
        p=dn*xhat
        small_ref[4*C:]+=jnp.sum(p.reshape(64,8,C),axis=0)
        g=dn*gamma_ref[...]
        gm=dot(g.astype(BF),ones)
        gx=dot((p*gamma_ref[...]).astype(BF),ones)
        dn_s[z]=(g-gm-xhat*gx)
        return carry
    lax.fori_loop(0,3,window,0)
    for zc in range(3):
        lo=dn_s[(zc+2)%3].reshape(64,8,C)
        hi=dn_s[zc].reshape(64,8,C)
        r=pltpu.roll(jnp.where(low,hi,lo),SHIFT,1)
        res=a[:,zc]+rstd_s[:,8*zc:8*zc+8]*r
        gin_ref[:,:,8*zc:8*zc+8]=res.astype(BF).reshape(8,8,8,C)

    if not first:
        @pl.when(step == pl.num_programs(0) - 1)
        def _():
            for h in range(HEADS):
                dbias_out[h] = dbias_ref[h].T.astype(BF)


def sublayer(first, blocks, operands):
    def whole(shape):
        return pl.BlockSpec(shape, lambda i: (0,) * len(shape))

    block = pl.BlockSpec((pl.Squeezed(), 8, 8, 24, C), lambda i: (i, 0, 0, 0, 0))
    square = (HEADS, T, T)
    ins = [block, block, whole((1, C)), whole((C, 3 * C)), whole((3 * C, C)), whole((C, C)), whole(square)]
    scratch = []
    if not first:
        ins += [whole(square), whole((4 * C + 8, C))]
        scratch = [pltpu.VMEM(square, F32)]
    scratch += [
        pltpu.VMEM(square, F32),
        pltpu.VMEM((3, T, C), F32),
        pltpu.VMEM((3, T, C), BF),
        pltpu.VMEM((64, 24, C), F32),
        pltpu.VMEM((HEADS, 2 * C, T), BF),
        pltpu.VMEM((HEADS, C, T), BF),
        pltpu.VMEM((T, 2 * C), BF),
        pltpu.VMEM((T, C), BF),
        pltpu.VMEM((C, T), BF),
        pltpu.VMEM((HEADS, 48, T), BF),
        pltpu.VMEM((C, T), BF),
        pltpu.VMEM((C, T), BF),
        pltpu.VMEM((3 * C, T), BF),
        pltpu.VMEM((3, T, C), F32),
        pltpu.VMEM((2, T, T), F32),
        pltpu.VMEM((2, T, T), BF),
        pltpu.VMEM((2, T, T), BF),
    ]
    return pl.pallas_call(
        functools.partial(kernel, first),
        grid=(blocks,),
        in_specs=ins,
        out_specs=[block, whole(square), whole((4 * C + 8, C))],
        out_shape=[
            jax.ShapeDtypeStruct((blocks, 8, 8, 24, C), BF),
            jax.ShapeDtypeStruct(square, F32 if first else BF),
            jax.ShapeDtypeStruct((4 * C + 8, C), F32),
        ],
        scratch_shapes=scratch,
        compiler_params=pltpu.CompilerParams(vmem_limit_bytes=58 * 1024 * 1024),
        cost_estimate=pl.CostEstimate(flops=blocks * 12 * 10**9, bytes_accessed=blocks * 10**7, transcendentals=0),
        name="window_grads",
    )(*operands)


def shifted(values, by_x, by_y):
    nx, ny = lax.axis_size("gx"), lax.axis_size("gy")
    if not by_y:
        return lax.ppermute(values, "gx", [(i, (i + by_x) % nx) for i in range(nx)])
    if not by_x:
        return lax.ppermute(values, "gy", [(i, (i + by_y) % ny) for i in range(ny)])
    pairs = [(i * ny + j, (i + by_x) % nx * ny + (j + by_y) % ny) for i in range(nx) for j in range(ny)]
    return lax.ppermute(values, ("gx", "gy"), pairs)


def flip_pairs(order):
    pairs = []
    for i in range(16):
        for j in range(8):
            axis, bit = order[i & 1]
            k, l = (i ^ bit, j) if axis == "gx" else (i, j ^ bit)
            pairs.append((i * 8 + j, k * 8 + l))
    return pairs


STEPS = [
    (("gx", 1), ("gx", 1)),
    (("gx", 2), ("gy", 1)),
    (("gx", 4), ("gy", 2)),
    (("gy", 1), ("gx", 2)),
    (("gy", 2), ("gx", 4)),
    (("gx", 8), ("gy", 4)),
    (("gy", 4), ("gx", 8)),
]


def my_bit(order):
    gx, gy = lax.axis_index("gx"), lax.axis_index("gy")
    bits = [((gx if axis == "gx" else gy) // bit) % 2 for axis, bit in order]
    return jnp.where(gx % 2 == 0, bits[0], bits[1])


def summed(values):
    for order in STEPS:
        half = values.shape[0] // 2
        mine = my_bit(order)
        away = lax.dynamic_slice_in_dim(values, (1 - mine) * half, half)
        keep = lax.dynamic_slice_in_dim(values, mine * half, half)
        got = lax.ppermute(away, ("gx", "gy"), flip_pairs(order))
        values = (keep.astype(F32) + got.astype(F32)).astype(BF)
    for order in reversed(STEPS):
        mine = my_bit(order)
        got = lax.ppermute(values, ("gx", "gy"), flip_pairs(order))
        values = jnp.where(mine == 0, jnp.concatenate([values, got]), jnp.concatenate([got, values]))
    return values


def body(retained_source, incoming_adjoint, rescale_multiplier, triple_projection_matrix, w_proj, pos_bias):
    both = jnp.stack([retained_source, incoming_adjoint])
    from_x = shifted(both[:, :4, 4:], -1, 0)
    from_y = shifted(both[:, 4:, :4], 0, -1)
    from_xy = shifted(both[:, :4, :4], -1, -1)
    params = (
        rescale_multiplier.reshape(1, C),
        triple_projection_matrix,
        triple_projection_matrix.T,
        w_proj,
        pos_bias,
    )
    inner = both[:, 4:12, 4:12]
    gin_a, acc, acc_small = sublayer(True, 1, (inner[0][None], inner[1][None]) + params)
    rim = jnp.stack(
        [
            jnp.concatenate([both[:, 12:, 4:12], from_x[:, :, :8]], axis=1),
            jnp.concatenate([both[:, 4:12, 12:], from_y[:, :8]], axis=2),
            jnp.concatenate(
                [
                    jnp.concatenate([both[:, 12:, 12:], from_y[:, 8:]], axis=2),
                    jnp.concatenate([from_x[:, :, 8:], from_xy], axis=2),
                ],
                axis=1,
            ),
        ],
        axis=1,
    )
    gin_b, grad_bias, small = sublayer(False, 3, (rim[0], rim[1]) + params + (acc, acc_small))
    bx, by, bc = gin_b[0], gin_b[1], gin_b[2]
    back_x = shifted(jnp.concatenate([bx[4:], bc[4:, :4]], axis=1), 1, 0)
    back_y = shifted(jnp.concatenate([by[:, 4:], bc[:4, 4:]], axis=0), 0, 1)
    back_xy = shifted(bc[4:, 4:], 1, 1)
    grad_input = jnp.concatenate(
        [
            jnp.concatenate([back_xy, back_x], axis=1),
            jnp.concatenate([back_y[:8], gin_a[0], by[:, :4]], axis=1),
            jnp.concatenate([back_y[8:], bx[:4], bc[:4, :4]], axis=1),
        ],
        axis=0,
    )
    rows = HEADS * T * T // C
    packed = jnp.concatenate([grad_bias.reshape(rows, C), small.astype(BF), jnp.zeros((1024 - small.shape[0], C), BF)])
    total = summed(packed)
    grad_bias = total[:rows].astype(F32).reshape(HEADS, T, T)
    rest = total[rows : rows + small.shape[0]].astype(F32)
    return (grad_input, grad_bias, rest[:C], rest[C : 4 * C].T, jnp.sum(rest[4 * C :], axis=0))


def solution(mesh):
    placed = (P("gx", "gy", None, None), P("gx", "gy", None, None), P(), P(), P(), P())
    return jax.shard_map(
        body,
        mesh=mesh,
        in_specs=placed,
        out_specs=(P("gx", "gy", None, None), P(), P(), P(), P()),
        check_vma=False,
    )
```

time: 644 us -> 235 us (0.36)
  matrix products: 219 us -> 0 us
  other arithmetic: 97.3 us -> 13.8 us
  Pallas kernels: 0 us -> 77.5 us
  waiting for transfers between devices: 148 us -> 76.8 us
  blocking collectives: 68.3 us -> 0 us
  local copies, waits for them, and re-layouts: 84.5 us -> 31.5 us
  starting transfers between devices: 10.1 us -> 33.8 us
  between operations: 14.3 us -> 1.08 us
    dot_general x99 -> x0, matrix products: 219 us -> none  [the longest x12 54.8 us: window_grads(): jnp.einsum('hqk,khd->qhd', prob_b, values, preferred_element_type=jnp.flo...]
    pallas_call x0 -> x2, Pallas kernels: none -> 77.5 us  [sublayer(): pl.pallas_call(functools.partial(kernel, first), grid=(blocks,), in_specs...]
    psum x1 -> x0, waiting for transfers between devices: 69 us -> none  [body(): lax.psum((bias_term, proj_term, qkv_term, multiplier_contribution), ('gx'...]
    psum x1 -> x0, blocking collectives: 68.3 us -> none  [body(): lax.psum((bias_term, proj_term, qkv_term, multiplier_contribution), ('gx'...]
    sub x12 -> x0, other arithmetic: 38.2 us -> none  [window_grads(): expo = jnp.exp(scores - top)]
    convert_element_type x14 -> x9, other arithmetic: 37.6 us -> 2.22 us  [the longest x7 2.18 us: summed(): values = (keep.astype(F32) + got.astype(F32)).astype(BF)]
    while x97 -> x0, local copies, waits for them, and re-layouts: 35 us -> none
    ppermute x4 -> x20, starting transfers between devices: 10.1 us -> 33.8 us  [the longest x7 17 us: summed(): got = lax.ppermute(values, ('gx', 'gy'), flip_pairs(order))]
  transfers between devices with their start and end apart: 5 -> 20, of which waited for: 5 -> 15; matrix products, arithmetic and copies ran while one was open for 5% -> 5% of each run, Pallas kernels for 0% -> 9%
where the time goes in v1:
time: 235 us; the launch traced here: 234 us
  Pallas kernels  77.5 us (33%)
  waiting for transfers between devices  76.8 us (33%)
  starting transfers between devices  33.8 us (14%)
  local copies, waits for them, and re-layouts  31.5 us (13%)
  other arithmetic  13.8 us (6%)
    pallas_call x2, Pallas kernels, sublayer(): pl.pallas_call(functools.partial(kernel, first), grid=(blocks,), in_specs...  77.5 us
    ppermute x7, waiting for transfers between devices, summed(): got = lax.ppermute(away, ('gx', 'gy'), flip_pairs(order))  33 us
    ppermute x7, waiting for transfers between devices, summed(): got = lax.ppermute(values, ('gx', 'gy'), flip_pairs(order))  29.1 us
    ppermute x7, starting transfers between devices, summed(): got = lax.ppermute(values, ('gx', 'gy'), flip_pairs(order))  17 us
    ppermute x2, waiting for transfers between devices, shifted(): return lax.ppermute(values, 'gy', [(i, (i + by_y) % ny) for i in range(ny)])  13.5 us
    reshape x2, local copies, waits for them, and re-layouts, body(): grad_bias = total[:rows].astype(F32).reshape(HEADS, T, T)  10.5 us
    ppermute x2, starting transfers between devices, shifted(): return lax.ppermute(values, ('gx', 'gy'), pairs)  7.92 us
    reshape x2, local copies, waits for them, and re-layouts, body(): grad_bias.reshape(rows, C)  5.99 us
  transfers between devices with their start and end apart: 20, of which 15 were waited for; matrix products, arithmetic and copies ran while one was open for 5% of the time, Pallas kernels for 9%

profile of v1, /device:TPU:1, one launch (start us, length us, event | category | flops | bytes accessed | tf_op | source)
XLA Modules:
  0.0 234.4 jit_solution(4221435541668170624)
XLA Ops:
  0.7 1.1 pad_maximum_fusion.8
  1.8 7.8 %collective-permute-start.2 = (bf16[2,4,4,24,128]{4,3,2,1,0:T(8,128)(2,1)S(1)}, bf16[2,4,4,24,128]{4,3,2,1,0:T(8,128)(2,1)S(1)}, u32[]{:S(2)}, u32[]{:S(2)}) collective-permute-start(bf16[2,4,4,24,128]{4,3,2,1,0:T(8,128)(2,1)S(1)} %pad_maximum_fusion.8), channel_id=1, source_target_pairs={{0,127},{1,120},{2,121},{3,122},{4,123},{5,124},{6,125},{7,126},{8... | collective-permute-start | bytes 589832 | tf_op jit(solution)/shard_map/ppermute | solution.py:253
  9.6 0.9 pad_maximum_fusion.4
  10.7 0.9 pad_maximum_fusion.5
  11.6 2.9 %collective-permute-start = (bf16[2,4,12,24,128]{4,3,2,1,0:T(8,128)(2,1)}, bf16[2,4,12,24,128]{4,3,2,1,0:T(8,128)(2,1)}, u32[]{:S(2)}, u32[]{:S(2)}) collective-permute-start(bf16[2,4,12,24,128]{4,3,2,1,0:T(8,128)(2,1)} %pad_maximum_fusion.5), channel_id=1, source_target_pairs={{0,120},{8,0},{16,8},{24,16},{32,24},{40,32},{48,40},{56,48},{64,5... | collective-permute-start | bytes 1769480 | tf_op jit(solution)/shard_map/ppermute | solution.py:249
  14.5 0.8 slice.146.refs_0_
  15.3 0.8 slice.147.refs_1_
  16.1 1.6 copy.19
  17.7 21.2 %window_grads.2 = (bf16[1,8,8,24,128]{4,3,2,1,0:T(8,128)(2,1)}, f32[4,512,512]{2,1,0:T(8,128)}, f32[520,128]{1,0:T(8,128)}) custom-call(bf16[1,8,8,24,128]{4,3,2,1,0:T(8,128)(2,1)} %slice.146.refs_0_, bf16[1,8,8,24,128]{4,3,2,1,0:T(8,128)(2,1)} %slice.147.refs_1_, f32[1,128]{1,0:T(1,128)} %bitcast.42, bf16[128,384]{1,0:T(8,128)(2,1)} %refs_3_.3, ...), custom_call_target="tpu_custom_call" | custom-call | flops 12000000000 | bytes 10000000 | tf_op jit(solution)/shard_map/window_grads/pallas_call | solution.py:229
  38.9 0.9 slice.142
  39.9 1.0 slice.141
  40.9 1.0 slice.143
  41.9 1.0 slice.140
  43.4 1.8 slice_bitcast_fusion
  45.3 56.3 %window_grads.3 = (bf16[3,8,8,24,128]{4,3,2,1,0:T(8,128)(2,1)}, bf16[4,512,512]{2,1,0:T(8,128)(2,1)}, f32[520,128]{1,0:T(8,128)}) custom-call(bf16[3,8,8,24,128]{4,3,2,1,0:T(8,128)(2,1)} %get-tuple-element.31.refs_0_, bf16[3,8,8,24,128]{4,3,2,1,0:T(8,128)(2,1)} %get-tuple-element.30.refs_1_, f32[1,128]{1,0:T(1,128)} %bitcast.43, bf16[128,384]{1,0:T(8,128)(2,1)} %refs_3_.3, ...), custom_call_target="tpu_custom_call" | custom-call | flops 35999997952 | bytes 30000000 | tf_op jit(solution)/shard_map/window_grads/pallas_call | solution.py:229
  101.5 3.1 %reshape.25 = bf16[8192,128]{1,0:T(8,128)(2,1)S(1)} reshape(bf16[4,512,512]{2,1,0:T(8,128)(2,1)} %get-tuple-element.15) | data formatting | bytes 4194304 | tf_op jit(solution)/shard_map/reshape | solution.py:340
  104.7 2.9 %copy.20 = bf16[8192,128]{0,1:T(8,128)(2,1)} copy(bf16[8192,128]{1,0:T(8,128)(2,1)S(1)} %reshape.25) | data formatting | bytes 4194304 | tf_op jit(solution)/shard_map/reshape | solution.py:340
  107.8 3.5 %concatenate.89 = bf16[9216,128]{0,1:T(8,128)(2,1)S(1)} concatenate(bf16[8192,128]{0,1:T(8,128)(2,1)} %copy.20, bf16[520,128]{0,1:T(8,128)(2,1)S(1)} %copy.21, bf16[504,128]{0,1:T(8,128)(2,1)S(1)} %broadcast_in_dim.3), dimensions={0} | concatenate | bytes 4718592 | tf_op jit(solution)/shard_map/concatenate | solution.py:340
  111.5 2.9 %collective-permute-done.6 = bf16[4608,128]{0,1:T(8,128)(2,1)} collective-permute-done((bf16[4608,128]{0,1:T(8,128)(2,1)S(1)}, bf16[4608,128]{0,1:T(8,128)(2,1)}, u32[]{:S(2)}, u32[]{:S(2)}) %collective-permute-start.6) | collective-permute-done | bytes 1179680 | tf_op jit(solution)/shard_map/ppermute | solution.py:289
  114.4 1.6 add_convert_fusion
  116.1 1.0 collective-permute-start.7
  117.1 8.1 %collective-permute-done.7 = bf16[2304,128]{0,1:T(8,128)(2,1)S(1)} collective-permute-done((bf16[2304,128]{0,1:T(8,128)(2,1)S(1)}, bf16[2304,128]{0,1:T(8,128)(2,1)S(1)}, u32[]{:S(2)}, u32[]{:S(2)}) %collective-permute-start.7) | collective-permute-done | bytes 589856 | tf_op jit(solution)/shard_map/ppermute | solution.py:289
  125.5 7.3 %collective-permute-done.8 = bf16[1152,128]{0,1:T(8,128)(2,1)S(1)} collective-permute-done((bf16[1152,128]{0,1:T(8,128)(2,1)S(1)}, bf16[1152,128]{0,1:T(8,128)(2,1)S(1)}, u32[]{:S(2)}, u32[]{:S(2)}) %collective-permute-start.8) | collective-permute-done | bytes 294944 | tf_op jit(solution)/shard_map/ppermute | solution.py:289
  133.2 4.1 %collective-permute-done.9 = bf16[576,128]{0,1:T(8,128)(2,1)S(1)} collective-permute-done((bf16[576,128]{0,1:T(8,128)(2,1)S(1)}, bf16[576,128]{0,1:T(8,128)(2,1)S(1)}, u32[]{:S(2)}, u32[]{:S(2)}) %collective-permute-start.9) | collective-permute-done | bytes 147488 | tf_op jit(solution)/shard_map/ppermute | solution.py:289
  138.1 4.5 %collective-permute-done.10 = bf16[288,128]{0,1:T(8,128)(2,1)S(1)} collective-permute-done((bf16[288,128]{0,1:T(8,128)(2,1)S(1)}, bf16[288,128]{0,1:T(8,128)(2,1)S(1)}, u32[]{:S(2)}, u32[]{:S(2)}) %collective-permute-start.10) | collective-permute-done | bytes 73760 | tf_op jit(solution)/shard_map/ppermute | solution.py:289
  142.8 1.3 collective-permute-start.11
  144.1 3.4 %collective-permute-done.11 = bf16[144,128]{0,1:T(8,128)(2,1)S(1)} collective-permute-done((bf16[144,128]{0,1:T(8,128)(2,1)S(1)}, bf16[144,128]{0,1:T(8,128)(2,1)S(1)}, u32[]{:S(2)}, u32[]{:S(2)}) %collective-permute-start.11) | collective-permute-done | bytes 36896 | tf_op jit(solution)/shard_map/ppermute | solution.py:289
  147.7 0.8 collective-permute-start.12
  148.5 2.7 %collective-permute-done.12 = bf16[72,128]{0,1:T(8,128)(2,1)S(1)} collective-permute-done((bf16[72,128]{0,1:T(8,128)(2,1)S(1)}, bf16[72,128]{0,1:T(8,128)(2,1)S(1)}, u32[]{:S(2)}, u32[]{:S(2)}) %collective-permute-start.12) | collective-permute-done | bytes 18464 | tf_op jit(solution)/shard_map/ppermute | solution.py:289
  151.3 0.8 collective-permute-start.13
  152.1 2.2 collective-permute-done.13
  154.4 1.4 collective-permute-start.14
  155.7 3.5 %collective-permute-done.14 = bf16[144,128]{0,1:T(8,128)(2,1)S(1)} collective-permute-done((bf16[144,128]{0,1:T(8,128)(2,1)S(1)}, bf16[144,128]{0,1:T(8,128)(2,1)S(1)}, u32[]{:S(2)}, u32[]{:S(2)}) %collective-permute-start.14) | collective-permute-done | bytes 36896 | tf_op jit(solution)/shard_map/ppermute | solution.py:293
  159.8 4.7 %collective-permute-done.15 = bf16[288,128]{0,1:T(8,128)(2,1)S(1)} collective-permute-done((bf16[288,128]{0,1:T(8,128)(2,1)S(1)}, bf16[288,128]{0,1:T(8,128)(2,1)S(1)}, u32[]{:S(2)}, u32[]{:S(2)}) %collective-permute-start.15) | collective-permute-done | bytes 73760 | tf_op jit(solution)/shard_map/ppermute | solution.py:293
  164.7 4.2 %collective-permute-done.16 = bf16[576,128]{0,1:T(8,128)(2,1)S(1)} collective-permute-done((bf16[576,128]{0,1:T(8,128)(2,1)S(1)}, bf16[576,128]{0,1:T(8,128)(2,1)S(1)}, u32[]{:S(2)}, u32[]{:S(2)}) %collective-permute-start.16) | collective-permute-done | bytes 147488 | tf_op jit(solution)/shard_map/ppermute | solution.py:293
  169.1 7.2 %collective-permute-done.17 = bf16[1152,128]{0,1:T(8,128)(2,1)S(1)} collective-permute-done((bf16[1152,128]{0,1:T(8,128)(2,1)S(1)}, bf16[1152,128]{0,1:T(8,128)(2,1)S(1)}, u32[]{:S(2)}, u32[]{:S(2)}) %collective-permute-start.17) | collective-permute-done | bytes 294944 | tf_op jit(solution)/shard_map/ppermute | solution.py:293
  176.5 2.3 collective-permute-start.18
  178.9 7.4 %collective-permute-done.18 = bf16[2304,128]{0,1:T(8,128)(2,1)S(1)} collective-permute-done((bf16[2304,128]{0,1:T(8,128)(2,1)S(1)}, bf16[2304,128]{0,1:T(8,128)(2,1)S(1)}, u32[]{:S(2)}, u32[]{:S(2)}) %collective-permute-start.18) | collective-permute-done | bytes 589856 | tf_op jit(solution)/shard_map/ppermute | solution.py:293
  186.6 11.9 %collective-permute-start.19 = (bf16[4608,128]{0,1:T(8,128)(2,1)S(1)}, bf16[4608,128]{0,1:T(8,128)(2,1)S(1)}, u32[]{:S(2)}, u32[]{:S(2)}) collective-permute-start(bf16[4608,128]{0,1:T(8,128)(2,1)S(1)} %maximum_select_fusion.1), channel_id=1, source_target_pairs={{0,8},{1,9},{2,10},{3,11},{4,12},{5,13},{6,14},{7,15},{8,0},{9,1},... | collective-permute-start | bytes 3538952 | tf_op jit(solution)/shard_map/ppermute | solution.py:293
  198.6 1.7 collective-permute-start.5
  200.5 13.5 %collective-permute-done.5 = bf16[12,4,24,128]{3,2,1,0:T(8,128)(2,1)S(1)} collective-permute-done((bf16[12,4,24,128]{3,2,1,0:T(8,128)(2,1)S(1)}, bf16[12,4,24,128]{3,2,1,0:T(8,128)(2,1)S(1)}, u32[]{:S(2)}, u32[]{:S(2)}) %collective-permute-start.5) | collective-permute-done | bytes 294944 | tf_op jit(solution)/shard_map/ppermute | solution.py:251
  214.1 1.1 collective-permute-done.3
  215.2 3.6 %maximum_maximum_fusion = bf16[16,16,24,128]{3,2,1,0:T(8,128)(2,1)} fusion(bf16[4,4,24,128]{3,2,1,0:T(8,128)(2,1)S(1)} %get-tuple-element.37, bf16[4,8,24,128]{3,2,1,0:T(8,128)(2,1)S(1)} %get-tuple-element.33, bf16[4,4,24,128]{3,2,1,0:T(8,128)(2,1)S(1)} %slice.154, bf16[8,4,24,128]{3,2,1,0:T(8,128)(2,1)S(1)} %get-tuple-element.40, ...), kind=kLoop, calls=%fused_computation.4 | loop fusion | flops 5505024 | bytes 3145728 | tf_op jit(solution)/shard_map/concatenate | solution.py:331
  220.1 0.7 slice_bitcast_fusion.4
  220.8 2.4 %slice_convert_fusion = f32[8192,128]{0,1:T(8,128)} fusion(bf16[9216,128]{0,1:T(8,128)(2,1)S(1)} %maximum_select_fusion), kind=kLoop, calls=%fused_computation.3 | loop fusion | flops 1048576 | bytes 6291456 | tf_op jit(solution)/shard_map/reshape | solution.py:342
  223.2 0.7 copy.23
  224.0 5.6 %copy.22 = f32[8192,128]{1,0:T(8,128)} copy(f32[8192,128]{0,1:T(8,128)} %slice_convert_fusion) | data formatting | bytes 8388608 | tf_op jit(solution)/shard_map/reshape | solution.py:342
  229.5 4.9 %reshape.29 = f32[4,512,512]{2,1,0:T(8,128)} reshape(f32[8192,128]{1,0:T(8,128)} %copy.22) | data formatting | bytes 8388608 | tf_op jit(solution)/shard_map/reshape | solution.py:342
  (61 shorter events, 6.1 us)
Async XLA Ops:
  0.6 9.0 %copy-start = (bf16[16,16,24,128]{3,2,1,0:T(8,128)(2,1)S(1)}, bf16[16,16,24,128]{3,2,1,0:T(8,128)(2,1)}, u32[]{:S(2)}) copy-start(bf16[16,16,24,128]{3,2,1,0:T(8,128)(2,1)} %param.7) | copy-start | bytes 4718596
  0.6 9.0 %copy-start.1 = (bf16[16,16,24,128]{3,2,1,0:T(8,128)(2,1)S(1)}, bf16[16,16,24,128]{3,2,1,0:T(8,128)(2,1)}, u32[]{:S(2)}) copy-start(bf16[16,16,24,128]{3,2,1,0:T(8,128)(2,1)} %param.6) | copy-start | bytes 4718596
  1.8 41.2 %collective-permute-start.2 = (bf16[2,4,4,24,128]{4,3,2,1,0:T(8,128)(2,1)S(1)}, bf16[2,4,4,24,128]{4,3,2,1,0:T(8,128)(2,1)S(1)}, u32[]{:S(2)}, u32[]{:S(2)}) collective-permute-start(bf16[2,4,4,24,128]{4,3,2,1,0:T(8,128)(2,1)S(1)} %pad_maximum_fusion.8), channel_id=1, source_target_pairs={{0,127},{1,120},{2,121},{3,122},{4,123},{5,124},{6,125},{7,126},{8... | collective-permute-start | bytes 589832 | tf_op jit(solution)/shard_map/ppermute | solution.py:253
  10.5 28.4 %collective-permute-start.1 = (bf16[2,12,4,24,128]{4,3,2,1,0:T(8,128)(2,1)}, bf16[2,12,4,24,128]{4,3,2,1,0:T(8,128)(2,1)}, u32[]{:S(2)}, u32[]{:S(2)}) collective-permute-start(bf16[2,12,4,24,128]{4,3,2,1,0:T(8,128)(2,1)} %pad_maximum_fusion.4), channel_id=1, source_target_pairs={{0,7},{1,0},{2,1},{3,2},{4,3},{5,4},{6,5},{7,6},{8,15},{9,8},{10,9... | collective-permute-start | bytes 1769480 | tf_op jit(solution)/shard_map/ppermute | solution.py:251
  11.6 29.3 %collective-permute-start = (bf16[2,4,12,24,128]{4,3,2,1,0:T(8,128)(2,1)}, bf16[2,4,12,24,128]{4,3,2,1,0:T(8,128)(2,1)}, u32[]{:S(2)}, u32[]{:S(2)}) collective-permute-start(bf16[2,4,12,24,128]{4,3,2,1,0:T(8,128)(2,1)} %pad_maximum_fusion.5), channel_id=1, source_target_pairs={{0,120},{8,0},{16,8},{24,16},{32,24},{40,32},{48,40},{56,48},{64,5... | collective-permute-start | bytes 1769480 | tf_op jit(solution)/shard_map/ppermute | solution.py:249
  104.6 2.9 %copy-start.4 = (f32[520,128]{1,0:T(8,128)S(1)}, f32[520,128]{1,0:T(8,128)}, u32[]{:S(2)}) copy-start(f32[520,128]{1,0:T(8,128)} %get-tuple-element.16) | copy-start | bytes 798724
  111.4 3.1 %collective-permute-start.6 = (bf16[4608,128]{0,1:T(8,128)(2,1)S(1)}, bf16[4608,128]{0,1:T(8,128)(2,1)}, u32[]{:S(2)}, u32[]{:S(2)}) collective-permute-start(bf16[4608,128]{0,1:T(8,128)(2,1)S(1)} %constant_dynamic-slice_fusion.6), channel_id=1, source_target_pairs={{0,8},{1,9},{2,10},{3,11},{4,12},{5,13},{6,14},{7,15},{8,0},{9,1},... | collective-permute-start | bytes 3538952 | tf_op jit(solution)/shard_map/ppermute | solution.py:289
  116.1 9.1 %collective-permute-start.7 = (bf16[2304,128]{0,1:T(8,128)(2,1)S(1)}, bf16[2304,128]{0,1:T(8,128)(2,1)S(1)}, u32[]{:S(2)}, u32[]{:S(2)}) collective-permute-start(bf16[2304,128]{0,1:T(8,128)(2,1)S(1)} %constant_dynamic-slice_fusion.5), channel_id=1, source_target_pairs={{0,16},{1,17},{2,18},{3,19},{4,20},{5,21},{6,22},{7,23},{8,9},{9,8... | collective-permute-start | bytes 1769480 | tf_op jit(solution)/shard_map/ppermute | solution.py:289
  125.4 7.5 %collective-permute-start.8 = (bf16[1152,128]{0,1:T(8,128)(2,1)S(1)}, bf16[1152,128]{0,1:T(8,128)(2,1)S(1)}, u32[]{:S(2)}, u32[]{:S(2)}) collective-permute-start(bf16[1152,128]{0,1:T(8,128)(2,1)S(1)} %constant_dynamic-slice_fusion.4), channel_id=1, source_target_pairs={{0,32},{1,33},{2,34},{3,35},{4,36},{5,37},{6,38},{7,39},{8,10},{9,... | collective-permute-start | bytes 884744 | tf_op jit(solution)/shard_map/ppermute | solution.py:289
  133.0 4.2 %collective-permute-start.9 = (bf16[576,128]{0,1:T(8,128)(2,1)S(1)}, bf16[576,128]{0,1:T(8,128)(2,1)S(1)}, u32[]{:S(2)}, u32[]{:S(2)}) collective-permute-start(bf16[576,128]{0,1:T(8,128)(2,1)S(1)} %constant_dynamic-slice_fusion.3), channel_id=1, source_target_pairs={{0,1},{1,0},{2,3},{3,2},{4,5},{5,4},{6,7},{7,6},{8,24},{9,25},{10,... | collective-permute-start | bytes 442376 | tf_op jit(solution)/shard_map/ppermute | solution.py:289
  137.5 5.1 %collective-permute-start.10 = (bf16[288,128]{0,1:T(8,128)(2,1)S(1)}, bf16[288,128]{0,1:T(8,128)(2,1)S(1)}, u32[]{:S(2)}, u32[]{:S(2)}) collective-permute-start(bf16[288,128]{0,1:T(8,128)(2,1)S(1)} %constant_dynamic-slice_fusion.2), channel_id=1, source_target_pairs={{0,2},{1,3},{2,0},{3,1},{4,6},{5,7},{6,4},{7,5},{8,40},{9,41},{10,... | collective-permute-start | bytes 221192 | tf_op jit(solution)/shard_map/ppermute | solution.py:289
  142.7 36.1 %copy-start.2 = (bf16[3,8,8,24,128]{4,3,2,1,0:T(8,128)(2,1)S(1)}, bf16[3,8,8,24,128]{4,3,2,1,0:T(8,128)(2,1)}, u32[]{:S(2)}) copy-start(bf16[3,8,8,24,128]{4,3,2,1,0:T(8,128)(2,1)} %get-tuple-element.13) | copy-start | bytes 3538948
  142.8 4.7 %collective-permute-start.11 = (bf16[144,128]{0,1:T(8,128)(2,1)S(1)}, bf16[144,128]{0,1:T(8,128)(2,1)S(1)}, u32[]{:S(2)}, u32[]{:S(2)}) collective-permute-start(bf16[144,128]{0,1:T(8,128)(2,1)S(1)} %constant_dynamic-slice_fusion.1), channel_id=1, source_target_pairs={{0,64},{1,65},{2,66},{3,67},{4,68},{5,69},{6,70},{7,71},{8,12},{9,... | collective-permute-start | bytes 110600 | tf_op jit(solution)/shard_map/ppermute | solution.py:289
  147.7 3.5 %collective-permute-start.12 = (bf16[72,128]{0,1:T(8,128)(2,1)S(1)}, bf16[72,128]{0,1:T(8,128)(2,1)S(1)}, u32[]{:S(2)}, u32[]{:S(2)}) collective-permute-start(bf16[72,128]{0,1:T(8,128)(2,1)S(1)} %constant_dynamic-slice_fusion), channel_id=1, source_target_pairs={{0,4},{1,5},{2,6},{3,7},{4,0},{5,1},{6,2},{7,3},{8,72},{9,73},{10,... | collective-permute-start | bytes 55304 | tf_op jit(solution)/shard_map/ppermute | solution.py:289
  151.3 3.0 %collective-permute-start.13 = (bf16[72,128]{0,1:T(8,128)(2,1)S(1)}, bf16[72,128]{0,1:T(8,128)(2,1)S(1)}, u32[]{:S(2)}, u32[]{:S(2)}) collective-permute-start(bf16[72,128]{0,1:T(8,128)(2,1)S(1)} %add_convert_fusion.6), channel_id=1, source_target_pairs={{0,4},{1,5},{2,6},{3,7},{4,0},{5,1},{6,2},{7,3},{8,72},{9,73},{10,... | collective-permute-start | bytes 55304 | tf_op jit(solution)/shard_map/ppermute | solution.py:293
  154.4 4.9 %collective-permute-start.14 = (bf16[144,128]{0,1:T(8,128)(2,1)S(1)}, bf16[144,128]{0,1:T(8,128)(2,1)S(1)}, u32[]{:S(2)}, u32[]{:S(2)}) collective-permute-start(bf16[144,128]{0,1:T(8,128)(2,1)S(1)} %maximum_select_fusion.6), channel_id=1, source_target_pairs={{0,64},{1,65},{2,66},{3,67},{4,68},{5,69},{6,70},{7,71},{8,12},{9,... | collective-permute-start | bytes 110600 | tf_op jit(solution)/shard_map/ppermute | solution.py:293
  159.4 5.1 %collective-permute-start.15 = (bf16[288,128]{0,1:T(8,128)(2,1)S(1)}, bf16[288,128]{0,1:T(8,128)(2,1)S(1)}, u32[]{:S(2)}, u32[]{:S(2)}) collective-permute-start(bf16[288,128]{0,1:T(8,128)(2,1)S(1)} %maximum_select_fusion.5), channel_id=1, source_target_pairs={{0,2},{1,3},{2,0},{3,1},{4,6},{5,7},{6,4},{7,5},{8,40},{9,41},{10,... | collective-permute-start | bytes 221192 | tf_op jit(solution)/shard_map/ppermute | solution.py:293
  164.6 4.2 %collective-permute-start.16 = (bf16[576,128]{0,1:T(8,128)(2,1)S(1)}, bf16[576,128]{0,1:T(8,128)(2,1)S(1)}, u32[]{:S(2)}, u32[]{:S(2)}) collective-permute-start(bf16[576,128]{0,1:T(8,128)(2,1)S(1)} %maximum_select_fusion.4), channel_id=1, source_target_pairs={{0,1},{1,0},{2,3},{3,2},{4,5},{5,4},{6,7},{7,6},{8,24},{9,25},{10,... | collective-permute-start | bytes 442376 | tf_op jit(solution)/shard_map/ppermute | solution.py:293
  169.0 7.3 %collective-permute-start.17 = (bf16[1152,128]{0,1:T(8,128)(2,1)S(1)}, bf16[1152,128]{0,1:T(8,128)(2,1)S(1)}, u32[]{:S(2)}, u32[]{:S(2)}) collective-permute-start(bf16[1152,128]{0,1:T(8,128)(2,1)S(1)} %maximum_select_fusion.3), channel_id=1, source_target_pairs={{0,32},{1,33},{2,34},{3,35},{4,36},{5,37},{6,38},{7,39},{8,10},{9,... | collective-permute-start | bytes 884744 | tf_op jit(solution)/shard_map/ppermute | solution.py:293
  176.5 9.9 %collective-permute-start.18 = (bf16[2304,128]{0,1:T(8,128)(2,1)S(1)}, bf16[2304,128]{0,1:T(8,128)(2,1)S(1)}, u32[]{:S(2)}, u32[]{:S(2)}) collective-permute-start(bf16[2304,128]{0,1:T(8,128)(2,1)S(1)} %maximum_select_fusion.2), channel_id=1, source_target_pairs={{0,16},{1,17},{2,18},{3,19},{4,20},{5,21},{6,22},{7,23},{8,9},{9,8... | collective-permute-start | bytes 1769480 | tf_op jit(solution)/shard_map/ppermute | solution.py:293
  186.6 32.2 %collective-permute-start.19 = (bf16[4608,128]{0,1:T(8,128)(2,1)S(1)}, bf16[4608,128]{0,1:T(8,128)(2,1)S(1)}, u32[]{:S(2)}, u32[]{:S(2)}) collective-permute-start(bf16[4608,128]{0,1:T(8,128)(2,1)S(1)} %maximum_select_fusion.1), channel_id=1, source_target_pairs={{0,8},{1,9},{2,10},{3,11},{4,12},{5,13},{6,14},{7,15},{8,0},{9,1},... | collective-permute-start | bytes 3538952 | tf_op jit(solution)/shard_map/ppermute | solution.py:293
  198.5 16.7 %copy-start.3 = (bf16[1,8,8,24,128]{4,3,2,1,0:T(8,128)(2,1)S(1)}, bf16[1,8,8,24,128]{4,3,2,1,0:T(8,128)(2,1)}, u32[]{:S(2)}) copy-start(bf16[1,8,8,24,128]{4,3,2,1,0:T(8,128)(2,1)} %get-tuple-element.14) | copy-start | bytes 1179652
  198.6 15.5 %collective-permute-start.5 = (bf16[12,4,24,128]{3,2,1,0:T(8,128)(2,1)S(1)}, bf16[12,4,24,128]{3,2,1,0:T(8,128)(2,1)S(1)}, u32[]{:S(2)}, u32[]{:S(2)}) collective-permute-start(bf16[12,4,24,128]{3,2,1,0:T(8,128)(2,1)S(1)} %pad_maximum_fusion.7), channel_id=1, source_target_pairs={{0,1},{1,2},{2,3},{3,4},{4,5},{5,6},{6,7},{7,0},{8,9},{9,10},{10,1... | collective-permute-start | bytes 884744 | tf_op jit(solution)/shard_map/ppermute | solution.py:251
  200.4 14.9 %collective-permute-start.4 = (bf16[4,12,24,128]{3,2,1,0:T(8,128)(2,1)S(1)}, bf16[4,12,24,128]{3,2,1,0:T(8,128)(2,1)S(1)}, u32[]{:S(2)}, u32[]{:S(2)}) collective-permute-start(bf16[4,12,24,128]{3,2,1,0:T(8,128)(2,1)S(1)} %pad_maximum_fusion.6), channel_id=1, source_target_pairs={{0,8},{8,16},{16,24},{24,32},{32,40},{40,48},{48,56},{56,64},{64,7... | collective-permute-start | bytes 884744 | tf_op jit(solution)/shard_map/ppermute | solution.py:249
  200.4 14.8 %collective-permute-start.3 = (bf16[4,4,24,128]{3,2,1,0:T(8,128)(2,1)S(1)}, bf16[4,4,24,128]{3,2,1,0:T(8,128)(2,1)S(1)}, u32[]{:S(2)}, u32[]{:S(2)}) collective-permute-start(bf16[4,4,24,128]{3,2,1,0:T(8,128)(2,1)S(1)} %get-tuple-element.36), channel_id=1, source_target_pairs={{0,9},{1,10},{2,11},{3,12},{4,13},{5,14},{6,15},{7,8},{8,17},{9,18... | collective-permute-start | bytes 294920 | tf_op jit(solution)/shard_map/ppermute | solution.py:253

commit v2 on v1

--- a/solution.py
+++ b/solution.py
@@ -13,6 +13,7 @@
 C = 128
 T = 512
 KC = 128
+HALF = 2 * T + C
 SHIFT = 4
 SCALE = HD**-0.5
 EXPC = SCALE / math.log(2.0)
@@ -53,21 +54,57 @@
     return out.astype(BF)
 
 
+INNER = [(0, 0, 4, 4, 0, 0, 8, 8)]
+RIM = [
+    (0, 0, 12, 4, 0, 0, 4, 8),
+    (0, 1, 0, 0, 4, 0, 4, 8),
+    (1, 0, 4, 12, 0, 0, 8, 4),
+    (1, 2, 0, 0, 0, 4, 8, 4),
+    (2, 0, 12, 12, 0, 0, 4, 4),
+    (2, 1, 0, 8, 4, 0, 4, 4),
+    (2, 2, 8, 0, 0, 4, 4, 4),
+    (2, 3, 0, 0, 4, 4, 4, 4),
+]
+
+
 def kernel(first, *refs):
-    xs_ref, adj_ref, gamma_ref, w_ref, wT_ref, wproj_ref, bias_ref = refs[:7]
+    pieces = INNER if first else RIM
+    xs_hbm, adj_hbm, gamma_ref, w_ref, wT_ref, wproj_ref, bias_ref = refs[:7]
     if first:
-        gin_ref, dbias_ref, small_ref = refs[7:10]
-        scratch = refs[10:]
+        gin_hbm, dbias_ref, small_ref = refs[7:10]
+        rest = refs[10:]
+        ends = [gin_hbm]
     else:
-        acc_ref, accs_ref = refs[7:9]
-        gin_ref, dbias_out, small_ref = refs[9:12]
-        dbias_ref = refs[12]
-        scratch = refs[13:]
-    (biasT_s, xh_s, adj_s, rstd_s, qext_s, gz_s, kext_s, v_s, kT_s, vT_s, gT_s, attT_s, dT_s, dn_s, u_s, e_s, ds_s) = scratch
+        halos = refs[7:10]
+        acc_ref, accs_ref, _ = refs[10:13]
+        ends = refs[13:17]
+        away_ref, keep_ref = refs[17:19]
+        dbias_ref, small_ref = refs[19:21]
+        rest = refs[21:]
+    in_sem, out_sem, blk_s, gin_s = rest[:4]
+    (biasT_s, xh_s, adj_s, rstd_s, qext_s, gz_s, kext_s, v_s, kT_s, vT_s, gT_s, attT_s, dT_s, dn_s, u_s, e_s, ds_s) = rest[4:]
+
+    def arriving(n, which):
+        block, origin, x, y, bx, by, ex, ey = pieces[n]
+        if origin:
+            src = halos[origin - 1].at[which, pl.ds(x, ex), pl.ds(y, ey)]
+        else:
+            src = (adj_hbm if which else xs_hbm).at[pl.ds(x, ex), pl.ds(y, ey)]
+        dst = blk_s.at[which, block, pl.ds(bx, ex), pl.ds(by, ey)]
+        return pltpu.make_async_copy(src, dst, in_sem.at[which, n])
+
+    def leaving(n):
+        block, origin, x, y, bx, by, ex, ey = pieces[n]
+        src = gin_s.at[block, pl.ds(bx, ex), pl.ds(by, ey)]
+        return pltpu.make_async_copy(src, ends[origin].at[pl.ds(x, ex), pl.ds(y, ey)], out_sem.at[n])
+
     step = pl.program_id(0)
 
     @pl.when(step == 0)
     def _():
+        for n in range(len(pieces)):
+            arriving(n, 0).start()
+            arriving(n, 1).start()
         for h in range(HEADS):
             biasT_s[h] = bias_ref[h].T * (1.0 / SCALE)
         if first:
@@ -86,16 +123,25 @@
     else:
         edge_x = (lax.axis_index("gx") == lax.axis_size("gx") - 1) & (step != 1)
         edge_y = (lax.axis_index("gy") == lax.axis_size("gy") - 1) & (step != 0)
+    for block in sorted({p[0] for p in pieces}):
+
+        @pl.when(step == block)
+        def _(block=block):
+            for n, piece in enumerate(pieces):
+                if piece[0] == block:
+                    arriving(n, 0).wait()
+                    arriving(n, 1).wait()
+
     ones = jnp.full((C, C), 1.0 / C, BF)
     low = lax.broadcasted_iota(jnp.int32, (64, 8, C), 1) < SHIFT
-    xb=xs_ref[...].reshape(64*24,C)
+    xb=blk_s[0, step].reshape(64*24,C)
     mu=dot(xb,ones)
     cen=xb.astype(F32)-mu
     var=dot((cen*cen).astype(BF),ones)
     rstd=lax.rsqrt(var+1e-5)
     rstd_s[...]=rstd.reshape(64,24,C)
     xh=(cen*rstd).reshape(64,3,8,C)
-    a=adj_ref[...].reshape(64,3,8,C).astype(F32)
+    a=blk_s[1, step].reshape(64,3,8,C).astype(F32)
     for z in range(3):
         z1=(z+1)%3
         xh_s[z]=pltpu.roll(jnp.where(low,xh[:,z1],xh[:,z]),SHIFT,1).reshape(T,C)
@@ -187,27 +233,61 @@
         hi=dn_s[zc].reshape(64,8,C)
         r=pltpu.roll(jnp.where(low,hi,lo),SHIFT,1)
         res=a[:,zc]+rstd_s[:,8*zc:8*zc+8]*r
-        gin_ref[:,:,8*zc:8*zc+8]=res.astype(BF).reshape(8,8,8,C)
-
-    if not first:
-        @pl.when(step == pl.num_programs(0) - 1)
-        def _():
-            for h in range(HEADS):
-                dbias_out[h] = dbias_ref[h].T.astype(BF)
-
-
-def sublayer(first, blocks, operands):
+        gin_s[step,:,:,8*zc:8*zc+8]=res.astype(BF).reshape(8,8,8,C)
+
+    for block in sorted({p[0] for p in pieces}):
+
+        @pl.when(step == block)
+        def _(block=block):
+            for n, piece in enumerate(pieces):
+                if piece[0] == block:
+                    leaving(n).start()
+
+    @pl.when(step == pl.num_programs(0) - 1)
+    def _():
+        if not first:
+            mine = lax.axis_index("gx") % 2
+            table = jnp.concatenate([small_ref[:C], small_ref[C : 4 * C].T], axis=1)
+            gain = jnp.concatenate(
+                [jnp.sum(small_ref[4 * C :], axis=0, keepdims=True), jnp.zeros((1, 3 * C), F32)], axis=1
+            )
+            gain = jnp.where(lax.broadcasted_iota(jnp.int32, (C, T), 0) == 0, gain, 0.0)
+            for j in range(2):
+                away_ref[j * T : (j + 1) * T] = dbias_ref[2 * (1 - mine) + j].T.astype(BF)
+                keep_ref[j * T : (j + 1) * T] = dbias_ref[2 * mine + j].T
+            away_ref[2 * T :] = jnp.where(mine == 1, table, gain).astype(BF)
+            keep_ref[2 * T :] = jnp.where(mine == 0, table, gain)
+        for n in range(len(pieces)):
+            leaving(n).wait()
+
+
+def sublayer(first, operands):
     def whole(shape):
         return pl.BlockSpec(shape, lambda i: (0,) * len(shape))
 
-    block = pl.BlockSpec((pl.Squeezed(), 8, 8, 24, C), lambda i: (i, 0, 0, 0, 0))
+    anywhere = pl.BlockSpec(memory_space=pl.ANY)
     square = (HEADS, T, T)
-    ins = [block, block, whole((1, C)), whole((C, 3 * C)), whole((3 * C, C)), whole((C, C)), whole(square)]
-    scratch = []
-    if not first:
-        ins += [whole(square), whole((4 * C + 8, C))]
-        scratch = [pltpu.VMEM(square, F32)]
+    small = (4 * C + 8, C)
+    grid_shape = (16, 16, 24, C)
+    blocks = 1 if first else 3
+    pieces = INNER if first else RIM
+    ins = [anywhere, anywhere, whole((1, C)), whole((C, 3 * C)), whole((3 * C, C)), whole((C, C)), whole(square)]
+    if first:
+        outs = [anywhere, whole(square), whole(small)]
+        shapes = [(grid_shape, BF), (square, F32), (small, F32)]
+        scratch = []
+        aliases = {}
+    else:
+        ins += [anywhere] * 3 + [whole(square), whole(small), anywhere]
+        outs = [anywhere] * 4 + [whole((HALF, T)), whole((HALF, T))]
+        shapes = [(grid_shape, BF), ((4, 12, 24, C), BF), ((12, 4, 24, C), BF), ((4, 4, 24, C), BF), ((HALF, T), BF), ((HALF, T), F32)]
+        scratch = [pltpu.VMEM(square, F32), pltpu.VMEM(small, F32)]
+        aliases = {12: 0}
     scratch += [
+        pltpu.SemaphoreType.DMA((2, len(pieces))),
+        pltpu.SemaphoreType.DMA((len(pieces),)),
+        pltpu.VMEM((2, blocks, 8, 8, 24, C), BF),
+        pltpu.VMEM((blocks, 8, 8, 24, C), BF),
         pltpu.VMEM(square, F32),
         pltpu.VMEM((3, T, C), F32),
         pltpu.VMEM((3, T, C), BF),
@@ -230,17 +310,41 @@
         functools.partial(kernel, first),
         grid=(blocks,),
         in_specs=ins,
-        out_specs=[block, whole(square), whole((4 * C + 8, C))],
-        out_shape=[
-            jax.ShapeDtypeStruct((blocks, 8, 8, 24, C), BF),
-            jax.ShapeDtypeStruct(square, F32 if first else BF),
-            jax.ShapeDtypeStruct((4 * C + 8, C), F32),
-        ],
+        out_specs=outs,
+        out_shape=[jax.ShapeDtypeStruct(shape, dtype) for shape, dtype in shapes],
         scratch_shapes=scratch,
+        input_output_aliases=aliases,
         compiler_params=pltpu.CompilerParams(vmem_limit_bytes=58 * 1024 * 1024),
         cost_estimate=pl.CostEstimate(flops=blocks * 12 * 10**9, bytes_accessed=blocks * 10**7, transcendentals=0),
-        name="window_grads",
+        name="inner_windows" if first else "rim_windows",
     )(*operands)
+
+
+def spread_kernel(mine_ref, own_ref, got_ref, out_ref):
+    @pl.when(pl.program_id(0) == 0)
+    def _():
+        out_ref[...] = own_ref[...].astype(F32)
+
+    @pl.when(pl.program_id(0) == 1)
+    def _():
+        out_ref[...] = got_ref[...].astype(F32)
+
+
+def spread(mine, own, got):
+    return pl.pallas_call(
+        spread_kernel,
+        grid_spec=pltpu.PrefetchScalarGridSpec(
+            num_scalar_prefetch=1,
+            grid=(2, 2),
+            in_specs=[
+                pl.BlockSpec((T, T), lambda s, j, m: (jnp.where(s == 0, j, 1), 0)),
+                pl.BlockSpec((T, T), lambda s, j, m: (jnp.where(s == 0, 0, j), 0)),
+            ],
+            out_specs=pl.BlockSpec((pl.Squeezed(), T, T), lambda s, j, m: (jnp.where(s == 0, m[0], 1 - m[0]) * 2 + j, 0, 0)),
+        ),
+        out_shape=jax.ShapeDtypeStruct((HEADS, T, T), F32),
+        name="spread",
+    )(mine.reshape(1), own, got)
 
 
 def shifted(values, by_x, by_y):
@@ -253,25 +357,27 @@
     return lax.ppermute(values, ("gx", "gy"), pairs)
 
 
-def flip_pairs(order):
+CORE = (("gx", 1), ("gx", 1))
+HALVED = [
+    (("gx", 2), ("gy", 1)),
+    (("gx", 4), ("gy", 2)),
+    (("gx", 8), ("gy", 4)),
+]
+WHOLE = [
+    (("gy", 1), ("gx", 2)),
+    (("gy", 2), ("gx", 4)),
+    (("gy", 4), ("gx", 8)),
+]
+
+
+def swap(values, order):
     pairs = []
     for i in range(16):
         for j in range(8):
             axis, bit = order[i & 1]
             k, l = (i ^ bit, j) if axis == "gx" else (i, j ^ bit)
             pairs.append((i * 8 + j, k * 8 + l))
-    return pairs
-
-
-STEPS = [
-    (("gx", 1), ("gx", 1)),
-    (("gx", 2), ("gy", 1)),
-    (("gx", 4), ("gy", 2)),
-    (("gy", 1), ("gx", 2)),
-    (("gy", 2), ("gx", 4)),
-    (("gx", 8), ("gy", 4)),
-    (("gy", 4), ("gx", 8)),
-]
+    return lax.ppermute(values, ("gx", "gy"), pairs)
 
 
 def my_bit(order):
@@ -280,26 +386,29 @@
     return jnp.where(gx % 2 == 0, bits[0], bits[1])
 
 
-def summed(values):
-    for order in STEPS:
+def summed(away, keep):
+    values = keep + swap(away, CORE).astype(F32)
+    for order in HALVED:
         half = values.shape[0] // 2
         mine = my_bit(order)
-        away = lax.dynamic_slice_in_dim(values, (1 - mine) * half, half)
+        away = lax.dynamic_slice_in_dim(values, (1 - mine) * half, half).astype(BF)
         keep = lax.dynamic_slice_in_dim(values, mine * half, half)
-        got = lax.ppermute(away, ("gx", "gy"), flip_pairs(order))
-        values = (keep.astype(F32) + got.astype(F32)).astype(BF)
-    for order in reversed(STEPS):
+        values = keep + swap(away, order).astype(F32)
+    for order in WHOLE:
+        values = values + swap(values, order)
+    values = values.astype(BF)
+    for order in reversed(HALVED):
         mine = my_bit(order)
-        got = lax.ppermute(values, ("gx", "gy"), flip_pairs(order))
+        got = swap(values, order)
         values = jnp.where(mine == 0, jnp.concatenate([values, got]), jnp.concatenate([got, values]))
-    return values
+    return values, swap(values, CORE)
 
 
 def body(retained_source, incoming_adjoint, rescale_multiplier, triple_projection_matrix, w_proj, pos_bias):
-    both = jnp.stack([retained_source, incoming_adjoint])
-    from_x = shifted(both[:, :4, 4:], -1, 0)
-    from_y = shifted(both[:, 4:, :4], 0, -1)
-    from_xy = shifted(both[:, :4, :4], -1, -1)
+    both = (retained_source, incoming_adjoint)
+    from_x = shifted(jnp.stack([v[:4, 4:] for v in both]), -1, 0)
+    from_y = shifted(jnp.stack([v[4:, :4] for v in both]), 0, -1)
+    from_xy = shifted(jnp.stack([v[:4, :4] for v in both]), -1, -1)
     params = (
         rescale_multiplier.reshape(1, C),
         triple_projection_matrix,
@@ -307,41 +416,20 @@
         w_proj,
         pos_bias,
     )
-    inner = both[:, 4:12, 4:12]
-    gin_a, acc, acc_small = sublayer(True, 1, (inner[0][None], inner[1][None]) + params)
-    rim = jnp.stack(
-        [
-            jnp.concatenate([both[:, 12:, 4:12], from_x[:, :, :8]], axis=1),
-            jnp.concatenate([both[:, 4:12, 12:], from_y[:, :8]], axis=2),
-            jnp.concatenate(
-                [
-                    jnp.concatenate([both[:, 12:, 12:], from_y[:, 8:]], axis=2),
-                    jnp.concatenate([from_x[:, :, 8:], from_xy], axis=2),
-                ],
-                axis=1,
-            ),
-        ],
-        axis=1,
-    )
-    gin_b, grad_bias, small = sublayer(False, 3, (rim[0], rim[1]) + params + (acc, acc_small))
-    bx, by, bc = gin_b[0], gin_b[1], gin_b[2]
-    back_x = shifted(jnp.concatenate([bx[4:], bc[4:, :4]], axis=1), 1, 0)
-    back_y = shifted(jnp.concatenate([by[:, 4:], bc[:4, 4:]], axis=0), 0, 1)
-    back_xy = shifted(bc[4:, 4:], 1, 1)
-    grad_input = jnp.concatenate(
-        [
-            jnp.concatenate([back_xy, back_x], axis=1),
-            jnp.concatenate([back_y[:8], gin_a[0], by[:, :4]], axis=1),
-            jnp.concatenate([back_y[8:], bx[:4], bc[:4, :4]], axis=1),
-        ],
-        axis=0,
-    )
-    rows = HEADS * T * T // C
-    packed = jnp.concatenate([grad_bias.reshape(rows, C), small.astype(BF), jnp.zeros((1024 - small.shape[0], C), BF)])
-    total = summed(packed)
-    grad_bias = total[:rows].astype(F32).reshape(HEADS, T, T)
-    rest = total[rows : rows + small.shape[0]].astype(F32)
-    return (grad_input, grad_bias, rest[:C], rest[C : 4 * C].T, jnp.sum(rest[4 * C :], axis=0))
+    gin, acc, acc_small = sublayer(True, both + params)
+    gin, back_x, back_y, back_xy, away, keep = sublayer(False, both + params + (from_x, from_y, from_xy, acc, acc_small, gin))
+    back_x = shifted(back_x, 1, 0)
+    back_y = shifted(back_y, 0, 1)
+    back_xy = shifted(back_xy, 1, 1)
+    gin = lax.dynamic_update_slice(gin, back_x, (0, 4, 0, 0))
+    gin = lax.dynamic_update_slice(gin, back_y, (4, 0, 0, 0))
+    gin = lax.dynamic_update_slice(gin, back_xy, (0, 0, 0, 0))
+    own, got = summed(away, keep)
+    mine = lax.axis_index("gx") % 2
+    grad_bias = spread(mine, own, got)
+    table = jnp.where(mine == 0, own[2 * T :], got[2 * T :]).astype(F32)
+    gain = jnp.where(mine == 0, got[2 * T, :C], own[2 * T, :C]).astype(F32)
+    return (gin, grad_bias, table[:, :C], table[:, C:], gain)
 
 
 def solution(mesh):

time: 235 us -> 201 us (0.86)
  local copies, waits for them, and re-layouts: 31.5 us -> 8.76 us
  starting transfers between devices: 33.8 us -> 22.6 us
  other arithmetic: 13.8 us -> 5.01 us
  Pallas kernels: 77.5 us -> 85 us
    reshape x4 -> x0, local copies, waits for them, and re-layouts: 16.5 us -> none  [the longest x2 10.5 us: body(): grad_bias = total[:rows].astype(F32).reshape(HEADS, T, T)]
    ppermute x14 -> x11, starting transfers between devices: 21 us -> 9.93 us  [swap(): return lax.ppermute(values, ('gx', 'gy'), pairs)]
    ppermute x2, starting transfers between devices: 1.87 us -> 7.95 us  [shifted(): return lax.ppermute(values, 'gy', [(i, (i + by_y) % ny) for i in range(ny)])]
    ppermute x2, starting transfers between devices: 7.92 us -> 3.28 us  [shifted(): return lax.ppermute(values, ('gx', 'gy'), pairs)]
    pallas_call x0 -> x1, Pallas kernels: none -> 4.52 us  [spread(): pl.pallas_call(spread_kernel, grid_spec=pltpu.PrefetchScalarGridSpec(num_...]
    slice x12 -> x2, local copies, waits for them, and re-layouts: 5.73 us -> 1.4 us  [body(): return (gin, grad_bias, table[:, :C], table[:, C:], gain)]
    concatenate x3 -> x0, other arithmetic: 3.69 us -> none  [the longest x1 3.63 us: body(): jnp.concatenate([jnp.concatenate([back_xy, back_x], axis=1), jnp.concaten...]
    concatenate x1 -> x0, local copies, waits for them, and re-layouts: 3.53 us -> none  [body(): jnp.concatenate([grad_bias.reshape(rows, C), small.astype(BF), jnp.zeros(...]
  transfers between devices with their start and end apart: 20 -> 17, of which waited for: 15 -> 13; matrix products, arithmetic and copies ran while one was open for 5% -> 3% of each run, Pallas kernels for 9% -> 11%
where the time goes in v2:
time: 201 us
  Pallas kernels  85 us (42%)
  waiting for transfers between devices  78.4 us (39%)
  starting transfers between devices  22.6 us (11%)
  local copies, waits for them, and re-layouts  8.76 us (4%)
  other arithmetic  5.01 us (2%)
    pallas_call x2, Pallas kernels, sublayer(): pl.pallas_call(functools.partial(kernel, first), grid=(blocks,), in_specs...  80.5 us
    ppermute x11, waiting for transfers between devices, swap(): return lax.ppermute(values, ('gx', 'gy'), pairs)  63.7 us
    ppermute x2, waiting for transfers between devices, shifted(): return lax.ppermute(values, 'gy', [(i, (i + by_y) % ny) for i in range(ny)])  11.8 us
    ppermute x11, starting transfers between devices, swap(): return lax.ppermute(values, ('gx', 'gy'), pairs)  9.93 us
    ppermute x2, starting transfers between devices, shifted(): return lax.ppermute(values, 'gy', [(i, (i + by_y) % ny) for i in range(ny)])  7.95 us
    pallas_call x1, Pallas kernels, spread(): pl.pallas_call(spread_kernel, grid_spec=pltpu.PrefetchScalarGridSpec(num_...  4.52 us
  transfers between devices with their start and end apart: 17, of which 13 were waited for; matrix products, arithmetic and copies ran while one was open for 3% of the time, Pallas kernels for 11%

profile of v2, /device:TPU:1, one launch (start us, length us, event | category | flops | bytes accessed | tf_op | source)
XLA Modules:
  0.0 201.0 jit_solution(103893884747491666)
XLA Ops:
  0.6 1.1 slice_bitcast_fusion.2
  1.8 1.5 collective-permute-start
  3.3 1.1 slice_bitcast_fusion
  4.5 6.5 %collective-permute-start.1 = (bf16[2,12,4,24,128]{4,3,2,1,0:T(8,128)(2,1)S(1)}, bf16[2,12,4,24,128]{4,3,2,1,0:T(8,128)(2,1)S(1)}, u32[]{:S(2)}, u32[]{:S(2)}) collective-permute-start(bf16[2,12,4,24,128]{4,3,2,1,0:T(8,128)(2,1)S(1)} %pad_maximum_fusion.1), channel_id=1, source_target_pairs={{0,7},{1,0},{2,1},{3,2},{4,3},{5,4},{6,5},{7,6},{8,15},{9,8},{10,9... | collective-permute-start | bytes 1769480 | tf_op jit(solution)/shard_map/ppermute | solution.py:355
  11.0 1.0 slice_bitcast_fusion.4
  12.0 3.3 %collective-permute-start.2 = (bf16[2,4,4,24,128]{4,3,2,1,0:T(8,128)(2,1)S(1)}, bf16[2,4,4,24,128]{4,3,2,1,0:T(8,128)(2,1)S(1)}, u32[]{:S(2)}, u32[]{:S(2)}) collective-permute-start(bf16[2,4,4,24,128]{4,3,2,1,0:T(8,128)(2,1)S(1)} %pad_maximum_fusion.2), channel_id=1, source_target_pairs={{0,127},{1,120},{2,121},{3,122},{4,123},{5,124},{6,125},{7,126},{8... | collective-permute-start | bytes 589832 | tf_op jit(solution)/shard_map/ppermute | solution.py:357
  15.3 0.7 copy.12
  16.1 23.0 %inner_windows.1 = (bf16[16,16,24,128]{3,2,1,0:T(8,128)(2,1)}, f32[4,512,512]{2,1,0:T(8,128)}, f32[520,128]{1,0:T(8,128)}) custom-call(bf16[16,16,24,128]{3,2,1,0:T(8,128)(2,1)} %refs_0_.3, bf16[16,16,24,128]{3,2,1,0:T(8,128)(2,1)} %refs_1_.3, f32[1,128]{1,0:T(1,128)} %bitcast.22, bf16[128,384]{1,0:T(8,128)(2,1)} %refs_3_.3, bf16[384,128]{1,0:T(8,128)(2,1)} %bitcast.20, ...), custom_call_target="tpu_custom_call" | custom-call | flops 12000000000 | bytes 10000000 | tf_op jit(solution)/shard_map/inner_windows/pallas_call | solution.py:309
  39.2 0.6 copy-done.7
  39.8 0.2 copy-done.3
  40.0 0.2 copy-done.4
  40.2 57.5 %rim_windows.1 = (bf16[16,16,24,128]{3,2,1,0:T(8,128)(2,1)}, bf16[4,12,24,128]{3,2,1,0:T(8,128)(2,1)}, bf16[12,4,24,128]{3,2,1,0:T(8,128)(2,1)}, bf16[4,4,24,128...) custom-call(bf16[16,16,24,128]{3,2,1,0:T(8,128)(2,1)} %refs_0_.3, ...), custom_call_target="tpu_custom_call", output_to_operand_aliasing={{0}: (12, {})} | custom-call | flops 35999997952 | bytes 30000000 | tf_op jit(solution)/shard_map/rim_windows/pallas_call | solution.py:309
  97.7 0.1 collective-permute-start.6
  97.9 3.0 %collective-permute-done.6 = bf16[1152,512]{1,0:T(8,128)(2,1)S(1)} collective-permute-done((bf16[1152,512]{1,0:T(8,128)(2,1)}, bf16[1152,512]{1,0:T(8,128)(2,1)S(1)}, u32[]{:S(2)}, u32[]{:S(2)}) %collective-permute-start.6) | collective-permute-done | bytes 1179680 | tf_op jit(solution)/shard_map/ppermute | solution.py:380
  100.8 2.0 %convert_add_fusion = f32[1152,512]{1,0:T(8,128)S(1)} fusion(f32[1152,512]{1,0:T(8,128)} %get-tuple-element.21, bf16[1152,512]{1,0:T(8,128)(2,1)S(1)} %collective-permute-done.6), kind=kLoop, calls=%fused_computation | loop fusion | flops 1179648 | bytes 5898240 | tf_op jit(solution)/shard_map/add | solution.py:390
  103.0 1.4 collective-permute-start.7
  104.4 7.8 %collective-permute-done.7 = bf16[576,512]{1,0:T(8,128)(2,1)} collective-permute-done((bf16[576,512]{1,0:T(8,128)(2,1)S(1)}, bf16[576,512]{1,0:T(8,128)(2,1)}, u32[]{:S(2)}, u32[]{:S(2)}) %collective-permute-start.7) | collective-permute-done | bytes 589856 | tf_op jit(solution)/shard_map/ppermute | solution.py:380
  112.2 1.2 convert_add_fusion.1
  113.5 0.1 collective-permute-start.8
  113.7 7.3 %collective-permute-done.8 = bf16[288,512]{1,0:T(8,128)(2,1)S(1)} collective-permute-done((bf16[288,512]{1,0:T(8,128)(2,1)S(1)}, bf16[288,512]{1,0:T(8,128)(2,1)S(1)}, u32[]{:S(2)}, u32[]{:S(2)}) %collective-permute-start.8) | collective-permute-done | bytes 294944 | tf_op jit(solution)/shard_map/ppermute | solution.py:380
  121.1 0.8 collective-permute-start.9
  121.8 6.0 %collective-permute-done.9 = bf16[144,512]{1,0:T(8,128)(2,1)S(1)} collective-permute-done((bf16[144,512]{1,0:T(8,128)(2,1)S(1)}, bf16[144,512]{1,0:T(8,128)(2,1)S(1)}, u32[]{:S(2)}, u32[]{:S(2)}) %collective-permute-start.9) | collective-permute-done | bytes 147488 | tf_op jit(solution)/shard_map/ppermute | solution.py:380
  127.9 0.1 collective-permute-start.10
  128.0 5.9 %collective-permute-done.10 = f32[144,512]{1,0:T(8,128)S(1)} collective-permute-done((f32[144,512]{1,0:T(8,128)S(1)}, f32[144,512]{1,0:T(8,128)S(1)}, u32[]{:S(2)}, u32[]{:S(2)}) %collective-permute-start.10) | collective-permute-done | bytes 294944 | tf_op jit(solution)/shard_map/ppermute | solution.py:380
  133.9 0.1 collective-permute-start.11
  134.0 7.4 %collective-permute-done.11 = f32[144,512]{1,0:T(8,128)S(1)} collective-permute-done((f32[144,512]{1,0:T(8,128)S(1)}, f32[144,512]{1,0:T(8,128)S(1)}, u32[]{:S(2)}, u32[]{:S(2)}) %collective-permute-start.11) | collective-permute-done | bytes 294944 | tf_op jit(solution)/shard_map/ppermute | solution.py:380
  141.4 0.4 collective-permute-start.12
  141.8 5.7 %collective-permute-done.12 = f32[144,512]{1,0:T(8,128)S(1)} collective-permute-done((f32[144,512]{1,0:T(8,128)S(1)}, f32[144,512]{1,0:T(8,128)S(1)}, u32[]{:S(2)}, u32[]{:S(2)}) %collective-permute-start.12) | collective-permute-done | bytes 294944 | tf_op jit(solution)/shard_map/ppermute | solution.py:380
  147.5 0.1 collective-permute-start.13
  147.6 5.5 %collective-permute-done.13 = bf16[144,512]{1,0:T(8,128)(2,1)S(1)} collective-permute-done((bf16[144,512]{1,0:T(8,128)(2,1)S(1)}, bf16[144,512]{1,0:T(8,128)(2,1)S(1)}, u32[]{:S(2)}, u32[]{:S(2)}) %collective-permute-start.13) | collective-permute-done | bytes 147488 | tf_op jit(solution)/shard_map/ppermute | solution.py:380
  153.2 0.1 collective-permute-start.14
  153.3 7.0 %collective-permute-done.14 = bf16[288,512]{1,0:T(8,128)(2,1)S(1)} collective-permute-done((bf16[288,512]{1,0:T(8,128)(2,1)S(1)}, bf16[288,512]{1,0:T(8,128)(2,1)S(1)}, u32[]{:S(2)}, u32[]{:S(2)}) %collective-permute-start.14) | collective-permute-done | bytes 294944 | tf_op jit(solution)/shard_map/ppermute | solution.py:380
  160.3 0.2 maximum_select_fusion.1
  160.6 0.9 collective-permute-start.15
  161.5 8.2 %collective-permute-done.15 = bf16[576,512]{1,0:T(8,128)(2,1)S(1)} collective-permute-done((bf16[576,512]{1,0:T(8,128)(2,1)S(1)}, bf16[576,512]{1,0:T(8,128)(2,1)S(1)}, u32[]{:S(2)}, u32[]{:S(2)}) %collective-permute-start.15) | collective-permute-done | bytes 589856 | tf_op jit(solution)/shard_map/ppermute | solution.py:380
  169.7 0.5 maximum_select_fusion.own_ref
  170.2 5.9 %collective-permute-start.16 = (bf16[1152,512]{1,0:T(8,128)(2,1)S(1)}, bf16[1152,512]{1,0:T(8,128)(2,1)S(1)}, u32[]{:S(2)}, u32[]{:S(2)}) collective-permute-start(bf16[1152,512]{1,0:T(8,128)(2,1)S(1)} %maximum_select_fusion.own_ref), channel_id=1, source_target_pairs={{0,8},{1,9},{2,10},{3,11},{4,12},{5,13},{6,14},{7,15},{8,0},{9,1},... | collective-permute-start | bytes 3538952 | tf_op jit(solution)/shard_map/ppermute | solution.py:380
  176.2 1.4 collective-permute-start.4
  177.6 2.2 %collective-permute-done.3 = bf16[4,12,24,128]{3,2,1,0:T(8,128)(2,1)S(1)} collective-permute-done((bf16[4,12,24,128]{3,2,1,0:T(8,128)(2,1)S(1)}, bf16[4,12,24,128]{3,2,1,0:T(8,128)(2,1)S(1)}, u32[]{:S(2)}, u32[]{:S(2)}) %collective-permute-start.3) | collective-permute-done | bytes 294944 | tf_op jit(solution)/shard_map/ppermute | solution.py:353
  179.8 0.8 constant_dynamic-update-slice_fusion.2
  180.6 11.8 %collective-permute-done.4 = bf16[12,4,24,128]{3,2,1,0:T(8,128)(2,1)S(1)} collective-permute-done((bf16[12,4,24,128]{3,2,1,0:T(8,128)(2,1)S(1)}, bf16[12,4,24,128]{3,2,1,0:T(8,128)(2,1)S(1)}, u32[]{:S(2)}, u32[]{:S(2)}) %collective-permute-start.4) | collective-permute-done | bytes 294944 | tf_op jit(solution)/shard_map/ppermute | solution.py:355
  192.4 0.8 constant_dynamic-update-slice_fusion.1
  193.1 0.7 collective-permute-done.5
  193.8 0.7 constant_dynamic-update-slice_fusion
  194.5 0.7 slice.50
  195.2 0.7 slice.51
  195.9 0.5 fusion.2
  196.4 4.5 %spread.1 = f32[4,512,512]{2,1,0:T(8,128)} custom-call(s32[1]{0:T(128)} %bitcast.8.mine_ref, bf16[1152,512]{1,0:T(8,128)(2,1)} %copy-done, bf16[1152,512]{1,0:T(8,128)(2,1)} %copy-done.1), custom_call_target="tpu_custom_call" | custom-call | tf_op jit(solution)/shard_map/spread/pallas_call | solution.py:334
  (34 shorter events, 0.7 us)
Async XLA Ops:
  1.8 13.5 %copy-start.2 = (bf16[128,384]{1,0:T(8,128)(2,1)S(1)}, bf16[128,384]{1,0:T(8,128)(2,1)}, u32[]{:S(2)}) copy-start(bf16[128,384]{1,0:T(8,128)(2,1)} %refs_3_.3) | copy-start | bytes 294916
  1.8 37.3 %collective-permute-start = (bf16[2,4,12,24,128]{4,3,2,1,0:T(8,128)(2,1)S(1)}, bf16[2,4,12,24,128]{4,3,2,1,0:T(8,128)(2,1)S(1)}, u32[]{:S(2)}, u32[]{:S(2)}) collective-permute-start(bf16[2,4,12,24,128]{4,3,2,1,0:T(8,128)(2,1)S(1)} %pad_maximum_fusion), channel_id=1, source_target_pairs={{0,120},{8,0},{16,8},{24,16},{32,24},{40,32},{48,40},{56,48},{64,5... | collective-permute-start | bytes 1769480 | tf_op jit(solution)/shard_map/ppermute | solution.py:353
  4.5 34.6 %collective-permute-start.1 = (bf16[2,12,4,24,128]{4,3,2,1,0:T(8,128)(2,1)S(1)}, bf16[2,12,4,24,128]{4,3,2,1,0:T(8,128)(2,1)S(1)}, u32[]{:S(2)}, u32[]{:S(2)}) collective-permute-start(bf16[2,12,4,24,128]{4,3,2,1,0:T(8,128)(2,1)S(1)} %pad_maximum_fusion.1), channel_id=1, source_target_pairs={{0,7},{1,0},{2,1},{3,2},{4,3},{5,4},{6,5},{7,6},{8,15},{9,8},{10,9... | collective-permute-start | bytes 1769480 | tf_op jit(solution)/shard_map/ppermute | solution.py:355
  12.0 27.1 %collective-permute-start.2 = (bf16[2,4,4,24,128]{4,3,2,1,0:T(8,128)(2,1)S(1)}, bf16[2,4,4,24,128]{4,3,2,1,0:T(8,128)(2,1)S(1)}, u32[]{:S(2)}, u32[]{:S(2)}) collective-permute-start(bf16[2,4,4,24,128]{4,3,2,1,0:T(8,128)(2,1)S(1)} %pad_maximum_fusion.2), channel_id=1, source_target_pairs={{0,127},{1,120},{2,121},{3,122},{4,123},{5,124},{6,125},{7,126},{8... | collective-permute-start | bytes 589832 | tf_op jit(solution)/shard_map/ppermute | solution.py:357
  39.1 0.7 copy-start.7
  39.1 0.8 copy-start.3
  39.1 1.1 copy-start.4
  97.7 3.1 %collective-permute-start.6 = (bf16[1152,512]{1,0:T(8,128)(2,1)}, bf16[1152,512]{1,0:T(8,128)(2,1)S(1)}, u32[]{:S(2)}, u32[]{:S(2)}) collective-permute-start(bf16[1152,512]{1,0:T(8,128)(2,1)} %get-tuple-element.22), channel_id=1, source_target_pairs={{0,8},{1,9},{2,10},{3,11},{4,12},{5,13},{6,14},{7,15},{8,0},{9,1},... | collective-permute-start | bytes 3538952 | tf_op jit(solution)/shard_map/ppermute | solution.py:380
  103.0 9.2 %collective-permute-start.7 = (bf16[576,512]{1,0:T(8,128)(2,1)S(1)}, bf16[576,512]{1,0:T(8,128)(2,1)}, u32[]{:S(2)}, u32[]{:S(2)}) collective-permute-start(bf16[576,512]{1,0:T(8,128)(2,1)S(1)} %dynamic-slice_convert_fusion), channel_id=1, source_target_pairs={{0,16},{1,17},{2,18},{3,19},{4,20},{5,21},{6,22},{7,23},{8,9},{9,8... | collective-permute-start | bytes 1769480 | tf_op jit(solution)/shard_map/ppermute | solution.py:380
  113.5 7.5 %collective-permute-start.8 = (bf16[288,512]{1,0:T(8,128)(2,1)S(1)}, bf16[288,512]{1,0:T(8,128)(2,1)S(1)}, u32[]{:S(2)}, u32[]{:S(2)}) collective-permute-start(bf16[288,512]{1,0:T(8,128)(2,1)S(1)} %dynamic-slice_convert_fusion.1), channel_id=1, source_target_pairs={{0,32},{1,33},{2,34},{3,35},{4,36},{5,37},{6,38},{7,39},{8,10},{9,... | collective-permute-start | bytes 884744 | tf_op jit(solution)/shard_map/ppermute | solution.py:380
  121.1 6.8 %collective-permute-start.9 = (bf16[144,512]{1,0:T(8,128)(2,1)S(1)}, bf16[144,512]{1,0:T(8,128)(2,1)S(1)}, u32[]{:S(2)}, u32[]{:S(2)}) collective-permute-start(bf16[144,512]{1,0:T(8,128)(2,1)S(1)} %dynamic-slice_convert_fusion.2), channel_id=1, source_target_pairs={{0,64},{1,65},{2,66},{3,67},{4,68},{5,69},{6,70},{7,71},{8,12},{9,... | collective-permute-start | bytes 442376 | tf_op jit(solution)/shard_map/ppermute | solution.py:380
  127.9 5.9 %collective-permute-start.10 = (f32[144,512]{1,0:T(8,128)S(1)}, f32[144,512]{1,0:T(8,128)S(1)}, u32[]{:S(2)}, u32[]{:S(2)}) collective-permute-start(f32[144,512]{1,0:T(8,128)S(1)} %convert_add_fusion.3), channel_id=1, source_target_pairs={{0,1},{1,0},{2,3},{3,2},{4,5},{5,4},{6,7},{7,6},{8,24},{9,25},{10,... | collective-permute-start | bytes 884744 | tf_op jit(solution)/shard_map/ppermute | solution.py:380
  133.9 7.5 %collective-permute-start.11 = (f32[144,512]{1,0:T(8,128)S(1)}, f32[144,512]{1,0:T(8,128)S(1)}, u32[]{:S(2)}, u32[]{:S(2)}) collective-permute-start(f32[144,512]{1,0:T(8,128)S(1)} %add.96), channel_id=1, source_target_pairs={{0,2},{1,3},{2,0},{3,1},{4,6},{5,7},{6,4},{7,5},{8,40},{9,41},{10,... | collective-permute-start | bytes 884744 | tf_op jit(solution)/shard_map/ppermute | solution.py:380
  141.4 6.1 %collective-permute-start.12 = (f32[144,512]{1,0:T(8,128)S(1)}, f32[144,512]{1,0:T(8,128)S(1)}, u32[]{:S(2)}, u32[]{:S(2)}) collective-permute-start(f32[144,512]{1,0:T(8,128)S(1)} %add.97), channel_id=1, source_target_pairs={{0,4},{1,5},{2,6},{3,7},{4,0},{5,1},{6,2},{7,3},{8,72},{9,73},{10,... | collective-permute-start | bytes 884744 | tf_op jit(solution)/shard_map/ppermute | solution.py:380
  147.5 5.6 %collective-permute-start.13 = (bf16[144,512]{1,0:T(8,128)(2,1)S(1)}, bf16[144,512]{1,0:T(8,128)(2,1)S(1)}, u32[]{:S(2)}, u32[]{:S(2)}) collective-permute-start(bf16[144,512]{1,0:T(8,128)(2,1)S(1)} %add_convert_fusion), channel_id=1, source_target_pairs={{0,64},{1,65},{2,66},{3,67},{4,68},{5,69},{6,70},{7,71},{8,12},{9,... | collective-permute-start | bytes 442376 | tf_op jit(solution)/shard_map/ppermute | solution.py:380
  153.2 7.2 %collective-permute-start.14 = (bf16[288,512]{1,0:T(8,128)(2,1)S(1)}, bf16[288,512]{1,0:T(8,128)(2,1)S(1)}, u32[]{:S(2)}, u32[]{:S(2)}) collective-permute-start(bf16[288,512]{1,0:T(8,128)(2,1)S(1)} %maximum_select_fusion.2), channel_id=1, source_target_pairs={{0,32},{1,33},{2,34},{3,35},{4,36},{5,37},{6,38},{7,39},{8,10},{9,... | collective-permute-start | bytes 884744 | tf_op jit(solution)/shard_map/ppermute | solution.py:380
  153.3 22.9 %copy-start.6 = (bf16[4,12,24,128]{3,2,1,0:T(8,128)(2,1)S(1)}, bf16[4,12,24,128]{3,2,1,0:T(8,128)(2,1)}, u32[]{:S(2)}) copy-start(bf16[4,12,24,128]{3,2,1,0:T(8,128)(2,1)} %get-tuple-element.18) | copy-start | bytes 884740
  153.3 22.9 %copy-start.5 = (bf16[12,4,24,128]{3,2,1,0:T(8,128)(2,1)S(1)}, bf16[12,4,24,128]{3,2,1,0:T(8,128)(2,1)}, u32[]{:S(2)}) copy-start(bf16[12,4,24,128]{3,2,1,0:T(8,128)(2,1)} %get-tuple-element.19) | copy-start | bytes 884740
  153.3 24.3 %copy-start.8 = (bf16[4,4,24,128]{3,2,1,0:T(8,128)(2,1)S(1)}, bf16[4,4,24,128]{3,2,1,0:T(8,128)(2,1)}, u32[]{:S(2)}) copy-start(bf16[4,4,24,128]{3,2,1,0:T(8,128)(2,1)} %get-tuple-element.20) | copy-start | bytes 294916
  160.6 9.1 %collective-permute-start.15 = (bf16[576,512]{1,0:T(8,128)(2,1)S(1)}, bf16[576,512]{1,0:T(8,128)(2,1)S(1)}, u32[]{:S(2)}, u32[]{:S(2)}) collective-permute-start(bf16[576,512]{1,0:T(8,128)(2,1)S(1)} %maximum_select_fusion.1), channel_id=1, source_target_pairs={{0,16},{1,17},{2,18},{3,19},{4,20},{5,21},{6,22},{7,23},{8,9},{9,8... | collective-permute-start | bytes 1769480 | tf_op jit(solution)/shard_map/ppermute | solution.py:380
  170.2 26.2 %copy-start = (bf16[1152,512]{1,0:T(8,128)(2,1)}, bf16[1152,512]{1,0:T(8,128)(2,1)S(1)}, u32[]{:S(2)}) copy-start(bf16[1152,512]{1,0:T(8,128)(2,1)S(1)} %maximum_select_fusion.own_ref) | copy-start | bytes 3538948
  170.2 24.3 %collective-permute-start.16 = (bf16[1152,512]{1,0:T(8,128)(2,1)S(1)}, bf16[1152,512]{1,0:T(8,128)(2,1)S(1)}, u32[]{:S(2)}, u32[]{:S(2)}) collective-permute-start(bf16[1152,512]{1,0:T(8,128)(2,1)S(1)} %maximum_select_fusion.own_ref), channel_id=1, source_target_pairs={{0,8},{1,9},{2,10},{3,11},{4,12},{5,13},{6,14},{7,15},{8,0},{9,1},... | collective-permute-start | bytes 3538952 | tf_op jit(solution)/shard_map/ppermute | solution.py:380
  176.2 3.7 %collective-permute-start.3 = (bf16[4,12,24,128]{3,2,1,0:T(8,128)(2,1)S(1)}, bf16[4,12,24,128]{3,2,1,0:T(8,128)(2,1)S(1)}, u32[]{:S(2)}, u32[]{:S(2)}) collective-permute-start(bf16[4,12,24,128]{3,2,1,0:T(8,128)(2,1)S(1)} %copy-done.6), channel_id=1, source_target_pairs={{0,8},{8,16},{16,24},{24,32},{32,40},{40,48},{48,56},{56,64},{64,7... | collective-permute-start | bytes 884744 | tf_op jit(solution)/shard_map/ppermute | solution.py:353
  176.2 16.2 %collective-permute-start.4 = (bf16[12,4,24,128]{3,2,1,0:T(8,128)(2,1)S(1)}, bf16[12,4,24,128]{3,2,1,0:T(8,128)(2,1)S(1)}, u32[]{:S(2)}, u32[]{:S(2)}) collective-permute-start(bf16[12,4,24,128]{3,2,1,0:T(8,128)(2,1)S(1)} %copy-done.5), channel_id=1, source_target_pairs={{0,1},{1,2},{2,3},{3,4},{4,5},{5,6},{6,7},{7,0},{8,9},{9,10},{10,1... | collective-permute-start | bytes 884744 | tf_op jit(solution)/shard_map/ppermute | solution.py:355
  177.6 16.3 %collective-permute-start.5 = (bf16[4,4,24,128]{3,2,1,0:T(8,128)(2,1)S(1)}, bf16[4,4,24,128]{3,2,1,0:T(8,128)(2,1)S(1)}, u32[]{:S(2)}, u32[]{:S(2)}) collective-permute-start(bf16[4,4,24,128]{3,2,1,0:T(8,128)(2,1)S(1)} %copy-done.8), channel_id=1, source_target_pairs={{0,9},{1,10},{2,11},{3,12},{4,13},{5,14},{6,15},{7,8},{8,17},{9,18... | collective-permute-start | bytes 294920 | tf_op jit(solution)/shard_map/ppermute | solution.py:357
  194.5 1.9 copy-start.1

commit v3 on v2

v3 whole, which is shorter than its diff:
```python
import functools
import math

import jax
import jax.numpy as jnp
from jax import lax
from jax.experimental import pallas as pl
from jax.experimental.pallas import tpu as pltpu
from jax.sharding import PartitionSpec as P

HEADS = 4
HD = 32
C = 128
T = 512
KC = 256
HALF = 2 * T + C
SHIFT = 4
SCALE = HD**-0.5
EXPC = SCALE / math.log(2.0)
BLOCKED = -(2.0**100)
F32 = jnp.float32
BF = jnp.bfloat16


def dot(a, b):
    return lax.dot_general(a, b, (((1,), (0,)), ((), ())), preferred_element_type=F32)


def dot_nt(a, b):
    return lax.dot_general(a, b, (((1,), (1,)), ((), ())), preferred_element_type=F32)


def half_bits(shape, dim):
    token = lax.broadcasted_iota(jnp.int32, shape, dim)
    return [lax.shift_right_logical(token, s) & 1 for s in (8, 5, 2)]


def key_regions():
    lane = lax.broadcasted_iota(jnp.int32, (T, C), 1)
    out = jnp.zeros((T, C), F32)
    for n, bit in enumerate(half_bits((T, C), 0)):
        out = jnp.where(lane == 2 * n, bit.astype(F32), out)
        out = jnp.where(lane == 2 * n + 1, 1.0 - bit.astype(F32), out)
    return out.astype(BF)


def query_regions(edges):
    row = lax.broadcasted_iota(jnp.int32, (16, T), 0)
    out = jnp.zeros((16, T), F32)
    for n, (bit, edge) in enumerate(zip(half_bits((16, T), 1), edges)):
        weight = jnp.where(edge, BLOCKED, 0.0)
        out = jnp.where(row == 2 * n, (1.0 - bit.astype(F32)) * weight, out)
        out = jnp.where(row == 2 * n + 1, bit.astype(F32) * weight, out)
    return out.astype(BF)


INNER = [(0, 0, 4, 4, 0, 0, 8, 8)]
RIM = [
    (0, 0, 12, 4, 0, 0, 4, 8),
    (0, 1, 0, 0, 4, 0, 4, 8),
    (1, 0, 4, 12, 0, 0, 8, 4),
    (1, 2, 0, 0, 0, 4, 8, 4),
    (2, 0, 12, 12, 0, 0, 4, 4),
    (2, 1, 0, 8, 4, 0, 4, 4),
    (2, 2, 8, 0, 0, 4, 4, 4),
    (2, 3, 0, 0, 4, 4, 4, 4),
]


def arriving(pieces, arrays, blk_s, sem, n, which):
    block, origin, x, y, bx, by, ex, ey = pieces[n]
    if origin:
        src = arrays[1 + origin].at[which, pl.ds(x, ex), pl.ds(y, ey)]
    else:
        src = arrays[which].at[pl.ds(x, ex), pl.ds(y, ey)]
    return pltpu.make_async_copy(src, blk_s.at[which, block, pl.ds(bx, ex), pl.ds(by, ey)], sem.at[which, n])


def start_all(pieces, arrays, blk_s, sem):
    for n in range(len(pieces)):
        for which in range(2):
            arriving(pieces, arrays, blk_s, sem, n, which).start()


def wait_block(pieces, arrays, blk_s, sem, step):
    for block in sorted({p[0] for p in pieces}):

        @pl.when(step == block)
        def _(block=block):
            for n, piece in enumerate(pieces):
                if piece[0] == block:
                    for which in range(2):
                        arriving(pieces, arrays, blk_s, sem, n, which).wait()


def standardized(block):
    ones = jnp.full((C, C), 1.0 / C, BF)
    flat = block.reshape(64 * 24, C)
    centred = flat.astype(F32) - dot(flat, ones)
    rstd = lax.rsqrt(dot((centred * centred).astype(BF), ones) + 1e-5)
    return (centred * rstd).reshape(64, 3, 8, C), rstd.reshape(64, 3, 8, C)


def kernel(first, *refs):
    pieces = INNER if first else RIM
    arrays = refs[:2] if first else refs[:5]
    refs = refs[len(arrays) :]
    gamma_ref, w_ref, wT_ref, wproj_ref, bias_hbm = refs[:5]
    refs = refs[5:]
    if first:
        dT_ref, dbias_ref, small_ref = refs[:3]
        refs = refs[3:]
    else:
        acc_hbm, accs_ref = refs[:2]
        dT_ref, away_ref, keep_ref = refs[2:5]
        dbias_ref, small_ref, acc_s, acc_sem = refs[5:9]
        refs = refs[9:]
    (in_sem, bias_sem, blk_s, bias_s, biasT_s, xh_s, adj_s, qext_s, gz_s, kext_s, v_s, kT_s, vT_s, gT_s, attT_s, u_s, e_s, ds_s) = refs
    step = pl.program_id(0)

    def bias_copy(h):
        return pltpu.make_async_copy(bias_hbm.at[h], bias_s.at[h], bias_sem.at[h])

    @pl.when(step == 0)
    def _():
        start_all(pieces, arrays, blk_s, in_sem)
        for h in range(HEADS):
            bias_copy(h).start()
        if not first:
            pltpu.make_async_copy(acc_hbm, acc_s, acc_sem).start()
        dbias_ref[...] = jnp.zeros_like(dbias_ref)
        small_ref[...] = jnp.zeros_like(small_ref)
        qext_s[...] = jnp.zeros_like(qext_s)
        gz_s[...] = jnp.zeros_like(gz_s)
        vT_s[...] = jnp.ones_like(vT_s)
        kext_s[:, C:] = key_regions()

    if first:
        edge_x = edge_y = False
    else:
        edge_x = (lax.axis_index("gx") == lax.axis_size("gx") - 1) & (step != 1)
        edge_y = (lax.axis_index("gy") == lax.axis_size("gy") - 1) & (step != 0)
    wait_block(pieces, arrays, blk_s, in_sem, step)
    low = lax.broadcasted_iota(jnp.int32, (64, 8, C), 1) < SHIFT
    xh, _ = standardized(blk_s[0, step])
    a = blk_s[1, step].reshape(64, 3, 8, C).astype(F32)
    for z in range(3):
        z1 = (z + 1) % 3
        xh_s[z] = pltpu.roll(jnp.where(low, xh[:, z1], xh[:, z]) * gamma_ref[...], SHIFT, 1).reshape(T, C).astype(BF)
        adj_s[z] = pltpu.roll(jnp.where(low, a[:, z1], a[:, z]), SHIFT, 1).reshape(T, C).astype(BF)

    @pl.when(step == 0)
    def _():
        for h in range(HEADS):
            bias_copy(h).wait()
            biasT_s[h] = bias_s[h].T * (1.0 / SCALE)

    def window(z, carry):
        nrm = xh_s[z]
        adj = adj_s[z]
        qkvT = dot_nt(wT_ref[...], nrm).astype(BF)
        kT_s[...] = qkvT[C : 2 * C]
        regions = query_regions((edge_x, edge_y, z == 2))
        for h in range(HEADS):
            vT_s[h, :HD] = qkvT[2 * C + HD * h : 2 * C + HD * (h + 1)]
            qext_s[h, HD * h : HD * (h + 1)] = qkvT[HD * h : HD * (h + 1)]
            qext_s[h, C : C + 16] = regions
        kv = dot(nrm, w_ref[:, C:]).astype(BF)
        kext_s[:, :C] = kv[:, :C]
        v_s[...] = kv[:, C:]
        gT_s[...] = dot_nt(wproj_ref[...], adj).astype(BF)
        chunks = T // KC
        held = {}

        def scores(h, c):
            ks = slice(c * KC, (c + 1) * KC)
            u = dot(kext_s[ks], qext_s[h]) + biasT_s[h, ks]
            u_s[h % 2, ks] = u
            top = jnp.max(u.reshape(KC // 8, 8, T), axis=0)
            held["top", h] = top if c == 0 else jnp.maximum(top, held["top", h])
            if c == chunks - 1:
                held["top", h] = jnp.max(held["top", h], axis=0, keepdims=True)

        def weights(h, c):
            ks = slice(c * KC, (c + 1) * KC)
            e = jnp.exp2((u_s[h % 2, ks] - held["top", h]) * EXPC).astype(BF)
            e_s[h % 3, ks] = e
            o = dot(vT_s[h, :, ks], e)
            held["o", h] = o if c == 0 else o + held["o", h]
            if c == chunks - 1:
                o = held["o", h]
                hs = slice(HD * h, HD * (h + 1))
                inverse = 1.0 / o[HD : HD + 1]
                gs = (gT_s[hs].astype(F32) * inverse).astype(BF)
                attended = o[:HD] * inverse
                attT_s[hs] = attended.astype(BF)
                held["delta", h] = jnp.sum(gs.astype(F32) * attended, axis=0, keepdims=True)
                gz_s[h, hs] = gs

        def score_grads(h, c):
            ks = slice(c * KC, (c + 1) * KC)
            dp = dot(v_s[ks], gz_s[h])
            ds = e_s[h % 3, ks].astype(F32) * (dp - held["delta", h])
            ds_s[h % 2, ks] = ds.astype(BF)
            dbias_ref[h, ks] += ds

        def qkv_grads(h, c):
            hs = slice(HD * h, HD * (h + 1))
            ks = slice(c * KC, (c + 1) * KC)
            dq = dot(kT_s[hs, ks], ds_s[h % 2, ks])
            held["dq", h] = dq if c == 0 else dq + held["dq", h]
            dT_ref[z, C + HD * h : C + HD * (h + 1), ks] = (dot_nt(qext_s[h, hs], ds_s[h % 2, ks]) * SCALE).astype(BF)
            dT_ref[z, 2 * C + HD * h : 2 * C + HD * (h + 1), ks] = dot_nt(gz_s[h, hs], e_s[h % 3, ks]).astype(BF)
            if c == chunks - 1:
                dT_ref[z, hs] = (held["dq", h] * SCALE).astype(BF)

        for turn in range(HEADS + 3):
            for c in range(chunks):
                for lag, stage in ((3, qkv_grads), (2, score_grads), (1, weights), (0, scores)):
                    if 0 <= turn - lag < HEADS:
                        stage(turn - lag, c)
        small_ref[:C] += dot(attT_s[...], adj)
        small_ref[C:] += dot(dT_ref[z], nrm)
        return carry

    lax.fori_loop(0, 3, window, 0)

    if not first:

        @pl.when(step == pl.num_programs(0) - 1)
        def _():
            pltpu.make_async_copy(acc_hbm, acc_s, acc_sem).wait()
            mine = lax.axis_index("gx") % 2
            small = small_ref[...] + accs_ref[...]
            table = jnp.concatenate([small[:C], small[C:].T], axis=1)
            for j in range(2):
                h = 2 * (1 - mine) + j
                away_ref[j * T : (j + 1) * T] = (dbias_ref[h] + acc_s[h]).T.astype(BF)
                h = 2 * mine + j
                keep_ref[j * T : (j + 1) * T] = (dbias_ref[h] + acc_s[h]).T
            away_ref[2 * T :] = jnp.where(mine == 1, table, 0.0).astype(BF)
            keep_ref[2 * T :] = jnp.where(mine == 0, table, 0.0)


def finish_kernel(first, *refs):
    pieces = INNER if first else RIM
    arrays = refs[:2] if first else refs[:5]
    refs = refs[len(arrays) :]
    gamma_ref, w_ref, dT_ref = refs[:3]
    ends = refs[4:5] if first else refs[3:7]
    in_sem, out_sem, blk_s, gin_s = refs[-4:]
    step = pl.program_id(0)

    def leaving(n):
        block, origin, x, y, bx, by, ex, ey = pieces[n]
        src = gin_s.at[block, pl.ds(bx, ex), pl.ds(by, ey)]
        return pltpu.make_async_copy(src, ends[origin].at[pl.ds(x, ex), pl.ds(y, ey)], out_sem.at[n])

    @pl.when(step == 0)
    def _():
        start_all(pieces, arrays, blk_s, in_sem)

    wait_block(pieces, arrays, blk_s, in_sem, step)
    low = lax.broadcasted_iota(jnp.int32, (64, 8, C), 1) < SHIFT
    ones = jnp.full((C, C), 1.0 / C, BF)
    xh, rstd = standardized(blk_s[0, step])
    a = blk_s[1, step].reshape(64, 3, 8, C).astype(F32)
    windows = [pltpu.roll(dot(w_ref[...], dT_ref[z]).T.reshape(64, 8, C), SHIFT, 1) for z in range(3)]
    for z in range(3):
        xhat = xh[:, z].reshape(T, C)
        g = jnp.where(low, windows[(z + 2) % 3], windows[z]).reshape(T, C) * gamma_ref[...]
        mean = dot(g.astype(BF), ones)
        slope = dot((g * xhat).astype(BF), ones)
        grad = a[:, z] + rstd[:, z] * (g - mean - xhat * slope).reshape(64, 8, C)
        gin_s[step, :, :, 8 * z : 8 * z + 8] = grad.astype(BF).reshape(8, 8, 8, C)
    for block in sorted({p[0] for p in pieces}):

        @pl.when(step == block)
        def _(block=block):
            for n, piece in enumerate(pieces):
                if piece[0] == block:
                    leaving(n).start()

    @pl.when(step == pl.num_programs(0) - 1)
    def _():
        for n in range(len(pieces)):
            leaving(n).wait()


def whole(shape):
    return pl.BlockSpec(shape, lambda i: (0,) * len(shape))


ANYWHERE = pl.BlockSpec(memory_space=pl.ANY)
DT_BLOCK = pl.BlockSpec((pl.Squeezed(), 3, 3 * C, T), lambda i: (i, 0, 0, 0))
DT_SHAPE = (3, 3 * C, T)


def sublayer(first, arrays, params, carried=()):
    square = (HEADS, T, T)
    small = (4 * C, C)
    blocks = 1 if first else 3
    pieces = INNER if first else RIM
    ins = [ANYWHERE] * len(arrays) + [whole((1, C)), whole((C, 3 * C)), whole((3 * C, C)), whole((C, C)), ANYWHERE]
    if first:
        outs = [DT_BLOCK, whole(square), whole(small)]
        shapes = [((blocks,) + DT_SHAPE, BF), (square, F32), (small, F32)]
        scratch = []
    else:
        ins += [ANYWHERE, whole(small)]
        outs = [DT_BLOCK, whole((HALF, T)), whole((HALF, T))]
        shapes = [((blocks,) + DT_SHAPE, BF), ((HALF, T), BF), ((HALF, T), F32)]
        scratch = [pltpu.VMEM(square, F32), pltpu.VMEM(small, F32), pltpu.VMEM(square, F32), pltpu.SemaphoreType.DMA]
    scratch += [
        pltpu.SemaphoreType.DMA((2, len(pieces))),
        pltpu.SemaphoreType.DMA((HEADS,)),
        pltpu.VMEM((2, blocks, 8, 8, 24, C), BF),
        pltpu.VMEM(square, F32),
        pltpu.VMEM(square, F32),
        pltpu.VMEM((3, T, C), BF),
        pltpu.VMEM((3, T, C), BF),
        pltpu.VMEM((HEADS, 2 * C, T), BF),
        pltpu.VMEM((HEADS, C, T), BF),
        pltpu.VMEM((T, 2 * C), BF),
        pltpu.VMEM((T, C), BF),
        pltpu.VMEM((C, T), BF),
        pltpu.VMEM((HEADS, 48, T), BF),
        pltpu.VMEM((C, T), BF),
        pltpu.VMEM((C, T), BF),
        pltpu.VMEM((2, T, T), F32),
        pltpu.VMEM((3, T, T), BF),
        pltpu.VMEM((2, T, T), BF),
    ]
    return pl.pallas_call(
        functools.partial(kernel, first),
        grid=(blocks,),
        in_specs=ins,
        out_specs=outs,
        out_shape=[jax.ShapeDtypeStruct(shape, dtype) for shape, dtype in shapes],
        scratch_shapes=scratch,
        compiler_params=pltpu.CompilerParams(vmem_limit_bytes=58 * 1024 * 1024),
        cost_estimate=pl.CostEstimate(flops=blocks * 12 * 10**9, bytes_accessed=blocks * 10**7, transcendentals=0),
        name="inner_windows" if first else "rim_windows",
    )(*arrays, *params, *carried)


def finish(first, arrays, gamma, w, dT, carried=()):
    blocks = 1 if first else 3
    pieces = INNER if first else RIM
    shapes = [(16, 16, 24, C)] if first else [(16, 16, 24, C), (4, 12, 24, C), (12, 4, 24, C), (4, 4, 24, C)]
    return pl.pallas_call(
        functools.partial(finish_kernel, first),
        grid=(blocks,),
        in_specs=[ANYWHERE] * len(arrays) + [whole((1, C)), whole((C, 3 * C)), DT_BLOCK] + [ANYWHERE] * len(carried),
        out_specs=[ANYWHERE] * len(shapes),
        out_shape=[jax.ShapeDtypeStruct(shape, BF) for shape in shapes],
        scratch_shapes=[
            pltpu.SemaphoreType.DMA((2, len(pieces))),
            pltpu.SemaphoreType.DMA((len(pieces),)),
            pltpu.VMEM((2, blocks, 8, 8, 24, C), BF),
            pltpu.VMEM((blocks, 8, 8, 24, C), BF),
        ],
        input_output_aliases={len(arrays) + 3: 0} if first else {},
        compiler_params=pltpu.CompilerParams(vmem_limit_bytes=32 * 1024 * 1024),
        cost_estimate=pl.CostEstimate(flops=blocks * 10**9, bytes_accessed=blocks * 3 * 10**6, transcendentals=0),
        name="inner_finish" if first else "rim_finish",
    )(*arrays, gamma, w, dT, *carried)


def spread_kernel(mine_ref, own_ref, got_ref, out_ref):
    @pl.when(pl.program_id(0) == 0)
    def _():
        out_ref[...] = own_ref[...].astype(F32)

    @pl.when(pl.program_id(0) == 1)
    def _():
        out_ref[...] = got_ref[...].astype(F32)


def spread(mine, own, got):
    return pl.pallas_call(
        spread_kernel,
        grid_spec=pltpu.PrefetchScalarGridSpec(
            num_scalar_prefetch=1,
            grid=(2, 2),
            in_specs=[
                pl.BlockSpec((T, T), lambda s, j, m: (jnp.where(s == 0, j, 1), 0)),
                pl.BlockSpec((T, T), lambda s, j, m: (jnp.where(s == 0, 0, j), 0)),
            ],
            out_specs=pl.BlockSpec((pl.Squeezed(), T, T), lambda s, j, m: (jnp.where(s == 0, m[0], 1 - m[0]) * 2 + j, 0, 0)),
        ),
        out_shape=jax.ShapeDtypeStruct((HEADS, T, T), F32),
        name="spread",
    )(mine.reshape(1), own, got)


def shifted(values, by_x, by_y):
    nx, ny = lax.axis_size("gx"), lax.axis_size("gy")
    if not by_y:
        return lax.ppermute(values, "gx", [(i, (i + by_x) % nx) for i in range(nx)])
    if not by_x:
        return lax.ppermute(values, "gy", [(i, (i + by_y) % ny) for i in range(ny)])
    pairs = [(i * ny + j, (i + by_x) % nx * ny + (j + by_y) % ny) for i in range(nx) for j in range(ny)]
    return lax.ppermute(values, ("gx", "gy"), pairs)


CORE = ("gx", 1, 2)
ACROSS_X = ("gx", 2, 4)
ACROSS_Z = ("gy", 1, 4)
ACROSS_Y = ("y", 0, 4)


def moved(i, j, digit, by):
    axis, stride, size = digit
    if axis == "y":
        y = (j // 4 * 2 + i // 8 + by) % 4
        return y % 2 * 8 + i % 8, y // 2 * 4 + j % 4
    place = i if axis == "gx" else j
    old = place // stride % size
    place += ((old + by) % size - old) * stride
    return (place, j) if axis == "gx" else (i, place)


def send(values, digits, by):
    pairs = []
    for i in range(16):
        for j in range(8):
            k, l = moved(i, j, digits[i % 2], by)
            pairs.append((i * 8 + j, k * 8 + l))
    return lax.ppermute(values, ("gx", "gy"), pairs)


def my_digit(digits):
    gx, gy = lax.axis_index("gx"), lax.axis_index("gy")
    return jnp.where(gx % 2 == 0, *[(gx if axis == "gx" else gy) // stride % size for axis, stride, size in digits])


def scattered(values, digits):
    mine = my_digit(digits)
    rows = values.shape[0] // 4
    got = [send(lax.dynamic_slice_in_dim(values, (mine + by) % 4 * rows, rows).astype(BF), digits, by) for by in (2, 1, 3)]
    values = lax.dynamic_slice_in_dim(values, mine * rows, rows)
    for part in got:
        values = values + part.astype(F32)
    return values


def gathered(values, digits):
    mine = my_digit(digits)
    rows = values.shape[0]
    out = jnp.zeros((4 * rows,) + values.shape[1:], values.dtype)
    out = lax.dynamic_update_slice_in_dim(out, values, mine * rows, 0)
    for by in (2, 1, 3):
        out = lax.dynamic_update_slice_in_dim(out, send(values, digits, by), (mine - by) % 4 * rows, 0)
    return out


def summed(away, keep, beside):
    values = keep + send(away, (CORE, CORE), 1).astype(F32)
    values = scattered(values, (ACROSS_X, ACROSS_Z))
    values = scattered(values, (ACROSS_Z, ACROSS_X))
    values, *beside = lax.optimization_barrier((values, *beside))
    got = {by: send(values, (ACROSS_Y, ACROSS_Y), by) for by in (2, 1, 3)}
    values = ((values + got[2]) + (got[1] + got[3])).astype(BF)
    values = gathered(values, (ACROSS_Z, ACROSS_X))
    values = gathered(values, (ACROSS_X, ACROSS_Z))
    return values, send(values, (CORE, CORE), 1), beside


def body(retained_source, incoming_adjoint, rescale_multiplier, triple_projection_matrix, w_proj, pos_bias):
    both = (retained_source, incoming_adjoint)
    from_x = shifted(jnp.stack([v[:4, 4:] for v in both]), -1, 0)
    from_y = shifted(jnp.stack([v[4:, :4] for v in both]), 0, -1)
    from_xy = shifted(jnp.stack([v[:4, :4] for v in both]), -1, -1)
    w = triple_projection_matrix
    gamma = rescale_multiplier.reshape(1, C)
    params = (gamma, w, w.T, w_proj, pos_bias)
    inner_dT, acc, acc_small = sublayer(True, both, params)
    around = both + (from_x, from_y, from_xy)
    rim_dT, away, keep = sublayer(False, around, params, (acc, acc_small))
    gin, back_x, back_y, back_xy = finish(False, around, gamma, w, rim_dT)
    back = (shifted(back_x, 1, 0), shifted(back_y, 0, 1), shifted(back_xy, 1, 1))
    own, got, back = summed(away, keep, back)
    (gin,) = finish(True, both, gamma, w, inner_dT, (gin,))
    for values, place in zip(back, ((0, 4), (4, 0), (0, 0))):
        gin = lax.dynamic_update_slice(gin, values, place + (0, 0))
    mine = lax.axis_index("gx") % 2
    grad_bias = spread(mine, own, got)
    table = jnp.where(mine == 0, own[2 * T :], got[2 * T :]).astype(F32)
    grad_qkv = table[:, C:]
    gain = jnp.sum(grad_qkv * w.astype(F32), axis=1) / rescale_multiplier
    return (gin, grad_bias, table[:, :C], grad_qkv, gain)


def solution(mesh):
    placed = (P("gx", "gy", None, None), P("gx", "gy", None, None), P(), P(), P(), P())
    return jax.shard_map(
        body,
        mesh=mesh,
        in_specs=placed,
        out_specs=(P("gx", "gy", None, None), P(), P(), P(), P()),
        check_vma=False,
    )
```

time: 201 us -> 178 us (0.89)
  waiting for transfers between devices: 78.4 us -> 41.8 us
  local copies, waits for them, and re-layouts: 8.76 us -> 20.7 us
  Pallas kernels: 85 us -> 74.4 us
  starting transfers between devices: 22.6 us -> 32 us
    ppermute x11 -> x17, waiting for transfers between devices: 63.7 us -> 26.3 us  [send(): return lax.ppermute(values, ('gx', 'gy'), pairs)]
    pallas_call x2, Pallas kernels: 80.5 us -> 63 us  [sublayer(): pl.pallas_call(functools.partial(kernel, first), grid=(blocks,), in_specs...]
    ppermute x2, waiting for transfers between devices: 0.71 us -> 15.5 us  [shifted(): return lax.ppermute(values, ('gx', 'gy'), pairs)]
    ppermute x2, waiting for transfers between devices: 11.8 us -> 0.01 us  [shifted(): return lax.ppermute(values, 'gy', [(i, (i + by_y) % ny) for i in range(ny)])]
    ppermute x11 -> x17, starting transfers between devices: 9.93 us -> 18.3 us  [send(): return lax.ppermute(values, ('gx', 'gy'), pairs)]
    pallas_call x0 -> x2, Pallas kernels: none -> 6.92 us  [finish(): pl.pallas_call(functools.partial(finish_kernel, first), grid=(blocks,), i...]
    unnamed x19 -> x41, local copies, waits for them, and re-layouts: 1.83 us -> 7.9 us
    dynamic_update_slice x3 -> x10, local copies, waits for them, and re-layouts: 2.19 us -> 7.05 us  [the longest x3 4.11 us: body(): gin = lax.dynamic_update_slice(gin, values, place + (0, 0))]
  transfers between devices with their start and end apart: 17 -> 23, of which waited for: 13 -> 11; matrix products, arithmetic and copies ran while one was open for 3% -> 6% of each run, Pallas kernels for 11% -> 15%
where the time goes in v3:
time: 178 us; the launch traced here: 177 us
  Pallas kernels  74.4 us (42%)
  waiting for transfers between devices  41.8 us (23%)
  starting transfers between devices  32 us (18%)
  local copies, waits for them, and re-layouts  20.7 us (12%)
  other arithmetic  6.52 us (4%)
    pallas_call x2, Pallas kernels, sublayer(): pl.pallas_call(functools.partial(kernel, first), grid=(blocks,), in_specs...  63 us
    ppermute x17, waiting for transfers between devices, send(): return lax.ppermute(values, ('gx', 'gy'), pairs)  26.3 us
    ppermute x17, starting transfers between devices, send(): return lax.ppermute(values, ('gx', 'gy'), pairs)  18.3 us
    ppermute x2, waiting for transfers between devices, shifted(): return lax.ppermute(values, ('gx', 'gy'), pairs)  15.5 us
    ppermute x2, starting transfers between devices, shifted(): return lax.ppermute(values, 'gy', [(i, (i + by_y) % ny) for i in range(ny)])  8.55 us
    unnamed x41, local copies, waits for them, and re-layouts  7.9 us
    pallas_call x2, Pallas kernels, finish(): pl.pallas_call(functools.partial(finish_kernel, first), grid=(blocks,), i...  6.92 us
    pallas_call x1, Pallas kernels, spread(): pl.pallas_call(spread_kernel, grid_spec=pltpu.PrefetchScalarGridSpec(num_...  4.5 us
  transfers between devices with their start and end apart: 23, of which 11 were waited for; matrix products, arithmetic and copies ran while one was open for 6% of the time, Pallas kernels for 15%

profile of v3, /device:TPU:1, one launch (start us, length us, event | category | flops | bytes accessed | tf_op | source)
XLA Modules:
  0.0 176.5 jit_solution(16559502931681743275)
XLA Ops:
  0.6 1.1 slice_bitcast_fusion.2
  1.8 1.5 collective-permute-start
  3.3 1.1 slice_bitcast_fusion
  4.5 6.5 %collective-permute-start.1 = (bf16[2,12,4,24,128]{4,3,2,1,0:T(8,128)(2,1)S(1)}, bf16[2,12,4,24,128]{4,3,2,1,0:T(8,128)(2,1)S(1)}, u32[]{:S(2)}, u32[]{:S(2)}) collective-permute-start(bf16[2,12,4,24,128]{4,3,2,1,0:T(8,128)(2,1)S(1)} %pad_maximum_fusion.1), channel_id=1, source_target_pairs={{0,7},{1,0},{2,1},{3,2},{4,3},{5,4},{6,5},{7,6},{8,15},{9,8},{10,9... | collective-permute-start | bytes 1769480 | tf_op jit(solution)/shard_map/ppermute | solution.py:402
  11.0 1.0 slice_bitcast_fusion.4
  12.0 3.3 %collective-permute-start.2 = (bf16[2,4,4,24,128]{4,3,2,1,0:T(8,128)(2,1)S(1)}, bf16[2,4,4,24,128]{4,3,2,1,0:T(8,128)(2,1)S(1)}, u32[]{:S(2)}, u32[]{:S(2)}) collective-permute-start(bf16[2,4,4,24,128]{4,3,2,1,0:T(8,128)(2,1)S(1)} %pad_maximum_fusion.2), channel_id=1, source_target_pairs={{0,127},{1,120},{2,121},{3,122},{4,123},{5,124},{6,125},{7,126},{8... | collective-permute-start | bytes 589832 | tf_op jit(solution)/shard_map/ppermute | solution.py:404
  15.3 0.7 copy.12
  16.1 18.8 %inner_windows.1 = (bf16[1,3,384,512]{3,2,1,0:T(8,128)(2,1)}, f32[4,512,512]{2,1,0:T(8,128)}, f32[512,128]{1,0:T(8,128)}) custom-call(bf16[16,16,24,128]{3,2,1,0:T(8,128)(2,1)} %refs_0_.7, bf16[16,16,24,128]{3,2,1,0:T(8,128)(2,1)} %refs_1_.7, f32[1,128]{1,0:T(1,128)} %bitcast.15, bf16[128,384]{1,0:T(8,128)(2,1)} %refs_3_.3, bf16[384,128]{1,0:T(8,128)(2,1)} %bitcast.19, ...), custom_call_target="tpu_custom_call" | custom-call | flops 12000000000 | bytes 10000000 | tf_op jit(solution)/shard_map/inner_windows/pallas_call | solution.py:334
  36.1 44.1 %rim_windows.1 = (bf16[3,3,384,512]{3,2,1,0:T(8,128)(2,1)}, bf16[1152,512]{1,0:T(8,128)(2,1)}, f32[1152,512]{1,0:T(8,128)}) custom-call(bf16[16,16,24,128]{3,2,1,0:T(8,128)(2,1)} %refs_0_.7, bf16[16,16,24,128]{3,2,1,0:T(8,128)(2,1)} %refs_1_.7, bf16[2,4,12,24,128]{4,3,2,1,0:T(8,128)(2,1)} %copy-done.6, bf16[2,12,4,24,128]{4,3,2,1,0:T(8,128)(2,1)} %copy-done.8, ...), custom_call_target="tpu_custom_call" | custom-call | flops 35999997952 | bytes 30000000 | tf_op jit(solution)/shard_map/rim_windows/pallas_call | solution.py:334
  80.4 2.9 %collective-permute-done.3 = bf16[1152,512]{1,0:T(8,128)(2,1)S(1)} collective-permute-done((bf16[1152,512]{1,0:T(8,128)(2,1)}, bf16[1152,512]{1,0:T(8,128)(2,1)S(1)}, u32[]{:S(2)}, u32[]{:S(2)}) %collective-permute-start.3) | collective-permute-done | bytes 1179680 | tf_op jit(solution)/shard_map/ppermute | solution.py:430
  83.3 2.0 %convert_add_fusion = f32[1152,512]{1,0:T(8,128)S(1)} fusion(f32[1152,512]{1,0:T(8,128)} %get-tuple-element.24, bf16[1152,512]{1,0:T(8,128)(2,1)S(1)} %collective-permute-done.3), kind=kLoop, calls=%fused_computation | loop fusion | flops 1179648 | bytes 5898240 | tf_op jit(solution)/shard_map/add | solution.py:459
  85.4 1.4 copy-done.14
  86.8 1.0 dynamic-slice_convert_fusion.2
  87.8 1.5 collective-permute-start.5
  89.2 1.7 collective-permute-start.4
  90.9 3.0 %collective-permute-done.6 = bf16[288,512]{1,0:T(8,128)(2,1)S(1)} collective-permute-done((bf16[288,512]{1,0:T(8,128)(2,1)}, bf16[288,512]{1,0:T(8,128)(2,1)S(1)}, u32[]{:S(2)}, u32[]{:S(2)}) %collective-permute-start.6) | collective-permute-done | bytes 294944 | tf_op jit(solution)/shard_map/ppermute | solution.py:430
  93.9 1.3 collective-permute-done.5
  95.2 3.2 %collective-permute-done.4 = bf16[288,512]{1,0:T(8,128)(2,1)} collective-permute-done((bf16[288,512]{1,0:T(8,128)(2,1)}, bf16[288,512]{1,0:T(8,128)(2,1)}, u32[]{:S(2)}, u32[]{:S(2)}) %collective-permute-start.4) | collective-permute-done | bytes 294944 | tf_op jit(solution)/shard_map/ppermute | solution.py:430
  98.5 1.4 convert_add_fusion.1
  99.9 0.8 dynamic-slice_convert_fusion.5
  100.7 2.9 %collective-permute-start.9 = (bf16[72,512]{1,0:T(8,128)(2,1)}, bf16[72,512]{1,0:T(8,128)(2,1)}, u32[]{:S(2)}, u32[]{:S(2)}) collective-permute-start(bf16[72,512]{1,0:T(8,128)(2,1)} %get-tuple-element.41), channel_id=1, source_target_pairs={{0,3},{1,0},{2,1},{3,2},{4,7},{5,4},{6,5},{7,6},{8,56},{9,57},{10,... | collective-permute-start | bytes 221192 | tf_op jit(solution)/shard_map/ppermute | solution.py:430
  103.5 1.2 collective-permute-start.7
  104.7 1.1 copy-done.9
  105.8 0.9 copy-done.11
  106.7 2.0 %copy-done.13 = bf16[3,3,384,512]{3,2,1,0:T(8,128)(2,1)S(1)} copy-done((bf16[3,3,384,512]{3,2,1,0:T(8,128)(2,1)S(1)}, bf16[3,3,384,512]{3,2,1,0:T(8,128)(2,1)}, u32[]{:S(2)}) %copy-start.13) | copy-done | bytes 3538968
  108.7 5.0 %rim_finish.1 = (bf16[16,16,24,128]{3,2,1,0:T(8,128)(2,1)}, bf16[4,12,24,128]{3,2,1,0:T(8,128)(2,1)}, bf16[12,4,24,128]{3,2,1,0:T(8,128)(2,1)S(1)}, bf16[4,4,24,128]{3,2,1,0:T(8,128)(2,1)S(1)}) custom-call(bf16[16,16,24,128]{3,2,1,0:T(8,128)(2,1)S(1)} %copy-done, bf16[16,16,24,128]{3,2,1,0:T(8,128)(2,1)S(1)} %copy-done.1, ...), custom_call_target="tpu_custom_call" | custom-call | flops 3000000000 | bytes 9000000 | tf_op jit(solution)/shard_map/rim_finish/pallas_call | solution.py:351
  114.4 2.0 %collective-permute-start.11 = (bf16[12,4,24,128]{3,2,1,0:T(8,128)(2,1)S(1)}, bf16[12,4,24,128]{3,2,1,0:T(8,128)(2,1)}, u32[]{:S(2)}, u32[]{:S(2)}) collective-permute-start(bf16[12,4,24,128]{3,2,1,0:T(8,128)(2,1)S(1)} %get-tuple-element.27), channel_id=1, source_target_pairs={{0,1},{1,2},{2,3},{3,4},{4,5},{5,6},{6,7},{7,0},{8,9},{9,10},{10,1... | collective-permute-start | bytes 884744 | tf_op jit(solution)/shard_map/ppermute | solution.py:402
  116.8 1.1 convert_add_fusion.2
  117.9 15.5 %collective-permute-done.12 = bf16[4,4,24,128]{3,2,1,0:T(8,128)(2,1)S(1)} collective-permute-done((bf16[4,4,24,128]{3,2,1,0:T(8,128)(2,1)}, bf16[4,4,24,128]{3,2,1,0:T(8,128)(2,1)S(1)}, u32[]{:S(2)}, u32[]{:S(2)}) %collective-permute-start.12) | collective-permute-done | bytes 98336 | tf_op jit(solution)/shard_map/ppermute | solution.py:404
  133.9 2.1 %collective-permute-start.15 = (f32[72,512]{1,0:T(8,128)S(1)}, f32[72,512]{1,0:T(8,128)S(1)}, u32[]{:S(2)}, u32[]{:S(2)}) collective-permute-start(f32[72,512]{1,0:T(8,128)S(1)} %convert_add_fusion.2), channel_id=1, source_target_pairs={{0,68},{1,69},{2,70},{3,71},{4,64},{5,65},{6,66},{7,67},{8,76},{9,... | collective-permute-start | bytes 442376 | tf_op jit(solution)/shard_map/ppermute | solution.py:430
  136.4 3.1 %collective-permute-done.14 = f32[72,512]{1,0:T(8,128)S(1)} collective-permute-done((f32[72,512]{1,0:T(8,128)S(1)}, f32[72,512]{1,0:T(8,128)S(1)}, u32[]{:S(2)}, u32[]{:S(2)}) %collective-permute-start.14) | collective-permute-done | bytes 147488 | tf_op jit(solution)/shard_map/ppermute | solution.py:430
  139.5 3.0 %collective-permute-done.15 = f32[72,512]{1,0:T(8,128)S(1)} collective-permute-done((f32[72,512]{1,0:T(8,128)S(1)}, f32[72,512]{1,0:T(8,128)S(1)}, u32[]{:S(2)}, u32[]{:S(2)}) %collective-permute-start.15) | collective-permute-done | bytes 147488 | tf_op jit(solution)/shard_map/ppermute | solution.py:430
  143.2 0.7 constant_dynamic-update-slice_fusion.7
  143.9 2.7 %collective-permute-start.18 = (bf16[72,512]{1,0:T(8,128)(2,1)}, bf16[72,512]{1,0:T(8,128)(2,1)S(1)}, u32[]{:S(2)}, u32[]{:S(2)}) collective-permute-start(bf16[72,512]{1,0:T(8,128)(2,1)} %get-tuple-element.36), channel_id=1, source_target_pairs={{0,3},{1,0},{2,1},{3,2},{4,7},{5,4},{6,5},{7,6},{8,56},{9,57},{10,... | collective-permute-start | bytes 221192 | tf_op jit(solution)/shard_map/ppermute | solution.py:430
  146.5 2.4 %collective-permute-done.16 = bf16[72,512]{1,0:T(8,128)(2,1)} collective-permute-done((bf16[72,512]{1,0:T(8,128)(2,1)}, bf16[72,512]{1,0:T(8,128)(2,1)}, u32[]{:S(2)}, u32[]{:S(2)}) %collective-permute-start.16) | collective-permute-done | bytes 73760 | tf_op jit(solution)/shard_map/ppermute | solution.py:430
  149.0 0.9 constant_dynamic-update-slice_fusion.6
  150.2 2.6 %collective-permute-start.21 = (bf16[288,512]{1,0:T(8,128)(2,1)S(1)}, bf16[288,512]{1,0:T(8,128)(2,1)S(1)}, u32[]{:S(2)}, u32[]{:S(2)}) collective-permute-start(bf16[288,512]{1,0:T(8,128)(2,1)S(1)} %constant_dynamic-update-slice_fusion.4), channel_id=1, source_target_pairs={{0,48},{1,49},{2,50},{3,51},{4,52},{5,53},{6,54},{7,55},{8,11},{9,... | collective-permute-start | bytes 884744 | tf_op jit(solution)/shard_map/ppermute | solution.py:430
  152.9 4.6 %collective-permute-done.19 = bf16[288,512]{1,0:T(8,128)(2,1)} collective-permute-done((bf16[288,512]{1,0:T(8,128)(2,1)S(1)}, bf16[288,512]{1,0:T(8,128)(2,1)}, u32[]{:S(2)}, u32[]{:S(2)}) %collective-permute-start.19) | collective-permute-done | bytes 294944 | tf_op jit(solution)/shard_map/ppermute | solution.py:430
  157.5 1.0 constant_dynamic-update-slice_fusion.2
  158.5 1.9 %collective-permute-done.20 = bf16[288,512]{1,0:T(8,128)(2,1)} collective-permute-done((bf16[288,512]{1,0:T(8,128)(2,1)S(1)}, bf16[288,512]{1,0:T(8,128)(2,1)}, u32[]{:S(2)}, u32[]{:S(2)}) %collective-permute-start.20) | collective-permute-done | bytes 294944 | tf_op jit(solution)/shard_map/ppermute | solution.py:430
  160.5 1.0 constant_dynamic-update-slice_fusion.1
  161.5 2.5 %collective-permute-start.22 = (bf16[1152,512]{1,0:T(8,128)(2,1)S(1)}, bf16[1152,512]{1,0:T(8,128)(2,1)S(1)}, u32[]{:S(2)}, u32[]{:S(2)}) collective-permute-start(bf16[1152,512]{1,0:T(8,128)(2,1)S(1)} %constant_dynamic-update-slice_fusion.own_ref), channel_id=1, source_target_pairs={{0,8},{1,9},{2,10},{3,11},{4,12},{5,13},{6,14},{7,15},{8,0},{9,1},... | collective-permute-start | bytes 3538952 | tf_op jit(solution)/shard_map/ppermute | solution.py:430
  164.0 1.9 %inner_finish.1 = bf16[16,16,24,128]{3,2,1,0:T(8,128)(2,1)} custom-call(bf16[16,16,24,128]{3,2,1,0:T(8,128)(2,1)S(1)} %copy-done, bf16[16,16,24,128]{3,2,1,0:T(8,128)(2,1)S(1)} %copy-done.1, f32[1,128]{1,0:T(1,128)S(1)} %bitcast.18, bf16[128,384]{1,0:T(8,128)(2,1)S(1)} %copy-done.4, ...), custom_call_target="tpu_custom_call", output_to_operand_aliasing={{}: (5, {})} | custom-call | flops 1000000000 | bytes 3000000 | tf_op jit(solution)/shard_map/inner_finish/pallas_call | solution.py:351
  165.9 1.7 constant_dynamic-update-slice_fusion.10
  167.7 1.7 constant_dynamic-update-slice_fusion.9
  170.1 0.7 slice.42
  170.8 0.7 multiply_reduce_fusion
  172.0 4.5 %spread.1 = f32[4,512,512]{2,1,0:T(8,128)} custom-call(s32[1]{0:T(128)} %bitcast.8.mine_ref, bf16[1152,512]{1,0:T(8,128)(2,1)} %copy-done.15, bf16[1152,512]{1,0:T(8,128)(2,1)} %copy-done.17), custom_call_target="tpu_custom_call" | custom-call | tf_op jit(solution)/shard_map/spread/pallas_call | solution.py:381
  (72 shorter events, 5.6 us)
Async XLA Ops:
  1.8 13.5 %copy-start.3 = (bf16[128,384]{1,0:T(8,128)(2,1)S(1)}, bf16[128,384]{1,0:T(8,128)(2,1)}, u32[]{:S(2)}) copy-start(bf16[128,384]{1,0:T(8,128)(2,1)} %refs_3_.3) | copy-start | bytes 294916
  1.8 33.1 %collective-permute-start = (bf16[2,4,12,24,128]{4,3,2,1,0:T(8,128)(2,1)S(1)}, bf16[2,4,12,24,128]{4,3,2,1,0:T(8,128)(2,1)S(1)}, u32[]{:S(2)}, u32[]{:S(2)}) collective-permute-start(bf16[2,4,12,24,128]{4,3,2,1,0:T(8,128)(2,1)S(1)} %pad_maximum_fusion), channel_id=1, source_target_pairs={{0,120},{8,0},{16,8},{24,16},{32,24},{40,32},{48,40},{56,48},{64,5... | collective-permute-start | bytes 1769480 | tf_op jit(solution)/shard_map/ppermute | solution.py:400
  4.5 30.5 %collective-permute-start.1 = (bf16[2,12,4,24,128]{4,3,2,1,0:T(8,128)(2,1)S(1)}, bf16[2,12,4,24,128]{4,3,2,1,0:T(8,128)(2,1)S(1)}, u32[]{:S(2)}, u32[]{:S(2)}) collective-permute-start(bf16[2,12,4,24,128]{4,3,2,1,0:T(8,128)(2,1)S(1)} %pad_maximum_fusion.1), channel_id=1, source_target_pairs={{0,7},{1,0},{2,1},{3,2},{4,3},{5,4},{6,5},{7,6},{8,15},{9,8},{10,9... | collective-permute-start | bytes 1769480 | tf_op jit(solution)/shard_map/ppermute | solution.py:402
  12.0 22.9 %collective-permute-start.2 = (bf16[2,4,4,24,128]{4,3,2,1,0:T(8,128)(2,1)S(1)}, bf16[2,4,4,24,128]{4,3,2,1,0:T(8,128)(2,1)S(1)}, u32[]{:S(2)}, u32[]{:S(2)}) collective-permute-start(bf16[2,4,4,24,128]{4,3,2,1,0:T(8,128)(2,1)S(1)} %pad_maximum_fusion.2), channel_id=1, source_target_pairs={{0,127},{1,120},{2,121},{3,122},{4,123},{5,124},{6,125},{7,126},{8... | collective-permute-start | bytes 589832 | tf_op jit(solution)/shard_map/ppermute | solution.py:404
  34.9 0.7 copy-start.10
  34.9 0.9 copy-start.6
  35.0 1.1 copy-start.8
  80.2 3.1 %collective-permute-start.3 = (bf16[1152,512]{1,0:T(8,128)(2,1)}, bf16[1152,512]{1,0:T(8,128)(2,1)S(1)}, u32[]{:S(2)}, u32[]{:S(2)}) collective-permute-start(bf16[1152,512]{1,0:T(8,128)(2,1)} %get-tuple-element.25), channel_id=1, source_target_pairs={{0,8},{1,9},{2,10},{3,11},{4,12},{5,13},{6,14},{7,15},{8,0},{9,1},... | collective-permute-start | bytes 3538952 | tf_op jit(solution)/shard_map/ppermute | solution.py:430
  85.4 1.4 copy-start.14
  86.8 17.9 %copy-start.1 = (bf16[16,16,24,128]{3,2,1,0:T(8,128)(2,1)S(1)}, bf16[16,16,24,128]{3,2,1,0:T(8,128)(2,1)}, u32[]{:S(2)}) copy-start(bf16[16,16,24,128]{3,2,1,0:T(8,128)(2,1)} %refs_1_.7) | copy-start | bytes 4718596
  87.7 17.0 %copy-start = (bf16[16,16,24,128]{3,2,1,0:T(8,128)(2,1)S(1)}, bf16[16,16,24,128]{3,2,1,0:T(8,128)(2,1)}, u32[]{:S(2)}) copy-start(bf16[16,16,24,128]{3,2,1,0:T(8,128)(2,1)} %refs_0_.7) | copy-start | bytes 4718596
  87.7 17.0 %copy-start.4 = (bf16[128,384]{1,0:T(8,128)(2,1)S(1)}, bf16[128,384]{1,0:T(8,128)(2,1)}, u32[]{:S(2)}) copy-start(bf16[128,384]{1,0:T(8,128)(2,1)} %refs_3_.3) | copy-start | bytes 294916
  87.7 17.0 %copy-start.5 = (f32[128]{0:T(128)S(1)}, f32[128]{0:T(128)}, u32[]{:S(2)}) copy-start(f32[128]{0:T(128)} %param.8) | copy-start | bytes 1540
  87.7 6.2 %collective-permute-start.6 = (bf16[288,512]{1,0:T(8,128)(2,1)}, bf16[288,512]{1,0:T(8,128)(2,1)S(1)}, u32[]{:S(2)}, u32[]{:S(2)}) collective-permute-start(bf16[288,512]{1,0:T(8,128)(2,1)} %get-tuple-element.38), channel_id=1, source_target_pairs={{0,48},{1,49},{2,50},{3,51},{4,52},{5,53},{6,54},{7,55},{8,11},{9,... | collective-permute-start | bytes 884744 | tf_op jit(solution)/shard_map/ppermute | solution.py:430
  87.8 7.5 %collective-permute-start.5 = (bf16[288,512]{1,0:T(8,128)(2,1)}, bf16[288,512]{1,0:T(8,128)(2,1)}, u32[]{:S(2)}, u32[]{:S(2)}) collective-permute-start(bf16[288,512]{1,0:T(8,128)(2,1)} %get-tuple-element.39), channel_id=1, source_target_pairs={{0,16},{1,17},{2,18},{3,19},{4,20},{5,21},{6,22},{7,23},{8,9},{9,1... | collective-permute-start | bytes 884744 | tf_op jit(solution)/shard_map/ppermute | solution.py:430
  89.2 9.3 %collective-permute-start.4 = (bf16[288,512]{1,0:T(8,128)(2,1)}, bf16[288,512]{1,0:T(8,128)(2,1)}, u32[]{:S(2)}, u32[]{:S(2)}) collective-permute-start(bf16[288,512]{1,0:T(8,128)(2,1)} %get-tuple-element.37), channel_id=1, source_target_pairs={{0,32},{1,33},{2,34},{3,35},{4,36},{5,37},{6,38},{7,39},{8,10},{9,... | collective-permute-start | bytes 884744 | tf_op jit(solution)/shard_map/ppermute | solution.py:430
  90.9 13.8 %copy-start.7 = (bf16[2,4,12,24,128]{4,3,2,1,0:T(8,128)(2,1)S(1)}, bf16[2,4,12,24,128]{4,3,2,1,0:T(8,128)(2,1)}, u32[]{:S(2)}) copy-start(bf16[2,4,12,24,128]{4,3,2,1,0:T(8,128)(2,1)} %copy-done.6) | copy-start | bytes 1769476
  99.9 4.8 %copy-start.16 = (f32[288,512]{1,0:T(8,128)}, f32[288,512]{1,0:T(8,128)S(1)}, u32[]{:S(2)}) copy-start(f32[288,512]{1,0:T(8,128)S(1)} %convert_add_fusion.1) | copy-start | bytes 1769476
  100.7 15.7 %collective-permute-start.9 = (bf16[72,512]{1,0:T(8,128)(2,1)}, bf16[72,512]{1,0:T(8,128)(2,1)}, u32[]{:S(2)}, u32[]{:S(2)}) collective-permute-start(bf16[72,512]{1,0:T(8,128)(2,1)} %get-tuple-element.41), channel_id=1, source_target_pairs={{0,3},{1,0},{2,1},{3,2},{4,7},{5,4},{6,5},{7,6},{8,56},{9,57},{10,... | collective-permute-start | bytes 221192 | tf_op jit(solution)/shard_map/ppermute | solution.py:430
  103.5 13.3 %collective-permute-start.8 = (bf16[72,512]{1,0:T(8,128)(2,1)}, bf16[72,512]{1,0:T(8,128)(2,1)}, u32[]{:S(2)}, u32[]{:S(2)}) collective-permute-start(bf16[72,512]{1,0:T(8,128)(2,1)} %get-tuple-element.42), channel_id=1, source_target_pairs={{0,1},{1,2},{2,3},{3,0},{4,5},{5,6},{6,7},{7,4},{8,24},{9,25},{10,... | collective-permute-start | bytes 221192 | tf_op jit(solution)/shard_map/ppermute | solution.py:430
  103.5 13.3 %collective-permute-start.7 = (bf16[72,512]{1,0:T(8,128)(2,1)}, bf16[72,512]{1,0:T(8,128)(2,1)}, u32[]{:S(2)}, u32[]{:S(2)}) collective-permute-start(bf16[72,512]{1,0:T(8,128)(2,1)} %get-tuple-element.40), channel_id=1, source_target_pairs={{0,2},{1,3},{2,0},{3,1},{4,6},{5,7},{6,4},{7,5},{8,40},{9,41},{10,... | collective-permute-start | bytes 221192 | tf_op jit(solution)/shard_map/ppermute | solution.py:430
  104.7 1.1 copy-start.9
  105.8 0.9 copy-start.11
  106.7 2.0 %copy-start.13 = (bf16[3,3,384,512]{3,2,1,0:T(8,128)(2,1)S(1)}, bf16[3,3,384,512]{3,2,1,0:T(8,128)(2,1)}, u32[]{:S(2)}) copy-start(bf16[3,3,384,512]{3,2,1,0:T(8,128)(2,1)} %get-tuple-element.22.refs_7_) | copy-start | bytes 10616836
  113.7 0.6 copy-start.12
  114.4 19.0 %collective-permute-start.10 = (bf16[4,12,24,128]{3,2,1,0:T(8,128)(2,1)}, bf16[4,12,24,128]{3,2,1,0:T(8,128)(2,1)}, u32[]{:S(2)}, u32[]{:S(2)}) collective-permute-start(bf16[4,12,24,128]{3,2,1,0:T(8,128)(2,1)} %get-tuple-element.26), channel_id=1, source_target_pairs={{0,8},{8,16},{16,24},{24,32},{32,40},{40,48},{48,56},{56,64},{64,7... | collective-permute-start | bytes 884744 | tf_op jit(solution)/shard_map/ppermute | solution.py:400
  114.4 19.0 %collective-permute-start.11 = (bf16[12,4,24,128]{3,2,1,0:T(8,128)(2,1)S(1)}, bf16[12,4,24,128]{3,2,1,0:T(8,128)(2,1)}, u32[]{:S(2)}, u32[]{:S(2)}) collective-permute-start(bf16[12,4,24,128]{3,2,1,0:T(8,128)(2,1)S(1)} %get-tuple-element.27), channel_id=1, source_target_pairs={{0,1},{1,2},{2,3},{3,4},{4,5},{5,6},{6,7},{7,0},{8,9},{9,10},{10,1... | collective-permute-start | bytes 884744 | tf_op jit(solution)/shard_map/ppermute | solution.py:402
  116.4 17.0 %collective-permute-start.12 = (bf16[4,4,24,128]{3,2,1,0:T(8,128)(2,1)}, bf16[4,4,24,128]{3,2,1,0:T(8,128)(2,1)S(1)}, u32[]{:S(2)}, u32[]{:S(2)}) collective-permute-start(bf16[4,4,24,128]{3,2,1,0:T(8,128)(2,1)} %copy-done.12), channel_id=1, source_target_pairs={{0,9},{1,10},{2,11},{3,12},{4,13},{5,14},{6,15},{7,8},{8,17},{9,18... | collective-permute-start | bytes 294920 | tf_op jit(solution)/shard_map/ppermute | solution.py:404
  133.3 9.8 %copy-start.18 = (bf16[4,4,24,128]{3,2,1,0:T(8,128)(2,1)}, bf16[4,4,24,128]{3,2,1,0:T(8,128)(2,1)S(1)}, u32[]{:S(2)}) copy-start(bf16[4,4,24,128]{3,2,1,0:T(8,128)(2,1)S(1)} %collective-permute-done.12) | copy-start | bytes 294916
  133.3 6.1 %collective-permute-start.14 = (f32[72,512]{1,0:T(8,128)S(1)}, f32[72,512]{1,0:T(8,128)S(1)}, u32[]{:S(2)}, u32[]{:S(2)}) collective-permute-start(f32[72,512]{1,0:T(8,128)S(1)} %convert_add_fusion.2), channel_id=1, source_target_pairs={{0,64},{1,65},{2,66},{3,67},{4,68},{5,69},{6,70},{7,71},{8,72},{9,... | collective-permute-start | bytes 442376 | tf_op jit(solution)/shard_map/ppermute | solution.py:430
  133.9 8.5 %collective-permute-start.15 = (f32[72,512]{1,0:T(8,128)S(1)}, f32[72,512]{1,0:T(8,128)S(1)}, u32[]{:S(2)}, u32[]{:S(2)}) collective-permute-start(f32[72,512]{1,0:T(8,128)S(1)} %convert_add_fusion.2), channel_id=1, source_target_pairs={{0,68},{1,69},{2,70},{3,71},{4,64},{5,65},{6,66},{7,67},{8,76},{9,... | collective-permute-start | bytes 442376 | tf_op jit(solution)/shard_map/ppermute | solution.py:430
  136.1 7.1 %collective-permute-start.13 = (f32[72,512]{1,0:T(8,128)S(1)}, f32[72,512]{1,0:T(8,128)S(1)}, u32[]{:S(2)}, u32[]{:S(2)}) collective-permute-start(f32[72,512]{1,0:T(8,128)S(1)} %convert_add_fusion.2), channel_id=1, source_target_pairs={{0,4},{1,5},{2,6},{3,7},{4,0},{5,1},{6,2},{7,3},{8,12},{9,13},{10,... | collective-permute-start | bytes 442376 | tf_op jit(solution)/shard_map/ppermute | solution.py:430
  143.9 5.1 %collective-permute-start.16 = (bf16[72,512]{1,0:T(8,128)(2,1)}, bf16[72,512]{1,0:T(8,128)(2,1)}, u32[]{:S(2)}, u32[]{:S(2)}) collective-permute-start(bf16[72,512]{1,0:T(8,128)(2,1)} %get-tuple-element.36), channel_id=1, source_target_pairs={{0,2},{1,3},{2,0},{3,1},{4,6},{5,7},{6,4},{7,5},{8,40},{9,41},{10,... | collective-permute-start | bytes 221192 | tf_op jit(solution)/shard_map/ppermute | solution.py:430
  143.9 6.0 %collective-permute-start.17 = (bf16[72,512]{1,0:T(8,128)(2,1)}, bf16[72,512]{1,0:T(8,128)(2,1)S(1)}, u32[]{:S(2)}, u32[]{:S(2)}) collective-permute-start(bf16[72,512]{1,0:T(8,128)(2,1)} %get-tuple-element.36), channel_id=1, source_target_pairs={{0,1},{1,2},{2,3},{3,0},{4,5},{5,6},{6,7},{7,4},{8,24},{9,25},{10,... | collective-permute-start | bytes 221192 | tf_op jit(solution)/shard_map/ppermute | solution.py:430
  143.9 6.0 %collective-permute-start.18 = (bf16[72,512]{1,0:T(8,128)(2,1)}, bf16[72,512]{1,0:T(8,128)(2,1)S(1)}, u32[]{:S(2)}, u32[]{:S(2)}) collective-permute-start(bf16[72,512]{1,0:T(8,128)(2,1)} %get-tuple-element.36), channel_id=1, source_target_pairs={{0,3},{1,0},{2,1},{3,2},{4,7},{5,4},{6,5},{7,6},{8,56},{9,57},{10,... | collective-permute-start | bytes 221192 | tf_op jit(solution)/shard_map/ppermute | solution.py:430
  149.9 7.6 %collective-permute-start.19 = (bf16[288,512]{1,0:T(8,128)(2,1)S(1)}, bf16[288,512]{1,0:T(8,128)(2,1)}, u32[]{:S(2)}, u32[]{:S(2)}) collective-permute-start(bf16[288,512]{1,0:T(8,128)(2,1)S(1)} %constant_dynamic-update-slice_fusion.4), channel_id=1, source_target_pairs={{0,32},{1,33},{2,34},{3,35},{4,36},{5,37},{6,38},{7,39},{8,10},{9,... | collective-permute-start | bytes 884744 | tf_op jit(solution)/shard_map/ppermute | solution.py:430
  150.0 10.4 %collective-permute-start.20 = (bf16[288,512]{1,0:T(8,128)(2,1)S(1)}, bf16[288,512]{1,0:T(8,128)(2,1)}, u32[]{:S(2)}, u32[]{:S(2)}) collective-permute-start(bf16[288,512]{1,0:T(8,128)(2,1)S(1)} %constant_dynamic-update-slice_fusion.4), channel_id=1, source_target_pairs={{0,16},{1,17},{2,18},{3,19},{4,20},{5,21},{6,22},{7,23},{8,9},{9,1... | collective-permute-start | bytes 884744 | tf_op jit(solution)/shard_map/ppermute | solution.py:430
  150.2 13.8 %copy-start.2 = (bf16[1,3,384,512]{3,2,1,0:T(8,128)(2,1)S(1)}, bf16[1,3,384,512]{3,2,1,0:T(8,128)(2,1)}, u32[]{:S(2)}) copy-start(bf16[1,3,384,512]{3,2,1,0:T(8,128)(2,1)} %get-tuple-element.19.refs_4_) | copy-start | bytes 3538948
  150.2 11.2 %collective-permute-start.21 = (bf16[288,512]{1,0:T(8,128)(2,1)S(1)}, bf16[288,512]{1,0:T(8,128)(2,1)S(1)}, u32[]{:S(2)}, u32[]{:S(2)}) collective-permute-start(bf16[288,512]{1,0:T(8,128)(2,1)S(1)} %constant_dynamic-update-slice_fusion.4), channel_id=1, source_target_pairs={{0,48},{1,49},{2,50},{3,51},{4,52},{5,53},{6,54},{7,55},{8,11},{9,... | collective-permute-start | bytes 884744 | tf_op jit(solution)/shard_map/ppermute | solution.py:430
  161.5 8.6 %copy-start.15 = (bf16[1152,512]{1,0:T(8,128)(2,1)}, bf16[1152,512]{1,0:T(8,128)(2,1)S(1)}, u32[]{:S(2)}) copy-start(bf16[1152,512]{1,0:T(8,128)(2,1)S(1)} %constant_dynamic-update-slice_fusion.own_ref) | copy-start | bytes 3538948
  161.5 8.6 %collective-permute-start.22 = (bf16[1152,512]{1,0:T(8,128)(2,1)S(1)}, bf16[1152,512]{1,0:T(8,128)(2,1)S(1)}, u32[]{:S(2)}, u32[]{:S(2)}) collective-permute-start(bf16[1152,512]{1,0:T(8,128)(2,1)S(1)} %constant_dynamic-update-slice_fusion.own_ref), channel_id=1, source_target_pairs={{0,8},{1,9},{2,10},{3,11},{4,12},{5,13},{6,14},{7,15},{8,0},{9,1},... | collective-permute-start | bytes 3538952 | tf_op jit(solution)/shard_map/ppermute | solution.py:430
  164.0 5.4 %copy-start.19 = (bf16[4,4,24,128]{3,2,1,0:T(8,128)(2,1)S(1)}, bf16[4,4,24,128]{3,2,1,0:T(8,128)(2,1)}, u32[]{:S(2)}) copy-start(bf16[4,4,24,128]{3,2,1,0:T(8,128)(2,1)} %copy-done.18) | copy-start | bytes 294916
  170.0 2.0 %copy-start.17 = (bf16[1152,512]{1,0:T(8,128)(2,1)}, bf16[1152,512]{1,0:T(8,128)(2,1)S(1)}, u32[]{:S(2)}) copy-start(bf16[1152,512]{1,0:T(8,128)(2,1)S(1)} %collective-permute-done.22.got_ref) | copy-start | bytes 3538948

commit v4 on v3

--- a/solution.py
+++ b/solution.py
@@ -113,8 +113,8 @@
     else:
         acc_hbm, accs_ref = refs[:2]
         dT_ref, away_ref, keep_ref = refs[2:5]
-        dbias_ref, small_ref, acc_s, acc_sem = refs[5:9]
-        refs = refs[9:]
+        dbias_ref, small_ref, acc_sem = refs[5:8]
+        refs = refs[8:]
     (in_sem, bias_sem, blk_s, bias_s, biasT_s, xh_s, adj_s, qext_s, gz_s, kext_s, v_s, kT_s, vT_s, gT_s, attT_s, u_s, e_s, ds_s) = refs
     step = pl.program_id(0)
 
@@ -126,10 +126,12 @@
         start_all(pieces, arrays, blk_s, in_sem)
         for h in range(HEADS):
             bias_copy(h).start()
-        if not first:
-            pltpu.make_async_copy(acc_hbm, acc_s, acc_sem).start()
-        dbias_ref[...] = jnp.zeros_like(dbias_ref)
-        small_ref[...] = jnp.zeros_like(small_ref)
+        if first:
+            dbias_ref[...] = jnp.zeros_like(dbias_ref)
+            small_ref[...] = jnp.zeros_like(small_ref)
+        else:
+            pltpu.make_async_copy(acc_hbm, dbias_ref, acc_sem).start()
+            small_ref[...] = accs_ref[...]
         qext_s[...] = jnp.zeros_like(qext_s)
         gz_s[...] = jnp.zeros_like(gz_s)
         vT_s[...] = jnp.ones_like(vT_s)
@@ -154,6 +156,8 @@
         for h in range(HEADS):
             bias_copy(h).wait()
             biasT_s[h] = bias_s[h].T * (1.0 / SCALE)
+        if not first:
+            pltpu.make_async_copy(acc_hbm, dbias_ref, acc_sem).wait()
 
     def window(z, carry):
         nrm = xh_s[z]
@@ -229,15 +233,11 @@
 
         @pl.when(step == pl.num_programs(0) - 1)
         def _():
-            pltpu.make_async_copy(acc_hbm, acc_s, acc_sem).wait()
             mine = lax.axis_index("gx") % 2
-            small = small_ref[...] + accs_ref[...]
-            table = jnp.concatenate([small[:C], small[C:].T], axis=1)
+            table = jnp.concatenate([small_ref[:C], small_ref[C:].T], axis=1)
             for j in range(2):
-                h = 2 * (1 - mine) + j
-                away_ref[j * T : (j + 1) * T] = (dbias_ref[h] + acc_s[h]).T.astype(BF)
-                h = 2 * mine + j
-                keep_ref[j * T : (j + 1) * T] = (dbias_ref[h] + acc_s[h]).T
+                away_ref[j * T : (j + 1) * T] = dbias_ref[2 * (1 - mine) + j].T.astype(BF)
+                keep_ref[j * T : (j + 1) * T] = dbias_ref[2 * mine + j].T
             away_ref[2 * T :] = jnp.where(mine == 1, table, 0.0).astype(BF)
             keep_ref[2 * T :] = jnp.where(mine == 0, table, 0.0)
 
@@ -310,7 +310,7 @@
         ins += [ANYWHERE, whole(small)]
         outs = [DT_BLOCK, whole((HALF, T)), whole((HALF, T))]
         shapes = [((blocks,) + DT_SHAPE, BF), ((HALF, T), BF), ((HALF, T), F32)]
-        scratch = [pltpu.VMEM(square, F32), pltpu.VMEM(small, F32), pltpu.VMEM(square, F32), pltpu.SemaphoreType.DMA]
+        scratch = [pltpu.VMEM(square, F32), pltpu.VMEM(small, F32), pltpu.SemaphoreType.DMA]
     scratch += [
         pltpu.SemaphoreType.DMA((2, len(pieces))),
         pltpu.SemaphoreType.DMA((HEADS,)),
@@ -361,37 +361,70 @@
             pltpu.VMEM((blocks, 8, 8, 24, C), BF),
         ],
         input_output_aliases={len(arrays) + 3: 0} if first else {},
-        compiler_params=pltpu.CompilerParams(vmem_limit_bytes=32 * 1024 * 1024),
+        compiler_params=pltpu.CompilerParams(vmem_limit_bytes=60 * 1024 * 1024),
         cost_estimate=pl.CostEstimate(flops=blocks * 10**9, bytes_accessed=blocks * 3 * 10**6, transcendentals=0),
         name="inner_finish" if first else "rim_finish",
     )(*arrays, gamma, w, dT, *carried)
 
 
-def spread_kernel(mine_ref, own_ref, got_ref, out_ref):
+def spread_own_kernel(mine_ref, own_ref, out_ref):
+    out_ref[...] = own_ref[...].astype(F32)
+
+
+def spread_own(mine, own):
+    return pl.pallas_call(
+        spread_own_kernel,
+        grid_spec=pltpu.PrefetchScalarGridSpec(
+            num_scalar_prefetch=1,
+            grid=(2,),
+            in_specs=[pl.BlockSpec((T, T), lambda j, m: (j, 0))],
+            out_specs=pl.BlockSpec((pl.Squeezed(), T, T), lambda j, m: (2 * m[0] + j, 0, 0)),
+        ),
+        out_shape=jax.ShapeDtypeStruct((HEADS, T, T), F32),
+        name="spread_own",
+    )(mine, own)
+
+
+def spread_got_kernel(mine_ref, got_ref, own_rest_ref, got_rest_ref, gamma_ref, w_ref, _, out_ref, proj_ref, qkv_ref, gain_ref):
+    out_ref[...] = got_ref[...].astype(F32)
+
     @pl.when(pl.program_id(0) == 0)
     def _():
-        out_ref[...] = own_ref[...].astype(F32)
-
-    @pl.when(pl.program_id(0) == 1)
-    def _():
-        out_ref[...] = got_ref[...].astype(F32)
-
-
-def spread(mine, own, got):
+        table = jnp.where(mine_ref[0] == 0, own_rest_ref[...].astype(F32), got_rest_ref[...].astype(F32))
+        proj_ref[...] = table[:, :C]
+        qkv_ref[...] = table[:, C:]
+        along = (table[:, C:] * w_ref[...].astype(F32)).T
+        gain_ref[...] = jnp.sum(along, axis=0, keepdims=True) / gamma_ref[...]
+
+
+def spread_got(mine, own, got, gamma, w, grad_bias):
+    rest = pl.BlockSpec((C, T), lambda j, m: (2 * T // C, 0))
+
+    def all_of(shape):
+        return pl.BlockSpec(shape, lambda j, m: (0,) * len(shape))
+
     return pl.pallas_call(
-        spread_kernel,
+        spread_got_kernel,
         grid_spec=pltpu.PrefetchScalarGridSpec(
             num_scalar_prefetch=1,
-            grid=(2, 2),
-            in_specs=[
-                pl.BlockSpec((T, T), lambda s, j, m: (jnp.where(s == 0, j, 1), 0)),
-                pl.BlockSpec((T, T), lambda s, j, m: (jnp.where(s == 0, 0, j), 0)),
+            grid=(2,),
+            in_specs=[pl.BlockSpec((T, T), lambda j, m: (j, 0)), rest, rest, all_of((1, C)), all_of((C, 3 * C)), ANYWHERE],
+            out_specs=[
+                pl.BlockSpec((pl.Squeezed(), T, T), lambda j, m: (2 * (1 - m[0]) + j, 0, 0)),
+                all_of((C, C)),
+                all_of((C, 3 * C)),
+                all_of((1, C)),
             ],
-            out_specs=pl.BlockSpec((pl.Squeezed(), T, T), lambda s, j, m: (jnp.where(s == 0, m[0], 1 - m[0]) * 2 + j, 0, 0)),
         ),
-        out_shape=jax.ShapeDtypeStruct((HEADS, T, T), F32),
-        name="spread",
-    )(mine.reshape(1), own, got)
+        out_shape=[
+            jax.ShapeDtypeStruct((HEADS, T, T), F32),
+            jax.ShapeDtypeStruct((C, C), F32),
+            jax.ShapeDtypeStruct((C, 3 * C), F32),
+            jax.ShapeDtypeStruct((1, C), F32),
+        ],
+        input_output_aliases={6: 0},
+        name="spread_got",
+    )(mine, got, own, got, gamma, w, grad_bias)
 
 
 def shifted(values, by_x, by_y):
@@ -435,36 +468,31 @@
     return jnp.where(gx % 2 == 0, *[(gx if axis == "gx" else gy) // stride % size for axis, stride, size in digits])
 
 
-def scattered(values, digits):
+def parts_sent(values, digits):
     mine = my_digit(digits)
     rows = values.shape[0] // 4
     got = [send(lax.dynamic_slice_in_dim(values, (mine + by) % 4 * rows, rows).astype(BF), digits, by) for by in (2, 1, 3)]
-    values = lax.dynamic_slice_in_dim(values, mine * rows, rows)
+    return lax.dynamic_slice_in_dim(values, mine * rows, rows), got
+
+
+def added(values, got):
     for part in got:
         values = values + part.astype(F32)
     return values
 
 
-def gathered(values, digits):
+def all_sent(values, digits):
+    return {by: send(values, digits, by) for by in (2, 1, 3)}
+
+
+def gathered(values, got, digits):
     mine = my_digit(digits)
     rows = values.shape[0]
     out = jnp.zeros((4 * rows,) + values.shape[1:], values.dtype)
     out = lax.dynamic_update_slice_in_dim(out, values, mine * rows, 0)
     for by in (2, 1, 3):
-        out = lax.dynamic_update_slice_in_dim(out, send(values, digits, by), (mine - by) % 4 * rows, 0)
+        out = lax.dynamic_update_slice_in_dim(out, got[by], (mine - by) % 4 * rows, 0)
     return out
-
-
-def summed(away, keep, beside):
-    values = keep + send(away, (CORE, CORE), 1).astype(F32)
-    values = scattered(values, (ACROSS_X, ACROSS_Z))
-    values = scattered(values, (ACROSS_Z, ACROSS_X))
-    values, *beside = lax.optimization_barrier((values, *beside))
-    got = {by: send(values, (ACROSS_Y, ACROSS_Y), by) for by in (2, 1, 3)}
-    values = ((values + got[2]) + (got[1] + got[3])).astype(BF)
-    values = gathered(values, (ACROSS_Z, ACROSS_X))
-    values = gathered(values, (ACROSS_X, ACROSS_Z))
-    return values, send(values, (CORE, CORE), 1), beside
 
 
 def body(retained_source, incoming_adjoint, rescale_multiplier, triple_projection_matrix, w_proj, pos_bias):
@@ -478,18 +506,33 @@
     inner_dT, acc, acc_small = sublayer(True, both, params)
     around = both + (from_x, from_y, from_xy)
     rim_dT, away, keep = sublayer(False, around, params, (acc, acc_small))
+
+    first, second, third = (ACROSS_X, ACROSS_Z), (ACROSS_Z, ACROSS_X), (ACROSS_Y, ACROSS_Y)
+    values = keep + send(away, (CORE, CORE), 1).astype(F32)
+    values, got = parts_sent(values, first)
     gin, back_x, back_y, back_xy = finish(False, around, gamma, w, rim_dT)
+    values, got, back_x, back_y, back_xy = lax.optimization_barrier((values, got, back_x, back_y, back_xy))
     back = (shifted(back_x, 1, 0), shifted(back_y, 0, 1), shifted(back_xy, 1, 1))
-    own, got, back = summed(away, keep, back)
+    values, got = parts_sent(added(values, got), second)
     (gin,) = finish(True, both, gamma, w, inner_dT, (gin,))
-    for values, place in zip(back, ((0, 4), (4, 0), (0, 0))):
-        gin = lax.dynamic_update_slice(gin, values, place + (0, 0))
-    mine = lax.axis_index("gx") % 2
-    grad_bias = spread(mine, own, got)
-    table = jnp.where(mine == 0, own[2 * T :], got[2 * T :]).astype(F32)
-    grad_qkv = table[:, C:]
-    gain = jnp.sum(grad_qkv * w.astype(F32), axis=1) / rescale_multiplier
-    return (gin, grad_bias, table[:, :C], grad_qkv, gain)
+    values, got, gin = lax.optimization_barrier((values, got, gin))
+    values = added(values, got)
+    got = all_sent(values, third)
+    values = ((values + got[2]) + (got[1] + got[3])).astype(BF)
+    got = all_sent(values, second)
+    values, got, back = lax.optimization_barrier((values, got, back))
+    values = gathered(values, got, second)
+    got = all_sent(values, first)
+    for part, place in zip(back, ((0, 4), (4, 0), (0, 0))):
+        gin = lax.dynamic_update_slice(gin, part, place + (0, 0))
+    values, got, gin = lax.optimization_barrier((values, got, gin))
+    own = gathered(values, got, first)
+    got = send(own, (CORE, CORE), 1)
+    mine = (lax.axis_index("gx") % 2).reshape(1)
+    grad_bias = spread_own(mine, own)
+    grad_bias, got = lax.optimization_barrier((grad_bias, got))
+    grad_bias, grad_proj, grad_qkv, gain = spread_got(mine, own, got, gamma, w, grad_bias)
+    return (gin, grad_bias, grad_proj, grad_qkv, gain.reshape(C))
 
 
 def solution(mesh):

time: 178 us -> 155 us (0.87)
  waiting for transfers between devices: 41.8 us -> 25.5 us
  local copies, waits for them, and re-layouts: 20.7 us -> 9.65 us
  Pallas kernels: 74.4 us -> 80.4 us
  other arithmetic: 6.52 us -> 2.39 us
  starting transfers between devices: 32 us -> 35.4 us
    ppermute x17, waiting for transfers between devices: 26.3 us -> 14.5 us  [send(): return lax.ppermute(values, ('gx', 'gy'), pairs)]
    dynamic_update_slice x9, local copies, waits for them, and re-layouts: 7.02 us -> 2.3 us  [the longest x3 2.19 us: body(): gin = lax.dynamic_update_slice(gin, part, place + (0, 0))]
    ppermute x2, waiting for transfers between devices: 15.5 us -> 11 us  [shifted(): return lax.ppermute(values, ('gx', 'gy'), pairs)]
    pallas_call x2, Pallas kernels: 6.92 us -> 11.3 us  [finish(): pl.pallas_call(functools.partial(finish_kernel, first), grid=(blocks,), i...]
    ppermute x2, starting transfers between devices: 1.49 us -> 5.84 us  [shifted(): return lax.ppermute(values, 'gx', [(i, (i + by_x) % nx) for i in range(nx)])]
    unnamed x41 -> x19, local copies, waits for them, and re-layouts: 7.9 us -> 3.79 us
    add x3, other arithmetic: 4.47 us -> 2.21 us  [the longest x1 2.03 us: body(): values = keep + send(away, (CORE, CORE), 1).astype(F32)]
    pallas_call x1 -> x2, Pallas kernels: 4.5 us -> 5.17 us  [the longest x1 2.75 us: spread_got(): pl.pallas_call(spread_got_kernel, grid_spec=pltpu.PrefetchScalarGridSpec(...]
  transfers between devices with their start and end apart: 23 -> 23, of which waited for: 11 -> 7; matrix products, arithmetic and copies ran while one was open for 6% -> 3% of each run, Pallas kernels for 15% -> 21%
where the time goes in v4:
time: 155 us
  Pallas kernels  80.4 us (52%)
  starting transfers between devices  35.4 us (23%)
  waiting for transfers between devices  25.5 us (16%)
  local copies, waits for them, and re-layouts  9.65 us (6%)
  other arithmetic  2.39 us (2%)
    pallas_call x2, Pallas kernels, sublayer(): pl.pallas_call(functools.partial(kernel, first), grid=(blocks,), in_specs...  63.9 us
    ppermute x17, starting transfers between devices, send(): return lax.ppermute(values, ('gx', 'gy'), pairs)  19.1 us
    ppermute x17, waiting for transfers between devices, send(): return lax.ppermute(values, ('gx', 'gy'), pairs)  14.5 us
    pallas_call x2, Pallas kernels, finish(): pl.pallas_call(functools.partial(finish_kernel, first), grid=(blocks,), i...  11.3 us
    ppermute x2, waiting for transfers between devices, shifted(): return lax.ppermute(values, ('gx', 'gy'), pairs)  11 us
    ppermute x2, starting transfers between devices, shifted(): return lax.ppermute(values, 'gy', [(i, (i + by_y) % ny) for i in range(ny)])  7.29 us
    ppermute x2, starting transfers between devices, shifted(): return lax.ppermute(values, 'gx', [(i, (i + by_x) % nx) for i in range(nx)])  5.84 us
    unnamed x19, local copies, waits for them, and re-layouts  3.79 us
  transfers between devices with their start and end apart: 23, of which 7 were waited for; matrix products, arithmetic and copies ran while one was open for 3% of the time, Pallas kernels for 21%

profile of v4, /device:TPU:1, one launch (start us, length us, event | category | flops | bytes accessed | tf_op | source)
XLA Modules:
  0.0 154.5 jit_solution(15144275762825537747)
XLA Ops:
  0.6 1.1 slice_bitcast_fusion
  1.8 7.3 %collective-permute-start.1 = (bf16[2,12,4,24,128]{4,3,2,1,0:T(8,128)(2,1)S(1)}, bf16[2,12,4,24,128]{4,3,2,1,0:T(8,128)(2,1)S(1)}, u32[]{:S(2)}, u32[]{:S(2)}) collective-permute-start(bf16[2,12,4,24,128]{4,3,2,1,0:T(8,128)(2,1)S(1)} %pad_maximum_fusion.1), channel_id=1, source_target_pairs={{0,7},{1,0},{2,1},{3,2},{4,3},{5,4},{6,5},{7,6},{8,15},{9,8},{10,9... | collective-permute-start | bytes 1769480 | tf_op jit(solution)/shard_map/ppermute | solution.py:435
  9.1 1.1 slice_bitcast_fusion.2
  10.3 1.0 collective-permute-start
  11.3 1.0 slice_bitcast_fusion.4
  12.3 2.7 %collective-permute-start.2 = (bf16[2,4,4,24,128]{4,3,2,1,0:T(8,128)(2,1)S(1)}, bf16[2,4,4,24,128]{4,3,2,1,0:T(8,128)(2,1)S(1)}, u32[]{:S(2)}, u32[]{:S(2)}) collective-permute-start(bf16[2,4,4,24,128]{4,3,2,1,0:T(8,128)(2,1)S(1)} %pad_maximum_fusion.2), channel_id=1, source_target_pairs={{0,127},{1,120},{2,121},{3,122},{4,123},{5,124},{6,125},{7,126},{8... | collective-permute-start | bytes 589832 | tf_op jit(solution)/shard_map/ppermute | solution.py:437
  15.0 0.8 copy.13
  15.8 18.8 %inner_windows.1 = (bf16[1,3,384,512]{3,2,1,0:T(8,128)(2,1)}, f32[4,512,512]{2,1,0:T(8,128)}, f32[512,128]{1,0:T(8,128)}) custom-call(bf16[16,16,24,128]{3,2,1,0:T(8,128)(2,1)} %refs_0_.7, bf16[16,16,24,128]{3,2,1,0:T(8,128)(2,1)} %refs_1_.7, f32[1,128]{1,0:T(1,128)} %bitcast.18, bf16[128,384]{1,0:T(8,128)(2,1)} %w_ref.1, bf16[384,128]{1,0:T(8,128)(2,1)} %bitcast.16, ...), custom_call_target="tpu_custom_call" | custom-call | flops 12000000000 | bytes 10000000 | tf_op jit(solution)/shard_map/inner_windows/pallas_call | solution.py:334
  34.7 0.6 copy-done.7
  35.3 0.2 copy-done.3
  35.6 0.2 copy-done.4
  35.7 45.0 %rim_windows.1 = (bf16[3,3,384,512]{3,2,1,0:T(8,128)(2,1)}, bf16[1152,512]{1,0:T(8,128)(2,1)}, f32[1152,512]{1,0:T(8,128)}) custom-call(bf16[16,16,24,128]{3,2,1,0:T(8,128)(2,1)} %refs_0_.7, bf16[16,16,24,128]{3,2,1,0:T(8,128)(2,1)} %refs_1_.7, bf16[2,4,12,24,128]{4,3,2,1,0:T(8,128)(2,1)} %copy-done.4, bf16[2,12,4,24,128]{4,3,2,1,0:T(8,128)(2,1)} %copy-done.3, ...), custom_call_target="tpu_custom_call" | custom-call | flops 35999997952 | bytes 30000000 | tf_op jit(solution)/shard_map/rim_windows/pallas_call | solution.py:334
  80.8 0.1 collective-permute-start.3
  81.1 2.9 %collective-permute-done.3 = bf16[1152,512]{1,0:T(8,128)(2,1)S(1)} collective-permute-done((bf16[1152,512]{1,0:T(8,128)(2,1)}, bf16[1152,512]{1,0:T(8,128)(2,1)S(1)}, u32[]{:S(2)}, u32[]{:S(2)}) %collective-permute-start.3) | collective-permute-done | bytes 1179680 | tf_op jit(solution)/shard_map/ppermute | solution.py:463
  83.9 2.0 %convert_add_fusion = f32[1152,512]{1,0:T(8,128)S(1)} fusion(f32[1152,512]{1,0:T(8,128)} %get-tuple-element.47, bf16[1152,512]{1,0:T(8,128)(2,1)S(1)} %collective-permute-done.3), kind=kLoop, calls=%fused_computation | loop fusion | flops 1179648 | bytes 5898240 | tf_op jit(solution)/shard_map/add | solution.py:511
  86.0 0.1 dynamic-slice_convert_fusion
  86.1 0.1 collective-permute-start.4
  86.2 1.2 collective-permute-start.5
  87.4 2.3 %collective-permute-start.6 = (bf16[288,512]{1,0:T(8,128)(2,1)S(1)}, bf16[288,512]{1,0:T(8,128)(2,1)S(1)}, u32[]{:S(2)}, u32[]{:S(2)}) collective-permute-start(bf16[288,512]{1,0:T(8,128)(2,1)S(1)} %get-tuple-element.85), channel_id=1, source_target_pairs={{0,48},{1,49},{2,50},{3,51},{4,52},{5,53},{6,54},{7,55},{8,11},{9,... | collective-permute-start | bytes 884744 | tf_op jit(solution)/shard_map/ppermute | solution.py:463
  89.7 7.0 %rim_finish.1 = (bf16[16,16,24,128]{3,2,1,0:T(8,128)(2,1)}, bf16[4,12,24,128]{3,2,1,0:T(8,128)(2,1)}, bf16[12,4,24,128]{3,2,1,0:T(8,128)(2,1)}, bf16[4,4,24,128]{3,2,1,0:T(8,128)(2,1)}) custom-call(bf16[16,16,24,128]{3,2,1,0:T(8,128)(2,1)} %refs_0_.7, bf16[16,16,24,128]{3,2,1,0:T(8,128)(2,1)} %refs_1_.7, bf16[2,4,12,24,128]{4,3,2,1,0:T(8,128)(2,1)} %copy-done.4, ...), custom_call_target="tpu_custom_call" | custom-call | flops 3000000000 | bytes 9000000 | tf_op jit(solution)/shard_map/rim_finish/pallas_call | solution.py:351
  96.7 4.3 %inner_finish.1 = bf16[16,16,24,128]{3,2,1,0:T(8,128)(2,1)} custom-call(bf16[16,16,24,128]{3,2,1,0:T(8,128)(2,1)} %refs_0_.7, bf16[16,16,24,128]{3,2,1,0:T(8,128)(2,1)} %refs_1_.7, f32[1,128]{1,0:T(1,128)} %bitcast.21, bf16[128,384]{1,0:T(8,128)(2,1)} %w_ref.1, bf16[1,3,384,512]{3,2,1,0:T(8,128)(2,1)} %get-tuple-element.57.refs_4_, ...), custom_call_target="tpu_custom_call", output_to_operand_aliasing={{}: (5, {})} | custom-call | flops 1000000000 | bytes 3000000 | tf_op jit(solution)/shard_map/inner_finish/pallas_call | solution.py:351
  101.2 0.1 convert_add_fusion.1
  101.4 0.5 collective-permute-start.7
  101.9 0.6 collective-permute-start.8
  102.5 2.1 %collective-permute-start.9 = (bf16[72,512]{1,0:T(8,128)(2,1)S(1)}, bf16[72,512]{1,0:T(8,128)(2,1)S(1)}, u32[]{:S(2)}, u32[]{:S(2)}) collective-permute-start(bf16[72,512]{1,0:T(8,128)(2,1)S(1)} %get-tuple-element.88), channel_id=1, source_target_pairs={{0,3},{1,0},{2,1},{3,2},{4,7},{5,4},{6,5},{7,6},{8,56},{9,57},{10,... | collective-permute-start | bytes 221192 | tf_op jit(solution)/shard_map/ppermute | solution.py:463
  104.6 1.7 %collective-permute-done.7 = bf16[72,512]{1,0:T(8,128)(2,1)S(1)} collective-permute-done((bf16[72,512]{1,0:T(8,128)(2,1)S(1)}, bf16[72,512]{1,0:T(8,128)(2,1)S(1)}, u32[]{:S(2)}, u32[]{:S(2)}) %collective-permute-start.7) | collective-permute-done | bytes 73760 | tf_op jit(solution)/shard_map/ppermute | solution.py:463
  106.3 1.0 collective-permute-done.8
  107.3 2.0 %collective-permute-start.10 = (f32[72,512]{1,0:T(8,128)S(1)}, f32[72,512]{1,0:T(8,128)S(1)}, u32[]{:S(2)}, u32[]{:S(2)}) collective-permute-start(f32[72,512]{1,0:T(8,128)S(1)} %convert_add_fusion.2), channel_id=1, source_target_pairs={{0,4},{1,5},{2,6},{3,7},{4,0},{5,1},{6,2},{7,3},{8,12},{9,13},{10,... | collective-permute-start | bytes 442376 | tf_op jit(solution)/shard_map/ppermute | solution.py:463
  109.3 2.7 %collective-permute-start.12 = (f32[72,512]{1,0:T(8,128)S(1)}, f32[72,512]{1,0:T(8,128)S(1)}, u32[]{:S(2)}, u32[]{:S(2)}) collective-permute-start(f32[72,512]{1,0:T(8,128)S(1)} %convert_add_fusion.2), channel_id=1, source_target_pairs={{0,68},{1,69},{2,70},{3,71},{4,64},{5,65},{6,66},{7,67},{8,76},{9,... | collective-permute-start | bytes 442376 | tf_op jit(solution)/shard_map/ppermute | solution.py:463
  112.0 4.8 %collective-permute-start.16 = (bf16[4,12,24,128]{3,2,1,0:T(8,128)(2,1)S(1)}, bf16[4,12,24,128]{3,2,1,0:T(8,128)(2,1)S(1)}, u32[]{:S(2)}, u32[]{:S(2)}) collective-permute-start(bf16[4,12,24,128]{3,2,1,0:T(8,128)(2,1)S(1)} %copy-done.6), channel_id=1, source_target_pairs={{0,8},{8,16},{16,24},{24,32},{32,40},{40,48},{48,56},{56,64},{64,7... | collective-permute-start | bytes 884744 | tf_op jit(solution)/shard_map/ppermute | solution.py:433
  116.8 0.5 collective-permute-start.18
  117.4 0.5 collective-permute-start.13
  117.9 4.3 %collective-permute-start.14 = (bf16[72,512]{1,0:T(8,128)(2,1)S(1)}, bf16[72,512]{1,0:T(8,128)(2,1)S(1)}, u32[]{:S(2)}, u32[]{:S(2)}) collective-permute-start(bf16[72,512]{1,0:T(8,128)(2,1)S(1)} %add_convert_fusion), channel_id=1, source_target_pairs={{0,2},{1,3},{2,0},{3,1},{4,6},{5,7},{6,4},{7,5},{8,40},{9,41},{10,... | collective-permute-start | bytes 221192 | tf_op jit(solution)/shard_map/ppermute | solution.py:463
  122.1 11.0 %collective-permute-done.18 = bf16[4,4,24,128]{3,2,1,0:T(8,128)(2,1)S(1)} collective-permute-done((bf16[4,4,24,128]{3,2,1,0:T(8,128)(2,1)S(1)}, bf16[4,4,24,128]{3,2,1,0:T(8,128)(2,1)S(1)}, u32[]{:S(2)}, u32[]{:S(2)}) %collective-permute-start.18) | collective-permute-done | bytes 98336 | tf_op jit(solution)/shard_map/ppermute | solution.py:437
  133.1 3.2 %collective-permute-done.15 = bf16[72,512]{1,0:T(8,128)(2,1)S(1)} collective-permute-done((bf16[72,512]{1,0:T(8,128)(2,1)S(1)}, bf16[72,512]{1,0:T(8,128)(2,1)S(1)}, u32[]{:S(2)}, u32[]{:S(2)}) %collective-permute-start.15) | collective-permute-done | bytes 73760 | tf_op jit(solution)/shard_map/ppermute | solution.py:463
  136.5 0.1 collective-permute-start.20
  136.6 2.6 %collective-permute-start.21 = (bf16[288,512]{1,0:T(8,128)(2,1)S(1)}, bf16[288,512]{1,0:T(8,128)(2,1)S(1)}, u32[]{:S(2)}, u32[]{:S(2)}) collective-permute-start(bf16[288,512]{1,0:T(8,128)(2,1)S(1)} %constant_dynamic-update-slice_fusion.7), channel_id=1, source_target_pairs={{0,48},{1,49},{2,50},{3,51},{4,52},{5,53},{6,54},{7,55},{8,11},{9,... | collective-permute-start | bytes 884744 | tf_op jit(solution)/shard_map/ppermute | solution.py:463
  139.2 0.8 constant_dynamic-update-slice_fusion.6
  140.0 0.8 constant_dynamic-update-slice_fusion.5
  140.7 0.7 constant_dynamic-update-slice_fusion.4
  141.4 5.1 %collective-permute-done.19 = bf16[288,512]{1,0:T(8,128)(2,1)S(1)} collective-permute-done((bf16[288,512]{1,0:T(8,128)(2,1)S(1)}, bf16[288,512]{1,0:T(8,128)(2,1)S(1)}, u32[]{:S(2)}, u32[]{:S(2)}) %collective-permute-start.19) | collective-permute-done | bytes 294944 | tf_op jit(solution)/shard_map/ppermute | solution.py:463
  146.5 0.6 collective-permute-done.21
  147.1 0.1 broadcast_in_dim.7
  147.3 0.1 collective-permute-start.22
  147.4 0.9 copy-done
  148.3 2.4 %spread_own.1._ = f32[4,512,512]{2,1,0:T(8,128)} custom-call(s32[1]{0:T(128)} %bitcast.8.mine_ref, bf16[1152,512]{1,0:T(8,128)(2,1)} %copy-done), custom_call_target="tpu_custom_call" | custom-call | tf_op jit(solution)/shard_map/spread_own/pallas_call | solution.py:375
  150.8 1.0 copy-done.1
  151.8 2.7 %spread_got.1 = (f32[4,512,512]{2,1,0:T(8,128)}, f32[128,128]{1,0:T(8,128)}, f32[128,384]{1,0:T(8,128)}, f32[1,128]{1,0:T(1,128)}) custom-call(s32[1]{0:T(128)} %bitcast.8.mine_ref, bf16[1152,512]{1,0:T(8,128)(2,1)} %copy-done.1, bf16[1152,512]{1,0:T(8,128)(2,1)} %copy-done, bf16[1152,512]{1,0:T(8,128)(2,1)} %copy-done.1, ...), custom_call_target="tpu_custom_call", output_to_operand_aliasing={{0}: (6, {})} | custom-call | tf_op jit(solution)/shard_map/spread_got/pallas_call | solution.py:406
  (50 shorter events, 0.7 us)
Async XLA Ops:
  1.8 13.2 %copy-start.2 = (bf16[128,384]{1,0:T(8,128)(2,1)S(1)}, bf16[128,384]{1,0:T(8,128)(2,1)}, u32[]{:S(2)}) copy-start(bf16[128,384]{1,0:T(8,128)(2,1)} %w_ref.1) | copy-start | bytes 294916
  1.8 32.8 %collective-permute-start.1 = (bf16[2,12,4,24,128]{4,3,2,1,0:T(8,128)(2,1)S(1)}, bf16[2,12,4,24,128]{4,3,2,1,0:T(8,128)(2,1)S(1)}, u32[]{:S(2)}, u32[]{:S(2)}) collective-permute-start(bf16[2,12,4,24,128]{4,3,2,1,0:T(8,128)(2,1)S(1)} %pad_maximum_fusion.1), channel_id=1, source_target_pairs={{0,7},{1,0},{2,1},{3,2},{4,3},{5,4},{6,5},{7,6},{8,15},{9,8},{10,9... | collective-permute-start | bytes 1769480 | tf_op jit(solution)/shard_map/ppermute | solution.py:435
  10.3 24.4 %collective-permute-start = (bf16[2,4,12,24,128]{4,3,2,1,0:T(8,128)(2,1)S(1)}, bf16[2,4,12,24,128]{4,3,2,1,0:T(8,128)(2,1)S(1)}, u32[]{:S(2)}, u32[]{:S(2)}) collective-permute-start(bf16[2,4,12,24,128]{4,3,2,1,0:T(8,128)(2,1)S(1)} %pad_maximum_fusion), channel_id=1, source_target_pairs={{0,120},{8,0},{16,8},{24,16},{32,24},{40,32},{48,40},{56,48},{64,5... | collective-permute-start | bytes 1769480 | tf_op jit(solution)/shard_map/ppermute | solution.py:433
  12.3 22.3 %collective-permute-start.2 = (bf16[2,4,4,24,128]{4,3,2,1,0:T(8,128)(2,1)S(1)}, bf16[2,4,4,24,128]{4,3,2,1,0:T(8,128)(2,1)S(1)}, u32[]{:S(2)}, u32[]{:S(2)}) collective-permute-start(bf16[2,4,4,24,128]{4,3,2,1,0:T(8,128)(2,1)S(1)} %pad_maximum_fusion.2), channel_id=1, source_target_pairs={{0,127},{1,120},{2,121},{3,122},{4,123},{5,124},{6,125},{7,126},{8... | collective-permute-start | bytes 589832 | tf_op jit(solution)/shard_map/ppermute | solution.py:437
  34.6 0.7 copy-start.7
  34.7 0.9 copy-start.3
  34.7 1.0 copy-start.4
  80.8 3.1 %collective-permute-start.3 = (bf16[1152,512]{1,0:T(8,128)(2,1)}, bf16[1152,512]{1,0:T(8,128)(2,1)S(1)}, u32[]{:S(2)}, u32[]{:S(2)}) collective-permute-start(bf16[1152,512]{1,0:T(8,128)(2,1)} %get-tuple-element.48), channel_id=1, source_target_pairs={{0,8},{1,9},{2,10},{3,11},{4,12},{5,13},{6,14},{7,15},{8,0},{9,1},... | collective-permute-start | bytes 3538952 | tf_op jit(solution)/shard_map/ppermute | solution.py:463
  86.1 15.0 %collective-permute-start.4 = (bf16[288,512]{1,0:T(8,128)(2,1)S(1)}, bf16[288,512]{1,0:T(8,128)(2,1)S(1)}, u32[]{:S(2)}, u32[]{:S(2)}) collective-permute-start(bf16[288,512]{1,0:T(8,128)(2,1)S(1)} %get-tuple-element.87), channel_id=1, source_target_pairs={{0,32},{1,33},{2,34},{3,35},{4,36},{5,37},{6,38},{7,39},{8,10},{9,... | collective-permute-start | bytes 884744 | tf_op jit(solution)/shard_map/ppermute | solution.py:463
  86.2 15.0 %collective-permute-start.5 = (bf16[288,512]{1,0:T(8,128)(2,1)S(1)}, bf16[288,512]{1,0:T(8,128)(2,1)S(1)}, u32[]{:S(2)}, u32[]{:S(2)}) collective-permute-start(bf16[288,512]{1,0:T(8,128)(2,1)S(1)} %get-tuple-element.86), channel_id=1, source_target_pairs={{0,16},{1,17},{2,18},{3,19},{4,20},{5,21},{6,22},{7,23},{8,9},{9,1... | collective-permute-start | bytes 884744 | tf_op jit(solution)/shard_map/ppermute | solution.py:463
  87.4 13.8 %collective-permute-start.6 = (bf16[288,512]{1,0:T(8,128)(2,1)S(1)}, bf16[288,512]{1,0:T(8,128)(2,1)S(1)}, u32[]{:S(2)}, u32[]{:S(2)}) collective-permute-start(bf16[288,512]{1,0:T(8,128)(2,1)S(1)} %get-tuple-element.85), channel_id=1, source_target_pairs={{0,48},{1,49},{2,50},{3,51},{4,52},{5,53},{6,54},{7,55},{8,11},{9,... | collective-permute-start | bytes 884744 | tf_op jit(solution)/shard_map/ppermute | solution.py:463
  101.2 10.8 %copy-start.6 = (bf16[4,12,24,128]{3,2,1,0:T(8,128)(2,1)S(1)}, bf16[4,12,24,128]{3,2,1,0:T(8,128)(2,1)}, u32[]{:S(2)}) copy-start(bf16[4,12,24,128]{3,2,1,0:T(8,128)(2,1)} %get-tuple-element.63) | copy-start | bytes 884740
  101.2 15.6 %copy-start.5 = (bf16[12,4,24,128]{3,2,1,0:T(8,128)(2,1)S(1)}, bf16[12,4,24,128]{3,2,1,0:T(8,128)(2,1)}, u32[]{:S(2)}) copy-start(bf16[12,4,24,128]{3,2,1,0:T(8,128)(2,1)} %get-tuple-element.64) | copy-start | bytes 884740
  101.2 15.6 %copy-start.8 = (bf16[4,4,24,128]{3,2,1,0:T(8,128)(2,1)S(1)}, bf16[4,4,24,128]{3,2,1,0:T(8,128)(2,1)}, u32[]{:S(2)}) copy-start(bf16[4,4,24,128]{3,2,1,0:T(8,128)(2,1)} %get-tuple-element.65) | copy-start | bytes 294916
  101.4 4.9 %collective-permute-start.7 = (bf16[72,512]{1,0:T(8,128)(2,1)S(1)}, bf16[72,512]{1,0:T(8,128)(2,1)S(1)}, u32[]{:S(2)}, u32[]{:S(2)}) collective-permute-start(bf16[72,512]{1,0:T(8,128)(2,1)S(1)} %get-tuple-element.90), channel_id=1, source_target_pairs={{0,2},{1,3},{2,0},{3,1},{4,6},{5,7},{6,4},{7,5},{8,40},{9,41},{10,... | collective-permute-start | bytes 221192 | tf_op jit(solution)/shard_map/ppermute | solution.py:463
  101.9 5.4 %collective-permute-start.8 = (bf16[72,512]{1,0:T(8,128)(2,1)S(1)}, bf16[72,512]{1,0:T(8,128)(2,1)S(1)}, u32[]{:S(2)}, u32[]{:S(2)}) collective-permute-start(bf16[72,512]{1,0:T(8,128)(2,1)S(1)} %get-tuple-element.89), channel_id=1, source_target_pairs={{0,1},{1,2},{2,3},{3,0},{4,5},{5,6},{6,7},{7,4},{8,24},{9,25},{10,... | collective-permute-start | bytes 221192 | tf_op jit(solution)/shard_map/ppermute | solution.py:463
  102.5 4.8 %collective-permute-start.9 = (bf16[72,512]{1,0:T(8,128)(2,1)S(1)}, bf16[72,512]{1,0:T(8,128)(2,1)S(1)}, u32[]{:S(2)}, u32[]{:S(2)}) collective-permute-start(bf16[72,512]{1,0:T(8,128)(2,1)S(1)} %get-tuple-element.88), channel_id=1, source_target_pairs={{0,3},{1,0},{2,1},{3,2},{4,7},{5,4},{6,5},{7,6},{8,56},{9,57},{10,... | collective-permute-start | bytes 221192 | tf_op jit(solution)/shard_map/ppermute | solution.py:463
  107.3 9.5 %collective-permute-start.10 = (f32[72,512]{1,0:T(8,128)S(1)}, f32[72,512]{1,0:T(8,128)S(1)}, u32[]{:S(2)}, u32[]{:S(2)}) collective-permute-start(f32[72,512]{1,0:T(8,128)S(1)} %convert_add_fusion.2), channel_id=1, source_target_pairs={{0,4},{1,5},{2,6},{3,7},{4,0},{5,1},{6,2},{7,3},{8,12},{9,13},{10,... | collective-permute-start | bytes 442376 | tf_op jit(solution)/shard_map/ppermute | solution.py:463
  109.3 8.0 %collective-permute-start.11 = (f32[72,512]{1,0:T(8,128)S(1)}, f32[72,512]{1,0:T(8,128)S(1)}, u32[]{:S(2)}, u32[]{:S(2)}) collective-permute-start(f32[72,512]{1,0:T(8,128)S(1)} %convert_add_fusion.2), channel_id=1, source_target_pairs={{0,64},{1,65},{2,66},{3,67},{4,68},{5,69},{6,70},{7,71},{8,72},{9,... | collective-permute-start | bytes 442376 | tf_op jit(solution)/shard_map/ppermute | solution.py:463
  109.3 8.0 %collective-permute-start.12 = (f32[72,512]{1,0:T(8,128)S(1)}, f32[72,512]{1,0:T(8,128)S(1)}, u32[]{:S(2)}, u32[]{:S(2)}) collective-permute-start(f32[72,512]{1,0:T(8,128)S(1)} %convert_add_fusion.2), channel_id=1, source_target_pairs={{0,68},{1,69},{2,70},{3,71},{4,64},{5,65},{6,66},{7,67},{8,76},{9,... | collective-permute-start | bytes 442376 | tf_op jit(solution)/shard_map/ppermute | solution.py:463
  112.0 24.4 %collective-permute-start.16 = (bf16[4,12,24,128]{3,2,1,0:T(8,128)(2,1)S(1)}, bf16[4,12,24,128]{3,2,1,0:T(8,128)(2,1)S(1)}, u32[]{:S(2)}, u32[]{:S(2)}) collective-permute-start(bf16[4,12,24,128]{3,2,1,0:T(8,128)(2,1)S(1)} %copy-done.6), channel_id=1, source_target_pairs={{0,8},{8,16},{16,24},{24,32},{32,40},{40,48},{48,56},{56,64},{64,7... | collective-permute-start | bytes 884744 | tf_op jit(solution)/shard_map/ppermute | solution.py:433
  116.8 19.5 %collective-permute-start.17 = (bf16[12,4,24,128]{3,2,1,0:T(8,128)(2,1)S(1)}, bf16[12,4,24,128]{3,2,1,0:T(8,128)(2,1)S(1)}, u32[]{:S(2)}, u32[]{:S(2)}) collective-permute-start(bf16[12,4,24,128]{3,2,1,0:T(8,128)(2,1)S(1)} %copy-done.5), channel_id=1, source_target_pairs={{0,1},{1,2},{2,3},{3,4},{4,5},{5,6},{6,7},{7,0},{8,9},{9,10},{10,1... | collective-permute-start | bytes 884744 | tf_op jit(solution)/shard_map/ppermute | solution.py:435
  116.8 16.3 %collective-permute-start.18 = (bf16[4,4,24,128]{3,2,1,0:T(8,128)(2,1)S(1)}, bf16[4,4,24,128]{3,2,1,0:T(8,128)(2,1)S(1)}, u32[]{:S(2)}, u32[]{:S(2)}) collective-permute-start(bf16[4,4,24,128]{3,2,1,0:T(8,128)(2,1)S(1)} %copy-done.8), channel_id=1, source_target_pairs={{0,9},{1,10},{2,11},{3,12},{4,13},{5,14},{6,15},{7,8},{8,17},{9,18... | collective-permute-start | bytes 294920 | tf_op jit(solution)/shard_map/ppermute | solution.py:437
  117.4 15.8 %collective-permute-start.13 = (bf16[72,512]{1,0:T(8,128)(2,1)S(1)}, bf16[72,512]{1,0:T(8,128)(2,1)S(1)}, u32[]{:S(2)}, u32[]{:S(2)}) collective-permute-start(bf16[72,512]{1,0:T(8,128)(2,1)S(1)} %add_convert_fusion), channel_id=1, source_target_pairs={{0,1},{1,2},{2,3},{3,0},{4,5},{5,6},{6,7},{7,4},{8,24},{9,25},{10,... | collective-permute-start | bytes 221192 | tf_op jit(solution)/shard_map/ppermute | solution.py:463
  117.9 15.3 %collective-permute-start.14 = (bf16[72,512]{1,0:T(8,128)(2,1)S(1)}, bf16[72,512]{1,0:T(8,128)(2,1)S(1)}, u32[]{:S(2)}, u32[]{:S(2)}) collective-permute-start(bf16[72,512]{1,0:T(8,128)(2,1)S(1)} %add_convert_fusion), channel_id=1, source_target_pairs={{0,2},{1,3},{2,0},{3,1},{4,6},{5,7},{6,4},{7,5},{8,40},{9,41},{10,... | collective-permute-start | bytes 221192 | tf_op jit(solution)/shard_map/ppermute | solution.py:463
  133.1 3.2 %collective-permute-start.15 = (bf16[72,512]{1,0:T(8,128)(2,1)S(1)}, bf16[72,512]{1,0:T(8,128)(2,1)S(1)}, u32[]{:S(2)}, u32[]{:S(2)}) collective-permute-start(bf16[72,512]{1,0:T(8,128)(2,1)S(1)} %add_convert_fusion), channel_id=1, source_target_pairs={{0,3},{1,0},{2,1},{3,2},{4,7},{5,4},{6,5},{7,6},{8,56},{9,57},{10,... | collective-permute-start | bytes 221192 | tf_op jit(solution)/shard_map/ppermute | solution.py:463
  136.4 10.0 %collective-permute-start.19 = (bf16[288,512]{1,0:T(8,128)(2,1)S(1)}, bf16[288,512]{1,0:T(8,128)(2,1)S(1)}, u32[]{:S(2)}, u32[]{:S(2)}) collective-permute-start(bf16[288,512]{1,0:T(8,128)(2,1)S(1)} %constant_dynamic-update-slice_fusion.7), channel_id=1, source_target_pairs={{0,16},{1,17},{2,18},{3,19},{4,20},{5,21},{6,22},{7,23},{8,9},{9,1... | collective-permute-start | bytes 884744 | tf_op jit(solution)/shard_map/ppermute | solution.py:463
  136.5 9.9 %collective-permute-start.20 = (bf16[288,512]{1,0:T(8,128)(2,1)S(1)}, bf16[288,512]{1,0:T(8,128)(2,1)S(1)}, u32[]{:S(2)}, u32[]{:S(2)}) collective-permute-start(bf16[288,512]{1,0:T(8,128)(2,1)S(1)} %constant_dynamic-update-slice_fusion.7), channel_id=1, source_target_pairs={{0,32},{1,33},{2,34},{3,35},{4,36},{5,37},{6,38},{7,39},{8,10},{9,... | collective-permute-start | bytes 884744 | tf_op jit(solution)/shard_map/ppermute | solution.py:463
  136.6 10.5 %collective-permute-start.21 = (bf16[288,512]{1,0:T(8,128)(2,1)S(1)}, bf16[288,512]{1,0:T(8,128)(2,1)S(1)}, u32[]{:S(2)}, u32[]{:S(2)}) collective-permute-start(bf16[288,512]{1,0:T(8,128)(2,1)S(1)} %constant_dynamic-update-slice_fusion.7), channel_id=1, source_target_pairs={{0,48},{1,49},{2,50},{3,51},{4,52},{5,53},{6,54},{7,55},{8,11},{9,... | collective-permute-start | bytes 884744 | tf_op jit(solution)/shard_map/ppermute | solution.py:463
  147.3 1.0 copy-start
  147.3 3.4 %collective-permute-start.22 = (bf16[1152,512]{1,0:T(8,128)(2,1)S(1)}, bf16[1152,512]{1,0:T(8,128)(2,1)S(1)}, u32[]{:S(2)}, u32[]{:S(2)}) collective-permute-start(bf16[1152,512]{1,0:T(8,128)(2,1)S(1)} %constant_dynamic-update-slice_fusion.own_ref.own_rest_ref), channel_id=1, source_target_pairs={{0,8},{1,9},{2,10},{3,11},{4,12},{5,13},{6,14},{7,15},{8,0},{9,1},... | collective-permute-start | bytes 3538952 | tf_op jit(solution)/shard_map/ppermute | solution.py:463
  150.8 1.0 copy-start.1

commit v5 on v4

--- a/solution.py
+++ b/solution.py
@@ -105,33 +105,37 @@
     pieces = INNER if first else RIM
     arrays = refs[:2] if first else refs[:5]
     refs = refs[len(arrays) :]
-    gamma_ref, w_ref, wT_ref, wproj_ref, bias_hbm = refs[:5]
-    refs = refs[5:]
+    gamma_ref, w_ref, wproj_ref, bias_hbm = refs[:4]
+    refs = refs[4:]
     if first:
-        dT_ref, dbias_ref, small_ref = refs[:3]
-        refs = refs[3:]
+        dT_ref, small_ref, acc_hbm, biasT_hbm = refs[:4]
+        bias_s, out_sem = refs[4:6]
+        refs = refs[6:]
     else:
         acc_hbm, accs_ref = refs[:2]
         dT_ref, away_ref, keep_ref = refs[2:5]
-        dbias_ref, small_ref, acc_sem = refs[5:8]
+        small_ref, acc_s, acc_sem = refs[5:8]
         refs = refs[8:]
-    (in_sem, bias_sem, blk_s, bias_s, biasT_s, xh_s, adj_s, qext_s, gz_s, kext_s, v_s, kT_s, vT_s, gT_s, attT_s, u_s, e_s, ds_s) = refs
+    (in_sem, bias_sem, blk_s, dbias_ref, biasT_s, wT_s, xh_s, adj_s, qext_s, gz_s, kext_s, v_s, kT_s, vT_s, gT_s, attT_s, u_s, e_s, ds_s) = refs
     step = pl.program_id(0)
 
     def bias_copy(h):
-        return pltpu.make_async_copy(bias_hbm.at[h], bias_s.at[h], bias_sem.at[h])
+        return pltpu.make_async_copy(bias_hbm.at[h], (bias_s if first else biasT_s).at[h], bias_sem.at[h])
+
+    def out_copy(n, h):
+        src, dst = ((dbias_ref, acc_hbm), (biasT_s, biasT_hbm))[n]
+        return pltpu.make_async_copy(src.at[h], dst.at[h], out_sem.at[n, h])
 
     @pl.when(step == 0)
     def _():
         start_all(pieces, arrays, blk_s, in_sem)
         for h in range(HEADS):
             bias_copy(h).start()
-        if first:
+        if not first:
+            pltpu.make_async_copy(acc_hbm, acc_s, acc_sem).start()
             dbias_ref[...] = jnp.zeros_like(dbias_ref)
-            small_ref[...] = jnp.zeros_like(small_ref)
-        else:
-            pltpu.make_async_copy(acc_hbm, dbias_ref, acc_sem).start()
-            small_ref[...] = accs_ref[...]
+        small_ref[...] = jnp.zeros_like(small_ref)
+        wT_s[...] = w_ref[...].astype(F32).T.astype(BF)
         qext_s[...] = jnp.zeros_like(qext_s)
         gz_s[...] = jnp.zeros_like(gz_s)
         vT_s[...] = jnp.ones_like(vT_s)
@@ -151,18 +155,17 @@
         xh_s[z] = pltpu.roll(jnp.where(low, xh[:, z1], xh[:, z]) * gamma_ref[...], SHIFT, 1).reshape(T, C).astype(BF)
         adj_s[z] = pltpu.roll(jnp.where(low, a[:, z1], a[:, z]), SHIFT, 1).reshape(T, C).astype(BF)
 
-    @pl.when(step == 0)
-    def _():
-        for h in range(HEADS):
-            bias_copy(h).wait()
-            biasT_s[h] = bias_s[h].T * (1.0 / SCALE)
-        if not first:
-            pltpu.make_async_copy(acc_hbm, dbias_ref, acc_sem).wait()
-
-    def window(z, carry):
+    if not first:
+
+        @pl.when(step == 0)
+        def _():
+            for h in range(HEADS):
+                bias_copy(h).wait()
+
+    def window(z, opening=False, closing=False):
         nrm = xh_s[z]
         adj = adj_s[z]
-        qkvT = dot_nt(wT_ref[...], nrm).astype(BF)
+        qkvT = dot_nt(wT_s[...], nrm).astype(BF)
         kT_s[...] = qkvT[C : 2 * C]
         regions = query_regions((edge_x, edge_y, z == 2))
         for h in range(HEADS):
@@ -178,6 +181,10 @@
 
         def scores(h, c):
             ks = slice(c * KC, (c + 1) * KC)
+            if opening and c == 0:
+                bias_copy(h).wait()
+                biasT_s[h] = bias_s[h].T * (1.0 / SCALE)
+                out_copy(1, h).start()
             u = dot(kext_s[ks], qext_s[h]) + biasT_s[h, ks]
             u_s[h % 2, ks] = u
             top = jnp.max(u.reshape(KC // 8, 8, T), axis=0)
@@ -206,17 +213,21 @@
             dp = dot(v_s[ks], gz_s[h])
             ds = e_s[h % 3, ks].astype(F32) * (dp - held["delta", h])
             ds_s[h % 2, ks] = ds.astype(BF)
-            dbias_ref[h, ks] += ds
+            if opening:
+                dbias_ref[h, ks] = ds
+            else:
+                dbias_ref[h, ks] += ds
+            if closing and c == chunks - 1:
+                out_copy(0, h).start()
 
         def qkv_grads(h, c):
             hs = slice(HD * h, HD * (h + 1))
-            ks = slice(c * KC, (c + 1) * KC)
-            dq = dot(kT_s[hs, ks], ds_s[h % 2, ks])
-            held["dq", h] = dq if c == 0 else dq + held["dq", h]
-            dT_ref[z, C + HD * h : C + HD * (h + 1), ks] = (dot_nt(qext_s[h, hs], ds_s[h % 2, ks]) * SCALE).astype(BF)
-            dT_ref[z, 2 * C + HD * h : 2 * C + HD * (h + 1), ks] = dot_nt(gz_s[h, hs], e_s[h % 3, ks]).astype(BF)
+            if c == 0:
+                dk = dot_nt(qext_s[h, hs], ds_s[h % 2]) * SCALE
+                dT_ref[z, C + HD * h : C + HD * (h + 1)] = dk.astype(BF)
             if c == chunks - 1:
-                dT_ref[z, hs] = (held["dq", h] * SCALE).astype(BF)
+                dT_ref[z, 2 * C + HD * h : 2 * C + HD * (h + 1)] = dot_nt(gz_s[h, hs], e_s[h % 3]).astype(BF)
+                dT_ref[z, hs] = (dot(kT_s[hs], ds_s[h % 2]) * SCALE).astype(BF)
 
         for turn in range(HEADS + 3):
             for c in range(chunks):
@@ -225,19 +236,27 @@
                         stage(turn - lag, c)
         small_ref[:C] += dot(attT_s[...], adj)
         small_ref[C:] += dot(dT_ref[z], nrm)
-        return carry
-
-    lax.fori_loop(0, 3, window, 0)
-
-    if not first:
+
+    if first:
+        for z in range(3):
+            window(z, opening=z == 0, closing=z == 2)
+        for h in range(HEADS):
+            for n in range(2):
+                out_copy(n, h).wait()
+    else:
+        lax.fori_loop(0, 3, lambda z, carry: (window(z), carry)[1], 0)
 
         @pl.when(step == pl.num_programs(0) - 1)
         def _():
+            pltpu.make_async_copy(acc_hbm, acc_s, acc_sem).wait()
             mine = lax.axis_index("gx") % 2
-            table = jnp.concatenate([small_ref[:C], small_ref[C:].T], axis=1)
+            small = small_ref[...] + accs_ref[...]
+            table = jnp.concatenate([small[:C], small[C:].T], axis=1)
             for j in range(2):
-                away_ref[j * T : (j + 1) * T] = dbias_ref[2 * (1 - mine) + j].T.astype(BF)
-                keep_ref[j * T : (j + 1) * T] = dbias_ref[2 * mine + j].T
+                h = 2 * (1 - mine) + j
+                away_ref[j * T : (j + 1) * T] = (dbias_ref[h] + acc_s[h]).T.astype(BF)
+                h = 2 * mine + j
+                keep_ref[j * T : (j + 1) * T] = (dbias_ref[h] + acc_s[h]).T
             away_ref[2 * T :] = jnp.where(mine == 1, table, 0.0).astype(BF)
             keep_ref[2 * T :] = jnp.where(mine == 0, table, 0.0)
 
@@ -301,22 +320,23 @@
     small = (4 * C, C)
     blocks = 1 if first else 3
     pieces = INNER if first else RIM
-    ins = [ANYWHERE] * len(arrays) + [whole((1, C)), whole((C, 3 * C)), whole((3 * C, C)), whole((C, C)), ANYWHERE]
+    ins = [ANYWHERE] * len(arrays) + [whole((1, C)), whole((C, 3 * C)), whole((C, C)), ANYWHERE]
     if first:
-        outs = [DT_BLOCK, whole(square), whole(small)]
-        shapes = [((blocks,) + DT_SHAPE, BF), (square, F32), (small, F32)]
-        scratch = []
+        outs = [DT_BLOCK, whole(small), ANYWHERE, ANYWHERE]
+        shapes = [((blocks,) + DT_SHAPE, BF), (small, F32), (square, F32), (square, F32)]
+        scratch = [pltpu.VMEM(square, F32), pltpu.SemaphoreType.DMA((2, HEADS))]
     else:
         ins += [ANYWHERE, whole(small)]
         outs = [DT_BLOCK, whole((HALF, T)), whole((HALF, T))]
         shapes = [((blocks,) + DT_SHAPE, BF), ((HALF, T), BF), ((HALF, T), F32)]
-        scratch = [pltpu.VMEM(square, F32), pltpu.VMEM(small, F32), pltpu.SemaphoreType.DMA]
+        scratch = [pltpu.VMEM(small, F32), pltpu.VMEM(square, F32), pltpu.SemaphoreType.DMA]
     scratch += [
         pltpu.SemaphoreType.DMA((2, len(pieces))),
         pltpu.SemaphoreType.DMA((HEADS,)),
         pltpu.VMEM((2, blocks, 8, 8, 24, C), BF),
         pltpu.VMEM(square, F32),
         pltpu.VMEM(square, F32),
+        pltpu.VMEM((3 * C, C), BF),
         pltpu.VMEM((3, T, C), BF),
         pltpu.VMEM((3, T, C), BF),
         pltpu.VMEM((HEADS, 2 * C, T), BF),
@@ -381,6 +401,7 @@
             out_specs=pl.BlockSpec((pl.Squeezed(), T, T), lambda j, m: (2 * m[0] + j, 0, 0)),
         ),
         out_shape=jax.ShapeDtypeStruct((HEADS, T, T), F32),
+        compiler_params=pltpu.CompilerParams(vmem_limit_bytes=60 * 1024 * 1024),
         name="spread_own",
     )(mine, own)
 
@@ -423,6 +444,7 @@
             jax.ShapeDtypeStruct((1, C), F32),
         ],
         input_output_aliases={6: 0},
+        compiler_params=pltpu.CompilerParams(vmem_limit_bytes=60 * 1024 * 1024),
         name="spread_got",
     )(mine, got, own, got, gamma, w, grad_bias)
 
@@ -502,10 +524,9 @@
     from_xy = shifted(jnp.stack([v[:4, :4] for v in both]), -1, -1)
     w = triple_projection_matrix
     gamma = rescale_multiplier.reshape(1, C)
-    params = (gamma, w, w.T, w_proj, pos_bias)
-    inner_dT, acc, acc_small = sublayer(True, both, params)
+    inner_dT, acc_small, acc, biasT = sublayer(True, both, (gamma, w, w_proj, pos_bias))
     around = both + (from_x, from_y, from_xy)
-    rim_dT, away, keep = sublayer(False, around, params, (acc, acc_small))
+    rim_dT, away, keep = sublayer(False, around, (gamma, w, w_proj, biasT), (acc, acc_small))
 
     first, second, third = (ACROSS_X, ACROSS_Z), (ACROSS_Z, ACROSS_X), (ACROSS_Y, ACROSS_Y)
     values = keep + send(away, (CORE, CORE), 1).astype(F32)
@@ -514,8 +535,6 @@
     values, got, back_x, back_y, back_xy = lax.optimization_barrier((values, got, back_x, back_y, back_xy))
     back = (shifted(back_x, 1, 0), shifted(back_y, 0, 1), shifted(back_xy, 1, 1))
     values, got = parts_sent(added(values, got), second)
-    (gin,) = finish(True, both, gamma, w, inner_dT, (gin,))
-    values, got, gin = lax.optimization_barrier((values, got, gin))
     values = added(values, got)
     got = all_sent(values, third)
     values = ((values + got[2]) + (got[1] + got[3])).astype(BF)
@@ -523,6 +542,8 @@
     values, got, back = lax.optimization_barrier((values, got, back))
     values = gathered(values, got, second)
     got = all_sent(values, first)
+    (gin, inner_dT) = lax.optimization_barrier((gin, inner_dT, values))[:2]
+    (gin,) = finish(True, both, gamma, w, inner_dT, (gin,))
     for part, place in zip(back, ((0, 4), (4, 0), (0, 0))):
         gin = lax.dynamic_update_slice(gin, part, place + (0, 0))
     values, got, gin = lax.optimization_barrier((values, got, gin))

time: 155 us -> 150 us (0.968)
  waiting for transfers between devices: 25.5 us -> 22.2 us
  Pallas kernels: 80.4 us -> 77.8 us
  starting transfers between devices: 35.4 us -> 37.3 us
    ppermute x17, waiting for transfers between devices: 14.5 us -> 10.9 us  [send(): return lax.ppermute(values, ('gx', 'gy'), pairs)]
    pallas_call x2, Pallas kernels: 63.9 us -> 61.3 us  [sublayer(): pl.pallas_call(functools.partial(kernel, first), grid=(blocks,), in_specs...]
    ppermute x17, starting transfers between devices: 19.1 us -> 20.8 us  [send(): return lax.ppermute(values, ('gx', 'gy'), pairs)]
    unnamed x19 -> x14, local copies, waits for them, and re-layouts: 3.79 us -> 3.01 us
  transfers between devices with their start and end apart: 23 -> 23, of which waited for: 7 -> 8; matrix products, arithmetic and copies ran while one was open for 3% -> 3% of each run, Pallas kernels for 21% -> 20%
where the time goes in v5:
time: 150 us
  Pallas kernels  77.8 us (52%)
  starting transfers between devices  37.3 us (25%)
  waiting for transfers between devices  22.2 us (15%)
  local copies, waits for them, and re-layouts  8.86 us (6%)
  other arithmetic  2.4 us (2%)
    pallas_call x2, Pallas kernels, sublayer(): pl.pallas_call(functools.partial(kernel, first), grid=(blocks,), in_specs...  61.3 us
    ppermute x17, starting transfers between devices, send(): return lax.ppermute(values, ('gx', 'gy'), pairs)  20.8 us
    pallas_call x2, Pallas kernels, finish(): pl.pallas_call(functools.partial(finish_kernel, first), grid=(blocks,), i...  11.3 us
    ppermute x2, waiting for transfers between devices, shifted(): return lax.ppermute(values, ('gx', 'gy'), pairs)  11.3 us
    ppermute x17, waiting for transfers between devices, send(): return lax.ppermute(values, ('gx', 'gy'), pairs)  10.9 us
    ppermute x2, starting transfers between devices, shifted(): return lax.ppermute(values, 'gy', [(i, (i + by_y) % ny) for i in range(ny)])  7.29 us
    ppermute x2, starting transfers between devices, shifted(): return lax.ppermute(values, 'gx', [(i, (i + by_x) % nx) for i in range(nx)])  5.93 us
    ppermute x2, starting transfers between devices, shifted(): return lax.ppermute(values, ('gx', 'gy'), pairs)  3.24 us
  transfers between devices with their start and end apart: 23, of which 8 were waited for; matrix products, arithmetic and copies ran while one was open for 3% of the time, Pallas kernels for 20%

profile of v5, /device:TPU:1, one launch (start us, length us, event | category | flops | bytes accessed | tf_op | source)
XLA Modules:
  0.0 149.7 jit_solution(13512628314850508912)
XLA Ops:
  0.6 1.1 slice_bitcast_fusion
  1.8 7.3 %collective-permute-start.1 = (bf16[2,12,4,24,128]{4,3,2,1,0:T(8,128)(2,1)S(1)}, bf16[2,12,4,24,128]{4,3,2,1,0:T(8,128)(2,1)S(1)}, u32[]{:S(2)}, u32[]{:S(2)}) collective-permute-start(bf16[2,12,4,24,128]{4,3,2,1,0:T(8,128)(2,1)S(1)} %pad_maximum_fusion.1), channel_id=1, source_target_pairs={{0,7},{1,0},{2,1},{3,2},{4,3},{5,4},{6,5},{7,6},{8,15},{9,8},{10,9... | collective-permute-start | bytes 1769480 | tf_op jit(solution)/shard_map/ppermute | solution.py:457
  9.1 1.1 slice_bitcast_fusion.2
  10.3 1.0 collective-permute-start
  11.3 1.0 slice_bitcast_fusion.4
  12.3 2.7 %collective-permute-start.2 = (bf16[2,4,4,24,128]{4,3,2,1,0:T(8,128)(2,1)S(1)}, bf16[2,4,4,24,128]{4,3,2,1,0:T(8,128)(2,1)S(1)}, u32[]{:S(2)}, u32[]{:S(2)}) collective-permute-start(bf16[2,4,4,24,128]{4,3,2,1,0:T(8,128)(2,1)S(1)} %pad_maximum_fusion.2), channel_id=1, source_target_pairs={{0,127},{1,120},{2,121},{3,122},{4,123},{5,124},{6,125},{7,126},{8... | collective-permute-start | bytes 589832 | tf_op jit(solution)/shard_map/ppermute | solution.py:459
  15.0 16.7 %inner_windows.1 = (bf16[1,3,384,512]{3,2,1,0:T(8,128)(2,1)}, f32[512,128]{1,0:T(8,128)}, f32[4,512,512]{2,1,0:T(8,128)}, f32[4,512,512]{2,1,0:T(8,128)}) custom-call(bf16[16,16,24,128]{3,2,1,0:T(8,128)(2,1)} %refs_0_.7, bf16[16,16,24,128]{3,2,1,0:T(8,128)(2,1)} %refs_1_.7, f32[1,128]{1,0:T(1,128)} %bitcast.15, bf16[128,384]{1,0:T(8,128)(2,1)} %w_ref.1, ...), custom_call_target="tpu_custom_call" | custom-call | flops 12000000000 | bytes 10000000 | tf_op jit(solution)/shard_map/inner_windows/pallas_call | solution.py:354
  31.8 0.6 copy-done.6
  32.4 0.2 copy-done.2
  32.7 0.2 copy-done.3
  32.8 44.6 %rim_windows.1 = (bf16[3,3,384,512]{3,2,1,0:T(8,128)(2,1)}, bf16[1152,512]{1,0:T(8,128)(2,1)}, f32[1152,512]{1,0:T(8,128)}) custom-call(bf16[16,16,24,128]{3,2,1,0:T(8,128)(2,1)} %refs_0_.7, bf16[16,16,24,128]{3,2,1,0:T(8,128)(2,1)} %refs_1_.7, bf16[2,4,12,24,128]{4,3,2,1,0:T(8,128)(2,1)} %copy-done.3, bf16[2,12,4,24,128]{4,3,2,1,0:T(8,128)(2,1)} %copy-done.2, ...), custom_call_target="tpu_custom_call" | custom-call | flops 35999997952 | bytes 30000000 | tf_op jit(solution)/shard_map/rim_windows/pallas_call | solution.py:354
  77.4 0.1 collective-permute-start.3
  77.7 2.9 %collective-permute-done.3 = bf16[1152,512]{1,0:T(8,128)(2,1)S(1)} collective-permute-done((bf16[1152,512]{1,0:T(8,128)(2,1)}, bf16[1152,512]{1,0:T(8,128)(2,1)S(1)}, u32[]{:S(2)}, u32[]{:S(2)}) %collective-permute-start.3) | collective-permute-done | bytes 1179680 | tf_op jit(solution)/shard_map/ppermute | solution.py:485
  80.5 2.0 %convert_add_fusion = f32[1152,512]{1,0:T(8,128)S(1)} fusion(f32[1152,512]{1,0:T(8,128)} %get-tuple-element.46, bf16[1152,512]{1,0:T(8,128)(2,1)S(1)} %collective-permute-done.3), kind=kLoop, calls=%fused_computation | loop fusion | flops 1179648 | bytes 5898240 | tf_op jit(solution)/shard_map/add | solution.py:532
  82.6 0.1 dynamic-slice_convert_fusion
  82.7 0.1 collective-permute-start.4
  82.8 1.2 collective-permute-start.5
  84.0 2.3 %collective-permute-start.6 = (bf16[288,512]{1,0:T(8,128)(2,1)S(1)}, bf16[288,512]{1,0:T(8,128)(2,1)S(1)}, u32[]{:S(2)}, u32[]{:S(2)}) collective-permute-start(bf16[288,512]{1,0:T(8,128)(2,1)S(1)} %get-tuple-element.81), channel_id=1, source_target_pairs={{0,48},{1,49},{2,50},{3,51},{4,52},{5,53},{6,54},{7,55},{8,11},{9,... | collective-permute-start | bytes 884744 | tf_op jit(solution)/shard_map/ppermute | solution.py:485
  86.3 7.0 %rim_finish.1 = (bf16[16,16,24,128]{3,2,1,0:T(8,128)(2,1)}, bf16[4,12,24,128]{3,2,1,0:T(8,128)(2,1)}, bf16[12,4,24,128]{3,2,1,0:T(8,128)(2,1)}, bf16[4,4,24,128]{3,2,1,0:T(8,128)(2,1)}) custom-call(bf16[16,16,24,128]{3,2,1,0:T(8,128)(2,1)} %refs_0_.7, bf16[16,16,24,128]{3,2,1,0:T(8,128)(2,1)} %refs_1_.7, bf16[2,4,12,24,128]{4,3,2,1,0:T(8,128)(2,1)} %copy-done.3, ...), custom_call_target="tpu_custom_call" | custom-call | flops 3000000000 | bytes 9000000 | tf_op jit(solution)/shard_map/rim_finish/pallas_call | solution.py:371
  93.5 0.1 convert_add_fusion.1
  93.7 0.5 collective-permute-start.7
  94.1 3.1 %collective-permute-start.8 = (bf16[72,512]{1,0:T(8,128)(2,1)S(1)}, bf16[72,512]{1,0:T(8,128)(2,1)S(1)}, u32[]{:S(2)}, u32[]{:S(2)}) collective-permute-start(bf16[72,512]{1,0:T(8,128)(2,1)S(1)} %get-tuple-element.86), channel_id=1, source_target_pairs={{0,1},{1,2},{2,3},{3,0},{4,5},{5,6},{6,7},{7,4},{8,24},{9,25},{10,... | collective-permute-start | bytes 221192 | tf_op jit(solution)/shard_map/ppermute | solution.py:485
  97.2 1.3 collective-permute-done.7
  98.5 0.7 collective-permute-done.8
  99.2 1.5 %collective-permute-done.9 = bf16[72,512]{1,0:T(8,128)(2,1)S(1)} collective-permute-done((bf16[72,512]{1,0:T(8,128)(2,1)S(1)}, bf16[72,512]{1,0:T(8,128)(2,1)S(1)}, u32[]{:S(2)}, u32[]{:S(2)}) %collective-permute-start.9) | collective-permute-done | bytes 73760 | tf_op jit(solution)/shard_map/ppermute | solution.py:485
  100.8 3.6 %collective-permute-start.10 = (f32[72,512]{1,0:T(8,128)S(1)}, f32[72,512]{1,0:T(8,128)S(1)}, u32[]{:S(2)}, u32[]{:S(2)}) collective-permute-start(f32[72,512]{1,0:T(8,128)S(1)} %convert_add_fusion.2), channel_id=1, source_target_pairs={{0,4},{1,5},{2,6},{3,7},{4,0},{5,1},{6,2},{7,3},{8,12},{9,13},{10,... | collective-permute-start | bytes 442376 | tf_op jit(solution)/shard_map/ppermute | solution.py:485
  104.4 2.7 %collective-permute-start.12 = (f32[72,512]{1,0:T(8,128)S(1)}, f32[72,512]{1,0:T(8,128)S(1)}, u32[]{:S(2)}, u32[]{:S(2)}) collective-permute-start(f32[72,512]{1,0:T(8,128)S(1)} %convert_add_fusion.2), channel_id=1, source_target_pairs={{0,68},{1,69},{2,70},{3,71},{4,64},{5,65},{6,66},{7,67},{8,76},{9,... | collective-permute-start | bytes 442376 | tf_op jit(solution)/shard_map/ppermute | solution.py:485
  107.0 4.9 %collective-permute-start.16 = (bf16[4,12,24,128]{3,2,1,0:T(8,128)(2,1)S(1)}, bf16[4,12,24,128]{3,2,1,0:T(8,128)(2,1)S(1)}, u32[]{:S(2)}, u32[]{:S(2)}) collective-permute-start(bf16[4,12,24,128]{3,2,1,0:T(8,128)(2,1)S(1)} %copy-done.5), channel_id=1, source_target_pairs={{0,8},{8,16},{16,24},{24,32},{32,40},{40,48},{48,56},{56,64},{64,7... | collective-permute-start | bytes 884744 | tf_op jit(solution)/shard_map/ppermute | solution.py:455
  112.0 0.5 collective-permute-start.18
  112.5 0.2 collective-permute-start.13
  112.7 4.3 %collective-permute-start.14 = (bf16[72,512]{1,0:T(8,128)(2,1)S(1)}, bf16[72,512]{1,0:T(8,128)(2,1)S(1)}, u32[]{:S(2)}, u32[]{:S(2)}) collective-permute-start(bf16[72,512]{1,0:T(8,128)(2,1)S(1)} %add_convert_fusion), channel_id=1, source_target_pairs={{0,2},{1,3},{2,0},{3,1},{4,6},{5,7},{6,4},{7,5},{8,40},{9,41},{10,... | collective-permute-start | bytes 221192 | tf_op jit(solution)/shard_map/ppermute | solution.py:485
  117.0 11.3 %collective-permute-done.18 = bf16[4,4,24,128]{3,2,1,0:T(8,128)(2,1)S(1)} collective-permute-done((bf16[4,4,24,128]{3,2,1,0:T(8,128)(2,1)}, bf16[4,4,24,128]{3,2,1,0:T(8,128)(2,1)S(1)}, u32[]{:S(2)}, u32[]{:S(2)}) %collective-permute-start.18) | collective-permute-done | bytes 98336 | tf_op jit(solution)/shard_map/ppermute | solution.py:459
  128.3 3.2 %collective-permute-done.15 = bf16[72,512]{1,0:T(8,128)(2,1)S(1)} collective-permute-done((bf16[72,512]{1,0:T(8,128)(2,1)S(1)}, bf16[72,512]{1,0:T(8,128)(2,1)S(1)}, u32[]{:S(2)}, u32[]{:S(2)}) %collective-permute-start.15) | collective-permute-done | bytes 73760 | tf_op jit(solution)/shard_map/ppermute | solution.py:485
  131.6 0.1 collective-permute-start.19
  131.7 0.1 collective-permute-start.20
  131.8 2.6 %collective-permute-start.21 = (bf16[288,512]{1,0:T(8,128)(2,1)S(1)}, bf16[288,512]{1,0:T(8,128)(2,1)S(1)}, u32[]{:S(2)}, u32[]{:S(2)}) collective-permute-start(bf16[288,512]{1,0:T(8,128)(2,1)S(1)} %constant_dynamic-update-slice_fusion.7), channel_id=1, source_target_pairs={{0,48},{1,49},{2,50},{3,51},{4,52},{5,53},{6,54},{7,55},{8,11},{9,... | collective-permute-start | bytes 884744 | tf_op jit(solution)/shard_map/ppermute | solution.py:485
  134.4 4.3 %inner_finish.1 = bf16[16,16,24,128]{3,2,1,0:T(8,128)(2,1)} custom-call(bf16[16,16,24,128]{3,2,1,0:T(8,128)(2,1)} %refs_0_.7, bf16[16,16,24,128]{3,2,1,0:T(8,128)(2,1)} %refs_1_.7, f32[1,128]{1,0:T(1,128)} %bitcast.18, bf16[128,384]{1,0:T(8,128)(2,1)} %w_ref.1, bf16[1,3,384,512]{3,2,1,0:T(8,128)(2,1)} %get-tuple-element.65.refs_4_, ...), custom_call_target="tpu_custom_call", output_to_operand_aliasing={{}: (5, {})} | custom-call | flops 1000000000 | bytes 3000000 | tf_op jit(solution)/shard_map/inner_finish/pallas_call | solution.py:371
  138.7 0.8 constant_dynamic-update-slice_fusion.6
  139.4 0.8 constant_dynamic-update-slice_fusion.5
  140.2 0.7 constant_dynamic-update-slice_fusion.4
  140.9 0.7 collective-permute-done.19
  141.6 0.6 collective-permute-done.21
  142.2 0.1 broadcast_in_dim.7
  142.5 0.1 collective-permute-start.22
  142.6 0.9 copy-done
  143.5 2.4 %spread_own.1._ = f32[4,512,512]{2,1,0:T(8,128)} custom-call(s32[1]{0:T(128)} %bitcast.7.mine_ref, bf16[1152,512]{1,0:T(8,128)(2,1)} %copy-done), custom_call_target="tpu_custom_call" | custom-call | tf_op jit(solution)/shard_map/spread_own/pallas_call | solution.py:395
  145.9 1.1 copy-done.1
  147.0 2.7 %spread_got.1 = (f32[4,512,512]{2,1,0:T(8,128)}, f32[128,128]{1,0:T(8,128)}, f32[128,384]{1,0:T(8,128)}, f32[1,128]{1,0:T(1,128)}) custom-call(s32[1]{0:T(128)} %bitcast.7.mine_ref, bf16[1152,512]{1,0:T(8,128)(2,1)} %copy-done.1, bf16[1152,512]{1,0:T(8,128)(2,1)} %copy-done, bf16[1152,512]{1,0:T(8,128)(2,1)} %copy-done.1, ...), custom_call_target="tpu_custom_call", output_to_operand_aliasing={{0}: (6, {})} | custom-call | tf_op jit(solution)/shard_map/spread_got/pallas_call | solution.py:427
  (44 shorter events, 0.6 us)
Async XLA Ops:
  1.8 29.9 %collective-permute-start.1 = (bf16[2,12,4,24,128]{4,3,2,1,0:T(8,128)(2,1)S(1)}, bf16[2,12,4,24,128]{4,3,2,1,0:T(8,128)(2,1)S(1)}, u32[]{:S(2)}, u32[]{:S(2)}) collective-permute-start(bf16[2,12,4,24,128]{4,3,2,1,0:T(8,128)(2,1)S(1)} %pad_maximum_fusion.1), channel_id=1, source_target_pairs={{0,7},{1,0},{2,1},{3,2},{4,3},{5,4},{6,5},{7,6},{8,15},{9,8},{10,9... | collective-permute-start | bytes 1769480 | tf_op jit(solution)/shard_map/ppermute | solution.py:457
  10.3 21.5 %collective-permute-start = (bf16[2,4,12,24,128]{4,3,2,1,0:T(8,128)(2,1)S(1)}, bf16[2,4,12,24,128]{4,3,2,1,0:T(8,128)(2,1)S(1)}, u32[]{:S(2)}, u32[]{:S(2)}) collective-permute-start(bf16[2,4,12,24,128]{4,3,2,1,0:T(8,128)(2,1)S(1)} %pad_maximum_fusion), channel_id=1, source_target_pairs={{0,120},{8,0},{16,8},{24,16},{32,24},{40,32},{48,40},{56,48},{64,5... | collective-permute-start | bytes 1769480 | tf_op jit(solution)/shard_map/ppermute | solution.py:455
  12.3 19.4 %collective-permute-start.2 = (bf16[2,4,4,24,128]{4,3,2,1,0:T(8,128)(2,1)S(1)}, bf16[2,4,4,24,128]{4,3,2,1,0:T(8,128)(2,1)S(1)}, u32[]{:S(2)}, u32[]{:S(2)}) collective-permute-start(bf16[2,4,4,24,128]{4,3,2,1,0:T(8,128)(2,1)S(1)} %pad_maximum_fusion.2), channel_id=1, source_target_pairs={{0,127},{1,120},{2,121},{3,122},{4,123},{5,124},{6,125},{7,126},{8... | collective-permute-start | bytes 589832 | tf_op jit(solution)/shard_map/ppermute | solution.py:459
  31.7 0.7 copy-start.6
  31.8 0.9 copy-start.2
  31.8 1.0 copy-start.3
  77.4 3.1 %collective-permute-start.3 = (bf16[1152,512]{1,0:T(8,128)(2,1)}, bf16[1152,512]{1,0:T(8,128)(2,1)S(1)}, u32[]{:S(2)}, u32[]{:S(2)}) collective-permute-start(bf16[1152,512]{1,0:T(8,128)(2,1)} %get-tuple-element.47), channel_id=1, source_target_pairs={{0,8},{1,9},{2,10},{3,11},{4,12},{5,13},{6,14},{7,15},{8,0},{9,1},... | collective-permute-start | bytes 3538952 | tf_op jit(solution)/shard_map/ppermute | solution.py:485
  82.7 10.7 %collective-permute-start.4 = (bf16[288,512]{1,0:T(8,128)(2,1)S(1)}, bf16[288,512]{1,0:T(8,128)(2,1)S(1)}, u32[]{:S(2)}, u32[]{:S(2)}) collective-permute-start(bf16[288,512]{1,0:T(8,128)(2,1)S(1)} %get-tuple-element.83), channel_id=1, source_target_pairs={{0,32},{1,33},{2,34},{3,35},{4,36},{5,37},{6,38},{7,39},{8,10},{9,... | collective-permute-start | bytes 884744 | tf_op jit(solution)/shard_map/ppermute | solution.py:485
  82.8 10.7 %collective-permute-start.5 = (bf16[288,512]{1,0:T(8,128)(2,1)S(1)}, bf16[288,512]{1,0:T(8,128)(2,1)S(1)}, u32[]{:S(2)}, u32[]{:S(2)}) collective-permute-start(bf16[288,512]{1,0:T(8,128)(2,1)S(1)} %get-tuple-element.82), channel_id=1, source_target_pairs={{0,16},{1,17},{2,18},{3,19},{4,20},{5,21},{6,22},{7,23},{8,9},{9,1... | collective-permute-start | bytes 884744 | tf_op jit(solution)/shard_map/ppermute | solution.py:485
  84.0 9.4 %collective-permute-start.6 = (bf16[288,512]{1,0:T(8,128)(2,1)S(1)}, bf16[288,512]{1,0:T(8,128)(2,1)S(1)}, u32[]{:S(2)}, u32[]{:S(2)}) collective-permute-start(bf16[288,512]{1,0:T(8,128)(2,1)S(1)} %get-tuple-element.81), channel_id=1, source_target_pairs={{0,48},{1,49},{2,50},{3,51},{4,52},{5,53},{6,54},{7,55},{8,11},{9,... | collective-permute-start | bytes 884744 | tf_op jit(solution)/shard_map/ppermute | solution.py:485
  93.4 13.6 %copy-start.5 = (bf16[4,12,24,128]{3,2,1,0:T(8,128)(2,1)S(1)}, bf16[4,12,24,128]{3,2,1,0:T(8,128)(2,1)}, u32[]{:S(2)}) copy-start(bf16[4,12,24,128]{3,2,1,0:T(8,128)(2,1)} %get-tuple-element.56) | copy-start | bytes 884740
  93.4 18.5 %copy-start.4 = (bf16[12,4,24,128]{3,2,1,0:T(8,128)(2,1)S(1)}, bf16[12,4,24,128]{3,2,1,0:T(8,128)(2,1)}, u32[]{:S(2)}) copy-start(bf16[12,4,24,128]{3,2,1,0:T(8,128)(2,1)} %get-tuple-element.57) | copy-start | bytes 884740
  93.7 4.9 %collective-permute-start.7 = (bf16[72,512]{1,0:T(8,128)(2,1)S(1)}, bf16[72,512]{1,0:T(8,128)(2,1)S(1)}, u32[]{:S(2)}, u32[]{:S(2)}) collective-permute-start(bf16[72,512]{1,0:T(8,128)(2,1)S(1)} %get-tuple-element.84), channel_id=1, source_target_pairs={{0,2},{1,3},{2,0},{3,1},{4,6},{5,7},{6,4},{7,5},{8,40},{9,41},{10,... | collective-permute-start | bytes 221192 | tf_op jit(solution)/shard_map/ppermute | solution.py:485
  94.1 5.1 %collective-permute-start.8 = (bf16[72,512]{1,0:T(8,128)(2,1)S(1)}, bf16[72,512]{1,0:T(8,128)(2,1)S(1)}, u32[]{:S(2)}, u32[]{:S(2)}) collective-permute-start(bf16[72,512]{1,0:T(8,128)(2,1)S(1)} %get-tuple-element.86), channel_id=1, source_target_pairs={{0,1},{1,2},{2,3},{3,0},{4,5},{5,6},{6,7},{7,4},{8,24},{9,25},{10,... | collective-permute-start | bytes 221192 | tf_op jit(solution)/shard_map/ppermute | solution.py:485
  97.2 3.5 %collective-permute-start.9 = (bf16[72,512]{1,0:T(8,128)(2,1)S(1)}, bf16[72,512]{1,0:T(8,128)(2,1)S(1)}, u32[]{:S(2)}, u32[]{:S(2)}) collective-permute-start(bf16[72,512]{1,0:T(8,128)(2,1)S(1)} %get-tuple-element.85), channel_id=1, source_target_pairs={{0,3},{1,0},{2,1},{3,2},{4,7},{5,4},{6,5},{7,6},{8,56},{9,57},{10,... | collective-permute-start | bytes 221192 | tf_op jit(solution)/shard_map/ppermute | solution.py:485
  100.8 11.2 %collective-permute-start.10 = (f32[72,512]{1,0:T(8,128)S(1)}, f32[72,512]{1,0:T(8,128)S(1)}, u32[]{:S(2)}, u32[]{:S(2)}) collective-permute-start(f32[72,512]{1,0:T(8,128)S(1)} %convert_add_fusion.2), channel_id=1, source_target_pairs={{0,4},{1,5},{2,6},{3,7},{4,0},{5,1},{6,2},{7,3},{8,12},{9,13},{10,... | collective-permute-start | bytes 442376 | tf_op jit(solution)/shard_map/ppermute | solution.py:485
  104.4 8.1 %collective-permute-start.11 = (f32[72,512]{1,0:T(8,128)S(1)}, f32[72,512]{1,0:T(8,128)S(1)}, u32[]{:S(2)}, u32[]{:S(2)}) collective-permute-start(f32[72,512]{1,0:T(8,128)S(1)} %convert_add_fusion.2), channel_id=1, source_target_pairs={{0,64},{1,65},{2,66},{3,67},{4,68},{5,69},{6,70},{7,71},{8,72},{9,... | collective-permute-start | bytes 442376 | tf_op jit(solution)/shard_map/ppermute | solution.py:485
  104.4 8.1 %collective-permute-start.12 = (f32[72,512]{1,0:T(8,128)S(1)}, f32[72,512]{1,0:T(8,128)S(1)}, u32[]{:S(2)}, u32[]{:S(2)}) collective-permute-start(f32[72,512]{1,0:T(8,128)S(1)} %convert_add_fusion.2), channel_id=1, source_target_pairs={{0,68},{1,69},{2,70},{3,71},{4,64},{5,65},{6,66},{7,67},{8,76},{9,... | collective-permute-start | bytes 442376 | tf_op jit(solution)/shard_map/ppermute | solution.py:485
  107.0 24.5 %collective-permute-start.16 = (bf16[4,12,24,128]{3,2,1,0:T(8,128)(2,1)S(1)}, bf16[4,12,24,128]{3,2,1,0:T(8,128)(2,1)S(1)}, u32[]{:S(2)}, u32[]{:S(2)}) collective-permute-start(bf16[4,12,24,128]{3,2,1,0:T(8,128)(2,1)S(1)} %copy-done.5), channel_id=1, source_target_pairs={{0,8},{8,16},{16,24},{24,32},{32,40},{40,48},{48,56},{56,64},{64,7... | collective-permute-start | bytes 884744 | tf_op jit(solution)/shard_map/ppermute | solution.py:455
  111.9 19.6 %collective-permute-start.17 = (bf16[12,4,24,128]{3,2,1,0:T(8,128)(2,1)S(1)}, bf16[12,4,24,128]{3,2,1,0:T(8,128)(2,1)S(1)}, u32[]{:S(2)}, u32[]{:S(2)}) collective-permute-start(bf16[12,4,24,128]{3,2,1,0:T(8,128)(2,1)S(1)} %copy-done.4), channel_id=1, source_target_pairs={{0,1},{1,2},{2,3},{3,4},{4,5},{5,6},{6,7},{7,0},{8,9},{9,10},{10,1... | collective-permute-start | bytes 884744 | tf_op jit(solution)/shard_map/ppermute | solution.py:457
  112.0 16.3 %collective-permute-start.18 = (bf16[4,4,24,128]{3,2,1,0:T(8,128)(2,1)}, bf16[4,4,24,128]{3,2,1,0:T(8,128)(2,1)S(1)}, u32[]{:S(2)}, u32[]{:S(2)}) collective-permute-start(bf16[4,4,24,128]{3,2,1,0:T(8,128)(2,1)} %get-tuple-element.58), channel_id=1, source_target_pairs={{0,9},{1,10},{2,11},{3,12},{4,13},{5,14},{6,15},{7,8},{8,17},{9,18... | collective-permute-start | bytes 294920 | tf_op jit(solution)/shard_map/ppermute | solution.py:459
  112.5 15.7 %collective-permute-start.13 = (bf16[72,512]{1,0:T(8,128)(2,1)S(1)}, bf16[72,512]{1,0:T(8,128)(2,1)S(1)}, u32[]{:S(2)}, u32[]{:S(2)}) collective-permute-start(bf16[72,512]{1,0:T(8,128)(2,1)S(1)} %add_convert_fusion), channel_id=1, source_target_pairs={{0,1},{1,2},{2,3},{3,0},{4,5},{5,6},{6,7},{7,4},{8,24},{9,25},{10,... | collective-permute-start | bytes 221192 | tf_op jit(solution)/shard_map/ppermute | solution.py:485
  112.7 15.5 %collective-permute-start.14 = (bf16[72,512]{1,0:T(8,128)(2,1)S(1)}, bf16[72,512]{1,0:T(8,128)(2,1)S(1)}, u32[]{:S(2)}, u32[]{:S(2)}) collective-permute-start(bf16[72,512]{1,0:T(8,128)(2,1)S(1)} %add_convert_fusion), channel_id=1, source_target_pairs={{0,2},{1,3},{2,0},{3,1},{4,6},{5,7},{6,4},{7,5},{8,40},{9,41},{10,... | collective-permute-start | bytes 221192 | tf_op jit(solution)/shard_map/ppermute | solution.py:485
  128.3 3.2 %collective-permute-start.15 = (bf16[72,512]{1,0:T(8,128)(2,1)S(1)}, bf16[72,512]{1,0:T(8,128)(2,1)S(1)}, u32[]{:S(2)}, u32[]{:S(2)}) collective-permute-start(bf16[72,512]{1,0:T(8,128)(2,1)S(1)} %add_convert_fusion), channel_id=1, source_target_pairs={{0,3},{1,0},{2,1},{3,2},{4,7},{5,4},{6,5},{7,6},{8,56},{9,57},{10,... | collective-permute-start | bytes 221192 | tf_op jit(solution)/shard_map/ppermute | solution.py:485
  131.6 10.0 %collective-permute-start.19 = (bf16[288,512]{1,0:T(8,128)(2,1)S(1)}, bf16[288,512]{1,0:T(8,128)(2,1)S(1)}, u32[]{:S(2)}, u32[]{:S(2)}) collective-permute-start(bf16[288,512]{1,0:T(8,128)(2,1)S(1)} %constant_dynamic-update-slice_fusion.7), channel_id=1, source_target_pairs={{0,16},{1,17},{2,18},{3,19},{4,20},{5,21},{6,22},{7,23},{8,9},{9,1... | collective-permute-start | bytes 884744 | tf_op jit(solution)/shard_map/ppermute | solution.py:485
  131.7 9.9 %collective-permute-start.20 = (bf16[288,512]{1,0:T(8,128)(2,1)S(1)}, bf16[288,512]{1,0:T(8,128)(2,1)S(1)}, u32[]{:S(2)}, u32[]{:S(2)}) collective-permute-start(bf16[288,512]{1,0:T(8,128)(2,1)S(1)} %constant_dynamic-update-slice_fusion.7), channel_id=1, source_target_pairs={{0,32},{1,33},{2,34},{3,35},{4,36},{5,37},{6,38},{7,39},{8,10},{9,... | collective-permute-start | bytes 884744 | tf_op jit(solution)/shard_map/ppermute | solution.py:485
  131.8 10.5 %collective-permute-start.21 = (bf16[288,512]{1,0:T(8,128)(2,1)S(1)}, bf16[288,512]{1,0:T(8,128)(2,1)S(1)}, u32[]{:S(2)}, u32[]{:S(2)}) collective-permute-start(bf16[288,512]{1,0:T(8,128)(2,1)S(1)} %constant_dynamic-update-slice_fusion.7), channel_id=1, source_target_pairs={{0,48},{1,49},{2,50},{3,51},{4,52},{5,53},{6,54},{7,55},{8,11},{9,... | collective-permute-start | bytes 884744 | tf_op jit(solution)/shard_map/ppermute | solution.py:485
  142.5 1.0 copy-start
  142.5 3.4 %collective-permute-start.22 = (bf16[1152,512]{1,0:T(8,128)(2,1)S(1)}, bf16[1152,512]{1,0:T(8,128)(2,1)S(1)}, u32[]{:S(2)}, u32[]{:S(2)}) collective-permute-start(bf16[1152,512]{1,0:T(8,128)(2,1)S(1)} %constant_dynamic-update-slice_fusion.own_ref.own_rest_ref), channel_id=1, source_target_pairs={{0,8},{1,9},{2,10},{3,11},{4,12},{5,13},{6,14},{7,15},{8,0},{9,1},... | collective-permute-start | bytes 3538952 | tf_op jit(solution)/shard_map/ppermute | solution.py:485
  145.9 1.1 copy-start.1

commit v6 on v5

--- a/solution.py
+++ b/solution.py
@@ -256,9 +256,9 @@
                 h = 2 * (1 - mine) + j
                 away_ref[j * T : (j + 1) * T] = (dbias_ref[h] + acc_s[h]).T.astype(BF)
                 h = 2 * mine + j
-                keep_ref[j * T : (j + 1) * T] = (dbias_ref[h] + acc_s[h]).T
+                keep_ref[j * T : (j + 1) * T] = (dbias_ref[h] + acc_s[h]).T.astype(BF)
             away_ref[2 * T :] = jnp.where(mine == 1, table, 0.0).astype(BF)
-            keep_ref[2 * T :] = jnp.where(mine == 0, table, 0.0)
+            keep_ref[2 * T :] = jnp.where(mine == 0, table, 0.0).astype(BF)
 
 
 def finish_kernel(first, *refs):
@@ -328,7 +328,7 @@
     else:
         ins += [ANYWHERE, whole(small)]
         outs = [DT_BLOCK, whole((HALF, T)), whole((HALF, T))]
-        shapes = [((blocks,) + DT_SHAPE, BF), ((HALF, T), BF), ((HALF, T), F32)]
+        shapes = [((blocks,) + DT_SHAPE, BF), ((HALF, T), BF), ((HALF, T), BF)]
         scratch = [pltpu.VMEM(small, F32), pltpu.VMEM(square, F32), pltpu.SemaphoreType.DMA]
     scratch += [
         pltpu.SemaphoreType.DMA((2, len(pieces))),
@@ -401,7 +401,7 @@
             out_specs=pl.BlockSpec((pl.Squeezed(), T, T), lambda j, m: (2 * m[0] + j, 0, 0)),
         ),
         out_shape=jax.ShapeDtypeStruct((HEADS, T, T), F32),
-        compiler_params=pltpu.CompilerParams(vmem_limit_bytes=60 * 1024 * 1024),
+        compiler_params=pltpu.CompilerParams(vmem_limit_bytes=8 * 1024 * 1024),
         name="spread_own",
     )(mine, own)
 
@@ -444,9 +444,33 @@
             jax.ShapeDtypeStruct((1, C), F32),
         ],
         input_output_aliases={6: 0},
-        compiler_params=pltpu.CompilerParams(vmem_limit_bytes=60 * 1024 * 1024),
+        compiler_params=pltpu.CompilerParams(vmem_limit_bytes=8 * 1024 * 1024),
         name="spread_got",
     )(mine, got, own, got, gamma, w, grad_bias)
+
+
+def rims_kernel(xs_hbm, adj_hbm, to_x, to_y, to_xy, sem):
+    copies = []
+    for which, src in enumerate((xs_hbm, adj_hbm)):
+        for n, (dst, x, y, ex, ey) in enumerate(((to_x, 0, 4, 4, 12), (to_y, 4, 0, 12, 4), (to_xy, 0, 0, 4, 4))):
+            part = src.at[pl.ds(x, ex), pl.ds(y, ey)]
+            copies.append(pltpu.make_async_copy(part, dst.at[which], sem.at[which, n]))
+    for copy in copies:
+        copy.start()
+    for copy in copies:
+        copy.wait()
+
+
+def rims(both):
+    return pl.pallas_call(
+        rims_kernel,
+        in_specs=[ANYWHERE] * 2,
+        out_specs=[ANYWHERE] * 3,
+        out_shape=[jax.ShapeDtypeStruct((2,) + shape + (24, C), BF) for shape in ((4, 12), (12, 4), (4, 4))],
+        scratch_shapes=[pltpu.SemaphoreType.DMA((2, 3))],
+        compiler_params=pltpu.CompilerParams(vmem_limit_bytes=60 * 1024 * 1024),
+        name="rims",
+    )(*both)
 
 
 def shifted(values, by_x, by_y):
@@ -519,9 +543,8 @@
 
 def body(retained_source, incoming_adjoint, rescale_multiplier, triple_projection_matrix, w_proj, pos_bias):
     both = (retained_source, incoming_adjoint)
-    from_x = shifted(jnp.stack([v[:4, 4:] for v in both]), -1, 0)
-    from_y = shifted(jnp.stack([v[4:, :4] for v in both]), 0, -1)
-    from_xy = shifted(jnp.stack([v[:4, :4] for v in both]), -1, -1)
+    to_x, to_y, to_xy = rims(both)
+    from_x, from_y, from_xy = shifted(to_x, -1, 0), shifted(to_y, 0, -1), shifted(to_xy, -1, -1)
     w = triple_projection_matrix
     gamma = rescale_multiplier.reshape(1, C)
     inner_dT, acc_small, acc, biasT = sublayer(True, both, (gamma, w, w_proj, pos_bias))
@@ -529,7 +552,7 @@
     rim_dT, away, keep = sublayer(False, around, (gamma, w, w_proj, biasT), (acc, acc_small))
 
     first, second, third = (ACROSS_X, ACROSS_Z), (ACROSS_Z, ACROSS_X), (ACROSS_Y, ACROSS_Y)
-    values = keep + send(away, (CORE, CORE), 1).astype(F32)
+    values = keep.astype(F32) + send(away, (CORE, CORE), 1).astype(F32)
     values, got = parts_sent(values, first)
     gin, back_x, back_y, back_xy = finish(False, around, gamma, w, rim_dT)
     values, got, back_x, back_y, back_xy = lax.optimization_barrier((values, got, back_x, back_y, back_xy))

time: 150 us -> 186 us (1.24)
  Pallas kernels: 77.8 us -> 118 us
  local copies, waits for them, and re-layouts: 8.86 us -> 3.71 us
    pallas_call x0 -> x1, Pallas kernels: none -> 42.8 us  [rims(): pl.pallas_call(rims_kernel, in_specs=[ANYWHERE] * 2, out_specs=[ANYWHERE]...]
    another operation x3 -> x0, local copies, waits for them, and re-layouts: 3.19 us -> none  [the longest x1 1.12 us: body(): from_y = shifted(jnp.stack([v[4:, :4] for v in both]), 0, -1)]
    ppermute x2, starting transfers between devices: 3.24 us -> 6.15 us  [shifted(): return lax.ppermute(values, ('gx', 'gy'), pairs)]
    unnamed x14, local copies, waits for them, and re-layouts: 3.01 us -> 1.05 us
  transfers between devices with their start and end apart: 23 -> 23, of which waited for: 8 -> 8; matrix products, arithmetic and copies ran while one was open for 3% -> 1% of each run, Pallas kernels for 20% -> 16%
where the time goes in v6:
time: 186 us
  Pallas kernels  118 us (63%)
  starting transfers between devices  38.3 us (21%)
  waiting for transfers between devices  23.3 us (13%)
  local copies, waits for them, and re-layouts  3.71 us (2%)
    pallas_call x2, Pallas kernels, sublayer(): pl.pallas_call(functools.partial(kernel, first), grid=(blocks,), in_specs...  60.5 us
    pallas_call x1, Pallas kernels, rims(): pl.pallas_call(rims_kernel, in_specs=[ANYWHERE] * 2, out_specs=[ANYWHERE]...  42.8 us
    ppermute x17, starting transfers between devices, send(): return lax.ppermute(values, ('gx', 'gy'), pairs)  19.6 us
    ppermute x17, waiting for transfers between devices, send(): return lax.ppermute(values, ('gx', 'gy'), pairs)  12.1 us
    pallas_call x2, Pallas kernels, finish(): pl.pallas_call(functools.partial(finish_kernel, first), grid=(blocks,), i...  11.3 us
    ppermute x2, waiting for transfers between devices, shifted(): return lax.ppermute(values, ('gx', 'gy'), pairs)  11.2 us
    ppermute x2, starting transfers between devices, shifted(): return lax.ppermute(values, 'gy', [(i, (i + by_y) % ny) for i in range(ny)])  6.47 us
    ppermute x2, starting transfers between devices, shifted(): return lax.ppermute(values, ('gx', 'gy'), pairs)  6.15 us
  transfers between devices with their start and end apart: 23, of which 8 were waited for; matrix products, arithmetic and copies ran while one was open for 1% of the time, Pallas kernels for 16%

profile of v6, /device:TPU:1, one launch (start us, length us, event | category | flops | bytes accessed | tf_op | source)
XLA Modules:
  0.0 186.1 jit_solution(10336491735895177568)
XLA Ops:
  0.6 42.8 %rims.1 = (bf16[2,4,12,24,128]{4,3,2,1,0:T(8,128)(2,1)}, bf16[2,12,4,24,128]{4,3,2,1,0:T(8,128)(2,1)}, bf16[2,4,4,24,128]{4,3,2,1,0:T(8,128)(2,1)}) custom-call(bf16[16,16,24,128]{3,2,1,0:T(8,128)(2,1)} %refs_0_.7, bf16[16,16,24,128]{3,2,1,0:T(8,128)(2,1)} %refs_1_.7), custom_call_target="tpu_custom_call" | custom-call | tf_op jit(solution)/shard_map/rims/pallas_call | solution.py:465
  43.5 1.5 collective-permute-start
  45.0 6.5 %collective-permute-start.1 = (bf16[2,12,4,24,128]{4,3,2,1,0:T(8,128)(2,1)}, bf16[2,12,4,24,128]{4,3,2,1,0:T(8,128)(2,1)S(1)}, u32[]{:S(2)}, u32[]{:S(2)}) collective-permute-start(bf16[2,12,4,24,128]{4,3,2,1,0:T(8,128)(2,1)} %get-tuple-element.47), channel_id=1, source_target_pairs={{0,7},{1,0},{2,1},{3,2},{4,3},{5,4},{6,5},{7,6},{8,15},{9,8},{10,9... | collective-permute-start | bytes 1769480 | tf_op jit(solution)/shard_map/ppermute | solution.py:481
  51.4 3.2 %collective-permute-start.2 = (bf16[2,4,4,24,128]{4,3,2,1,0:T(8,128)(2,1)}, bf16[2,4,4,24,128]{4,3,2,1,0:T(8,128)(2,1)S(1)}, u32[]{:S(2)}, u32[]{:S(2)}) collective-permute-start(bf16[2,4,4,24,128]{4,3,2,1,0:T(8,128)(2,1)} %get-tuple-element.48), channel_id=1, source_target_pairs={{0,127},{1,120},{2,121},{3,122},{4,123},{5,124},{6,125},{7,126},{8... | collective-permute-start | bytes 589832 | tf_op jit(solution)/shard_map/ppermute | solution.py:483
  54.7 16.7 %inner_windows.1 = (bf16[1,3,384,512]{3,2,1,0:T(8,128)(2,1)}, f32[512,128]{1,0:T(8,128)}, f32[4,512,512]{2,1,0:T(8,128)}, f32[4,512,512]{2,1,0:T(8,128)}) custom-call(bf16[16,16,24,128]{3,2,1,0:T(8,128)(2,1)} %refs_0_.7, bf16[16,16,24,128]{3,2,1,0:T(8,128)(2,1)} %refs_1_.7, f32[1,128]{1,0:T(1,128)} %bitcast.3, bf16[128,384]{1,0:T(8,128)(2,1)} %w_ref.1, ...), custom_call_target="tpu_custom_call" | custom-call | flops 12000000000 | bytes 10000000 | tf_op jit(solution)/shard_map/inner_windows/pallas_call | solution.py:354
  71.4 0.0 copy-start.5
  71.4 0.6 copy-done.5
  72.1 0.2 copy-done.2
  72.3 0.2 copy-done.3
  72.4 43.8 %rim_windows.1 = (bf16[3,3,384,512]{3,2,1,0:T(8,128)(2,1)}, bf16[1152,512]{1,0:T(8,128)(2,1)}, bf16[1152,512]{1,0:T(8,128)(2,1)}) custom-call(bf16[16,16,24,128]{3,2,1,0:T(8,128)(2,1)} %refs_0_.7, bf16[16,16,24,128]{3,2,1,0:T(8,128)(2,1)} %refs_1_.7, bf16[2,4,12,24,128]{4,3,2,1,0:T(8,128)(2,1)} %copy-done.2, bf16[2,12,4,24,128]{4,3,2,1,0:T(8,128)(2,1)} %copy-done.3, ...), custom_call_target="tpu_custom_call" | custom-call | flops 35999997952 | bytes 30000000 | tf_op jit(solution)/shard_map/rim_windows/pallas_call | solution.py:354
  116.3 0.1 collective-permute-start.3
  116.5 2.9 %collective-permute-done.3 = bf16[1152,512]{1,0:T(8,128)(2,1)S(1)} collective-permute-done((bf16[1152,512]{1,0:T(8,128)(2,1)}, bf16[1152,512]{1,0:T(8,128)(2,1)S(1)}, u32[]{:S(2)}, u32[]{:S(2)}) %collective-permute-start.3) | collective-permute-done | bytes 1179680 | tf_op jit(solution)/shard_map/ppermute | solution.py:509
  119.4 1.6 convert_add_fusion
  121.0 0.1 dynamic-slice_convert_fusion
  121.1 0.1 collective-permute-start.4
  121.2 1.4 collective-permute-start.5
  122.6 2.3 %collective-permute-start.6 = (bf16[288,512]{1,0:T(8,128)(2,1)S(1)}, bf16[288,512]{1,0:T(8,128)(2,1)S(1)}, u32[]{:S(2)}, u32[]{:S(2)}) collective-permute-start(bf16[288,512]{1,0:T(8,128)(2,1)S(1)} %get-tuple-element.87), channel_id=1, source_target_pairs={{0,48},{1,49},{2,50},{3,51},{4,52},{5,53},{6,54},{7,55},{8,11},{9,... | collective-permute-start | bytes 884744 | tf_op jit(solution)/shard_map/ppermute | solution.py:509
  125.0 7.0 %rim_finish.1 = (bf16[16,16,24,128]{3,2,1,0:T(8,128)(2,1)}, bf16[4,12,24,128]{3,2,1,0:T(8,128)(2,1)}, bf16[12,4,24,128]{3,2,1,0:T(8,128)(2,1)}, bf16[4,4,24,128]{3,2,1,0:T(8,128)(2,1)}) custom-call(bf16[16,16,24,128]{3,2,1,0:T(8,128)(2,1)} %refs_0_.7, bf16[16,16,24,128]{3,2,1,0:T(8,128)(2,1)} %refs_1_.7, bf16[2,4,12,24,128]{4,3,2,1,0:T(8,128)(2,1)} %copy-done.2, ...), custom_call_target="tpu_custom_call" | custom-call | flops 3000000000 | bytes 9000000 | tf_op jit(solution)/shard_map/rim_finish/pallas_call | solution.py:371
  132.1 0.1 convert_add_fusion.1
  132.3 0.8 collective-permute-start.7
  133.1 5.2 %collective-permute-start.8 = (bf16[72,512]{1,0:T(8,128)(2,1)S(1)}, bf16[72,512]{1,0:T(8,128)(2,1)S(1)}, u32[]{:S(2)}, u32[]{:S(2)}) collective-permute-start(bf16[72,512]{1,0:T(8,128)(2,1)S(1)} %get-tuple-element.92), channel_id=1, source_target_pairs={{0,1},{1,2},{2,3},{3,0},{4,5},{5,6},{6,7},{7,4},{8,24},{9,25},{10,... | collective-permute-start | bytes 221192 | tf_op jit(solution)/shard_map/ppermute | solution.py:509
  138.3 1.4 collective-permute-done.8
  139.7 1.8 collective-permute-done.9
  141.6 0.5 collective-permute-start.10
  142.1 0.9 collective-permute-start.11
  143.0 1.8 collective-permute-start.12
  144.8 4.6 %collective-permute-start.16 = (bf16[4,12,24,128]{3,2,1,0:T(8,128)(2,1)}, bf16[4,12,24,128]{3,2,1,0:T(8,128)(2,1)S(1)}, u32[]{:S(2)}, u32[]{:S(2)}) collective-permute-start(bf16[4,12,24,128]{3,2,1,0:T(8,128)(2,1)} %get-tuple-element.62), channel_id=1, source_target_pairs={{0,8},{8,16},{16,24},{24,32},{32,40},{40,48},{48,56},{56,64},{64,7... | collective-permute-start | bytes 884744 | tf_op jit(solution)/shard_map/ppermute | solution.py:479
  149.4 2.9 %collective-permute-start.18 = (bf16[4,4,24,128]{3,2,1,0:T(8,128)(2,1)S(1)}, bf16[4,4,24,128]{3,2,1,0:T(8,128)(2,1)S(1)}, u32[]{:S(2)}, u32[]{:S(2)}) collective-permute-start(bf16[4,4,24,128]{3,2,1,0:T(8,128)(2,1)S(1)} %copy-done.6), channel_id=1, source_target_pairs={{0,9},{1,10},{2,11},{3,12},{4,13},{5,14},{6,15},{7,8},{8,17},{9,18... | collective-permute-start | bytes 294920 | tf_op jit(solution)/shard_map/ppermute | solution.py:483
  152.3 0.2 collective-permute-start.13
  152.5 3.6 %collective-permute-start.14 = (bf16[72,512]{1,0:T(8,128)(2,1)S(1)}, bf16[72,512]{1,0:T(8,128)(2,1)S(1)}, u32[]{:S(2)}, u32[]{:S(2)}) collective-permute-start(bf16[72,512]{1,0:T(8,128)(2,1)S(1)} %add_convert_fusion), channel_id=1, source_target_pairs={{0,2},{1,3},{2,0},{3,1},{4,6},{5,7},{6,4},{7,5},{8,40},{9,41},{10,... | collective-permute-start | bytes 221192 | tf_op jit(solution)/shard_map/ppermute | solution.py:509
  156.1 11.2 %collective-permute-done.18 = bf16[4,4,24,128]{3,2,1,0:T(8,128)(2,1)S(1)} collective-permute-done((bf16[4,4,24,128]{3,2,1,0:T(8,128)(2,1)S(1)}, bf16[4,4,24,128]{3,2,1,0:T(8,128)(2,1)S(1)}, u32[]{:S(2)}, u32[]{:S(2)}) %collective-permute-start.18) | collective-permute-done | bytes 98336 | tf_op jit(solution)/shard_map/ppermute | solution.py:483
  167.3 3.2 %collective-permute-done.15 = bf16[72,512]{1,0:T(8,128)(2,1)S(1)} collective-permute-done((bf16[72,512]{1,0:T(8,128)(2,1)S(1)}, bf16[72,512]{1,0:T(8,128)(2,1)S(1)}, u32[]{:S(2)}, u32[]{:S(2)}) %collective-permute-start.15) | collective-permute-done | bytes 73760 | tf_op jit(solution)/shard_map/ppermute | solution.py:509
  170.6 0.1 collective-permute-start.19
  170.7 0.1 collective-permute-start.20
  170.8 2.6 %collective-permute-start.21 = (bf16[288,512]{1,0:T(8,128)(2,1)S(1)}, bf16[288,512]{1,0:T(8,128)(2,1)S(1)}, u32[]{:S(2)}, u32[]{:S(2)}) collective-permute-start(bf16[288,512]{1,0:T(8,128)(2,1)S(1)} %constant_dynamic-update-slice_fusion.7), channel_id=1, source_target_pairs={{0,48},{1,49},{2,50},{3,51},{4,52},{5,53},{6,54},{7,55},{8,11},{9,... | collective-permute-start | bytes 884744 | tf_op jit(solution)/shard_map/ppermute | solution.py:509
  173.4 4.3 %inner_finish.1 = bf16[16,16,24,128]{3,2,1,0:T(8,128)(2,1)} custom-call(bf16[16,16,24,128]{3,2,1,0:T(8,128)(2,1)} %refs_0_.7, bf16[16,16,24,128]{3,2,1,0:T(8,128)(2,1)} %refs_1_.7, f32[1,128]{1,0:T(1,128)} %bitcast.6, bf16[128,384]{1,0:T(8,128)(2,1)} %w_ref.1, bf16[1,3,384,512]{3,2,1,0:T(8,128)(2,1)} %get-tuple-element.71.refs_4_, ...), custom_call_target="tpu_custom_call", output_to_operand_aliasing={{}: (5, {})} | custom-call | flops 1000000000 | bytes 3000000 | tf_op jit(solution)/shard_map/inner_finish/pallas_call | solution.py:371
  177.7 0.8 constant_dynamic-update-slice_fusion.6
  178.5 0.8 constant_dynamic-update-slice_fusion.5
  179.2 0.7 constant_dynamic-update-slice_fusion.4
  179.9 0.7 collective-permute-done.19
  180.7 0.6 collective-permute-done.21
  181.3 0.1 broadcast_in_dim.7
  181.5 0.1 collective-permute-start.22
  181.6 0.0 copy-start
  181.6 0.0 copy-start.1
  181.6 1.4 spread_own.1._
  183.0 1.4 collective-permute-done.22.got_ref.got_rest_ref
  184.4 1.6 spread_got.1
  (39 shorter events, 0.4 us)
Async XLA Ops:
  43.5 27.9 %collective-permute-start = (bf16[2,4,12,24,128]{4,3,2,1,0:T(8,128)(2,1)}, bf16[2,4,12,24,128]{4,3,2,1,0:T(8,128)(2,1)S(1)}, u32[]{:S(2)}, u32[]{:S(2)}) collective-permute-start(bf16[2,4,12,24,128]{4,3,2,1,0:T(8,128)(2,1)} %get-tuple-element.46), channel_id=1, source_target_pairs={{0,120},{8,0},{16,8},{24,16},{32,24},{40,32},{48,40},{56,48},{64,5... | collective-permute-start | bytes 1769480 | tf_op jit(solution)/shard_map/ppermute | solution.py:479
  45.0 26.4 %collective-permute-start.1 = (bf16[2,12,4,24,128]{4,3,2,1,0:T(8,128)(2,1)}, bf16[2,12,4,24,128]{4,3,2,1,0:T(8,128)(2,1)S(1)}, u32[]{:S(2)}, u32[]{:S(2)}) collective-permute-start(bf16[2,12,4,24,128]{4,3,2,1,0:T(8,128)(2,1)} %get-tuple-element.47), channel_id=1, source_target_pairs={{0,7},{1,0},{2,1},{3,2},{4,3},{5,4},{6,5},{7,6},{8,15},{9,8},{10,9... | collective-permute-start | bytes 1769480 | tf_op jit(solution)/shard_map/ppermute | solution.py:481
  51.4 19.9 %collective-permute-start.2 = (bf16[2,4,4,24,128]{4,3,2,1,0:T(8,128)(2,1)}, bf16[2,4,4,24,128]{4,3,2,1,0:T(8,128)(2,1)S(1)}, u32[]{:S(2)}, u32[]{:S(2)}) collective-permute-start(bf16[2,4,4,24,128]{4,3,2,1,0:T(8,128)(2,1)} %get-tuple-element.48), channel_id=1, source_target_pairs={{0,127},{1,120},{2,121},{3,122},{4,123},{5,124},{6,125},{7,126},{8... | collective-permute-start | bytes 589832 | tf_op jit(solution)/shard_map/ppermute | solution.py:483
  71.4 0.7 copy-start.5
  71.4 0.9 copy-start.2
  71.4 1.0 copy-start.3
  116.3 3.1 %collective-permute-start.3 = (bf16[1152,512]{1,0:T(8,128)(2,1)}, bf16[1152,512]{1,0:T(8,128)(2,1)S(1)}, u32[]{:S(2)}, u32[]{:S(2)}) collective-permute-start(bf16[1152,512]{1,0:T(8,128)(2,1)} %get-tuple-element.53), channel_id=1, source_target_pairs={{0,8},{1,9},{2,10},{3,11},{4,12},{5,13},{6,14},{7,15},{8,0},{9,1},... | collective-permute-start | bytes 3538952 | tf_op jit(solution)/shard_map/ppermute | solution.py:509
  121.1 10.9 %collective-permute-start.4 = (bf16[288,512]{1,0:T(8,128)(2,1)S(1)}, bf16[288,512]{1,0:T(8,128)(2,1)S(1)}, u32[]{:S(2)}, u32[]{:S(2)}) collective-permute-start(bf16[288,512]{1,0:T(8,128)(2,1)S(1)} %get-tuple-element.89), channel_id=1, source_target_pairs={{0,32},{1,33},{2,34},{3,35},{4,36},{5,37},{6,38},{7,39},{8,10},{9,... | collective-permute-start | bytes 884744 | tf_op jit(solution)/shard_map/ppermute | solution.py:509
  121.2 10.9 %collective-permute-start.5 = (bf16[288,512]{1,0:T(8,128)(2,1)S(1)}, bf16[288,512]{1,0:T(8,128)(2,1)S(1)}, u32[]{:S(2)}, u32[]{:S(2)}) collective-permute-start(bf16[288,512]{1,0:T(8,128)(2,1)S(1)} %get-tuple-element.88), channel_id=1, source_target_pairs={{0,16},{1,17},{2,18},{3,19},{4,20},{5,21},{6,22},{7,23},{8,9},{9,1... | collective-permute-start | bytes 884744 | tf_op jit(solution)/shard_map/ppermute | solution.py:509
  122.6 9.5 %collective-permute-start.6 = (bf16[288,512]{1,0:T(8,128)(2,1)S(1)}, bf16[288,512]{1,0:T(8,128)(2,1)S(1)}, u32[]{:S(2)}, u32[]{:S(2)}) collective-permute-start(bf16[288,512]{1,0:T(8,128)(2,1)S(1)} %get-tuple-element.87), channel_id=1, source_target_pairs={{0,48},{1,49},{2,50},{3,51},{4,52},{5,53},{6,54},{7,55},{8,11},{9,... | collective-permute-start | bytes 884744 | tf_op jit(solution)/shard_map/ppermute | solution.py:509
  132.1 17.3 %copy-start.4 = (bf16[12,4,24,128]{3,2,1,0:T(8,128)(2,1)S(1)}, bf16[12,4,24,128]{3,2,1,0:T(8,128)(2,1)}, u32[]{:S(2)}) copy-start(bf16[12,4,24,128]{3,2,1,0:T(8,128)(2,1)} %get-tuple-element.63) | copy-start | bytes 884740
  132.1 17.3 %copy-start.6 = (bf16[4,4,24,128]{3,2,1,0:T(8,128)(2,1)S(1)}, bf16[4,4,24,128]{3,2,1,0:T(8,128)(2,1)}, u32[]{:S(2)}) copy-start(bf16[4,4,24,128]{3,2,1,0:T(8,128)(2,1)} %get-tuple-element.64) | copy-start | bytes 294916
  132.3 6.0 %collective-permute-start.7 = (bf16[72,512]{1,0:T(8,128)(2,1)S(1)}, bf16[72,512]{1,0:T(8,128)(2,1)S(1)}, u32[]{:S(2)}, u32[]{:S(2)}) collective-permute-start(bf16[72,512]{1,0:T(8,128)(2,1)S(1)} %get-tuple-element.90), channel_id=1, source_target_pairs={{0,2},{1,3},{2,0},{3,1},{4,6},{5,7},{6,4},{7,5},{8,40},{9,41},{10,... | collective-permute-start | bytes 221192 | tf_op jit(solution)/shard_map/ppermute | solution.py:509
  133.1 6.6 %collective-permute-start.8 = (bf16[72,512]{1,0:T(8,128)(2,1)S(1)}, bf16[72,512]{1,0:T(8,128)(2,1)S(1)}, u32[]{:S(2)}, u32[]{:S(2)}) collective-permute-start(bf16[72,512]{1,0:T(8,128)(2,1)S(1)} %get-tuple-element.92), channel_id=1, source_target_pairs={{0,1},{1,2},{2,3},{3,0},{4,5},{5,6},{6,7},{7,4},{8,24},{9,25},{10,... | collective-permute-start | bytes 221192 | tf_op jit(solution)/shard_map/ppermute | solution.py:509
  138.3 3.2 %collective-permute-start.9 = (bf16[72,512]{1,0:T(8,128)(2,1)S(1)}, bf16[72,512]{1,0:T(8,128)(2,1)S(1)}, u32[]{:S(2)}, u32[]{:S(2)}) collective-permute-start(bf16[72,512]{1,0:T(8,128)(2,1)S(1)} %get-tuple-element.91), channel_id=1, source_target_pairs={{0,3},{1,0},{2,1},{3,2},{4,7},{5,4},{6,5},{7,6},{8,56},{9,57},{10,... | collective-permute-start | bytes 221192 | tf_op jit(solution)/shard_map/ppermute | solution.py:509
  141.6 7.7 %collective-permute-start.10 = (f32[72,512]{1,0:T(8,128)S(1)}, f32[72,512]{1,0:T(8,128)S(1)}, u32[]{:S(2)}, u32[]{:S(2)}) collective-permute-start(f32[72,512]{1,0:T(8,128)S(1)} %convert_add_fusion.2), channel_id=1, source_target_pairs={{0,4},{1,5},{2,6},{3,7},{4,0},{5,1},{6,2},{7,3},{8,12},{9,13},{10,... | collective-permute-start | bytes 442376 | tf_op jit(solution)/shard_map/ppermute | solution.py:509
  142.1 10.2 %collective-permute-start.11 = (f32[72,512]{1,0:T(8,128)S(1)}, f32[72,512]{1,0:T(8,128)S(1)}, u32[]{:S(2)}, u32[]{:S(2)}) collective-permute-start(f32[72,512]{1,0:T(8,128)S(1)} %convert_add_fusion.2), channel_id=1, source_target_pairs={{0,64},{1,65},{2,66},{3,67},{4,68},{5,69},{6,70},{7,71},{8,72},{9,... | collective-permute-start | bytes 442376 | tf_op jit(solution)/shard_map/ppermute | solution.py:509
  143.0 9.3 %collective-permute-start.12 = (f32[72,512]{1,0:T(8,128)S(1)}, f32[72,512]{1,0:T(8,128)S(1)}, u32[]{:S(2)}, u32[]{:S(2)}) collective-permute-start(f32[72,512]{1,0:T(8,128)S(1)} %convert_add_fusion.2), channel_id=1, source_target_pairs={{0,68},{1,69},{2,70},{3,71},{4,64},{5,65},{6,66},{7,67},{8,76},{9,... | collective-permute-start | bytes 442376 | tf_op jit(solution)/shard_map/ppermute | solution.py:509
  144.8 25.8 %collective-permute-start.16 = (bf16[4,12,24,128]{3,2,1,0:T(8,128)(2,1)}, bf16[4,12,24,128]{3,2,1,0:T(8,128)(2,1)S(1)}, u32[]{:S(2)}, u32[]{:S(2)}) collective-permute-start(bf16[4,12,24,128]{3,2,1,0:T(8,128)(2,1)} %get-tuple-element.62), channel_id=1, source_target_pairs={{0,8},{8,16},{16,24},{24,32},{32,40},{40,48},{48,56},{56,64},{64,7... | collective-permute-start | bytes 884744 | tf_op jit(solution)/shard_map/ppermute | solution.py:479
  149.3 21.2 %collective-permute-start.17 = (bf16[12,4,24,128]{3,2,1,0:T(8,128)(2,1)S(1)}, bf16[12,4,24,128]{3,2,1,0:T(8,128)(2,1)S(1)}, u32[]{:S(2)}, u32[]{:S(2)}) collective-permute-start(bf16[12,4,24,128]{3,2,1,0:T(8,128)(2,1)S(1)} %copy-done.4), channel_id=1, source_target_pairs={{0,1},{1,2},{2,3},{3,4},{4,5},{5,6},{6,7},{7,0},{8,9},{9,10},{10,1... | collective-permute-start | bytes 884744 | tf_op jit(solution)/shard_map/ppermute | solution.py:481
  149.4 18.0 %collective-permute-start.18 = (bf16[4,4,24,128]{3,2,1,0:T(8,128)(2,1)S(1)}, bf16[4,4,24,128]{3,2,1,0:T(8,128)(2,1)S(1)}, u32[]{:S(2)}, u32[]{:S(2)}) collective-permute-start(bf16[4,4,24,128]{3,2,1,0:T(8,128)(2,1)S(1)} %copy-done.6), channel_id=1, source_target_pairs={{0,9},{1,10},{2,11},{3,12},{4,13},{5,14},{6,15},{7,8},{8,17},{9,18... | collective-permute-start | bytes 294920 | tf_op jit(solution)/shard_map/ppermute | solution.py:483
  152.3 15.0 %collective-permute-start.13 = (bf16[72,512]{1,0:T(8,128)(2,1)S(1)}, bf16[72,512]{1,0:T(8,128)(2,1)S(1)}, u32[]{:S(2)}, u32[]{:S(2)}) collective-permute-start(bf16[72,512]{1,0:T(8,128)(2,1)S(1)} %add_convert_fusion), channel_id=1, source_target_pairs={{0,1},{1,2},{2,3},{3,0},{4,5},{5,6},{6,7},{7,4},{8,24},{9,25},{10,... | collective-permute-start | bytes 221192 | tf_op jit(solution)/shard_map/ppermute | solution.py:509
  152.5 14.8 %collective-permute-start.14 = (bf16[72,512]{1,0:T(8,128)(2,1)S(1)}, bf16[72,512]{1,0:T(8,128)(2,1)S(1)}, u32[]{:S(2)}, u32[]{:S(2)}) collective-permute-start(bf16[72,512]{1,0:T(8,128)(2,1)S(1)} %add_convert_fusion), channel_id=1, source_target_pairs={{0,2},{1,3},{2,0},{3,1},{4,6},{5,7},{6,4},{7,5},{8,40},{9,41},{10,... | collective-permute-start | bytes 221192 | tf_op jit(solution)/shard_map/ppermute | solution.py:509
  167.3 3.2 %collective-permute-start.15 = (bf16[72,512]{1,0:T(8,128)(2,1)S(1)}, bf16[72,512]{1,0:T(8,128)(2,1)S(1)}, u32[]{:S(2)}, u32[]{:S(2)}) collective-permute-start(bf16[72,512]{1,0:T(8,128)(2,1)S(1)} %add_convert_fusion), channel_id=1, source_target_pairs={{0,3},{1,0},{2,1},{3,2},{4,7},{5,4},{6,5},{7,6},{8,56},{9,57},{10,... | collective-permute-start | bytes 221192 | tf_op jit(solution)/shard_map/ppermute | solution.py:509
  170.6 10.0 %collective-permute-start.19 = (bf16[288,512]{1,0:T(8,128)(2,1)S(1)}, bf16[288,512]{1,0:T(8,128)(2,1)S(1)}, u32[]{:S(2)}, u32[]{:S(2)}) collective-permute-start(bf16[288,512]{1,0:T(8,128)(2,1)S(1)} %constant_dynamic-update-slice_fusion.7), channel_id=1, source_target_pairs={{0,16},{1,17},{2,18},{3,19},{4,20},{5,21},{6,22},{7,23},{8,9},{9,1... | collective-permute-start | bytes 884744 | tf_op jit(solution)/shard_map/ppermute | solution.py:509
  170.7 9.9 %collective-permute-start.20 = (bf16[288,512]{1,0:T(8,128)(2,1)S(1)}, bf16[288,512]{1,0:T(8,128)(2,1)S(1)}, u32[]{:S(2)}, u32[]{:S(2)}) collective-permute-start(bf16[288,512]{1,0:T(8,128)(2,1)S(1)} %constant_dynamic-update-slice_fusion.7), channel_id=1, source_target_pairs={{0,32},{1,33},{2,34},{3,35},{4,36},{5,37},{6,38},{7,39},{8,10},{9,... | collective-permute-start | bytes 884744 | tf_op jit(solution)/shard_map/ppermute | solution.py:509
  170.8 10.5 %collective-permute-start.21 = (bf16[288,512]{1,0:T(8,128)(2,1)S(1)}, bf16[288,512]{1,0:T(8,128)(2,1)S(1)}, u32[]{:S(2)}, u32[]{:S(2)}) collective-permute-start(bf16[288,512]{1,0:T(8,128)(2,1)S(1)} %constant_dynamic-update-slice_fusion.7), channel_id=1, source_target_pairs={{0,48},{1,49},{2,50},{3,51},{4,52},{5,53},{6,54},{7,55},{8,11},{9,... | collective-permute-start | bytes 884744 | tf_op jit(solution)/shard_map/ppermute | solution.py:509
  181.5 2.9 %collective-permute-start.22 = (bf16[1152,512]{1,0:T(8,128)(2,1)S(1)}, bf16[1152,512]{1,0:T(8,128)(2,1)S(1)}, u32[]{:S(2)}, u32[]{:S(2)}) collective-permute-start(bf16[1152,512]{1,0:T(8,128)(2,1)S(1)} %constant_dynamic-update-slice_fusion.own_ref.own_rest_ref), channel_id=1, source_target_pairs={{0,8},{1,9},{2,10},{3,11},{4,12},{5,13},{6,14},{7,15},{8,0},{9,1},... | collective-permute-start | bytes 3538952 | tf_op jit(solution)/shard_map/ppermute | solution.py:509
  181.6 2.8 %copy-start = (bf16[128,384]{1,0:T(8,128)(2,1)S(1)}, bf16[128,384]{1,0:T(8,128)(2,1)}, u32[]{:S(2)}) copy-start(bf16[128,384]{1,0:T(8,128)(2,1)} %w_ref.1) | copy-start | bytes 294916
  181.6 2.8 %copy-start.1 = (f32[128]{0:T(128)S(1)}, f32[128]{0:T(128)}, u32[]{:S(2)}) copy-start(f32[128]{0:T(128)} %param.8) | copy-start | bytes 1540

commit v7 on v5

--- a/solution.py
+++ b/solution.py
@@ -256,9 +256,9 @@
                 h = 2 * (1 - mine) + j
                 away_ref[j * T : (j + 1) * T] = (dbias_ref[h] + acc_s[h]).T.astype(BF)
                 h = 2 * mine + j
-                keep_ref[j * T : (j + 1) * T] = (dbias_ref[h] + acc_s[h]).T
+                keep_ref[j * T : (j + 1) * T] = (dbias_ref[h] + acc_s[h]).T.astype(BF)
             away_ref[2 * T :] = jnp.where(mine == 1, table, 0.0).astype(BF)
-            keep_ref[2 * T :] = jnp.where(mine == 0, table, 0.0)
+            keep_ref[2 * T :] = jnp.where(mine == 0, table, 0.0).astype(BF)
 
 
 def finish_kernel(first, *refs):
@@ -328,7 +328,7 @@
     else:
         ins += [ANYWHERE, whole(small)]
         outs = [DT_BLOCK, whole((HALF, T)), whole((HALF, T))]
-        shapes = [((blocks,) + DT_SHAPE, BF), ((HALF, T), BF), ((HALF, T), F32)]
+        shapes = [((blocks,) + DT_SHAPE, BF), ((HALF, T), BF), ((HALF, T), BF)]
         scratch = [pltpu.VMEM(small, F32), pltpu.VMEM(square, F32), pltpu.SemaphoreType.DMA]
     scratch += [
         pltpu.SemaphoreType.DMA((2, len(pieces))),
@@ -401,7 +401,7 @@
             out_specs=pl.BlockSpec((pl.Squeezed(), T, T), lambda j, m: (2 * m[0] + j, 0, 0)),
         ),
         out_shape=jax.ShapeDtypeStruct((HEADS, T, T), F32),
-        compiler_params=pltpu.CompilerParams(vmem_limit_bytes=60 * 1024 * 1024),
+        compiler_params=pltpu.CompilerParams(vmem_limit_bytes=8 * 1024 * 1024),
         name="spread_own",
     )(mine, own)
 
@@ -444,7 +444,7 @@
             jax.ShapeDtypeStruct((1, C), F32),
         ],
         input_output_aliases={6: 0},
-        compiler_params=pltpu.CompilerParams(vmem_limit_bytes=60 * 1024 * 1024),
+        compiler_params=pltpu.CompilerParams(vmem_limit_bytes=8 * 1024 * 1024),
         name="spread_got",
     )(mine, got, own, got, gamma, w, grad_bias)
 
@@ -529,7 +529,7 @@
     rim_dT, away, keep = sublayer(False, around, (gamma, w, w_proj, biasT), (acc, acc_small))
 
     first, second, third = (ACROSS_X, ACROSS_Z), (ACROSS_Z, ACROSS_X), (ACROSS_Y, ACROSS_Y)
-    values = keep + send(away, (CORE, CORE), 1).astype(F32)
+    values = keep.astype(F32) + send(away, (CORE, CORE), 1).astype(F32)
     values, got = parts_sent(values, first)
     gin, back_x, back_y, back_xy = finish(False, around, gamma, w, rim_dT)
     values, got, back_x, back_y, back_xy = lax.optimization_barrier((values, got, back_x, back_y, back_xy))

time: 150 us -> 146 us (0.973)
  Pallas kernels: 77.8 us -> 74.9 us
  local copies, waits for them, and re-layouts: 8.86 us -> 6.92 us
  waiting for transfers between devices: 22.2 us -> 23.8 us
    unnamed x14, local copies, waits for them, and re-layouts: 3.01 us -> 1.06 us
  transfers between devices with their start and end apart: 23 -> 23, of which waited for: 8 -> 9; matrix products, arithmetic and copies ran while one was open for 3% -> 3% of each run, Pallas kernels for 20% -> 20%
where the time goes in v7:
time: 146 us
  Pallas kernels  74.9 us (51%)
  starting transfers between devices  37.3 us (26%)
  waiting for transfers between devices  23.8 us (16%)
  local copies, waits for them, and re-layouts  6.92 us (5%)
  other arithmetic  1.98 us (1%)
    pallas_call x2, Pallas kernels, sublayer(): pl.pallas_call(functools.partial(kernel, first), grid=(blocks,), in_specs...  60.5 us
    ppermute x17, starting transfers between devices, send(): return lax.ppermute(values, ('gx', 'gy'), pairs)  20.8 us
    ppermute x17, waiting for transfers between devices, send(): return lax.ppermute(values, ('gx', 'gy'), pairs)  12.3 us
    ppermute x2, waiting for transfers between devices, shifted(): return lax.ppermute(values, ('gx', 'gy'), pairs)  11.5 us
    pallas_call x2, Pallas kernels, finish(): pl.pallas_call(functools.partial(finish_kernel, first), grid=(blocks,), i...  11.4 us
    ppermute x2, starting transfers between devices, shifted(): return lax.ppermute(values, 'gy', [(i, (i + by_y) % ny) for i in range(ny)])  7.29 us
    ppermute x2, starting transfers between devices, shifted(): return lax.ppermute(values, 'gx', [(i, (i + by_x) % nx) for i in range(nx)])  5.95 us
    ppermute x2, starting transfers between devices, shifted(): return lax.ppermute(values, ('gx', 'gy'), pairs)  3.24 us
  transfers between devices with their start and end apart: 23, of which 9 were waited for; matrix products, arithmetic and copies ran while one was open for 3% of the time, Pallas kernels for 20%

profile of v7, /device:TPU:1, one launch (start us, length us, event | category | flops | bytes accessed | tf_op | source)
XLA Modules:
  0.0 146.1 jit_solution(3957903450497736480)
XLA Ops:
  0.6 1.1 slice_bitcast_fusion
  1.8 0.1 pad_maximum_fusion.1
  1.8 7.3 %collective-permute-start.1 = (bf16[2,12,4,24,128]{4,3,2,1,0:T(8,128)(2,1)S(1)}, bf16[2,12,4,24,128]{4,3,2,1,0:T(8,128)(2,1)S(1)}, u32[]{:S(2)}, u32[]{:S(2)}) collective-permute-start(bf16[2,12,4,24,128]{4,3,2,1,0:T(8,128)(2,1)S(1)} %pad_maximum_fusion.1), channel_id=1, source_target_pairs={{0,7},{1,0},{2,1},{3,2},{4,3},{5,4},{6,5},{7,6},{8,15},{9,8},{10,9... | collective-permute-start | bytes 1769480 | tf_op jit(solution)/shard_map/ppermute | solution.py:457
  9.1 1.1 slice_bitcast_fusion.2
  10.3 1.0 collective-permute-start
  11.3 1.0 slice_bitcast_fusion.4
  12.3 2.7 %collective-permute-start.2 = (bf16[2,4,4,24,128]{4,3,2,1,0:T(8,128)(2,1)S(1)}, bf16[2,4,4,24,128]{4,3,2,1,0:T(8,128)(2,1)S(1)}, u32[]{:S(2)}, u32[]{:S(2)}) collective-permute-start(bf16[2,4,4,24,128]{4,3,2,1,0:T(8,128)(2,1)S(1)} %pad_maximum_fusion.2), channel_id=1, source_target_pairs={{0,127},{1,120},{2,121},{3,122},{4,123},{5,124},{6,125},{7,126},{8... | collective-permute-start | bytes 589832 | tf_op jit(solution)/shard_map/ppermute | solution.py:459
  15.0 16.7 %inner_windows.1 = (bf16[1,3,384,512]{3,2,1,0:T(8,128)(2,1)}, f32[512,128]{1,0:T(8,128)}, f32[4,512,512]{2,1,0:T(8,128)}, f32[4,512,512]{2,1,0:T(8,128)}) custom-call(bf16[16,16,24,128]{3,2,1,0:T(8,128)(2,1)} %refs_0_.7, bf16[16,16,24,128]{3,2,1,0:T(8,128)(2,1)} %refs_1_.7, f32[1,128]{1,0:T(1,128)} %bitcast.15, bf16[128,384]{1,0:T(8,128)(2,1)} %w_ref.1, ...), custom_call_target="tpu_custom_call" | custom-call | flops 12000000000 | bytes 10000000 | tf_op jit(solution)/shard_map/inner_windows/pallas_call | solution.py:354
  31.8 0.6 copy-done.5
  32.4 0.2 copy-done.2
  32.6 0.2 copy-done.3
  32.8 43.8 %rim_windows.1 = (bf16[3,3,384,512]{3,2,1,0:T(8,128)(2,1)}, bf16[1152,512]{1,0:T(8,128)(2,1)}, bf16[1152,512]{1,0:T(8,128)(2,1)}) custom-call(bf16[16,16,24,128]{3,2,1,0:T(8,128)(2,1)} %refs_0_.7, bf16[16,16,24,128]{3,2,1,0:T(8,128)(2,1)} %refs_1_.7, bf16[2,4,12,24,128]{4,3,2,1,0:T(8,128)(2,1)} %copy-done.3, bf16[2,12,4,24,128]{4,3,2,1,0:T(8,128)(2,1)} %copy-done.2, ...), custom_call_target="tpu_custom_call" | custom-call | flops 35999997952 | bytes 30000000 | tf_op jit(solution)/shard_map/rim_windows/pallas_call | solution.py:354
  76.7 0.1 collective-permute-start.3
  76.9 2.9 %collective-permute-done.3 = bf16[1152,512]{1,0:T(8,128)(2,1)S(1)} collective-permute-done((bf16[1152,512]{1,0:T(8,128)(2,1)}, bf16[1152,512]{1,0:T(8,128)(2,1)S(1)}, u32[]{:S(2)}, u32[]{:S(2)}) %collective-permute-start.3) | collective-permute-done | bytes 1179680 | tf_op jit(solution)/shard_map/ppermute | solution.py:485
  79.8 1.6 %convert_add_fusion = f32[1152,512]{1,0:T(8,128)S(1)} fusion(bf16[1152,512]{1,0:T(8,128)(2,1)S(1)} %collective-permute-done.3, bf16[1152,512]{1,0:T(8,128)(2,1)} %get-tuple-element.46), kind=kLoop, calls=%fused_computation | loop fusion | flops 1769472 | bytes 4718592 | tf_op jit(solution)/shard_map/add | solution.py:532
  81.4 0.1 dynamic-slice_convert_fusion
  81.6 0.1 collective-permute-start.4
  81.6 1.2 collective-permute-start.5
  82.9 2.3 %collective-permute-start.6 = (bf16[288,512]{1,0:T(8,128)(2,1)S(1)}, bf16[288,512]{1,0:T(8,128)(2,1)S(1)}, u32[]{:S(2)}, u32[]{:S(2)}) collective-permute-start(bf16[288,512]{1,0:T(8,128)(2,1)S(1)} %get-tuple-element.81), channel_id=1, source_target_pairs={{0,48},{1,49},{2,50},{3,51},{4,52},{5,53},{6,54},{7,55},{8,11},{9,... | collective-permute-start | bytes 884744 | tf_op jit(solution)/shard_map/ppermute | solution.py:485
  85.2 7.0 %rim_finish.1 = (bf16[16,16,24,128]{3,2,1,0:T(8,128)(2,1)}, bf16[4,12,24,128]{3,2,1,0:T(8,128)(2,1)}, bf16[12,4,24,128]{3,2,1,0:T(8,128)(2,1)}, bf16[4,4,24,128]{3,2,1,0:T(8,128)(2,1)}) custom-call(bf16[16,16,24,128]{3,2,1,0:T(8,128)(2,1)} %refs_0_.7, bf16[16,16,24,128]{3,2,1,0:T(8,128)(2,1)} %refs_1_.7, bf16[2,4,12,24,128]{4,3,2,1,0:T(8,128)(2,1)} %copy-done.3, ...), custom_call_target="tpu_custom_call" | custom-call | flops 3000000000 | bytes 9000000 | tf_op jit(solution)/shard_map/rim_finish/pallas_call | solution.py:371
  92.3 0.1 convert_add_fusion.1
  92.5 0.5 collective-permute-start.7
  93.0 3.1 %collective-permute-start.8 = (bf16[72,512]{1,0:T(8,128)(2,1)S(1)}, bf16[72,512]{1,0:T(8,128)(2,1)S(1)}, u32[]{:S(2)}, u32[]{:S(2)}) collective-permute-start(bf16[72,512]{1,0:T(8,128)(2,1)S(1)} %get-tuple-element.86), channel_id=1, source_target_pairs={{0,1},{1,2},{2,3},{3,0},{4,5},{5,6},{6,7},{7,4},{8,24},{9,25},{10,... | collective-permute-start | bytes 221192 | tf_op jit(solution)/shard_map/ppermute | solution.py:485
  96.1 1.3 collective-permute-done.7
  97.4 0.7 collective-permute-done.8
  98.1 1.5 %collective-permute-done.9 = bf16[72,512]{1,0:T(8,128)(2,1)S(1)} collective-permute-done((bf16[72,512]{1,0:T(8,128)(2,1)S(1)}, bf16[72,512]{1,0:T(8,128)(2,1)S(1)}, u32[]{:S(2)}, u32[]{:S(2)}) %collective-permute-start.9) | collective-permute-done | bytes 73760 | tf_op jit(solution)/shard_map/ppermute | solution.py:485
  99.6 3.6 %collective-permute-start.10 = (f32[72,512]{1,0:T(8,128)S(1)}, f32[72,512]{1,0:T(8,128)S(1)}, u32[]{:S(2)}, u32[]{:S(2)}) collective-permute-start(f32[72,512]{1,0:T(8,128)S(1)} %convert_add_fusion.2), channel_id=1, source_target_pairs={{0,4},{1,5},{2,6},{3,7},{4,0},{5,1},{6,2},{7,3},{8,12},{9,13},{10,... | collective-permute-start | bytes 442376 | tf_op jit(solution)/shard_map/ppermute | solution.py:485
  103.2 2.7 %collective-permute-start.12 = (f32[72,512]{1,0:T(8,128)S(1)}, f32[72,512]{1,0:T(8,128)S(1)}, u32[]{:S(2)}, u32[]{:S(2)}) collective-permute-start(f32[72,512]{1,0:T(8,128)S(1)} %convert_add_fusion.2), channel_id=1, source_target_pairs={{0,68},{1,69},{2,70},{3,71},{4,64},{5,65},{6,66},{7,67},{8,76},{9,... | collective-permute-start | bytes 442376 | tf_op jit(solution)/shard_map/ppermute | solution.py:485
  105.9 4.9 %collective-permute-start.16 = (bf16[4,12,24,128]{3,2,1,0:T(8,128)(2,1)}, bf16[4,12,24,128]{3,2,1,0:T(8,128)(2,1)S(1)}, u32[]{:S(2)}, u32[]{:S(2)}) collective-permute-start(bf16[4,12,24,128]{3,2,1,0:T(8,128)(2,1)} %get-tuple-element.56), channel_id=1, source_target_pairs={{0,8},{8,16},{16,24},{24,32},{32,40},{40,48},{48,56},{56,64},{64,7... | collective-permute-start | bytes 884744 | tf_op jit(solution)/shard_map/ppermute | solution.py:455
  110.8 0.5 collective-permute-start.18
  111.4 0.2 collective-permute-start.13
  111.6 4.3 %collective-permute-start.14 = (bf16[72,512]{1,0:T(8,128)(2,1)S(1)}, bf16[72,512]{1,0:T(8,128)(2,1)S(1)}, u32[]{:S(2)}, u32[]{:S(2)}) collective-permute-start(bf16[72,512]{1,0:T(8,128)(2,1)S(1)} %add_convert_fusion), channel_id=1, source_target_pairs={{0,2},{1,3},{2,0},{3,1},{4,6},{5,7},{6,4},{7,5},{8,40},{9,41},{10,... | collective-permute-start | bytes 221192 | tf_op jit(solution)/shard_map/ppermute | solution.py:485
  115.9 11.5 %collective-permute-done.18 = bf16[4,4,24,128]{3,2,1,0:T(8,128)(2,1)S(1)} collective-permute-done((bf16[4,4,24,128]{3,2,1,0:T(8,128)(2,1)S(1)}, bf16[4,4,24,128]{3,2,1,0:T(8,128)(2,1)S(1)}, u32[]{:S(2)}, u32[]{:S(2)}) %collective-permute-start.18) | collective-permute-done | bytes 98336 | tf_op jit(solution)/shard_map/ppermute | solution.py:459
  127.3 3.2 %collective-permute-done.15 = bf16[72,512]{1,0:T(8,128)(2,1)S(1)} collective-permute-done((bf16[72,512]{1,0:T(8,128)(2,1)S(1)}, bf16[72,512]{1,0:T(8,128)(2,1)S(1)}, u32[]{:S(2)}, u32[]{:S(2)}) %collective-permute-start.15) | collective-permute-done | bytes 73760 | tf_op jit(solution)/shard_map/ppermute | solution.py:485
  130.7 0.1 collective-permute-start.19
  130.7 0.1 collective-permute-start.20
  130.8 2.6 %collective-permute-start.21 = (bf16[288,512]{1,0:T(8,128)(2,1)S(1)}, bf16[288,512]{1,0:T(8,128)(2,1)S(1)}, u32[]{:S(2)}, u32[]{:S(2)}) collective-permute-start(bf16[288,512]{1,0:T(8,128)(2,1)S(1)} %constant_dynamic-update-slice_fusion.7), channel_id=1, source_target_pairs={{0,48},{1,49},{2,50},{3,51},{4,52},{5,53},{6,54},{7,55},{8,11},{9,... | collective-permute-start | bytes 884744 | tf_op jit(solution)/shard_map/ppermute | solution.py:485
  133.4 4.3 %inner_finish.1 = bf16[16,16,24,128]{3,2,1,0:T(8,128)(2,1)} custom-call(bf16[16,16,24,128]{3,2,1,0:T(8,128)(2,1)} %refs_0_.7, bf16[16,16,24,128]{3,2,1,0:T(8,128)(2,1)} %refs_1_.7, f32[1,128]{1,0:T(1,128)} %bitcast.18, bf16[128,384]{1,0:T(8,128)(2,1)} %w_ref.1, bf16[1,3,384,512]{3,2,1,0:T(8,128)(2,1)} %get-tuple-element.65.refs_4_, ...), custom_call_target="tpu_custom_call", output_to_operand_aliasing={{}: (5, {})} | custom-call | flops 1000000000 | bytes 3000000 | tf_op jit(solution)/shard_map/inner_finish/pallas_call | solution.py:371
  137.7 0.8 constant_dynamic-update-slice_fusion.6
  138.5 0.8 constant_dynamic-update-slice_fusion.5
  139.3 0.7 constant_dynamic-update-slice_fusion.4
  139.9 0.7 collective-permute-done.19
  140.7 0.6 collective-permute-done.21
  141.3 0.1 broadcast_in_dim.7
  141.5 0.1 collective-permute-start.22
  141.6 1.4 spread_own.1._
  143.0 1.4 collective-permute-done.22.got_ref.got_rest_ref
  144.4 1.6 %spread_got.1 = (f32[4,512,512]{2,1,0:T(8,128)}, f32[128,128]{1,0:T(8,128)}, f32[128,384]{1,0:T(8,128)}, f32[1,128]{1,0:T(1,128)}) custom-call(s32[1]{0:T(128)} %bitcast.7.mine_ref, bf16[1152,512]{1,0:T(8,128)(2,1)S(1)} %collective-permute-done.22.got_ref.got_rest_ref, ...), custom_call_target="tpu_custom_call", output_to_operand_aliasing={{0}: (6, {})} | custom-call | tf_op jit(solution)/shard_map/spread_got/pallas_call | solution.py:427
  (44 shorter events, 0.5 us)
Async XLA Ops:
  1.8 30.0 %collective-permute-start.1 = (bf16[2,12,4,24,128]{4,3,2,1,0:T(8,128)(2,1)S(1)}, bf16[2,12,4,24,128]{4,3,2,1,0:T(8,128)(2,1)S(1)}, u32[]{:S(2)}, u32[]{:S(2)}) collective-permute-start(bf16[2,12,4,24,128]{4,3,2,1,0:T(8,128)(2,1)S(1)} %pad_maximum_fusion.1), channel_id=1, source_target_pairs={{0,7},{1,0},{2,1},{3,2},{4,3},{5,4},{6,5},{7,6},{8,15},{9,8},{10,9... | collective-permute-start | bytes 1769480 | tf_op jit(solution)/shard_map/ppermute | solution.py:457
  10.3 21.5 %collective-permute-start = (bf16[2,4,12,24,128]{4,3,2,1,0:T(8,128)(2,1)S(1)}, bf16[2,4,12,24,128]{4,3,2,1,0:T(8,128)(2,1)S(1)}, u32[]{:S(2)}, u32[]{:S(2)}) collective-permute-start(bf16[2,4,12,24,128]{4,3,2,1,0:T(8,128)(2,1)S(1)} %pad_maximum_fusion), channel_id=1, source_target_pairs={{0,120},{8,0},{16,8},{24,16},{32,24},{40,32},{48,40},{56,48},{64,5... | collective-permute-start | bytes 1769480 | tf_op jit(solution)/shard_map/ppermute | solution.py:455
  12.3 19.4 %collective-permute-start.2 = (bf16[2,4,4,24,128]{4,3,2,1,0:T(8,128)(2,1)S(1)}, bf16[2,4,4,24,128]{4,3,2,1,0:T(8,128)(2,1)S(1)}, u32[]{:S(2)}, u32[]{:S(2)}) collective-permute-start(bf16[2,4,4,24,128]{4,3,2,1,0:T(8,128)(2,1)S(1)} %pad_maximum_fusion.2), channel_id=1, source_target_pairs={{0,127},{1,120},{2,121},{3,122},{4,123},{5,124},{6,125},{7,126},{8... | collective-permute-start | bytes 589832 | tf_op jit(solution)/shard_map/ppermute | solution.py:459
  31.8 0.7 copy-start.5
  31.8 0.9 copy-start.2
  31.8 1.0 copy-start.3
  76.7 3.1 %collective-permute-start.3 = (bf16[1152,512]{1,0:T(8,128)(2,1)}, bf16[1152,512]{1,0:T(8,128)(2,1)S(1)}, u32[]{:S(2)}, u32[]{:S(2)}) collective-permute-start(bf16[1152,512]{1,0:T(8,128)(2,1)} %get-tuple-element.47), channel_id=1, source_target_pairs={{0,8},{1,9},{2,10},{3,11},{4,12},{5,13},{6,14},{7,15},{8,0},{9,1},... | collective-permute-start | bytes 3538952 | tf_op jit(solution)/shard_map/ppermute | solution.py:485
  81.6 10.8 %collective-permute-start.4 = (bf16[288,512]{1,0:T(8,128)(2,1)S(1)}, bf16[288,512]{1,0:T(8,128)(2,1)S(1)}, u32[]{:S(2)}, u32[]{:S(2)}) collective-permute-start(bf16[288,512]{1,0:T(8,128)(2,1)S(1)} %get-tuple-element.83), channel_id=1, source_target_pairs={{0,32},{1,33},{2,34},{3,35},{4,36},{5,37},{6,38},{7,39},{8,10},{9,... | collective-permute-start | bytes 884744 | tf_op jit(solution)/shard_map/ppermute | solution.py:485
  81.6 10.7 %collective-permute-start.5 = (bf16[288,512]{1,0:T(8,128)(2,1)S(1)}, bf16[288,512]{1,0:T(8,128)(2,1)S(1)}, u32[]{:S(2)}, u32[]{:S(2)}) collective-permute-start(bf16[288,512]{1,0:T(8,128)(2,1)S(1)} %get-tuple-element.82), channel_id=1, source_target_pairs={{0,16},{1,17},{2,18},{3,19},{4,20},{5,21},{6,22},{7,23},{8,9},{9,1... | collective-permute-start | bytes 884744 | tf_op jit(solution)/shard_map/ppermute | solution.py:485
  82.9 9.5 %collective-permute-start.6 = (bf16[288,512]{1,0:T(8,128)(2,1)S(1)}, bf16[288,512]{1,0:T(8,128)(2,1)S(1)}, u32[]{:S(2)}, u32[]{:S(2)}) collective-permute-start(bf16[288,512]{1,0:T(8,128)(2,1)S(1)} %get-tuple-element.81), channel_id=1, source_target_pairs={{0,48},{1,49},{2,50},{3,51},{4,52},{5,53},{6,54},{7,55},{8,11},{9,... | collective-permute-start | bytes 884744 | tf_op jit(solution)/shard_map/ppermute | solution.py:485
  92.3 18.5 %copy-start.4 = (bf16[12,4,24,128]{3,2,1,0:T(8,128)(2,1)S(1)}, bf16[12,4,24,128]{3,2,1,0:T(8,128)(2,1)}, u32[]{:S(2)}) copy-start(bf16[12,4,24,128]{3,2,1,0:T(8,128)(2,1)} %get-tuple-element.57) | copy-start | bytes 884740
  92.3 18.5 %copy-start.6 = (bf16[4,4,24,128]{3,2,1,0:T(8,128)(2,1)S(1)}, bf16[4,4,24,128]{3,2,1,0:T(8,128)(2,1)}, u32[]{:S(2)}) copy-start(bf16[4,4,24,128]{3,2,1,0:T(8,128)(2,1)} %get-tuple-element.58) | copy-start | bytes 294916
  92.5 4.9 %collective-permute-start.7 = (bf16[72,512]{1,0:T(8,128)(2,1)S(1)}, bf16[72,512]{1,0:T(8,128)(2,1)S(1)}, u32[]{:S(2)}, u32[]{:S(2)}) collective-permute-start(bf16[72,512]{1,0:T(8,128)(2,1)S(1)} %get-tuple-element.84), channel_id=1, source_target_pairs={{0,2},{1,3},{2,0},{3,1},{4,6},{5,7},{6,4},{7,5},{8,40},{9,41},{10,... | collective-permute-start | bytes 221192 | tf_op jit(solution)/shard_map/ppermute | solution.py:485
  93.0 5.1 %collective-permute-start.8 = (bf16[72,512]{1,0:T(8,128)(2,1)S(1)}, bf16[72,512]{1,0:T(8,128)(2,1)S(1)}, u32[]{:S(2)}, u32[]{:S(2)}) collective-permute-start(bf16[72,512]{1,0:T(8,128)(2,1)S(1)} %get-tuple-element.86), channel_id=1, source_target_pairs={{0,1},{1,2},{2,3},{3,0},{4,5},{5,6},{6,7},{7,4},{8,24},{9,25},{10,... | collective-permute-start | bytes 221192 | tf_op jit(solution)/shard_map/ppermute | solution.py:485
  96.1 3.5 %collective-permute-start.9 = (bf16[72,512]{1,0:T(8,128)(2,1)S(1)}, bf16[72,512]{1,0:T(8,128)(2,1)S(1)}, u32[]{:S(2)}, u32[]{:S(2)}) collective-permute-start(bf16[72,512]{1,0:T(8,128)(2,1)S(1)} %get-tuple-element.85), channel_id=1, source_target_pairs={{0,3},{1,0},{2,1},{3,2},{4,7},{5,4},{6,5},{7,6},{8,56},{9,57},{10,... | collective-permute-start | bytes 221192 | tf_op jit(solution)/shard_map/ppermute | solution.py:485
  99.6 11.2 %collective-permute-start.10 = (f32[72,512]{1,0:T(8,128)S(1)}, f32[72,512]{1,0:T(8,128)S(1)}, u32[]{:S(2)}, u32[]{:S(2)}) collective-permute-start(f32[72,512]{1,0:T(8,128)S(1)} %convert_add_fusion.2), channel_id=1, source_target_pairs={{0,4},{1,5},{2,6},{3,7},{4,0},{5,1},{6,2},{7,3},{8,12},{9,13},{10,... | collective-permute-start | bytes 442376 | tf_op jit(solution)/shard_map/ppermute | solution.py:485
  103.2 8.2 %collective-permute-start.11 = (f32[72,512]{1,0:T(8,128)S(1)}, f32[72,512]{1,0:T(8,128)S(1)}, u32[]{:S(2)}, u32[]{:S(2)}) collective-permute-start(f32[72,512]{1,0:T(8,128)S(1)} %convert_add_fusion.2), channel_id=1, source_target_pairs={{0,64},{1,65},{2,66},{3,67},{4,68},{5,69},{6,70},{7,71},{8,72},{9,... | collective-permute-start | bytes 442376 | tf_op jit(solution)/shard_map/ppermute | solution.py:485
  103.2 8.2 %collective-permute-start.12 = (f32[72,512]{1,0:T(8,128)S(1)}, f32[72,512]{1,0:T(8,128)S(1)}, u32[]{:S(2)}, u32[]{:S(2)}) collective-permute-start(f32[72,512]{1,0:T(8,128)S(1)} %convert_add_fusion.2), channel_id=1, source_target_pairs={{0,68},{1,69},{2,70},{3,71},{4,64},{5,65},{6,66},{7,67},{8,76},{9,... | collective-permute-start | bytes 442376 | tf_op jit(solution)/shard_map/ppermute | solution.py:485
  105.9 24.7 %collective-permute-start.16 = (bf16[4,12,24,128]{3,2,1,0:T(8,128)(2,1)}, bf16[4,12,24,128]{3,2,1,0:T(8,128)(2,1)S(1)}, u32[]{:S(2)}, u32[]{:S(2)}) collective-permute-start(bf16[4,12,24,128]{3,2,1,0:T(8,128)(2,1)} %get-tuple-element.56), channel_id=1, source_target_pairs={{0,8},{8,16},{16,24},{24,32},{32,40},{40,48},{48,56},{56,64},{64,7... | collective-permute-start | bytes 884744 | tf_op jit(solution)/shard_map/ppermute | solution.py:455
  110.8 19.7 %collective-permute-start.17 = (bf16[12,4,24,128]{3,2,1,0:T(8,128)(2,1)S(1)}, bf16[12,4,24,128]{3,2,1,0:T(8,128)(2,1)S(1)}, u32[]{:S(2)}, u32[]{:S(2)}) collective-permute-start(bf16[12,4,24,128]{3,2,1,0:T(8,128)(2,1)S(1)} %copy-done.4), channel_id=1, source_target_pairs={{0,1},{1,2},{2,3},{3,4},{4,5},{5,6},{6,7},{7,0},{8,9},{9,10},{10,1... | collective-permute-start | bytes 884744 | tf_op jit(solution)/shard_map/ppermute | solution.py:457
  110.8 16.5 %collective-permute-start.18 = (bf16[4,4,24,128]{3,2,1,0:T(8,128)(2,1)S(1)}, bf16[4,4,24,128]{3,2,1,0:T(8,128)(2,1)S(1)}, u32[]{:S(2)}, u32[]{:S(2)}) collective-permute-start(bf16[4,4,24,128]{3,2,1,0:T(8,128)(2,1)S(1)} %copy-done.6), channel_id=1, source_target_pairs={{0,9},{1,10},{2,11},{3,12},{4,13},{5,14},{6,15},{7,8},{8,17},{9,18... | collective-permute-start | bytes 294920 | tf_op jit(solution)/shard_map/ppermute | solution.py:459
  111.4 15.9 %collective-permute-start.13 = (bf16[72,512]{1,0:T(8,128)(2,1)S(1)}, bf16[72,512]{1,0:T(8,128)(2,1)S(1)}, u32[]{:S(2)}, u32[]{:S(2)}) collective-permute-start(bf16[72,512]{1,0:T(8,128)(2,1)S(1)} %add_convert_fusion), channel_id=1, source_target_pairs={{0,1},{1,2},{2,3},{3,0},{4,5},{5,6},{6,7},{7,4},{8,24},{9,25},{10,... | collective-permute-start | bytes 221192 | tf_op jit(solution)/shard_map/ppermute | solution.py:485
  111.6 15.7 %collective-permute-start.14 = (bf16[72,512]{1,0:T(8,128)(2,1)S(1)}, bf16[72,512]{1,0:T(8,128)(2,1)S(1)}, u32[]{:S(2)}, u32[]{:S(2)}) collective-permute-start(bf16[72,512]{1,0:T(8,128)(2,1)S(1)} %add_convert_fusion), channel_id=1, source_target_pairs={{0,2},{1,3},{2,0},{3,1},{4,6},{5,7},{6,4},{7,5},{8,40},{9,41},{10,... | collective-permute-start | bytes 221192 | tf_op jit(solution)/shard_map/ppermute | solution.py:485
  127.3 3.2 %collective-permute-start.15 = (bf16[72,512]{1,0:T(8,128)(2,1)S(1)}, bf16[72,512]{1,0:T(8,128)(2,1)S(1)}, u32[]{:S(2)}, u32[]{:S(2)}) collective-permute-start(bf16[72,512]{1,0:T(8,128)(2,1)S(1)} %add_convert_fusion), channel_id=1, source_target_pairs={{0,3},{1,0},{2,1},{3,2},{4,7},{5,4},{6,5},{7,6},{8,56},{9,57},{10,... | collective-permute-start | bytes 221192 | tf_op jit(solution)/shard_map/ppermute | solution.py:485
  130.7 10.0 %collective-permute-start.19 = (bf16[288,512]{1,0:T(8,128)(2,1)S(1)}, bf16[288,512]{1,0:T(8,128)(2,1)S(1)}, u32[]{:S(2)}, u32[]{:S(2)}) collective-permute-start(bf16[288,512]{1,0:T(8,128)(2,1)S(1)} %constant_dynamic-update-slice_fusion.7), channel_id=1, source_target_pairs={{0,16},{1,17},{2,18},{3,19},{4,20},{5,21},{6,22},{7,23},{8,9},{9,1... | collective-permute-start | bytes 884744 | tf_op jit(solution)/shard_map/ppermute | solution.py:485
  130.7 9.9 %collective-permute-start.20 = (bf16[288,512]{1,0:T(8,128)(2,1)S(1)}, bf16[288,512]{1,0:T(8,128)(2,1)S(1)}, u32[]{:S(2)}, u32[]{:S(2)}) collective-permute-start(bf16[288,512]{1,0:T(8,128)(2,1)S(1)} %constant_dynamic-update-slice_fusion.7), channel_id=1, source_target_pairs={{0,32},{1,33},{2,34},{3,35},{4,36},{5,37},{6,38},{7,39},{8,10},{9,... | collective-permute-start | bytes 884744 | tf_op jit(solution)/shard_map/ppermute | solution.py:485
  130.8 10.5 %collective-permute-start.21 = (bf16[288,512]{1,0:T(8,128)(2,1)S(1)}, bf16[288,512]{1,0:T(8,128)(2,1)S(1)}, u32[]{:S(2)}, u32[]{:S(2)}) collective-permute-start(bf16[288,512]{1,0:T(8,128)(2,1)S(1)} %constant_dynamic-update-slice_fusion.7), channel_id=1, source_target_pairs={{0,48},{1,49},{2,50},{3,51},{4,52},{5,53},{6,54},{7,55},{8,11},{9,... | collective-permute-start | bytes 884744 | tf_op jit(solution)/shard_map/ppermute | solution.py:485
  141.5 2.9 %collective-permute-start.22 = (bf16[1152,512]{1,0:T(8,128)(2,1)S(1)}, bf16[1152,512]{1,0:T(8,128)(2,1)S(1)}, u32[]{:S(2)}, u32[]{:S(2)}) collective-permute-start(bf16[1152,512]{1,0:T(8,128)(2,1)S(1)} %constant_dynamic-update-slice_fusion.own_ref.own_rest_ref), channel_id=1, source_target_pairs={{0,8},{1,9},{2,10},{3,11},{4,12},{5,13},{6,14},{7,15},{8,0},{9,1},... | collective-permute-start | bytes 3538952 | tf_op jit(solution)/shard_map/ppermute | solution.py:485
  141.6 2.8 %copy-start = (bf16[128,384]{1,0:T(8,128)(2,1)S(1)}, bf16[128,384]{1,0:T(8,128)(2,1)}, u32[]{:S(2)}) copy-start(bf16[128,384]{1,0:T(8,128)(2,1)} %w_ref.1) | copy-start | bytes 294916
  141.6 2.8 %copy-start.1 = (f32[128]{0:T(128)S(1)}, f32[128]{0:T(128)}, u32[]{:S(2)}) copy-start(f32[128]{0:T(128)} %param.8) | copy-start | bytes 1540

commit v8 on v7

--- a/solution.py
+++ b/solution.py
@@ -539,11 +539,11 @@
     got = all_sent(values, third)
     values = ((values + got[2]) + (got[1] + got[3])).astype(BF)
     got = all_sent(values, second)
-    values, got, back = lax.optimization_barrier((values, got, back))
+    gin, inner_dT, _ = lax.optimization_barrier((gin, inner_dT, values))
+    (gin,) = finish(True, both, gamma, w, inner_dT, (gin,))
+    values, got, back, gin = lax.optimization_barrier((values, got, back, gin))
     values = gathered(values, got, second)
     got = all_sent(values, first)
-    (gin, inner_dT) = lax.optimization_barrier((gin, inner_dT, values))[:2]
-    (gin,) = finish(True, both, gamma, w, inner_dT, (gin,))
     for part, place in zip(back, ((0, 4), (4, 0), (0, 0))):
         gin = lax.dynamic_update_slice(gin, part, place + (0, 0))
     values, got, gin = lax.optimization_barrier((values, got, gin))

time: 146 us -> 147 us (level)
  transfers between devices with their start and end apart: 23 -> 23, of which waited for: 9 -> 8; matrix products, arithmetic and copies ran while one was open for 3% -> 3% of each run, Pallas kernels for 20% -> 20%
where the time goes in v8:
time: 147 us
  Pallas kernels  74.9 us (51%)
  starting transfers between devices  37.6 us (26%)
  waiting for transfers between devices  24.5 us (17%)
  local copies, waits for them, and re-layouts  6.9 us (5%)
  other arithmetic  1.99 us (1%)
    pallas_call x2, Pallas kernels, sublayer(): pl.pallas_call(functools.partial(kernel, first), grid=(blocks,), in_specs...  60.5 us
    ppermute x17, starting transfers between devices, send(): return lax.ppermute(values, ('gx', 'gy'), pairs)  21.1 us
    ppermute x17, waiting for transfers between devices, send(): return lax.ppermute(values, ('gx', 'gy'), pairs)  13.2 us
    pallas_call x2, Pallas kernels, finish(): pl.pallas_call(functools.partial(finish_kernel, first), grid=(blocks,), i...  11.3 us
    ppermute x2, waiting for transfers between devices, shifted(): return lax.ppermute(values, ('gx', 'gy'), pairs)  11.3 us
    ppermute x2, starting transfers between devices, shifted(): return lax.ppermute(values, 'gy', [(i, (i + by_y) % ny) for i in range(ny)])  7.29 us
    ppermute x2, starting transfers between devices, shifted(): return lax.ppermute(values, 'gx', [(i, (i + by_x) % nx) for i in range(nx)])  5.94 us
    ppermute x2, starting transfers between devices, shifted(): return lax.ppermute(values, ('gx', 'gy'), pairs)  3.23 us
  transfers between devices with their start and end apart: 23, of which 8 were waited for; matrix products, arithmetic and copies ran while one was open for 3% of the time, Pallas kernels for 20%

profile of v8, /device:TPU:1, one launch (start us, length us, event | category | flops | bytes accessed | tf_op | source)
XLA Modules:
  0.0 147.0 jit_solution(12085270232401956423)
XLA Ops:
  0.6 1.1 slice_bitcast_fusion
  1.8 0.1 pad_maximum_fusion.1
  1.8 7.3 %collective-permute-start.1 = (bf16[2,12,4,24,128]{4,3,2,1,0:T(8,128)(2,1)S(1)}, bf16[2,12,4,24,128]{4,3,2,1,0:T(8,128)(2,1)S(1)}, u32[]{:S(2)}, u32[]{:S(2)}) collective-permute-start(bf16[2,12,4,24,128]{4,3,2,1,0:T(8,128)(2,1)S(1)} %pad_maximum_fusion.1), channel_id=1, source_target_pairs={{0,7},{1,0},{2,1},{3,2},{4,3},{5,4},{6,5},{7,6},{8,15},{9,8},{10,9... | collective-permute-start | bytes 1769480 | tf_op jit(solution)/shard_map/ppermute | solution.py:457
  9.1 1.1 slice_bitcast_fusion.2
  10.2 0.1 pad_maximum_fusion
  10.3 1.0 collective-permute-start
  11.3 1.0 slice_bitcast_fusion.4
  12.3 2.7 %collective-permute-start.2 = (bf16[2,4,4,24,128]{4,3,2,1,0:T(8,128)(2,1)S(1)}, bf16[2,4,4,24,128]{4,3,2,1,0:T(8,128)(2,1)S(1)}, u32[]{:S(2)}, u32[]{:S(2)}) collective-permute-start(bf16[2,4,4,24,128]{4,3,2,1,0:T(8,128)(2,1)S(1)} %pad_maximum_fusion.2), channel_id=1, source_target_pairs={{0,127},{1,120},{2,121},{3,122},{4,123},{5,124},{6,125},{7,126},{8... | collective-permute-start | bytes 589832 | tf_op jit(solution)/shard_map/ppermute | solution.py:459
  15.0 16.7 %inner_windows.1 = (bf16[1,3,384,512]{3,2,1,0:T(8,128)(2,1)}, f32[512,128]{1,0:T(8,128)}, f32[4,512,512]{2,1,0:T(8,128)}, f32[4,512,512]{2,1,0:T(8,128)}) custom-call(bf16[16,16,24,128]{3,2,1,0:T(8,128)(2,1)} %refs_0_.7, bf16[16,16,24,128]{3,2,1,0:T(8,128)(2,1)} %refs_1_.7, f32[1,128]{1,0:T(1,128)} %bitcast.15, bf16[128,384]{1,0:T(8,128)(2,1)} %w_ref.1, ...), custom_call_target="tpu_custom_call" | custom-call | flops 12000000000 | bytes 10000000 | tf_op jit(solution)/shard_map/inner_windows/pallas_call | solution.py:354
  31.8 0.6 copy-done.6
  32.4 0.2 copy-done.2
  32.6 0.2 copy-done.3
  32.8 43.8 %rim_windows.1 = (bf16[3,3,384,512]{3,2,1,0:T(8,128)(2,1)}, bf16[1152,512]{1,0:T(8,128)(2,1)}, bf16[1152,512]{1,0:T(8,128)(2,1)}) custom-call(bf16[16,16,24,128]{3,2,1,0:T(8,128)(2,1)} %refs_0_.7, bf16[16,16,24,128]{3,2,1,0:T(8,128)(2,1)} %refs_1_.7, bf16[2,4,12,24,128]{4,3,2,1,0:T(8,128)(2,1)} %copy-done.3, bf16[2,12,4,24,128]{4,3,2,1,0:T(8,128)(2,1)} %copy-done.2, ...), custom_call_target="tpu_custom_call" | custom-call | flops 35999997952 | bytes 30000000 | tf_op jit(solution)/shard_map/rim_windows/pallas_call | solution.py:354
  76.6 0.1 collective-permute-start.3
  76.9 2.9 %collective-permute-done.3 = bf16[1152,512]{1,0:T(8,128)(2,1)S(1)} collective-permute-done((bf16[1152,512]{1,0:T(8,128)(2,1)}, bf16[1152,512]{1,0:T(8,128)(2,1)S(1)}, u32[]{:S(2)}, u32[]{:S(2)}) %collective-permute-start.3) | collective-permute-done | bytes 1179680 | tf_op jit(solution)/shard_map/ppermute | solution.py:485
  79.8 1.6 %convert_add_fusion = f32[1152,512]{1,0:T(8,128)S(1)} fusion(bf16[1152,512]{1,0:T(8,128)(2,1)S(1)} %collective-permute-done.3, bf16[1152,512]{1,0:T(8,128)(2,1)} %get-tuple-element.47), kind=kLoop, calls=%fused_computation | loop fusion | flops 1769472 | bytes 4718592 | tf_op jit(solution)/shard_map/add | solution.py:532
  81.4 0.1 dynamic-slice_convert_fusion
  81.5 0.1 collective-permute-start.4
  81.6 1.2 collective-permute-start.5
  82.8 2.3 %collective-permute-start.6 = (bf16[288,512]{1,0:T(8,128)(2,1)S(1)}, bf16[288,512]{1,0:T(8,128)(2,1)S(1)}, u32[]{:S(2)}, u32[]{:S(2)}) collective-permute-start(bf16[288,512]{1,0:T(8,128)(2,1)S(1)} %get-tuple-element.83), channel_id=1, source_target_pairs={{0,48},{1,49},{2,50},{3,51},{4,52},{5,53},{6,54},{7,55},{8,11},{9,... | collective-permute-start | bytes 884744 | tf_op jit(solution)/shard_map/ppermute | solution.py:485
  85.1 7.0 %rim_finish.1 = (bf16[16,16,24,128]{3,2,1,0:T(8,128)(2,1)}, bf16[4,12,24,128]{3,2,1,0:T(8,128)(2,1)}, bf16[12,4,24,128]{3,2,1,0:T(8,128)(2,1)}, bf16[4,4,24,128]{3,2,1,0:T(8,128)(2,1)}) custom-call(bf16[16,16,24,128]{3,2,1,0:T(8,128)(2,1)} %refs_0_.7, bf16[16,16,24,128]{3,2,1,0:T(8,128)(2,1)} %refs_1_.7, bf16[2,4,12,24,128]{4,3,2,1,0:T(8,128)(2,1)} %copy-done.3, ...), custom_call_target="tpu_custom_call" | custom-call | flops 3000000000 | bytes 9000000 | tf_op jit(solution)/shard_map/rim_finish/pallas_call | solution.py:371
  92.3 0.1 convert_add_fusion.1
  92.5 0.5 collective-permute-start.7
  93.0 3.1 %collective-permute-start.8 = (bf16[72,512]{1,0:T(8,128)(2,1)S(1)}, bf16[72,512]{1,0:T(8,128)(2,1)S(1)}, u32[]{:S(2)}, u32[]{:S(2)}) collective-permute-start(bf16[72,512]{1,0:T(8,128)(2,1)S(1)} %get-tuple-element.88), channel_id=1, source_target_pairs={{0,1},{1,2},{2,3},{3,0},{4,5},{5,6},{6,7},{7,4},{8,24},{9,25},{10,... | collective-permute-start | bytes 221192 | tf_op jit(solution)/shard_map/ppermute | solution.py:485
  96.1 1.3 collective-permute-done.7
  97.4 0.7 collective-permute-done.8
  98.1 1.5 %collective-permute-done.9 = bf16[72,512]{1,0:T(8,128)(2,1)S(1)} collective-permute-done((bf16[72,512]{1,0:T(8,128)(2,1)S(1)}, bf16[72,512]{1,0:T(8,128)(2,1)S(1)}, u32[]{:S(2)}, u32[]{:S(2)}) %collective-permute-start.9) | collective-permute-done | bytes 73760 | tf_op jit(solution)/shard_map/ppermute | solution.py:485
  99.6 3.6 %collective-permute-start.10 = (f32[72,512]{1,0:T(8,128)S(1)}, f32[72,512]{1,0:T(8,128)S(1)}, u32[]{:S(2)}, u32[]{:S(2)}) collective-permute-start(f32[72,512]{1,0:T(8,128)S(1)} %convert_add_fusion.2), channel_id=1, source_target_pairs={{0,4},{1,5},{2,6},{3,7},{4,0},{5,1},{6,2},{7,3},{8,12},{9,13},{10,... | collective-permute-start | bytes 442376 | tf_op jit(solution)/shard_map/ppermute | solution.py:485
  103.2 2.7 %collective-permute-start.12 = (f32[72,512]{1,0:T(8,128)S(1)}, f32[72,512]{1,0:T(8,128)S(1)}, u32[]{:S(2)}, u32[]{:S(2)}) collective-permute-start(f32[72,512]{1,0:T(8,128)S(1)} %convert_add_fusion.2), channel_id=1, source_target_pairs={{0,68},{1,69},{2,70},{3,71},{4,64},{5,65},{6,66},{7,67},{8,76},{9,... | collective-permute-start | bytes 442376 | tf_op jit(solution)/shard_map/ppermute | solution.py:485
  105.9 4.9 %collective-permute-start.16 = (bf16[4,12,24,128]{3,2,1,0:T(8,128)(2,1)S(1)}, bf16[4,12,24,128]{3,2,1,0:T(8,128)(2,1)S(1)}, u32[]{:S(2)}, u32[]{:S(2)}) collective-permute-start(bf16[4,12,24,128]{3,2,1,0:T(8,128)(2,1)S(1)} %copy-done.5), channel_id=1, source_target_pairs={{0,8},{8,16},{16,24},{24,32},{32,40},{40,48},{48,56},{56,64},{64,7... | collective-permute-start | bytes 884744 | tf_op jit(solution)/shard_map/ppermute | solution.py:455
  110.8 0.5 collective-permute-start.18
  111.4 0.2 collective-permute-start.13
  111.6 4.3 %collective-permute-start.14 = (bf16[72,512]{1,0:T(8,128)(2,1)S(1)}, bf16[72,512]{1,0:T(8,128)(2,1)S(1)}, u32[]{:S(2)}, u32[]{:S(2)}) collective-permute-start(bf16[72,512]{1,0:T(8,128)(2,1)S(1)} %add_convert_fusion), channel_id=1, source_target_pairs={{0,2},{1,3},{2,0},{3,1},{4,6},{5,7},{6,4},{7,5},{8,40},{9,41},{10,... | collective-permute-start | bytes 221192 | tf_op jit(solution)/shard_map/ppermute | solution.py:485
  115.8 11.3 %collective-permute-done.18 = bf16[4,4,24,128]{3,2,1,0:T(8,128)(2,1)S(1)} collective-permute-done((bf16[4,4,24,128]{3,2,1,0:T(8,128)(2,1)S(1)}, bf16[4,4,24,128]{3,2,1,0:T(8,128)(2,1)S(1)}, u32[]{:S(2)}, u32[]{:S(2)}) %collective-permute-start.18) | collective-permute-done | bytes 98336 | tf_op jit(solution)/shard_map/ppermute | solution.py:459
  127.1 4.3 %inner_finish.1 = bf16[16,16,24,128]{3,2,1,0:T(8,128)(2,1)} custom-call(bf16[16,16,24,128]{3,2,1,0:T(8,128)(2,1)} %refs_0_.7, bf16[16,16,24,128]{3,2,1,0:T(8,128)(2,1)} %refs_1_.7, f32[1,128]{1,0:T(1,128)} %bitcast.18, bf16[128,384]{1,0:T(8,128)(2,1)} %w_ref.1, bf16[1,3,384,512]{3,2,1,0:T(8,128)(2,1)} %get-tuple-element.62.refs_4_, ...), custom_call_target="tpu_custom_call", output_to_operand_aliasing={{}: (5, {})} | custom-call | flops 1000000000 | bytes 3000000 | tf_op jit(solution)/shard_map/inner_finish/pallas_call | solution.py:371
  131.6 0.1 collective-permute-start.19
  131.7 0.1 collective-permute-start.20
  131.8 2.6 %collective-permute-start.21 = (bf16[288,512]{1,0:T(8,128)(2,1)S(1)}, bf16[288,512]{1,0:T(8,128)(2,1)S(1)}, u32[]{:S(2)}, u32[]{:S(2)}) collective-permute-start(bf16[288,512]{1,0:T(8,128)(2,1)S(1)} %constant_dynamic-update-slice_fusion.7), channel_id=1, source_target_pairs={{0,48},{1,49},{2,50},{3,51},{4,52},{5,53},{6,54},{7,55},{8,11},{9,... | collective-permute-start | bytes 884744 | tf_op jit(solution)/shard_map/ppermute | solution.py:485
  134.3 0.8 constant_dynamic-update-slice_fusion.6
  135.1 0.8 constant_dynamic-update-slice_fusion.5
  135.9 0.7 constant_dynamic-update-slice_fusion.4
  136.5 5.1 %collective-permute-done.19 = bf16[288,512]{1,0:T(8,128)(2,1)S(1)} collective-permute-done((bf16[288,512]{1,0:T(8,128)(2,1)S(1)}, bf16[288,512]{1,0:T(8,128)(2,1)S(1)}, u32[]{:S(2)}, u32[]{:S(2)}) %collective-permute-start.19) | collective-permute-done | bytes 294944 | tf_op jit(solution)/shard_map/ppermute | solution.py:485
  141.6 0.6 collective-permute-done.21
  142.2 0.1 broadcast_in_dim.7
  142.5 0.4 collective-permute-start.22
  142.8 1.4 spread_own.1._
  144.2 1.1 collective-permute-done.22.got_ref.got_rest_ref
  145.4 1.6 %spread_got.1 = (f32[4,512,512]{2,1,0:T(8,128)}, f32[128,128]{1,0:T(8,128)}, f32[128,384]{1,0:T(8,128)}, f32[1,128]{1,0:T(1,128)}) custom-call(s32[1]{0:T(128)} %bitcast.7.mine_ref, bf16[1152,512]{1,0:T(8,128)(2,1)S(1)} %collective-permute-done.22.got_ref.got_rest_ref, ...), custom_call_target="tpu_custom_call", output_to_operand_aliasing={{0}: (6, {})} | custom-call | tf_op jit(solution)/shard_map/spread_got/pallas_call | solution.py:427
  (46 shorter events, 0.5 us)
Async XLA Ops:
  1.8 29.9 %collective-permute-start.1 = (bf16[2,12,4,24,128]{4,3,2,1,0:T(8,128)(2,1)S(1)}, bf16[2,12,4,24,128]{4,3,2,1,0:T(8,128)(2,1)S(1)}, u32[]{:S(2)}, u32[]{:S(2)}) collective-permute-start(bf16[2,12,4,24,128]{4,3,2,1,0:T(8,128)(2,1)S(1)} %pad_maximum_fusion.1), channel_id=1, source_target_pairs={{0,7},{1,0},{2,1},{3,2},{4,3},{5,4},{6,5},{7,6},{8,15},{9,8},{10,9... | collective-permute-start | bytes 1769480 | tf_op jit(solution)/shard_map/ppermute | solution.py:457
  10.3 21.5 %collective-permute-start = (bf16[2,4,12,24,128]{4,3,2,1,0:T(8,128)(2,1)S(1)}, bf16[2,4,12,24,128]{4,3,2,1,0:T(8,128)(2,1)S(1)}, u32[]{:S(2)}, u32[]{:S(2)}) collective-permute-start(bf16[2,4,12,24,128]{4,3,2,1,0:T(8,128)(2,1)S(1)} %pad_maximum_fusion), channel_id=1, source_target_pairs={{0,120},{8,0},{16,8},{24,16},{32,24},{40,32},{48,40},{56,48},{64,5... | collective-permute-start | bytes 1769480 | tf_op jit(solution)/shard_map/ppermute | solution.py:455
  12.3 19.4 %collective-permute-start.2 = (bf16[2,4,4,24,128]{4,3,2,1,0:T(8,128)(2,1)S(1)}, bf16[2,4,4,24,128]{4,3,2,1,0:T(8,128)(2,1)S(1)}, u32[]{:S(2)}, u32[]{:S(2)}) collective-permute-start(bf16[2,4,4,24,128]{4,3,2,1,0:T(8,128)(2,1)S(1)} %pad_maximum_fusion.2), channel_id=1, source_target_pairs={{0,127},{1,120},{2,121},{3,122},{4,123},{5,124},{6,125},{7,126},{8... | collective-permute-start | bytes 589832 | tf_op jit(solution)/shard_map/ppermute | solution.py:459
  31.8 0.7 copy-start.6
  31.8 0.9 copy-start.2
  31.8 1.0 copy-start.3
  76.6 3.1 %collective-permute-start.3 = (bf16[1152,512]{1,0:T(8,128)(2,1)}, bf16[1152,512]{1,0:T(8,128)(2,1)S(1)}, u32[]{:S(2)}, u32[]{:S(2)}) collective-permute-start(bf16[1152,512]{1,0:T(8,128)(2,1)} %get-tuple-element.48), channel_id=1, source_target_pairs={{0,8},{1,9},{2,10},{3,11},{4,12},{5,13},{6,14},{7,15},{8,0},{9,1},... | collective-permute-start | bytes 3538952 | tf_op jit(solution)/shard_map/ppermute | solution.py:485
  81.5 10.7 %collective-permute-start.4 = (bf16[288,512]{1,0:T(8,128)(2,1)S(1)}, bf16[288,512]{1,0:T(8,128)(2,1)S(1)}, u32[]{:S(2)}, u32[]{:S(2)}) collective-permute-start(bf16[288,512]{1,0:T(8,128)(2,1)S(1)} %get-tuple-element.85), channel_id=1, source_target_pairs={{0,32},{1,33},{2,34},{3,35},{4,36},{5,37},{6,38},{7,39},{8,10},{9,... | collective-permute-start | bytes 884744 | tf_op jit(solution)/shard_map/ppermute | solution.py:485
  81.6 10.6 %collective-permute-start.5 = (bf16[288,512]{1,0:T(8,128)(2,1)S(1)}, bf16[288,512]{1,0:T(8,128)(2,1)S(1)}, u32[]{:S(2)}, u32[]{:S(2)}) collective-permute-start(bf16[288,512]{1,0:T(8,128)(2,1)S(1)} %get-tuple-element.84), channel_id=1, source_target_pairs={{0,16},{1,17},{2,18},{3,19},{4,20},{5,21},{6,22},{7,23},{8,9},{9,1... | collective-permute-start | bytes 884744 | tf_op jit(solution)/shard_map/ppermute | solution.py:485
  82.8 9.4 %collective-permute-start.6 = (bf16[288,512]{1,0:T(8,128)(2,1)S(1)}, bf16[288,512]{1,0:T(8,128)(2,1)S(1)}, u32[]{:S(2)}, u32[]{:S(2)}) collective-permute-start(bf16[288,512]{1,0:T(8,128)(2,1)S(1)} %get-tuple-element.83), channel_id=1, source_target_pairs={{0,48},{1,49},{2,50},{3,51},{4,52},{5,53},{6,54},{7,55},{8,11},{9,... | collective-permute-start | bytes 884744 | tf_op jit(solution)/shard_map/ppermute | solution.py:485
  92.3 13.6 %copy-start.5 = (bf16[4,12,24,128]{3,2,1,0:T(8,128)(2,1)S(1)}, bf16[4,12,24,128]{3,2,1,0:T(8,128)(2,1)}, u32[]{:S(2)}) copy-start(bf16[4,12,24,128]{3,2,1,0:T(8,128)(2,1)} %get-tuple-element.57) | copy-start | bytes 884740
  92.3 18.5 %copy-start.4 = (bf16[12,4,24,128]{3,2,1,0:T(8,128)(2,1)S(1)}, bf16[12,4,24,128]{3,2,1,0:T(8,128)(2,1)}, u32[]{:S(2)}) copy-start(bf16[12,4,24,128]{3,2,1,0:T(8,128)(2,1)} %get-tuple-element.58) | copy-start | bytes 884740
  92.3 18.5 %copy-start.7 = (bf16[4,4,24,128]{3,2,1,0:T(8,128)(2,1)S(1)}, bf16[4,4,24,128]{3,2,1,0:T(8,128)(2,1)}, u32[]{:S(2)}) copy-start(bf16[4,4,24,128]{3,2,1,0:T(8,128)(2,1)} %get-tuple-element.59) | copy-start | bytes 294916
  92.5 4.9 %collective-permute-start.7 = (bf16[72,512]{1,0:T(8,128)(2,1)S(1)}, bf16[72,512]{1,0:T(8,128)(2,1)S(1)}, u32[]{:S(2)}, u32[]{:S(2)}) collective-permute-start(bf16[72,512]{1,0:T(8,128)(2,1)S(1)} %get-tuple-element.86), channel_id=1, source_target_pairs={{0,2},{1,3},{2,0},{3,1},{4,6},{5,7},{6,4},{7,5},{8,40},{9,41},{10,... | collective-permute-start | bytes 221192 | tf_op jit(solution)/shard_map/ppermute | solution.py:485
  93.0 5.1 %collective-permute-start.8 = (bf16[72,512]{1,0:T(8,128)(2,1)S(1)}, bf16[72,512]{1,0:T(8,128)(2,1)S(1)}, u32[]{:S(2)}, u32[]{:S(2)}) collective-permute-start(bf16[72,512]{1,0:T(8,128)(2,1)S(1)} %get-tuple-element.88), channel_id=1, source_target_pairs={{0,1},{1,2},{2,3},{3,0},{4,5},{5,6},{6,7},{7,4},{8,24},{9,25},{10,... | collective-permute-start | bytes 221192 | tf_op jit(solution)/shard_map/ppermute | solution.py:485
  96.1 3.5 %collective-permute-start.9 = (bf16[72,512]{1,0:T(8,128)(2,1)S(1)}, bf16[72,512]{1,0:T(8,128)(2,1)S(1)}, u32[]{:S(2)}, u32[]{:S(2)}) collective-permute-start(bf16[72,512]{1,0:T(8,128)(2,1)S(1)} %get-tuple-element.87), channel_id=1, source_target_pairs={{0,3},{1,0},{2,1},{3,2},{4,7},{5,4},{6,5},{7,6},{8,56},{9,57},{10,... | collective-permute-start | bytes 221192 | tf_op jit(solution)/shard_map/ppermute | solution.py:485
  99.6 11.2 %collective-permute-start.10 = (f32[72,512]{1,0:T(8,128)S(1)}, f32[72,512]{1,0:T(8,128)S(1)}, u32[]{:S(2)}, u32[]{:S(2)}) collective-permute-start(f32[72,512]{1,0:T(8,128)S(1)} %convert_add_fusion.2), channel_id=1, source_target_pairs={{0,4},{1,5},{2,6},{3,7},{4,0},{5,1},{6,2},{7,3},{8,12},{9,13},{10,... | collective-permute-start | bytes 442376 | tf_op jit(solution)/shard_map/ppermute | solution.py:485
  103.2 8.1 %collective-permute-start.11 = (f32[72,512]{1,0:T(8,128)S(1)}, f32[72,512]{1,0:T(8,128)S(1)}, u32[]{:S(2)}, u32[]{:S(2)}) collective-permute-start(f32[72,512]{1,0:T(8,128)S(1)} %convert_add_fusion.2), channel_id=1, source_target_pairs={{0,64},{1,65},{2,66},{3,67},{4,68},{5,69},{6,70},{7,71},{8,72},{9,... | collective-permute-start | bytes 442376 | tf_op jit(solution)/shard_map/ppermute | solution.py:485
  103.2 8.1 %collective-permute-start.12 = (f32[72,512]{1,0:T(8,128)S(1)}, f32[72,512]{1,0:T(8,128)S(1)}, u32[]{:S(2)}, u32[]{:S(2)}) collective-permute-start(f32[72,512]{1,0:T(8,128)S(1)} %convert_add_fusion.2), channel_id=1, source_target_pairs={{0,68},{1,69},{2,70},{3,71},{4,64},{5,65},{6,66},{7,67},{8,76},{9,... | collective-permute-start | bytes 442376 | tf_op jit(solution)/shard_map/ppermute | solution.py:485
  105.9 25.6 %collective-permute-start.16 = (bf16[4,12,24,128]{3,2,1,0:T(8,128)(2,1)S(1)}, bf16[4,12,24,128]{3,2,1,0:T(8,128)(2,1)S(1)}, u32[]{:S(2)}, u32[]{:S(2)}) collective-permute-start(bf16[4,12,24,128]{3,2,1,0:T(8,128)(2,1)S(1)} %copy-done.5), channel_id=1, source_target_pairs={{0,8},{8,16},{16,24},{24,32},{32,40},{40,48},{48,56},{56,64},{64,7... | collective-permute-start | bytes 884744 | tf_op jit(solution)/shard_map/ppermute | solution.py:455
  110.8 20.7 %collective-permute-start.17 = (bf16[12,4,24,128]{3,2,1,0:T(8,128)(2,1)S(1)}, bf16[12,4,24,128]{3,2,1,0:T(8,128)(2,1)S(1)}, u32[]{:S(2)}, u32[]{:S(2)}) collective-permute-start(bf16[12,4,24,128]{3,2,1,0:T(8,128)(2,1)S(1)} %copy-done.4), channel_id=1, source_target_pairs={{0,1},{1,2},{2,3},{3,4},{4,5},{5,6},{6,7},{7,0},{8,9},{9,10},{10,1... | collective-permute-start | bytes 884744 | tf_op jit(solution)/shard_map/ppermute | solution.py:457
  110.8 16.3 %collective-permute-start.18 = (bf16[4,4,24,128]{3,2,1,0:T(8,128)(2,1)S(1)}, bf16[4,4,24,128]{3,2,1,0:T(8,128)(2,1)S(1)}, u32[]{:S(2)}, u32[]{:S(2)}) collective-permute-start(bf16[4,4,24,128]{3,2,1,0:T(8,128)(2,1)S(1)} %copy-done.7), channel_id=1, source_target_pairs={{0,9},{1,10},{2,11},{3,12},{4,13},{5,14},{6,15},{7,8},{8,17},{9,18... | collective-permute-start | bytes 294920 | tf_op jit(solution)/shard_map/ppermute | solution.py:459
  111.4 20.1 %collective-permute-start.13 = (bf16[72,512]{1,0:T(8,128)(2,1)S(1)}, bf16[72,512]{1,0:T(8,128)(2,1)S(1)}, u32[]{:S(2)}, u32[]{:S(2)}) collective-permute-start(bf16[72,512]{1,0:T(8,128)(2,1)S(1)} %add_convert_fusion), channel_id=1, source_target_pairs={{0,1},{1,2},{2,3},{3,0},{4,5},{5,6},{6,7},{7,4},{8,24},{9,25},{10,... | collective-permute-start | bytes 221192 | tf_op jit(solution)/shard_map/ppermute | solution.py:485
  111.6 19.9 %collective-permute-start.14 = (bf16[72,512]{1,0:T(8,128)(2,1)S(1)}, bf16[72,512]{1,0:T(8,128)(2,1)S(1)}, u32[]{:S(2)}, u32[]{:S(2)}) collective-permute-start(bf16[72,512]{1,0:T(8,128)(2,1)S(1)} %add_convert_fusion), channel_id=1, source_target_pairs={{0,2},{1,3},{2,0},{3,1},{4,6},{5,7},{6,4},{7,5},{8,40},{9,41},{10,... | collective-permute-start | bytes 221192 | tf_op jit(solution)/shard_map/ppermute | solution.py:485
  127.1 4.3 %collective-permute-start.15 = (bf16[72,512]{1,0:T(8,128)(2,1)S(1)}, bf16[72,512]{1,0:T(8,128)(2,1)S(1)}, u32[]{:S(2)}, u32[]{:S(2)}) collective-permute-start(bf16[72,512]{1,0:T(8,128)(2,1)S(1)} %add_convert_fusion), channel_id=1, source_target_pairs={{0,3},{1,0},{2,1},{3,2},{4,7},{5,4},{6,5},{7,6},{8,56},{9,57},{10,... | collective-permute-start | bytes 221192 | tf_op jit(solution)/shard_map/ppermute | solution.py:485
  131.6 10.0 %collective-permute-start.19 = (bf16[288,512]{1,0:T(8,128)(2,1)S(1)}, bf16[288,512]{1,0:T(8,128)(2,1)S(1)}, u32[]{:S(2)}, u32[]{:S(2)}) collective-permute-start(bf16[288,512]{1,0:T(8,128)(2,1)S(1)} %constant_dynamic-update-slice_fusion.7), channel_id=1, source_target_pairs={{0,16},{1,17},{2,18},{3,19},{4,20},{5,21},{6,22},{7,23},{8,9},{9,1... | collective-permute-start | bytes 884744 | tf_op jit(solution)/shard_map/ppermute | solution.py:485
  131.7 9.9 %collective-permute-start.20 = (bf16[288,512]{1,0:T(8,128)(2,1)S(1)}, bf16[288,512]{1,0:T(8,128)(2,1)S(1)}, u32[]{:S(2)}, u32[]{:S(2)}) collective-permute-start(bf16[288,512]{1,0:T(8,128)(2,1)S(1)} %constant_dynamic-update-slice_fusion.7), channel_id=1, source_target_pairs={{0,32},{1,33},{2,34},{3,35},{4,36},{5,37},{6,38},{7,39},{8,10},{9,... | collective-permute-start | bytes 884744 | tf_op jit(solution)/shard_map/ppermute | solution.py:485
  131.8 10.5 %collective-permute-start.21 = (bf16[288,512]{1,0:T(8,128)(2,1)S(1)}, bf16[288,512]{1,0:T(8,128)(2,1)S(1)}, u32[]{:S(2)}, u32[]{:S(2)}) collective-permute-start(bf16[288,512]{1,0:T(8,128)(2,1)S(1)} %constant_dynamic-update-slice_fusion.7), channel_id=1, source_target_pairs={{0,48},{1,49},{2,50},{3,51},{4,52},{5,53},{6,54},{7,55},{8,11},{9,... | collective-permute-start | bytes 884744 | tf_op jit(solution)/shard_map/ppermute | solution.py:485
  142.5 2.9 %collective-permute-start.22 = (bf16[1152,512]{1,0:T(8,128)(2,1)S(1)}, bf16[1152,512]{1,0:T(8,128)(2,1)S(1)}, u32[]{:S(2)}, u32[]{:S(2)}) collective-permute-start(bf16[1152,512]{1,0:T(8,128)(2,1)S(1)} %constant_dynamic-update-slice_fusion.own_ref.own_rest_ref), channel_id=1, source_target_pairs={{0,8},{1,9},{2,10},{3,11},{4,12},{5,13},{6,14},{7,15},{8,0},{9,1},... | collective-permute-start | bytes 3538952 | tf_op jit(solution)/shard_map/ppermute | solution.py:485
  142.8 2.5 %copy-start = (bf16[128,384]{1,0:T(8,128)(2,1)S(1)}, bf16[128,384]{1,0:T(8,128)(2,1)}, u32[]{:S(2)}) copy-start(bf16[128,384]{1,0:T(8,128)(2,1)} %w_ref.1) | copy-start | bytes 294916
  142.8 2.5 %copy-start.1 = (f32[128]{0:T(128)S(1)}, f32[128]{0:T(128)}, u32[]{:S(2)}) copy-start(f32[128]{0:T(128)} %param.8) | copy-start | bytes 1540

commit v9 on v7

--- a/solution.py
+++ b/solution.py
@@ -231,7 +231,7 @@
 
         for turn in range(HEADS + 3):
             for c in range(chunks):
-                for lag, stage in ((3, qkv_grads), (2, score_grads), (1, weights), (0, scores)):
+                for lag, stage in ((0, scores), (3, qkv_grads), (2, score_grads), (1, weights)):
                     if 0 <= turn - lag < HEADS:
                         stage(turn - lag, c)
         small_ref[:C] += dot(attT_s[...], adj)

time: 146 us -> 146 us (level)
  no operation moved by 1% of the time
where the time goes in v9:
time: 146 us; the launch traced here: 145 us
  Pallas kernels  74.1 us (51%)
  starting transfers between devices  37.4 us (26%)
  waiting for transfers between devices  23.8 us (16%)
  local copies, waits for them, and re-layouts  6.92 us (5%)
  other arithmetic  1.98 us (1%)
    pallas_call x2, Pallas kernels, sublayer(): pl.pallas_call(functools.partial(kernel, first), grid=(blocks,), in_specs...  59.7 us
    ppermute x17, starting transfers between devices, send(): return lax.ppermute(values, ('gx', 'gy'), pairs)  21 us
    ppermute x17, waiting for transfers between devices, send(): return lax.ppermute(values, ('gx', 'gy'), pairs)  12.3 us
    ppermute x2, waiting for transfers between devices, shifted(): return lax.ppermute(values, ('gx', 'gy'), pairs)  11.5 us
    pallas_call x2, Pallas kernels, finish(): pl.pallas_call(functools.partial(finish_kernel, first), grid=(blocks,), i...  11.4 us
    ppermute x2, starting transfers between devices, shifted(): return lax.ppermute(values, 'gy', [(i, (i + by_y) % ny) for i in range(ny)])  7.29 us
    ppermute x2, starting transfers between devices, shifted(): return lax.ppermute(values, 'gx', [(i, (i + by_x) % nx) for i in range(nx)])  5.95 us
    ppermute x2, starting transfers between devices, shifted(): return lax.ppermute(values, ('gx', 'gy'), pairs)  3.23 us
  transfers between devices with their start and end apart: 23, of which 9 were waited for; matrix products, arithmetic and copies ran while one was open for 3% of the time, Pallas kernels for 20%

profile of v9, /device:TPU:1, one launch (start us, length us, event | category | flops | bytes accessed | tf_op | source)
XLA Modules:
  0.0 145.4 jit_solution(11125349628206622235)
XLA Ops:
  0.6 1.1 slice_bitcast_fusion
  1.8 0.1 pad_maximum_fusion.1
  1.8 7.3 %collective-permute-start.1 = (bf16[2,12,4,24,128]{4,3,2,1,0:T(8,128)(2,1)S(1)}, bf16[2,12,4,24,128]{4,3,2,1,0:T(8,128)(2,1)S(1)}, u32[]{:S(2)}, u32[]{:S(2)}) collective-permute-start(bf16[2,12,4,24,128]{4,3,2,1,0:T(8,128)(2,1)S(1)} %pad_maximum_fusion.1), channel_id=1, source_target_pairs={{0,7},{1,0},{2,1},{3,2},{4,3},{5,4},{6,5},{7,6},{8,15},{9,8},{10,9... | collective-permute-start | bytes 1769480 | tf_op jit(solution)/shard_map/ppermute | solution.py:457
  9.1 1.1 slice_bitcast_fusion.2
  10.3 1.0 collective-permute-start
  11.3 1.0 slice_bitcast_fusion.4
  12.3 2.7 %collective-permute-start.2 = (bf16[2,4,4,24,128]{4,3,2,1,0:T(8,128)(2,1)S(1)}, bf16[2,4,4,24,128]{4,3,2,1,0:T(8,128)(2,1)S(1)}, u32[]{:S(2)}, u32[]{:S(2)}) collective-permute-start(bf16[2,4,4,24,128]{4,3,2,1,0:T(8,128)(2,1)S(1)} %pad_maximum_fusion.2), channel_id=1, source_target_pairs={{0,127},{1,120},{2,121},{3,122},{4,123},{5,124},{6,125},{7,126},{8... | collective-permute-start | bytes 589832 | tf_op jit(solution)/shard_map/ppermute | solution.py:459
  15.0 16.5 %inner_windows.1 = (bf16[1,3,384,512]{3,2,1,0:T(8,128)(2,1)}, f32[512,128]{1,0:T(8,128)}, f32[4,512,512]{2,1,0:T(8,128)}, f32[4,512,512]{2,1,0:T(8,128)}) custom-call(bf16[16,16,24,128]{3,2,1,0:T(8,128)(2,1)} %refs_0_.7, bf16[16,16,24,128]{3,2,1,0:T(8,128)(2,1)} %refs_1_.7, f32[1,128]{1,0:T(1,128)} %bitcast.15, bf16[128,384]{1,0:T(8,128)(2,1)} %w_ref.1, ...), custom_call_target="tpu_custom_call" | custom-call | flops 12000000000 | bytes 10000000 | tf_op jit(solution)/shard_map/inner_windows/pallas_call | solution.py:354
  31.6 0.6 copy-done.5
  32.3 0.2 copy-done.2
  32.5 0.2 copy-done.3
  32.7 43.1 %rim_windows.1 = (bf16[3,3,384,512]{3,2,1,0:T(8,128)(2,1)}, bf16[1152,512]{1,0:T(8,128)(2,1)}, bf16[1152,512]{1,0:T(8,128)(2,1)}) custom-call(bf16[16,16,24,128]{3,2,1,0:T(8,128)(2,1)} %refs_0_.7, bf16[16,16,24,128]{3,2,1,0:T(8,128)(2,1)} %refs_1_.7, bf16[2,4,12,24,128]{4,3,2,1,0:T(8,128)(2,1)} %copy-done.3, bf16[2,12,4,24,128]{4,3,2,1,0:T(8,128)(2,1)} %copy-done.2, ...), custom_call_target="tpu_custom_call" | custom-call | flops 35999997952 | bytes 30000000 | tf_op jit(solution)/shard_map/rim_windows/pallas_call | solution.py:354
  75.8 0.1 collective-permute-start.3
  76.1 2.9 %collective-permute-done.3 = bf16[1152,512]{1,0:T(8,128)(2,1)S(1)} collective-permute-done((bf16[1152,512]{1,0:T(8,128)(2,1)}, bf16[1152,512]{1,0:T(8,128)(2,1)S(1)}, u32[]{:S(2)}, u32[]{:S(2)}) %collective-permute-start.3) | collective-permute-done | bytes 1179680 | tf_op jit(solution)/shard_map/ppermute | solution.py:485
  78.9 1.6 %convert_add_fusion = f32[1152,512]{1,0:T(8,128)S(1)} fusion(bf16[1152,512]{1,0:T(8,128)(2,1)S(1)} %collective-permute-done.3, bf16[1152,512]{1,0:T(8,128)(2,1)} %get-tuple-element.46), kind=kLoop, calls=%fused_computation | loop fusion | flops 1769472 | bytes 4718592 | tf_op jit(solution)/shard_map/add | solution.py:532
  80.6 0.1 dynamic-slice_convert_fusion
  80.7 0.1 collective-permute-start.4
  80.8 1.2 collective-permute-start.5
  82.0 2.3 %collective-permute-start.6 = (bf16[288,512]{1,0:T(8,128)(2,1)S(1)}, bf16[288,512]{1,0:T(8,128)(2,1)S(1)}, u32[]{:S(2)}, u32[]{:S(2)}) collective-permute-start(bf16[288,512]{1,0:T(8,128)(2,1)S(1)} %get-tuple-element.81), channel_id=1, source_target_pairs={{0,48},{1,49},{2,50},{3,51},{4,52},{5,53},{6,54},{7,55},{8,11},{9,... | collective-permute-start | bytes 884744 | tf_op jit(solution)/shard_map/ppermute | solution.py:485
  84.3 7.0 %rim_finish.1 = (bf16[16,16,24,128]{3,2,1,0:T(8,128)(2,1)}, bf16[4,12,24,128]{3,2,1,0:T(8,128)(2,1)}, bf16[12,4,24,128]{3,2,1,0:T(8,128)(2,1)}, bf16[4,4,24,128]{3,2,1,0:T(8,128)(2,1)}) custom-call(bf16[16,16,24,128]{3,2,1,0:T(8,128)(2,1)} %refs_0_.7, bf16[16,16,24,128]{3,2,1,0:T(8,128)(2,1)} %refs_1_.7, bf16[2,4,12,24,128]{4,3,2,1,0:T(8,128)(2,1)} %copy-done.3, ...), custom_call_target="tpu_custom_call" | custom-call | flops 3000000000 | bytes 9000000 | tf_op jit(solution)/shard_map/rim_finish/pallas_call | solution.py:371
  91.5 0.1 convert_add_fusion.1
  91.7 0.5 collective-permute-start.7
  92.2 3.2 %collective-permute-start.8 = (bf16[72,512]{1,0:T(8,128)(2,1)S(1)}, bf16[72,512]{1,0:T(8,128)(2,1)S(1)}, u32[]{:S(2)}, u32[]{:S(2)}) collective-permute-start(bf16[72,512]{1,0:T(8,128)(2,1)S(1)} %get-tuple-element.86), channel_id=1, source_target_pairs={{0,1},{1,2},{2,3},{3,0},{4,5},{5,6},{6,7},{7,4},{8,24},{9,25},{10,... | collective-permute-start | bytes 221192 | tf_op jit(solution)/shard_map/ppermute | solution.py:485
  95.4 1.1 collective-permute-done.7
  96.5 0.7 collective-permute-done.8
  97.2 1.7 %collective-permute-done.9 = bf16[72,512]{1,0:T(8,128)(2,1)S(1)} collective-permute-done((bf16[72,512]{1,0:T(8,128)(2,1)S(1)}, bf16[72,512]{1,0:T(8,128)(2,1)S(1)}, u32[]{:S(2)}, u32[]{:S(2)}) %collective-permute-start.9) | collective-permute-done | bytes 73760 | tf_op jit(solution)/shard_map/ppermute | solution.py:485
  98.9 3.6 %collective-permute-start.10 = (f32[72,512]{1,0:T(8,128)S(1)}, f32[72,512]{1,0:T(8,128)S(1)}, u32[]{:S(2)}, u32[]{:S(2)}) collective-permute-start(f32[72,512]{1,0:T(8,128)S(1)} %convert_add_fusion.2), channel_id=1, source_target_pairs={{0,4},{1,5},{2,6},{3,7},{4,0},{5,1},{6,2},{7,3},{8,12},{9,13},{10,... | collective-permute-start | bytes 442376 | tf_op jit(solution)/shard_map/ppermute | solution.py:485
  102.5 2.7 %collective-permute-start.12 = (f32[72,512]{1,0:T(8,128)S(1)}, f32[72,512]{1,0:T(8,128)S(1)}, u32[]{:S(2)}, u32[]{:S(2)}) collective-permute-start(f32[72,512]{1,0:T(8,128)S(1)} %convert_add_fusion.2), channel_id=1, source_target_pairs={{0,68},{1,69},{2,70},{3,71},{4,64},{5,65},{6,66},{7,67},{8,76},{9,... | collective-permute-start | bytes 442376 | tf_op jit(solution)/shard_map/ppermute | solution.py:485
  105.2 4.9 %collective-permute-start.16 = (bf16[4,12,24,128]{3,2,1,0:T(8,128)(2,1)}, bf16[4,12,24,128]{3,2,1,0:T(8,128)(2,1)S(1)}, u32[]{:S(2)}, u32[]{:S(2)}) collective-permute-start(bf16[4,12,24,128]{3,2,1,0:T(8,128)(2,1)} %get-tuple-element.56), channel_id=1, source_target_pairs={{0,8},{8,16},{16,24},{24,32},{32,40},{40,48},{48,56},{56,64},{64,7... | collective-permute-start | bytes 884744 | tf_op jit(solution)/shard_map/ppermute | solution.py:455
  110.1 0.5 collective-permute-start.18
  110.7 0.2 collective-permute-start.13
  110.9 4.3 %collective-permute-start.14 = (bf16[72,512]{1,0:T(8,128)(2,1)S(1)}, bf16[72,512]{1,0:T(8,128)(2,1)S(1)}, u32[]{:S(2)}, u32[]{:S(2)}) collective-permute-start(bf16[72,512]{1,0:T(8,128)(2,1)S(1)} %add_convert_fusion), channel_id=1, source_target_pairs={{0,2},{1,3},{2,0},{3,1},{4,6},{5,7},{6,4},{7,5},{8,40},{9,41},{10,... | collective-permute-start | bytes 221192 | tf_op jit(solution)/shard_map/ppermute | solution.py:485
  115.2 11.5 %collective-permute-done.18 = bf16[4,4,24,128]{3,2,1,0:T(8,128)(2,1)S(1)} collective-permute-done((bf16[4,4,24,128]{3,2,1,0:T(8,128)(2,1)S(1)}, bf16[4,4,24,128]{3,2,1,0:T(8,128)(2,1)S(1)}, u32[]{:S(2)}, u32[]{:S(2)}) %collective-permute-start.18) | collective-permute-done | bytes 98336 | tf_op jit(solution)/shard_map/ppermute | solution.py:459
  126.6 3.2 %collective-permute-done.15 = bf16[72,512]{1,0:T(8,128)(2,1)S(1)} collective-permute-done((bf16[72,512]{1,0:T(8,128)(2,1)S(1)}, bf16[72,512]{1,0:T(8,128)(2,1)S(1)}, u32[]{:S(2)}, u32[]{:S(2)}) %collective-permute-start.15) | collective-permute-done | bytes 73760 | tf_op jit(solution)/shard_map/ppermute | solution.py:485
  130.0 0.1 collective-permute-start.19
  130.0 0.1 collective-permute-start.20
  130.1 2.6 %collective-permute-start.21 = (bf16[288,512]{1,0:T(8,128)(2,1)S(1)}, bf16[288,512]{1,0:T(8,128)(2,1)S(1)}, u32[]{:S(2)}, u32[]{:S(2)}) collective-permute-start(bf16[288,512]{1,0:T(8,128)(2,1)S(1)} %constant_dynamic-update-slice_fusion.7), channel_id=1, source_target_pairs={{0,48},{1,49},{2,50},{3,51},{4,52},{5,53},{6,54},{7,55},{8,11},{9,... | collective-permute-start | bytes 884744 | tf_op jit(solution)/shard_map/ppermute | solution.py:485
  132.7 4.3 %inner_finish.1 = bf16[16,16,24,128]{3,2,1,0:T(8,128)(2,1)} custom-call(bf16[16,16,24,128]{3,2,1,0:T(8,128)(2,1)} %refs_0_.7, bf16[16,16,24,128]{3,2,1,0:T(8,128)(2,1)} %refs_1_.7, f32[1,128]{1,0:T(1,128)} %bitcast.18, bf16[128,384]{1,0:T(8,128)(2,1)} %w_ref.1, bf16[1,3,384,512]{3,2,1,0:T(8,128)(2,1)} %get-tuple-element.65.refs_4_, ...), custom_call_target="tpu_custom_call", output_to_operand_aliasing={{}: (5, {})} | custom-call | flops 1000000000 | bytes 3000000 | tf_op jit(solution)/shard_map/inner_finish/pallas_call | solution.py:371
  137.0 0.8 constant_dynamic-update-slice_fusion.6
  137.8 0.8 constant_dynamic-update-slice_fusion.5
  138.6 0.7 constant_dynamic-update-slice_fusion.4
  139.2 0.7 collective-permute-done.19
  140.0 0.6 collective-permute-done.21
  140.6 0.1 broadcast_in_dim.7
  140.8 0.1 collective-permute-start.22
  140.9 1.4 spread_own.1._
  142.3 1.4 collective-permute-done.22.got_ref.got_rest_ref
  143.7 1.6 %spread_got.1 = (f32[4,512,512]{2,1,0:T(8,128)}, f32[128,128]{1,0:T(8,128)}, f32[128,384]{1,0:T(8,128)}, f32[1,128]{1,0:T(1,128)}) custom-call(s32[1]{0:T(128)} %bitcast.7.mine_ref, bf16[1152,512]{1,0:T(8,128)(2,1)S(1)} %collective-permute-done.22.got_ref.got_rest_ref, ...), custom_call_target="tpu_custom_call", output_to_operand_aliasing={{0}: (6, {})} | custom-call | tf_op jit(solution)/shard_map/spread_got/pallas_call | solution.py:427
  (44 shorter events, 0.5 us)
Async XLA Ops:
  1.8 29.8 %collective-permute-start.1 = (bf16[2,12,4,24,128]{4,3,2,1,0:T(8,128)(2,1)S(1)}, bf16[2,12,4,24,128]{4,3,2,1,0:T(8,128)(2,1)S(1)}, u32[]{:S(2)}, u32[]{:S(2)}) collective-permute-start(bf16[2,12,4,24,128]{4,3,2,1,0:T(8,128)(2,1)S(1)} %pad_maximum_fusion.1), channel_id=1, source_target_pairs={{0,7},{1,0},{2,1},{3,2},{4,3},{5,4},{6,5},{7,6},{8,15},{9,8},{10,9... | collective-permute-start | bytes 1769480 | tf_op jit(solution)/shard_map/ppermute | solution.py:457
  10.3 21.3 %collective-permute-start = (bf16[2,4,12,24,128]{4,3,2,1,0:T(8,128)(2,1)S(1)}, bf16[2,4,12,24,128]{4,3,2,1,0:T(8,128)(2,1)S(1)}, u32[]{:S(2)}, u32[]{:S(2)}) collective-permute-start(bf16[2,4,12,24,128]{4,3,2,1,0:T(8,128)(2,1)S(1)} %pad_maximum_fusion), channel_id=1, source_target_pairs={{0,120},{8,0},{16,8},{24,16},{32,24},{40,32},{48,40},{56,48},{64,5... | collective-permute-start | bytes 1769480 | tf_op jit(solution)/shard_map/ppermute | solution.py:455
  12.3 19.3 %collective-permute-start.2 = (bf16[2,4,4,24,128]{4,3,2,1,0:T(8,128)(2,1)S(1)}, bf16[2,4,4,24,128]{4,3,2,1,0:T(8,128)(2,1)S(1)}, u32[]{:S(2)}, u32[]{:S(2)}) collective-permute-start(bf16[2,4,4,24,128]{4,3,2,1,0:T(8,128)(2,1)S(1)} %pad_maximum_fusion.2), channel_id=1, source_target_pairs={{0,127},{1,120},{2,121},{3,122},{4,123},{5,124},{6,125},{7,126},{8... | collective-permute-start | bytes 589832 | tf_op jit(solution)/shard_map/ppermute | solution.py:459
  31.6 0.7 copy-start.5
  31.6 0.9 copy-start.2
  31.6 1.0 copy-start.3
  75.8 3.1 %collective-permute-start.3 = (bf16[1152,512]{1,0:T(8,128)(2,1)}, bf16[1152,512]{1,0:T(8,128)(2,1)S(1)}, u32[]{:S(2)}, u32[]{:S(2)}) collective-permute-start(bf16[1152,512]{1,0:T(8,128)(2,1)} %get-tuple-element.47), channel_id=1, source_target_pairs={{0,8},{1,9},{2,10},{3,11},{4,12},{5,13},{6,14},{7,15},{8,0},{9,1},... | collective-permute-start | bytes 3538952 | tf_op jit(solution)/shard_map/ppermute | solution.py:485
  80.7 10.8 %collective-permute-start.4 = (bf16[288,512]{1,0:T(8,128)(2,1)S(1)}, bf16[288,512]{1,0:T(8,128)(2,1)S(1)}, u32[]{:S(2)}, u32[]{:S(2)}) collective-permute-start(bf16[288,512]{1,0:T(8,128)(2,1)S(1)} %get-tuple-element.83), channel_id=1, source_target_pairs={{0,32},{1,33},{2,34},{3,35},{4,36},{5,37},{6,38},{7,39},{8,10},{9,... | collective-permute-start | bytes 884744 | tf_op jit(solution)/shard_map/ppermute | solution.py:485
  80.8 10.7 %collective-permute-start.5 = (bf16[288,512]{1,0:T(8,128)(2,1)S(1)}, bf16[288,512]{1,0:T(8,128)(2,1)S(1)}, u32[]{:S(2)}, u32[]{:S(2)}) collective-permute-start(bf16[288,512]{1,0:T(8,128)(2,1)S(1)} %get-tuple-element.82), channel_id=1, source_target_pairs={{0,16},{1,17},{2,18},{3,19},{4,20},{5,21},{6,22},{7,23},{8,9},{9,1... | collective-permute-start | bytes 884744 | tf_op jit(solution)/shard_map/ppermute | solution.py:485
  82.0 9.5 %collective-permute-start.6 = (bf16[288,512]{1,0:T(8,128)(2,1)S(1)}, bf16[288,512]{1,0:T(8,128)(2,1)S(1)}, u32[]{:S(2)}, u32[]{:S(2)}) collective-permute-start(bf16[288,512]{1,0:T(8,128)(2,1)S(1)} %get-tuple-element.81), channel_id=1, source_target_pairs={{0,48},{1,49},{2,50},{3,51},{4,52},{5,53},{6,54},{7,55},{8,11},{9,... | collective-permute-start | bytes 884744 | tf_op jit(solution)/shard_map/ppermute | solution.py:485
  91.4 18.7 %copy-start.4 = (bf16[12,4,24,128]{3,2,1,0:T(8,128)(2,1)S(1)}, bf16[12,4,24,128]{3,2,1,0:T(8,128)(2,1)}, u32[]{:S(2)}) copy-start(bf16[12,4,24,128]{3,2,1,0:T(8,128)(2,1)} %get-tuple-element.57) | copy-start | bytes 884740
  91.4 18.7 %copy-start.6 = (bf16[4,4,24,128]{3,2,1,0:T(8,128)(2,1)S(1)}, bf16[4,4,24,128]{3,2,1,0:T(8,128)(2,1)}, u32[]{:S(2)}) copy-start(bf16[4,4,24,128]{3,2,1,0:T(8,128)(2,1)} %get-tuple-element.58) | copy-start | bytes 294916
  91.7 4.8 %collective-permute-start.7 = (bf16[72,512]{1,0:T(8,128)(2,1)S(1)}, bf16[72,512]{1,0:T(8,128)(2,1)S(1)}, u32[]{:S(2)}, u32[]{:S(2)}) collective-permute-start(bf16[72,512]{1,0:T(8,128)(2,1)S(1)} %get-tuple-element.84), channel_id=1, source_target_pairs={{0,2},{1,3},{2,0},{3,1},{4,6},{5,7},{6,4},{7,5},{8,40},{9,41},{10,... | collective-permute-start | bytes 221192 | tf_op jit(solution)/shard_map/ppermute | solution.py:485
  92.2 5.1 %collective-permute-start.8 = (bf16[72,512]{1,0:T(8,128)(2,1)S(1)}, bf16[72,512]{1,0:T(8,128)(2,1)S(1)}, u32[]{:S(2)}, u32[]{:S(2)}) collective-permute-start(bf16[72,512]{1,0:T(8,128)(2,1)S(1)} %get-tuple-element.86), channel_id=1, source_target_pairs={{0,1},{1,2},{2,3},{3,0},{4,5},{5,6},{6,7},{7,4},{8,24},{9,25},{10,... | collective-permute-start | bytes 221192 | tf_op jit(solution)/shard_map/ppermute | solution.py:485
  95.4 3.5 %collective-permute-start.9 = (bf16[72,512]{1,0:T(8,128)(2,1)S(1)}, bf16[72,512]{1,0:T(8,128)(2,1)S(1)}, u32[]{:S(2)}, u32[]{:S(2)}) collective-permute-start(bf16[72,512]{1,0:T(8,128)(2,1)S(1)} %get-tuple-element.85), channel_id=1, source_target_pairs={{0,3},{1,0},{2,1},{3,2},{4,7},{5,4},{6,5},{7,6},{8,56},{9,57},{10,... | collective-permute-start | bytes 221192 | tf_op jit(solution)/shard_map/ppermute | solution.py:485
  98.9 11.2 %collective-permute-start.10 = (f32[72,512]{1,0:T(8,128)S(1)}, f32[72,512]{1,0:T(8,128)S(1)}, u32[]{:S(2)}, u32[]{:S(2)}) collective-permute-start(f32[72,512]{1,0:T(8,128)S(1)} %convert_add_fusion.2), channel_id=1, source_target_pairs={{0,4},{1,5},{2,6},{3,7},{4,0},{5,1},{6,2},{7,3},{8,12},{9,13},{10,... | collective-permute-start | bytes 442376 | tf_op jit(solution)/shard_map/ppermute | solution.py:485
  102.5 8.1 %collective-permute-start.11 = (f32[72,512]{1,0:T(8,128)S(1)}, f32[72,512]{1,0:T(8,128)S(1)}, u32[]{:S(2)}, u32[]{:S(2)}) collective-permute-start(f32[72,512]{1,0:T(8,128)S(1)} %convert_add_fusion.2), channel_id=1, source_target_pairs={{0,64},{1,65},{2,66},{3,67},{4,68},{5,69},{6,70},{7,71},{8,72},{9,... | collective-permute-start | bytes 442376 | tf_op jit(solution)/shard_map/ppermute | solution.py:485
  102.5 8.1 %collective-permute-start.12 = (f32[72,512]{1,0:T(8,128)S(1)}, f32[72,512]{1,0:T(8,128)S(1)}, u32[]{:S(2)}, u32[]{:S(2)}) collective-permute-start(f32[72,512]{1,0:T(8,128)S(1)} %convert_add_fusion.2), channel_id=1, source_target_pairs={{0,68},{1,69},{2,70},{3,71},{4,64},{5,65},{6,66},{7,67},{8,76},{9,... | collective-permute-start | bytes 442376 | tf_op jit(solution)/shard_map/ppermute | solution.py:485
  105.2 24.7 %collective-permute-start.16 = (bf16[4,12,24,128]{3,2,1,0:T(8,128)(2,1)}, bf16[4,12,24,128]{3,2,1,0:T(8,128)(2,1)S(1)}, u32[]{:S(2)}, u32[]{:S(2)}) collective-permute-start(bf16[4,12,24,128]{3,2,1,0:T(8,128)(2,1)} %get-tuple-element.56), channel_id=1, source_target_pairs={{0,8},{8,16},{16,24},{24,32},{32,40},{40,48},{48,56},{56,64},{64,7... | collective-permute-start | bytes 884744 | tf_op jit(solution)/shard_map/ppermute | solution.py:455
  110.1 19.7 %collective-permute-start.17 = (bf16[12,4,24,128]{3,2,1,0:T(8,128)(2,1)S(1)}, bf16[12,4,24,128]{3,2,1,0:T(8,128)(2,1)S(1)}, u32[]{:S(2)}, u32[]{:S(2)}) collective-permute-start(bf16[12,4,24,128]{3,2,1,0:T(8,128)(2,1)S(1)} %copy-done.4), channel_id=1, source_target_pairs={{0,1},{1,2},{2,3},{3,4},{4,5},{5,6},{6,7},{7,0},{8,9},{9,10},{10,1... | collective-permute-start | bytes 884744 | tf_op jit(solution)/shard_map/ppermute | solution.py:457
  110.1 16.5 %collective-permute-start.18 = (bf16[4,4,24,128]{3,2,1,0:T(8,128)(2,1)S(1)}, bf16[4,4,24,128]{3,2,1,0:T(8,128)(2,1)S(1)}, u32[]{:S(2)}, u32[]{:S(2)}) collective-permute-start(bf16[4,4,24,128]{3,2,1,0:T(8,128)(2,1)S(1)} %copy-done.6), channel_id=1, source_target_pairs={{0,9},{1,10},{2,11},{3,12},{4,13},{5,14},{6,15},{7,8},{8,17},{9,18... | collective-permute-start | bytes 294920 | tf_op jit(solution)/shard_map/ppermute | solution.py:459
  110.7 15.9 %collective-permute-start.13 = (bf16[72,512]{1,0:T(8,128)(2,1)S(1)}, bf16[72,512]{1,0:T(8,128)(2,1)S(1)}, u32[]{:S(2)}, u32[]{:S(2)}) collective-permute-start(bf16[72,512]{1,0:T(8,128)(2,1)S(1)} %add_convert_fusion), channel_id=1, source_target_pairs={{0,1},{1,2},{2,3},{3,0},{4,5},{5,6},{6,7},{7,4},{8,24},{9,25},{10,... | collective-permute-start | bytes 221192 | tf_op jit(solution)/shard_map/ppermute | solution.py:485
  110.9 15.7 %collective-permute-start.14 = (bf16[72,512]{1,0:T(8,128)(2,1)S(1)}, bf16[72,512]{1,0:T(8,128)(2,1)S(1)}, u32[]{:S(2)}, u32[]{:S(2)}) collective-permute-start(bf16[72,512]{1,0:T(8,128)(2,1)S(1)} %add_convert_fusion), channel_id=1, source_target_pairs={{0,2},{1,3},{2,0},{3,1},{4,6},{5,7},{6,4},{7,5},{8,40},{9,41},{10,... | collective-permute-start | bytes 221192 | tf_op jit(solution)/shard_map/ppermute | solution.py:485
  126.6 3.2 %collective-permute-start.15 = (bf16[72,512]{1,0:T(8,128)(2,1)S(1)}, bf16[72,512]{1,0:T(8,128)(2,1)S(1)}, u32[]{:S(2)}, u32[]{:S(2)}) collective-permute-start(bf16[72,512]{1,0:T(8,128)(2,1)S(1)} %add_convert_fusion), channel_id=1, source_target_pairs={{0,3},{1,0},{2,1},{3,2},{4,7},{5,4},{6,5},{7,6},{8,56},{9,57},{10,... | collective-permute-start | bytes 221192 | tf_op jit(solution)/shard_map/ppermute | solution.py:485
  130.0 10.0 %collective-permute-start.19 = (bf16[288,512]{1,0:T(8,128)(2,1)S(1)}, bf16[288,512]{1,0:T(8,128)(2,1)S(1)}, u32[]{:S(2)}, u32[]{:S(2)}) collective-permute-start(bf16[288,512]{1,0:T(8,128)(2,1)S(1)} %constant_dynamic-update-slice_fusion.7), channel_id=1, source_target_pairs={{0,16},{1,17},{2,18},{3,19},{4,20},{5,21},{6,22},{7,23},{8,9},{9,1... | collective-permute-start | bytes 884744 | tf_op jit(solution)/shard_map/ppermute | solution.py:485
  130.0 9.9 %collective-permute-start.20 = (bf16[288,512]{1,0:T(8,128)(2,1)S(1)}, bf16[288,512]{1,0:T(8,128)(2,1)S(1)}, u32[]{:S(2)}, u32[]{:S(2)}) collective-permute-start(bf16[288,512]{1,0:T(8,128)(2,1)S(1)} %constant_dynamic-update-slice_fusion.7), channel_id=1, source_target_pairs={{0,32},{1,33},{2,34},{3,35},{4,36},{5,37},{6,38},{7,39},{8,10},{9,... | collective-permute-start | bytes 884744 | tf_op jit(solution)/shard_map/ppermute | solution.py:485
  130.1 10.5 %collective-permute-start.21 = (bf16[288,512]{1,0:T(8,128)(2,1)S(1)}, bf16[288,512]{1,0:T(8,128)(2,1)S(1)}, u32[]{:S(2)}, u32[]{:S(2)}) collective-permute-start(bf16[288,512]{1,0:T(8,128)(2,1)S(1)} %constant_dynamic-update-slice_fusion.7), channel_id=1, source_target_pairs={{0,48},{1,49},{2,50},{3,51},{4,52},{5,53},{6,54},{7,55},{8,11},{9,... | collective-permute-start | bytes 884744 | tf_op jit(solution)/shard_map/ppermute | solution.py:485
  140.8 2.9 %collective-permute-start.22 = (bf16[1152,512]{1,0:T(8,128)(2,1)S(1)}, bf16[1152,512]{1,0:T(8,128)(2,1)S(1)}, u32[]{:S(2)}, u32[]{:S(2)}) collective-permute-start(bf16[1152,512]{1,0:T(8,128)(2,1)S(1)} %constant_dynamic-update-slice_fusion.own_ref.own_rest_ref), channel_id=1, source_target_pairs={{0,8},{1,9},{2,10},{3,11},{4,12},{5,13},{6,14},{7,15},{8,0},{9,1},... | collective-permute-start | bytes 3538952 | tf_op jit(solution)/shard_map/ppermute | solution.py:485
  140.9 2.8 %copy-start = (bf16[128,384]{1,0:T(8,128)(2,1)S(1)}, bf16[128,384]{1,0:T(8,128)(2,1)}, u32[]{:S(2)}) copy-start(bf16[128,384]{1,0:T(8,128)(2,1)} %w_ref.1) | copy-start | bytes 294916
  140.9 2.8 %copy-start.1 = (f32[128]{0:T(128)S(1)}, f32[128]{0:T(128)}, u32[]{:S(2)}) copy-start(f32[128]{0:T(128)} %param.8) | copy-start | bytes 1540
